TPU v7x, 32 devices: a whole 2x2x4 slice. The times are simulated.
32 devices in a mesh: dev: 8 (over z, x), ha: 2 (over y), wa: 2 (over core).
Axes of the slice: x: 2, y: 2, z: 4, core: 2. Of those that a mesh axis runs over, the one named last changes fastest.
Arguments:
- tokens: bfloat16 [2352, 768], P(('dev', 'ha'), 'wa'), may hold values from -6 to 6
- cotangent: bfloat16 [2352, 768], P(('dev', 'ha'), 'wa'), may hold values from -6 to 6
- conv_taps: float32 [2, 9, 768], P(None, None, 'wa'), may hold values from -2 to 2
- norm_gain: float32 [4, 768], P(None, 'wa'), may hold values from 0.1 to 1.9
- norm_shift: float32 [4, 768], P(None, 'wa'), may hold values from -2 to 2
- w_qkv: bfloat16 [2, 768, 3, 768], P(None, 'wa', None, 'ha'), may hold values from -0.21875 to 0.21875
- w_proj: bfloat16 [2, 768, 768], P(None, 'ha', 'wa'), may hold values from -0.625 to 0.625
- w_up: bfloat16 [2, 768, 3072], P(None, 'wa', 'ha'), may hold values from -0.21875 to 0.21875
- w_down: bfloat16 [2, 3072, 768], P(None, 'ha', 'wa'), may hold values from -0.109375 to 0.109375
- valid: int32 [48, 49], P('dev'), may hold values from 0 to 1, as said below
Outputs:
- output: float32 [2352, 768], P(('dev', 'ha'), 'wa')
- grad_tokens: float32 [2352, 768], P(('dev', 'ha'), 'wa')
- grad_taps: float32 [2, 9, 768], P(None, None, 'wa')
- grad_gain: float32 [4, 768], P(None, 'wa')
- grad_shift: float32 [4, 768], P(None, 'wa')
- grad_qkv: float32 [2, 768, 3, 768], P(None, 'wa', None, ('ha', 'dev'))
- grad_proj: float32 [2, 768, 768], P(None, 'ha', ('wa', 'dev'))
- grad_up: float32 [2, 768, 3072], P(None, 'wa', ('ha', 'dev'))
- grad_down: float32 [2, 3072, 768], P(None, 'ha', ('wa', 'dev'))
Inputs may be any that keep to these rules, and one draw needn't show every extreme that they name: For each image the patches with valid = 1 form the top-left rectangle of its 7 x 7 grid, of height and width each from 3 to 7.
All inputs are finite; a program needn't handle non-finite values.
Results may differ from a plain program's by a relative error of at most 0.02.
Values may be sent and summed in bfloat16 or wider, within the bound.
No kernel may reach another device: no remote copies, remote signals or barrier semaphores. Data moves between devices by JAX's collectives and lax.ppermute only.
A program may use at most 128 MiB of HBM per device.

v0:
```python
from functools import partial

import jax
import jax.numpy as jnp
from jax import lax
from jax.sharding import PartitionSpec as P

WIN = 7
HEAD_DIM = 32
PATCHES = 49


EPS = 1e-05


def contract(left_mat, right_mat, left_dim, right_dim):
    return lax.dot_general(
        left_mat,
        right_mat,
        (((left_dim,), (right_dim,)), ((), ())),
        preferred_element_type=jnp.float32,
    )


def width_sums(first_arr, second_arr):
    return lax.psum((jnp.sum(first_arr, axis=1), jnp.sum(second_arr, axis=1)), "wa")


def head_rows(values):
    return lax.all_gather(values, "ha", axis=0, tiled=True)


def width_rows(values):
    return lax.all_gather(values, "wa", axis=0, tiled=True)


def over_width(left_mat, right_mat, right_dim):
    return lax.psum_scatter(
        contract(left_mat, right_mat, 1, right_dim), "wa", scatter_dimension=0, tiled=True
    )


def over_heads(left_mat, right_mat, right_dim):
    return lax.psum_scatter(
        contract(left_mat, right_mat, 1, right_dim), "ha", scatter_dimension=0, tiled=True
    )


def normalize(stream, gain, shift):
    width = stream.shape[1] * lax.axis_size("wa")
    totals, squares = width_sums(stream, stream * stream)
    center = totals / width
    inv_std = lax.rsqrt(squares / width - center * center + EPS)
    unit_rows = (stream - center[:, None]) * inv_std[:, None]
    return (unit_rows, inv_std, (unit_rows * gain + shift).astype(jnp.bfloat16))


def norm_back(upstream, unit_rows, inv_std, gain):
    width = upstream.shape[1] * lax.axis_size("wa")
    scaled = upstream * gain
    totals, projected = width_sums(scaled, scaled * unit_rows)
    grad_stream = inv_std[:, None] * (
        scaled - (totals / width)[:, None] - unit_rows * (projected / width)[:, None]
    )
    return (grad_stream, jnp.sum(upstream * unit_rows, axis=0), jnp.sum(upstream, axis=0))


def conv_embed(stream, taps):
    images = stream.reshape(-1, WIN, WIN, stream.shape[1])
    padded = jnp.pad(images, ((0, 0), (1, 1), (1, 1), (0, 0)))
    result = images
    for tap_row in range(3):
        for tap_col in range(3):
            result = (
                result
                + padded[:, tap_row : tap_row + WIN, tap_col : tap_col + WIN, :]
                * taps[tap_row * 3 + tap_col]
            )
    return result.reshape(stream.shape)


def conv_back(upstream, stream, taps):
    images = stream.reshape(-1, WIN, WIN, stream.shape[1])
    grads = upstream.reshape(images.shape)
    padded = jnp.pad(images, ((0, 0), (1, 1), (1, 1), (0, 0)))
    padded_grad = jnp.pad(grads, ((0, 0), (1, 1), (1, 1), (0, 0)))
    grad_stream = grads
    tap_grads = []
    for tap_row in range(3):
        for tap_col in range(3):
            tap_index = tap_row * 3 + tap_col
            shifted = padded[:, tap_row : tap_row + WIN, tap_col : tap_col + WIN, :]
            tap_grads.append(jnp.sum(grads * shifted, axis=(0, 1, 2)))
            grad_stream = (
                grad_stream
                + padded_grad[
                    :, 2 - tap_row : 2 - tap_row + WIN, 2 - tap_col : 2 - tap_col + WIN, :
                ]
                * taps[tap_index]
            )
    return (grad_stream.reshape(upstream.shape), jnp.stack(tap_grads))


def split_heads(packed):
    row_total = packed.shape[0]
    local_width = packed.shape[1] // 3
    parts = packed.reshape(row_total // PATCHES, PATCHES, 3, local_width // HEAD_DIM, HEAD_DIM)
    return (parts[:, :, 0], parts[:, :, 1], parts[:, :, 2])


def window_forward(pre_act):
    packed = pre_act.astype(jnp.bfloat16)
    queries, key_rows, value_rows = split_heads(packed)
    scaling = HEAD_DIM ** (-0.5)
    scores = (
        jnp.einsum("iqhd,ikhd->ihqk", queries, key_rows, preferred_element_type=jnp.float32)
        * scaling
    )
    attn_probs = jax.nn.softmax(scores, axis=-1)
    rounded = attn_probs.astype(jnp.bfloat16)
    mixed = jnp.einsum("ihqk,ikhd->iqhd", rounded, value_rows, preferred_element_type=jnp.float32)
    return (mixed.reshape(pre_act.shape[0], -1), (packed, attn_probs, rounded))


def window_backward(stored, upstream):
    packed, attn_probs, rounded = stored
    queries, key_rows, value_rows = split_heads(packed)
    scaling = HEAD_DIM ** (-0.5)
    grad_mixed = upstream.reshape(queries.shape)
    grad_probs = jnp.einsum(
        "iqhd,ikhd->ihqk", grad_mixed, value_rows, preferred_element_type=jnp.float32
    )
    grad_values = jnp.einsum(
        "ihqk,iqhd->ikhd", rounded, grad_mixed, preferred_element_type=jnp.float32
    )
    grad_scores = (
        attn_probs * (grad_probs - jnp.sum(grad_probs * attn_probs, axis=-1, keepdims=True))
    ).astype(jnp.bfloat16)
    grad_queries = (
        jnp.einsum("ihqk,ikhd->iqhd", grad_scores, key_rows, preferred_element_type=jnp.float32)
        * scaling
    )
    grad_keys = (
        jnp.einsum("ihqk,iqhd->ikhd", grad_scores, queries, preferred_element_type=jnp.float32)
        * scaling
    )
    return jnp.stack([grad_queries, grad_keys, grad_values], axis=2).reshape(packed.shape)


def channel_forward(pre_act, mask):
    packed = pre_act.astype(jnp.bfloat16)
    queries, key_rows, value_rows = split_heads(packed)
    scaling = HEAD_DIM ** (-0.5)
    masked = queries * mask[:, :, None, None]
    scores = (
        jnp.einsum("ingc,ingd->igcd", masked, key_rows, preferred_element_type=jnp.float32)
        * scaling
    )
    attn_probs = jax.nn.softmax(scores, axis=-1)
    rounded = attn_probs.astype(jnp.bfloat16)
    mixed = jnp.einsum("ingd,igcd->ingc", value_rows, rounded, preferred_element_type=jnp.float32)
    return (mixed.reshape(pre_act.shape[0], -1), (packed, attn_probs, rounded))


def channel_backward(stored, upstream, mask):
    packed, attn_probs, rounded = stored
    queries, key_rows, value_rows = split_heads(packed)
    scaling = HEAD_DIM ** (-0.5)
    masked = queries * mask[:, :, None, None]
    grad_mixed = upstream.reshape(queries.shape)
    grad_probs = jnp.einsum(
        "ingc,ingd->igcd", grad_mixed, value_rows, preferred_element_type=jnp.float32
    )
    grad_values = jnp.einsum(
        "ingc,igcd->ingd", grad_mixed, rounded, preferred_element_type=jnp.float32
    )
    grad_scores = (
        attn_probs * (grad_probs - jnp.sum(grad_probs * attn_probs, axis=-1, keepdims=True))
    ).astype(jnp.bfloat16)
    grad_queries = (
        jnp.einsum("igcd,ingd->ingc", grad_scores, key_rows, preferred_element_type=jnp.float32)
        * scaling
        * mask[:, :, None, None]
    )
    grad_keys = (
        jnp.einsum("igcd,ingc->ingd", grad_scores, masked, preferred_element_type=jnp.float32)
        * scaling
    )
    return jnp.stack([grad_queries, grad_keys, grad_values], axis=2).reshape(packed.shape)


def gelu_exact(values):
    return jax.nn.gelu(values, approximate=False)


def mlp_forward(pre_act):
    return (gelu_exact(pre_act), pre_act)


def mlp_backward(stored, upstream):
    unused_out, pull = jax.vjp(gelu_exact, stored)
    return pull(upstream.astype(jnp.float32))[0]


def branch_forward(stream, gain, shift, w_in, w_out, inner_forward):
    unit_rows, inv_std, normed = normalize(stream, gain, shift)
    normed_all = head_rows(normed)
    post_act, inner_saved = inner_forward(over_width(normed_all, w_in, 0))
    post_low = post_act.astype(jnp.bfloat16)
    post_all = width_rows(post_low)
    branch_out = over_heads(post_all, w_out, 0)
    kept_mats = (normed_all, post_all, w_in, w_out)
    return (stream + branch_out, (unit_rows, inv_std, kept_mats, inner_saved))


def branch_backward(gradient, gain, cached, inner_backward):
    unit_rows, inv_std, kept_mats, inner_saved = cached
    grad_all = head_rows(gradient.astype(jnp.bfloat16))
    normed_all, post_all, w_in, w_out = kept_mats
    grad_w_out = contract(post_all, grad_all, 0, 0)
    grad_post = over_width(grad_all, w_out, 1)
    grad_pre = inner_backward(inner_saved, grad_post.astype(jnp.bfloat16)).astype(jnp.bfloat16)
    grad_pre_all = width_rows(grad_pre)
    grad_w_in = contract(normed_all, grad_pre_all, 0, 0)
    grad_normed = over_heads(grad_pre_all, w_in, 1)
    grad_stream, grad_gain, grad_shift = norm_back(grad_normed, unit_rows, inv_std, gain)
    return (gradient + grad_stream, grad_w_in, grad_w_out, grad_gain, grad_shift)


def on_device(
    tokens, cotangent, conv_taps, norm_gain, norm_shift, w_qkv, w_proj, w_up, w_down, valid
):
    image_share = valid.shape[0] // lax.axis_size("wa")
    mask = lax.dynamic_slice_in_dim(
        valid, lax.axis_index("wa") * image_share, image_share, 0
    ).astype(jnp.bfloat16)
    width_half = w_qkv.shape[1]
    head_width = w_qkv.shape[3]
    qkv_flat = [
        w_qkv[section_index].reshape(width_half, 3 * head_width) for section_index in range(2)
    ]
    channel_fwd = partial(channel_forward, mask=mask)
    channel_bwd = partial(channel_backward, mask=mask)
    stream_zero = tokens.astype(jnp.float32)
    stream_one = conv_embed(stream_zero, conv_taps[0])
    stream_two, cached_one = branch_forward(
        stream_one, norm_gain[0], norm_shift[0], qkv_flat[0], w_proj[0], window_forward
    )
    stream_three, cached_two = branch_forward(
        stream_two, norm_gain[1], norm_shift[1], w_up[0], w_down[0], mlp_forward
    )
    stream_four = conv_embed(stream_three, conv_taps[1])
    stream_five, cached_three = branch_forward(
        stream_four, norm_gain[2], norm_shift[2], qkv_flat[1], w_proj[1], channel_fwd
    )
    stream_six, cached_four = branch_forward(
        stream_five, norm_gain[3], norm_shift[3], w_up[1], w_down[1], mlp_forward
    )
    gradient = cotangent.astype(jnp.float32)
    gradient, up_grad_one, down_grad_one, gain_three, shift_three = branch_backward(
        gradient, norm_gain[3], cached_four, mlp_backward
    )
    gradient, qkv_grad_one, proj_grad_one, gain_two, shift_two = branch_backward(
        gradient, norm_gain[2], cached_three, channel_bwd
    )
    gradient, taps_one = conv_back(gradient, stream_three, conv_taps[1])
    gradient, up_grad_zero, down_grad_zero, gain_one, shift_one = branch_backward(
        gradient, norm_gain[1], cached_two, mlp_backward
    )
    gradient, qkv_grad_zero, proj_grad_zero, gain_zero, shift_zero = branch_backward(
        gradient, norm_gain[0], cached_one, window_backward
    )
    gradient, taps_zero = conv_back(gradient, stream_zero, conv_taps[0])
    grad_taps, grad_gain, grad_shift = lax.psum(
        (
            jnp.stack([taps_zero, taps_one]),
            jnp.stack([gain_zero, gain_one, gain_two, gain_three]),
            jnp.stack([shift_zero, shift_one, shift_two, shift_three]),
        ),
        ("dev", "ha"),
    )
    qkv_local = jnp.stack([qkv_grad_zero, qkv_grad_one]).reshape(2, width_half, 3, head_width)
    proj_local = jnp.stack([proj_grad_zero, proj_grad_one])
    up_local = jnp.stack([up_grad_zero, up_grad_one])
    down_local = jnp.stack([down_grad_zero, down_grad_one])
    grad_qkv, grad_proj, grad_up, grad_down = (
        lax.psum_scatter(qkv_local, "dev", scatter_dimension=3, tiled=True),
        lax.psum_scatter(proj_local, "dev", scatter_dimension=2, tiled=True),
        lax.psum_scatter(up_local, "dev", scatter_dimension=2, tiled=True),
        lax.psum_scatter(down_local, "dev", scatter_dimension=2, tiled=True),
    )
    return (
        stream_six,
        gradient,
        grad_taps,
        grad_gain,
        grad_shift,
        grad_qkv,
        grad_proj,
        grad_up,
        grad_down,
    )


def solution(mesh):
    placed = (
        P(("dev", "ha"), "wa"),
        P(("dev", "ha"), "wa"),
        P(None, None, "wa"),
        P(None, "wa"),
        P(None, "wa"),
        P(None, "wa", None, "ha"),
        P(None, "ha", "wa"),
        P(None, "wa", "ha"),
        P(None, "ha", "wa"),
        P("dev", None),
    )
    return jax.shard_map(
        on_device,
        mesh=mesh,
        in_specs=placed,
        out_specs=(
            P(("dev", "ha"), "wa"),
            P(("dev", "ha"), "wa"),
            P(None, None, "wa"),
            P(None, "wa"),
            P(None, "wa"),
            P(None, "wa", None, ("ha", "dev")),
            P(None, "ha", ("wa", "dev")),
            P(None, "wa", ("ha", "dev")),
            P(None, "ha", ("wa", "dev")),
        ),
        check_vma=False,
    )
```

profile of v0, /device:TPU:0, one launch (start us, length us, event | category | flops | bytes accessed | tf_op | source)
XLA Modules:
  0.0 831.6 jit_solution(8307729382552010500)
XLA Ops:
  15.2 7.0 all-gather
  50.5 11.2 %fusion.1 = f32[160,384]{1,0:T(8,128)S(1)} fusion(f32[294,384]{1,0:T(8,128)S(1)} %fusion.95), kind=kCustom, calls=%all-reduce-scatter.1 | all-reduce-scatter fusion | flops 122881 | bytes 697856
  69.1 6.5 all-gather.2
  97.3 11.2 %fusion.3 = f32[160,384]{1,0:T(8,128)S(1)} fusion(f32[294,384]{1,0:T(8,128)S(1)} %fusion.36), kind=kCustom, calls=%all-reduce-scatter.3 | all-reduce-scatter fusion | flops 122881 | bytes 697856
  117.9 5.9 all-gather.4
  125.6 5.1 fusion.4
  133.1 5.5 all-gather.8
  152.3 10.0 %fusion.5 = f32[160,384]{1,0:T(8,128)S(1)} fusion(f32[294,384]{1,0:T(8,128)S(1)} %fusion.91), kind=kCustom, calls=%all-reduce-scatter.5 | all-reduce-scatter fusion | flops 122881 | bytes 697856
  174.5 6.1 all-gather.6
  184.9 7.9 fusion.173
  212.8 11.4 %fusion.9 = f32[160,384]{1,0:T(8,128)S(1)} fusion(f32[294,384]{1,0:T(8,128)S(1)} %fusion.30), kind=kCustom, calls=%all-reduce-scatter.9 | all-reduce-scatter fusion | flops 122881 | bytes 697856
  241.0 6.0 all-gather.10
  279.2 6.0 all-gather.11
  290.0 11.3 %fusion.11 = f32[160,384]{1,0:T(8,128)} fusion(f32[294,384]{1,0:T(8,128)} %fusion.190), kind=kCustom, calls=%all-reduce-scatter.11 | all-reduce-scatter fusion | flops 122881 | bytes 697856
  324.9 6.0 all-gather.12
  338.2 6.4 fusion.12
  351.8 8.3 %copy.112 = f32[2,1536,384]{1,0,2:T(2,128)} copy(f32[2,1536,384]{2,1,0:T(8,128)} %pad_maximum_fusion.1) | data formatting | bytes 9437184 | tf_op jit(solution)/shard_map/stack | solution.py:285
  369.5 11.7 %fusion.13 = f32[160,384]{1,0:T(8,128)S(1)} fusion(f32[294,384]{1,0:T(8,128)} %fusion.38), kind=kCustom, calls=%all-reduce-scatter.13 | all-reduce-scatter fusion | flops 122881 | bytes 697856
  387.8 8.2 copy.111
  400.0 5.9 all-gather.14
  434.8 15.3 %fusion.174 = (f32[160,384]{1,0:T(8,128)S(1)}, f32[160,384]{1,0:T(8,128)S(1)}) fusion(f32[294,384]{1,0:T(8,128)S(1)} %fusion.28, f32[294,384]{1,0:T(8,128)S(1)} %fusion.191), kind=kCustom, calls=%all-reduce-scatter.17 | all-reduce-scatter fusion | flops 245761 | bytes 1395200
  460.0 80.4 %all-reduce.39 = (f32[2,9,384]{2,1,0:T(8,128)S(1)}, f32[4,384]{1,0:T(4,128)}, f32[4,384]{1,0:T(4,128)}) all-reduce(f32[2,9,384]{2,1,0:T(8,128)S(1)} %pad_maximum_fusion.6, f32[4,384]{1,0:T(4,128)S(1)} %pad_maximum_fusion.7, f32[4,384]{1,0:T(4,128)S(1)} %pad_maximum_fusion.8), channel_id=1, replica_groups=mesh['dev'=8,'ha'=2,'wa'=2] {'dev','ha'}, use_global_device_ids=true, to_apply=%region_72.73 | all-reduce | flops 9984 | bytes 79872 | tf_op jit(solution)/shard_map/psum | solution.py:274
  542.8 199.4 %all-reduce.53.cloned.1.call-done = (f32[2,384,384]{1,0,2:T(2,128)}, f32[2,384,1536]{1,0,2:T(2,128)}, f32[2,1536,384]{1,0,2:T(2,128)}) async-done(((f32[2,384,384]{1,0,2:T(2,128)}, f32[2,384,1536]{1,0,2:T(2,128)}, f32[2,1536,384]{1,0,2:T(2,128)}), (f32[2,384,384]{1,0,2:T(2,128)}, f32[2,384,1536]{1,0,2:T(2,128)}, f32[2,1536,384]{1,0,2:T(2,128)})) %all-reduce.53.cloned.1.call-update) | async-done | bytes 10616848
  747.9 76.4 %reduce-scatter.34.cloned.1.call-done = f32[2,384,3,48]{1,3,2,0:T(8,128)} async-done(((f32[2,384,3,384]{1,3,2,0:T(8,128)}), f32[2,384,3,48]{1,3,2,0:T(8,128)}) %reduce-scatter.34.cloned.1.call-update) | async-done | bytes 442384 | tf_op jit(solution)/shard_map/reduce_scatter | solution.py:287
  (513 shorter events, 282.2 us)
Async XLA Ops:
  7.2 734.9 %all-reduce.53.cloned.1.call-start = ((), (), s32[]{:S(2)}) async-start(), calls=%async_computation.2 | async-start | bytes 21233664
  10.4 55.3 %copy-start.9 = (f32[147,384]{1,0:T(8,128)}, f32[147,384]{1,0:T(8,128)S(1)}, u32[]{:S(2)}) copy-start(f32[147,384]{1,0:T(8,128)S(1)} %reshape.155) | copy-start | bytes 677380
  34.0 3.5 collective-permute-start
  50.1 25.4 %copy-start.31 = (bf16[294,384]{1,0:T(8,128)(2,1)}, bf16[294,384]{1,0:T(8,128)(2,1)S(1)}, u32[]{:S(2)}) copy-start(bf16[294,384]{1,0:T(8,128)(2,1)S(1)} %reshape.169) | copy-start | bytes 677380
  61.7 3.7 collective-permute-start.1
  65.9 48.6 %copy-start.11 = (f32[147,384]{1,0:T(8,128)}, f32[147,384]{1,0:T(8,128)S(1)}, u32[]{:S(2)}) copy-start(f32[147,384]{1,0:T(8,128)S(1)} %get-tuple-element.148) | copy-start | bytes 677380
  82.9 3.4 collective-permute-start.2
  108.6 5.5 collective-permute-start.3
  115.3 55.5 %copy-start.8 = (f32[147,384]{1,0:T(8,128)}, f32[147,384]{1,0:T(8,128)S(1)}, u32[]{:S(2)}) copy-start(f32[147,384]{1,0:T(8,128)S(1)} %reshape.158) | copy-start | bytes 677380
  130.8 7.9 collective-permute-start.4
  138.6 27.9 %copy-start.38 = (bf16[294,384]{1,0:T(8,128)(2,1)}, bf16[294,384]{1,0:T(8,128)(2,1)S(1)}, u32[]{:S(2)}) copy-start(bf16[294,384]{1,0:T(8,128)(2,1)S(1)} %reshape.183) | copy-start | bytes 677380
  163.1 5.4 collective-permute-start.5
  193.7 9.4 %collective-permute-start.6 = (f32[5,1536]{1,0:T(8,128)S(1)}, f32[5,1536]{1,0:T(8,128)S(1)}, u32[]{:S(2)}, u32[]{:S(2)}) collective-permute-start(f32[5,1536]{1,0:T(8,128)S(1)} %slice.390), channel_id=1, source_target_pairs={{0,1},{2,3},{4,5},{6,7},{8,9},{10,11},{12,13},{14,15},{16,17},{18,... | collective-permute-start | bytes 92168
  196.6 2.1 collective-permute-start.8
  224.9 8.0 collective-permute-start.9
  256.3 5.8 collective-permute-start.10
  302.1 5.9 collective-permute-start.11
  345.3 14.7 %collective-permute-start.12 = (bf16[5,1536]{1,0:T(8,128)(2,1)S(1)}, bf16[5,1536]{1,0:T(8,128)(2,1)S(1)}, u32[]{:S(2)}, u32[]{:S(2)}) collective-permute-start(bf16[5,1536]{1,0:T(8,128)(2,1)S(1)} %slice.396), channel_id=1, source_target_pairs={{0,1},{2,3},{4,5},{6,7},{8,9},{10,11},{12,13},{14,15},{16,17},{18,... | collective-permute-start | bytes 46088
  381.2 14.8 %collective-permute-start.13 = (f32[13,384]{1,0:T(8,128)S(1)}, f32[13,384]{1,0:T(8,128)S(1)}, u32[]{:S(2)}, u32[]{:S(2)}) collective-permute-start(f32[13,384]{1,0:T(8,128)S(1)} %slice.397), channel_id=1, source_target_pairs={{0,2},{1,3},{4,6},{5,7},{8,10},{9,11},{12,14},{13,15},{16,18},{17,... | collective-permute-start | bytes 59912
  408.5 415.9 %reduce-scatter.34.cloned.1.call-start = ((), (), s32[]{:S(2)}) async-start(), calls=%async_computation.1 | async-start | bytes 3981312 | tf_op jit(solution)/shard_map/reduce_scatter | solution.py:287
  413.2 4.7 collective-permute-start.14
  450.1 5.6 collective-permute-start.15
  454.4 87.2 %collective-permute-start.7 = (f32[13,384]{1,0:T(8,128)S(1)}, f32[13,384]{1,0:T(8,128)S(1)}, u32[]{:S(2)}, u32[]{:S(2)}) collective-permute-start(f32[13,384]{1,0:T(8,128)S(1)} %slice.391), channel_id=1, source_target_pairs={{0,2},{1,3},{4,6},{5,7},{8,10},{9,11},{12,14},{13,15},{16,18},{17,... | collective-permute-start | bytes 59912
  458.9 83.1 %copy-start.7 = (f32[147,384]{1,0:T(8,128)S(1)}, f32[147,384]{1,0:T(8,128)}, u32[]{:S(2)}) copy-start(f32[147,384]{1,0:T(8,128)} %copy-done.6) | copy-start | bytes 677380
  (116 other events, 1102.1 us)
Sparse Core Ops, SparseCore 0:
  408.6 333.5 all-reduce.52
  746.3 77.9 reduce-scatter.33
where the time goes:
time: 843 us; the launch traced here: 832 us
  blocking collectives  290 us (34%)
  waiting for transfers between devices  277 us (33%)
  local copies, waits for them, and re-layouts  116 us (14%)
  matrix products  53.4 us (6%)
  other arithmetic  38.1 us (5%)
  starting transfers between devices  37.7 us (4%)
  between operations  20.2 us (2%)
    unnamed x19, waiting for transfers between devices  200 us
    unnamed x14, blocking collectives  118 us
    psum x1, blocking collectives, on_device(): lax.psum((jnp.stack([taps_zero, taps_one]), jnp.stack([gain_zero, gain_on...  80.4 us
    reduce_scatter x1, waiting for transfers between devices, on_device(): lax.psum_scatter(qkv_local, 'dev', scatter_dimension=3, tiled=True)  76.4 us
    unnamed x315, local copies, waits for them, and re-layouts  75 us
    all_gather x8, blocking collectives, head_rows(): return lax.all_gather(values, 'ha', axis=0, tiled=True)  49.1 us
    dot_general x24, matrix products, contract(): lax.dot_general(left_mat, right_mat, (((left_dim,), (right_dim,)), ((), (...  45.1 us
    unnamed x17, starting transfers between devices  37.6 us
  transfers between devices with their start and end apart: 18, of which 4 were waited for; matrix products, arithmetic and copies ran while one was open for 11% of the time, Pallas kernels for 0%

commit v1 on v0

v1 whole, which is shorter than its diff:
```python
from functools import partial

import jax
import jax.numpy as jnp
import numpy as np
from jax import lax
from jax.experimental import pallas as pl
from jax.experimental.pallas import tpu as pltpu
from jax.sharding import PartitionSpec as P

WIN = 7
GRID_COLS = 8
PATCHES = 49
PADDED = WIN * GRID_COLS
HEAD_DIM = 32
LANES = 128
HEADS_TILE = LANES // HEAD_DIM
EPS = 1e-05
NEG = -1e30
BF16 = jnp.bfloat16
F32 = jnp.float32
VMEM_LIMIT = 40 * 2**20


def mm(left, right, left_dim, right_dim):
    return lax.dot_general(
        left, right, (((left_dim,), (right_dim,)), ((), ())), preferred_element_type=F32
    )


def kernel_call(body, name, ins, outs, scratch=(), flops=0):
    specs, arrays = [], []
    for item in ins:
        if isinstance(item, tuple):
            array, section = item
            specs.append(
                pl.BlockSpec(
                    (None,) + array.shape[1:],
                    lambda step, section=section, rest=array.ndim - 1: (section,) + (0,) * rest,
                )
            )
        else:
            array = item
            if array.dtype == jnp.int32:
                specs.append(pl.BlockSpec(memory_space=pltpu.SMEM))
            else:
                specs.append(
                    pl.BlockSpec(array.shape, lambda step, rest=array.ndim: (0,) * rest)
                )
        arrays.append(array)
    moved = sum(int(np.prod(o.shape)) * o.dtype.itemsize for o in outs) + sum(
        int(np.prod(a.shape)) * a.dtype.itemsize for a in arrays
    )
    return pl.pallas_call(
        body,
        grid=(1,),
        in_specs=specs,
        out_specs=[pl.BlockSpec(o.shape, lambda step, rest=len(o.shape): (0,) * rest) for o in outs],
        out_shape=list(outs),
        scratch_shapes=list(scratch),
        compiler_params=pltpu.CompilerParams(vmem_limit_bytes=VMEM_LIMIT),
        cost_estimate=pl.CostEstimate(flops=flops, bytes_accessed=moved, transcendentals=0),
        name=name,
    )(*arrays)


def sds(shape, dtype=F32):
    return jax.ShapeDtypeStruct(shape, dtype)


def column_mask(rows):
    return (lax.broadcasted_iota(jnp.int32, (rows, 1), 0) % GRID_COLS) < WIN


def side_shifts(values):
    rows = values.shape[0]
    return (pltpu.roll(values, 1, 0), values, pltpu.roll(values, rows - 1, 0))


def as_grid(values):
    return values.reshape(-1, WIN, GRID_COLS, values.shape[-1])


def move_rows(values, step):
    grid = as_grid(values)
    zeros = jnp.zeros_like(grid[:, :1])
    if step > 0:
        moved = jnp.concatenate([zeros, grid[:, :-1]], axis=1)
    else:
        moved = jnp.concatenate([grid[:, 1:], zeros], axis=1)
    return moved.reshape(values.shape)


def conv_cols(values, taps, keep):
    shifted = side_shifts(values)
    line = [
        sum(shifted[col] * taps[3 * row + col] for col in range(3)) for row in range(3)
    ]
    total = values + line[1] + move_rows(line[0], 1) + move_rows(line[2], -1)
    return jnp.where(keep, total, 0.0)


def tap_sums(grads, values):
    shifted = side_shifts(values)
    grad_grid = as_grid(grads)
    sums = []
    for row in range(3):
        for col in range(3):
            moved = as_grid(shifted[col])
            if row == 0:
                prod = grad_grid[:, 1:] * moved[:, :-1]
            elif row == 1:
                prod = grad_grid * moved
            else:
                prod = grad_grid[:, :-1] * moved[:, 1:]
            flat = prod.reshape(-1, GRID_COLS, prod.shape[-1])
            sums.append(jnp.sum(jnp.sum(flat, axis=0), axis=0, keepdims=True))
    return sums


def norm_stats(stream):
    width = stream.shape[1]
    center = jnp.sum(stream, axis=1, keepdims=True) * (1.0 / width)
    moved = stream - center
    inv_std = lax.rsqrt(jnp.sum(moved * moved, axis=1, keepdims=True) * (1.0 / width) + EPS)
    return moved * inv_std, inv_std


def norm_back(upstream, units, inv_std, gain):
    width = upstream.shape[1]
    scaled = upstream * gain
    first = jnp.sum(scaled, axis=1, keepdims=True) * (1.0 / width)
    second = jnp.sum(scaled * units, axis=1, keepdims=True) * (1.0 / width)
    return inv_std * (scaled - first - units * second)


def gelu_parts(values):
    z = jnp.abs(values) * (0.5**0.5)
    t = 1.0 / (1.0 + 0.3275911 * z)
    bell = jnp.exp(-z * z)
    poly = t * (
        0.254829592
        + t * (-0.284496736 + t * (1.421413741 + t * (-1.453152027 + t * 1.061405429)))
    )
    tail = 0.5 * poly * bell
    return jnp.where(values < 0, tail, 1.0 - tail), bell * float(1.0 / np.sqrt(2.0 * np.pi))


def head_mask(index):
    return (lax.broadcasted_iota(jnp.int32, (1, LANES), 1) // HEAD_DIM) == index


def spread_heads(tile):
    return jnp.concatenate(
        [jnp.where(head_mask(j), tile, 0.0) for j in range(HEADS_TILE)], axis=0
    ).astype(BF16)


def gather_heads(stacked):
    rows = stacked.shape[0] // HEADS_TILE
    total = jnp.where(head_mask(0), stacked[:rows], 0.0)
    for j in range(1, HEADS_TILE):
        total = jnp.where(head_mask(j), stacked[j * rows : (j + 1) * rows], total)
    return total


def softmax_rows(scores):
    top = jnp.max(scores, axis=0, keepdims=True)
    weights = jnp.exp(scores - top)
    return weights / jnp.sum(weights, axis=0, keepdims=True)


SCALE = HEAD_DIM**-0.5


def window_tile(q, k, v):
    keys_ok = column_mask(PADDED)
    scores = mm(k.astype(BF16), spread_heads(q), 1, 1) * SCALE
    probs = softmax_rows(jnp.where(keys_ok, scores, NEG))
    return probs, gather_heads(mm(probs.astype(BF16), v.astype(BF16), 0, 0))


def window_tile_back(q, k, v, probs, grad):
    low = probs.astype(BF16)
    q_big, g_big = spread_heads(q), spread_heads(grad)
    grad_probs = mm(v.astype(BF16), g_big, 1, 1)
    grad_v = mm(low, g_big, 1, 0)
    grad_scores = (
        probs * (grad_probs - jnp.sum(grad_probs * probs, axis=0, keepdims=True))
    ).astype(BF16)
    grad_k = mm(grad_scores, q_big, 1, 0) * SCALE
    grad_q = gather_heads(mm(grad_scores, k.astype(BF16), 0, 0)) * SCALE
    return grad_q, grad_k, grad_v


def same_head():
    first = lax.broadcasted_iota(jnp.int32, (LANES, LANES), 0) // HEAD_DIM
    second = lax.broadcasted_iota(jnp.int32, (LANES, LANES), 1) // HEAD_DIM
    return first == second


def channel_tile(q, k, v, mask):
    scores = mm(k.astype(BF16), (q * mask).astype(BF16), 0, 0) * SCALE
    probs = softmax_rows(jnp.where(same_head(), scores, NEG))
    return probs, mm(v.astype(BF16), probs.astype(BF16), 1, 0)


def channel_tile_back(q, k, v, probs, grad, mask):
    low = probs.astype(BF16)
    grad_low = grad.astype(BF16)
    grad_probs = mm(v.astype(BF16), grad_low, 0, 0)
    grad_v = mm(grad_low, low, 1, 1)
    grad_scores = (
        probs * (grad_probs - jnp.sum(grad_probs * probs, axis=0, keepdims=True))
    ).astype(BF16)
    grad_q = mm(k.astype(BF16), grad_scores, 1, 0) * SCALE * mask
    grad_k = mm((q * mask).astype(BF16), grad_scores, 1, 1) * SCALE
    return grad_q, grad_k, grad_v


def solution(mesh):
    n_dev = mesh.shape["dev"]
    bits = n_dev.bit_length() - 1
    assert n_dev == 1 << bits and mesh.shape["ha"] == 2 and mesh.shape["wa"] == 2

    swap = [(0, 1), (1, 0)]
    pair = ("ha", "wa")
    near_in = [(0, 2), (3, 1), (1, 0), (2, 3)]
    near_out = [(2, 0), (1, 3), (0, 1), (3, 2)]
    cross = [(1, 2), (2, 1)]

    def over_ha(values):
        return lax.ppermute(values, "ha", swap)

    def over_wa(values):
        return lax.ppermute(values, "wa", swap)

    def over_dev(values, bit):
        return lax.ppermute(values, "dev", [(i, i ^ (1 << bit)) for i in range(n_dev)])

    def reverse_bits(value):
        return sum(((value >> b) & 1) << (bits - 1 - b) for b in range(bits))

    def on_device(
        tokens, cotangent, conv_taps, norm_gain, norm_shift, w_qkv, w_proj, w_up, w_down, valid
    ):
        rows_in, half = tokens.shape
        images = rows_in // PATCHES
        rows = images * PADDED
        width = 2 * half
        heads_width = w_qkv.shape[3]
        hidden = w_up.shape[2]
        tiles = heads_width // LANES
        dev, ha, wa = (lax.axis_index(name) for name in ("dev", "ha", "wa"))
        flag = (ha == wa).astype(jnp.int32).reshape(1)
        first_ha = (ha == 0).astype(jnp.int32).reshape(1)
        chunk_at = jnp.stack([reverse_bits(p) ^ dev for p in range(n_dev)]).astype(jnp.int32)

        place = np.zeros((rows, rows_in), np.float32)
        for image in range(images):
            for patch in range(PATCHES):
                place[
                    image * PADDED + (patch // WIN) * GRID_COLS + patch % WIN,
                    image * PATCHES + patch,
                ] = 1.0
        spread = jnp.asarray(place, BF16)
        compact = jnp.asarray(place.T, BF16)

        wq_own = jnp.transpose(w_qkv, (0, 2, 1, 3))
        small = jnp.concatenate(
            [conv_taps.reshape(18, half), norm_gain, norm_shift], axis=0
        )
        near_tokens = lax.ppermute(tokens, pair, near_in)
        cross_tokens = lax.ppermute(tokens, pair, cross)
        params = jnp.concatenate([small, over_wa(small)], axis=1)
        wq_oth, wp_oth = over_wa(wq_own), over_wa(w_proj)
        wu_oth, wd_oth = over_wa(w_up), over_wa(w_down)
        near_cot = lax.ppermute(cotangent, pair, near_in)
        cross_cot = lax.ppermute(cotangent, pair, cross)

        mask = lax.dynamic_slice_in_dim(valid, wa * images, images, 0).reshape(images, WIN, WIN)
        mask = jnp.pad(mask, ((0, 0), (0, 0), (0, GRID_COLS - WIN))).reshape(rows, 1).astype(F32)

        def row(ref, index):
            return ref[index : index + 1, :]

        def unpack(flag_ref, mine, near, far, spread_ref):
            same = flag_ref[0] == 1
            own = jnp.where(same, mine[...], near[...])
            oth = jnp.where(same, near[...], far[...])
            return mm(spread_ref[...], jnp.concatenate([own, oth], axis=1), 1, 0)

        def project_in(normed, own_ref, oth_ref):
            return mm(normed[:, :half], own_ref, 1, 0) + mm(normed[:, half:], oth_ref, 1, 0)

        def to_normed(stream, params_ref, branch):
            units, _ = norm_stats(stream)
            return (units * row(params_ref, 18 + branch) + row(params_ref, 22 + branch)).astype(
                BF16
            )

        def attention_part(window, normed, mask_ref, wq_a, wq_b, qkv_ref, probs_ref):
            packed = [project_in(normed, wq_a[part], wq_b[part]).astype(BF16) for part in range(3)]
            for part in range(3):
                qkv_ref[part] = packed[part]
            wide = [part.astype(F32) for part in packed]
            mixed = []
            for image in range(images):
                line = []
                for tile in range(tiles):
                    q, k, v = (
                        part[
                            image * PADDED : (image + 1) * PADDED,
                            tile * LANES : (tile + 1) * LANES,
                        ]
                        for part in wide
                    )
                    if window:
                        probs, out = window_tile(q, k, v)
                    else:
                        valid_rows = mask_ref[image * PADDED : (image + 1) * PADDED, :]
                        probs, out = channel_tile(q, k, v, valid_rows)
                    probs_ref[image * tiles + tile] = probs
                    line.append(out)
                mixed.append(jnp.concatenate(line, axis=1))
            return jnp.concatenate(mixed, axis=0).astype(BF16)

        def attention_part_back(window, grad_mixed, mask_ref, qkv_ref, probs_ref, dpk_ref):
            wide = [qkv_ref[part].astype(F32) for part in range(3)]
            grad = grad_mixed.astype(F32)
            found = [[], [], []]
            for image in range(images):
                lines = [[], [], []]
                for tile in range(tiles):
                    rows_at = slice(image * PADDED, (image + 1) * PADDED)
                    lanes_at = slice(tile * LANES, (tile + 1) * LANES)
                    q, k, v = (part[rows_at, lanes_at] for part in wide)
                    probs = probs_ref[image * tiles + tile]
                    if window:
                        parts = window_tile_back(q, k, v, probs, grad[rows_at, lanes_at])
                    else:
                        parts = channel_tile_back(
                            q, k, v, probs, grad[rows_at, lanes_at], mask_ref[rows_at, :]
                        )
                    for line, part in zip(lines, parts):
                        line.append(part)
                for part in range(3):
                    found[part].append(jnp.concatenate(lines[part], axis=1))
            packed = [jnp.concatenate(part, axis=0).astype(BF16) for part in found]
            for part in range(3):
                dpk_ref[part] = packed[part]
            return packed

        def put_both(own_ref, oth_ref, values):
            own_ref[...] = values[:, :half]
            oth_ref[...] = values[:, half:]

        def mul_out(left, own_ref, oth_ref, out_ref):
            out_ref[:, :half] = mm(left, own_ref[...], 1, 0).astype(BF16)
            out_ref[:, half:] = mm(left, oth_ref[...], 1, 0).astype(BF16)

        def both_nt(values, own_ref, oth_ref):
            return mm(values[:, :half], own_ref[...], 1, 1) + mm(
                values[:, half:], oth_ref[...], 1, 1
            )

        def conv_into(out_ref, values, taps_at, params_ref, keep):
            for col in range(0, width, LANES):
                taps = [params_ref[taps_at + t : taps_at + t + 1, col : col + LANES] for t in range(9)]
                out_ref[:, col : col + LANES] = conv_cols(values[:, col : col + LANES], taps, keep)

        def conv_back_into(out_ref, sums_ref, sums_at, grads, values, taps_at, params_ref, keep):
            for col in range(0, width, LANES):
                lanes_at = slice(col, col + LANES)
                taps = [
                    params_ref[taps_at + 8 - t : taps_at + 9 - t, lanes_at] for t in range(9)
                ]
                for t, total in enumerate(tap_sums(grads[:, lanes_at], values[:, lanes_at])):
                    sums_ref[sums_at + t : sums_at + t + 1, lanes_at] = total
                out_ref[:, lanes_at] = conv_cols(grads[:, lanes_at], taps, keep)

        probs_shape = {
            True: (images * tiles, PADDED, HEADS_TILE * PADDED),
            False: (images * tiles, LANES, LANES),
        }
        full, full_low = sds((rows, width)), sds((rows, width), BF16)
        half_low = sds((rows, half), BF16)
        hid_low = sds((rows, hidden), BF16)
        qkv_low = sds((3, rows, heads_width), BF16)
        mixed_low = sds((rows, heads_width), BF16)

        def first_body(
            flag_ref, mine, near, far, spread_ref, params_ref, wq_a, wq_b, wp_a, wp_b,
            x_ref, s_ref, n_own, n_oth, qkv_ref, probs_ref, mixed_ref, part_ref,
        ):
            keep = column_mask(rows)
            stream = unpack(flag_ref, mine, near, far, spread_ref)
            x_ref[...] = stream.astype(BF16)
            conv_into(s_ref, stream, 0, params_ref, keep)
            normed = to_normed(s_ref[...], params_ref, 0)
            put_both(n_own, n_oth, normed)
            mixed = attention_part(True, normed, None, wq_a, wq_b, qkv_ref, probs_ref)
            mixed_ref[...] = mixed
            mul_out(mixed, wp_a, wp_b, part_ref)

        attn_flops = 2 * rows * (4 * width * heads_width)
        mlp_flops = 2 * rows * (2 * width * hidden)
        (x0, s1, n0_own, n0_oth, qkv0, probs0, mixed0, part0) = kernel_call(
            first_body, "attn_a",
            [flag, tokens, near_tokens, cross_tokens, spread, params,
             (wq_own, 0), (wq_oth, 0), (w_proj, 0), (wp_oth, 0)],
            [full_low, full, half_low, half_low, qkv_low, sds(probs_shape[True]), mixed_low, full_low],
            flops=attn_flops,
        )
        far0 = over_ha(part0)

        def mlp_body(
            s_in, part_a, part_b, params_ref, wu_a, wu_b, wd_a, wd_b,
            s_ref, n_own, n_oth, hid_ref, slope_ref, part_ref,
        ):
            s_ref[...] = s_in[...] + part_a[...].astype(F32) + part_b[...].astype(F32)
            normed = to_normed(s_ref[...], params_ref, 1)
            put_both(n_own, n_oth, normed)
            pre = project_in(normed, wu_a[...], wu_b[...])
            below, bell = gelu_parts(pre)
            hid = (pre * below).astype(BF16)
            hid_ref[...] = hid
            slope_ref[...] = below + pre * bell
            mul_out(hid, wd_a, wd_b, part_ref)

        (s2, n1_own, n1_oth, hid1, slope1, part1) = kernel_call(
            mlp_body, "mlp_b",
            [s1, part0, far0, params, (w_up, 0), (wu_oth, 0), (w_down, 0), (wd_oth, 0)],
            [full, half_low, half_low, hid_low, sds((rows, hidden)), full_low],
            flops=mlp_flops,
        )
        far1 = over_ha(part1)

        def channel_body(
            s_in, part_a, part_b, params_ref, mask_ref, wq_a, wq_b, wp_a, wp_b,
            s_before, s_ref, n_own, n_oth, qkv_ref, probs_ref, mixed_ref, part_ref,
        ):
            keep = column_mask(rows)
            total = s_in[...] + part_a[...].astype(F32) + part_b[...].astype(F32)
            s_before[...] = jnp.where(keep, total, 0.0)
            conv_into(s_ref, s_before, 9, params_ref, keep)
            normed = to_normed(s_ref[...], params_ref, 2)
            put_both(n_own, n_oth, normed)
            mixed = attention_part(False, normed, mask_ref, wq_a, wq_b, qkv_ref, probs_ref)
            mixed_ref[...] = mixed
            mul_out(mixed, wp_a, wp_b, part_ref)

        (s3, s4, n2_own, n2_oth, qkv2, probs2, mixed2, part2) = kernel_call(
            channel_body, "attn_c",
            [s2, part1, far1, params, mask, (wq_own, 1), (wq_oth, 1), (w_proj, 1), (wp_oth, 1)],
            [full, full, half_low, half_low, qkv_low, sds(probs_shape[False]), mixed_low, full_low],
            flops=attn_flops,
        )
        far2 = over_ha(part2)

        def cot_body(flag_ref, mine, near, far, spread_ref, wd_a, wd_b, g_own, g_oth, dhid_ref):
            grad = unpack(flag_ref, mine, near, far, spread_ref).astype(BF16)
            put_both(g_own, g_oth, grad)
            dhid_ref[...] = both_nt(grad, wd_a, wd_b).astype(BF16)

        g3_own, g3_oth, dhid3 = kernel_call(
            cot_body, "cot_d",
            [flag, cotangent, near_cot, cross_cot, spread, (w_down, 1), (wd_oth, 1)],
            [half_low, half_low, hid_low],
            flops=mlp_flops // 2,
        )

        def last_body(
            s_in, part_a, part_b, params_ref, dhid_ref, wu_a, wu_b,
            s_ref, n_own, n_oth, hid_ref, dpre_ref, part_ref,
        ):
            s_ref[...] = s_in[...] + part_a[...].astype(F32) + part_b[...].astype(F32)
            normed = to_normed(s_ref[...], params_ref, 3)
            put_both(n_own, n_oth, normed)
            pre = project_in(normed, wu_a[...], wu_b[...])
            below, bell = gelu_parts(pre)
            hid_ref[...] = (pre * below).astype(BF16)
            dpre = (dhid_ref[...].astype(F32) * (below + pre * bell)).astype(BF16)
            dpre_ref[...] = dpre
            part_ref[:, :half] = mm(dpre, wu_a[...], 1, 1).astype(BF16)
            part_ref[:, half:] = mm(dpre, wu_b[...], 1, 1).astype(BF16)

        (s5, n3_own, n3_oth, hid3, dpre3, back3) = kernel_call(
            last_body, "mlp_d",
            [s4, part2, far2, params, dhid3, (w_up, 1), (wu_oth, 1)],
            [full, half_low, half_low, hid_low, hid_low, full_low],
            flops=mlp_flops,
        )
        far_back3 = over_ha(back3)

        def ship(flag_ref, total, compact_ref, kept, sent, crossed):
            packed = mm(compact_ref[...], total.astype(BF16), 1, 0).astype(BF16)
            own, oth = packed[:, :half], packed[:, half:]
            kept[...] = own
            sent[...] = jnp.where(flag_ref[0] == 1, oth, own)
            crossed[...] = oth

        shipped = [sds((rows_in, half), BF16)] * 3

        def join(flag_ref, kept, near, far, out_ref):
            mine = jnp.where(flag_ref[0] == 1, kept[...], far[...])
            out_ref[...] = near[...].astype(F32) + mine.astype(F32)

        def deliver(kept, sent, crossed, name):
            near = lax.ppermute(sent, pair, near_out)
            far = lax.ppermute(crossed, pair, cross)
            return kernel_call(join, name, [flag, kept, near, far], [sds((rows_in, half))])[0]

        def out_body(flag_ref, ha_ref, s_in, hid_ref, wd_a, wd_b, compact_ref, kept, sent, crossed):
            hid = hid_ref[...]
            base = jnp.where(ha_ref[0] == 1, s_in[...], 0.0)
            branch = jnp.concatenate(
                [mm(hid, wd_a[...], 1, 0), mm(hid, wd_b[...], 1, 0)], axis=1
            )
            ship(flag_ref, base + branch, compact_ref, kept, sent, crossed)

        output_parts = kernel_call(
            out_body, "out_d",
            [flag, first_ha, s5, hid3, (w_down, 1), (wd_oth, 1), compact],
            shipped, flops=mlp_flops // 2,
        )
        output = deliver(*output_parts, "join_out")

        def reduce_chunks(kept, sent):
            for bit in range(bits):
                received = over_dev(sent, bit)
                total = kept.astype(F32) + received.astype(F32)
                if bit == bits - 1:
                    return total[0]
                total = total.astype(BF16)
                cut = total.shape[0] // 2
                kept, sent = total[:cut], total[cut:]

        def scatter_chunks(scratch, chunk_ref, kept, sent):
            cut = n_dev // 2
            for position in range(n_dev):
                target = kept if position < cut else sent
                target[position % cut] = scratch[chunk_ref[position]].astype(BF16)

        up_rows, down_rows = hidden // n_dev, half // n_dev
        folds = hidden // half
        mlp_rows = up_rows + folds * down_rows

        def mlp_weights_body(
            chunk_ref, dpre_a, dpre_b, n_a, n_b, g_a, g_b, hid_a, hid_b, kept, sent, scratch
        ):
            up = mm(dpre_a[...], n_a[...], 0, 0) + mm(dpre_b[...], n_b[...], 0, 0)
            for chunk in range(n_dev):
                scratch[chunk, :up_rows, :] = up[chunk * up_rows : (chunk + 1) * up_rows]
            down = mm(g_a[...], hid_a[...], 0, 0) + mm(g_b[...], hid_b[...], 0, 0)
            for chunk in range(n_dev):
                for fold in range(folds):
                    at = up_rows + fold * down_rows
                    scratch[chunk, at : at + down_rows, :] = down[
                        chunk * down_rows : (chunk + 1) * down_rows,
                        fold * half : (fold + 1) * half,
                    ]
            scatter_chunks(scratch, chunk_ref, kept, sent)

        def mlp_weights(dpre, n_own, n_oth, g_own, g_oth, hid, name):
            kept, sent = kernel_call(
                mlp_weights_body, name,
                [chunk_at, dpre, over_wa(dpre), n_own, over_wa(n_oth),
                 g_own, over_wa(g_oth), hid, over_wa(hid)],
                [sds((n_dev // 2, mlp_rows, half), BF16)] * 2,
                scratch=[pltpu.VMEM((n_dev, mlp_rows, half), F32)],
                flops=2 * 4 * rows * half * hidden,
            )
            total = reduce_chunks(kept, sent)
            up = total[:up_rows]
            down = total[up_rows:].reshape(folds, down_rows, half)
            return up, jnp.transpose(down, (1, 0, 2)).reshape(down_rows, hidden)

        qkv_rows, proj_rows = heads_width // n_dev, half // n_dev
        attn_rows = 3 * qkv_rows + proj_rows
        assert heads_width == half

        def attn_weights_body(
            chunk_ref, dpk_a, dpk_b, n_a, n_b, g_a, g_b, mix_a, mix_b, kept, sent, scratch
        ):
            for part in range(3):
                qkv = mm(dpk_a[part], n_a[...], 0, 0) + mm(dpk_b[part], n_b[...], 0, 0)
                for chunk in range(n_dev):
                    scratch[chunk, part * qkv_rows : (part + 1) * qkv_rows, :] = qkv[
                        chunk * qkv_rows : (chunk + 1) * qkv_rows
                    ]
            proj = mm(g_a[...], mix_a[...], 0, 0) + mm(g_b[...], mix_b[...], 0, 0)
            for chunk in range(n_dev):
                scratch[chunk, 3 * qkv_rows :, :] = proj[
                    chunk * proj_rows : (chunk + 1) * proj_rows
                ]
            scatter_chunks(scratch, chunk_ref, kept, sent)

        def attn_weights(dpk, n_own, n_oth, g_own, g_oth, mixed, name):
            kept, sent = kernel_call(
                attn_weights_body, name,
                [chunk_at, dpk, over_wa(dpk), n_own, over_wa(n_oth),
                 g_own, over_wa(g_oth), mixed, over_wa(mixed)],
                [sds((n_dev // 2, attn_rows, half), BF16)] * 2,
                scratch=[pltpu.VMEM((n_dev, attn_rows, half), F32)],
                flops=2 * 2 * rows * half * 4 * heads_width,
            )
            total = reduce_chunks(kept, sent)
            return total[: 3 * qkv_rows].reshape(3, qkv_rows, half), total[3 * qkv_rows :]

        def add_norm_back(grad, part_a, part_b, stream, params_ref, branch, sums_ref):
            upstream = part_a[...].astype(F32) + part_b[...].astype(F32)
            units, inv_std = norm_stats(stream)
            sums_ref[0:1, :] = jnp.sum(upstream * units, axis=0, keepdims=True)
            sums_ref[1:2, :] = jnp.sum(upstream, axis=0, keepdims=True)
            return grad + norm_back(upstream, units, inv_std, row(params_ref, 18 + branch))

        def qkv_back(packed, wq_a, wq_b):
            return [
                sum(mm(packed[part], ref[part], 1, 1) for part in range(3)) for ref in (wq_a, wq_b)
            ]

        def channel_back_body(
            g_in_own, g_in_oth, part_a, part_b, s_in, params_ref, mask_ref, qkv_ref, probs_ref,
            wp_a, wp_b, wq_a, wq_b, g_ref, g_own, g_oth, dpk_ref, part_ref, sums_ref,
        ):
            grad = jnp.concatenate([g_in_own[...], g_in_oth[...]], axis=1).astype(F32)
            grad = add_norm_back(grad, part_a, part_b, s_in[...], params_ref, 3, sums_ref)
            g_ref[...] = grad
            low = grad.astype(BF16)
            put_both(g_own, g_oth, low)
            grad_mixed = both_nt(low, wp_a, wp_b).astype(BF16)
            packed = attention_part_back(False, grad_mixed, mask_ref, qkv_ref, probs_ref, dpk_ref)
            own, oth = qkv_back(packed, wq_a, wq_b)
            part_ref[:, :half] = own.astype(BF16)
            part_ref[:, half:] = oth.astype(BF16)

        (g2, g2_own, g2_oth, dpk2, back2, sums3) = kernel_call(
            channel_back_body, "back_c",
            [g3_own, g3_oth, back3, far_back3, s5, params, mask, qkv2, probs2,
             (w_proj, 1), (wp_oth, 1), (wq_own, 1), (wq_oth, 1)],
            [full, half_low, half_low, qkv_low, full_low, sds((2, width))],
            flops=attn_flops,
        )
        far_back2 = over_ha(back2)
        up_one, down_one = mlp_weights(dpre3, n3_own, n3_oth, g3_own, g3_oth, hid3, "wgrad_d")

        def mlp_back_body(
            g_in, part_a, part_b, s_in, s_before, params_ref, slope_ref, wd_a, wd_b, wu_a, wu_b,
            g_ref, g_own, g_oth, dpre_ref, part_ref, sums_ref,
        ):
            keep = column_mask(rows)
            grad = add_norm_back(g_in[...], part_a, part_b, s_in[...], params_ref, 2, sums_ref)
            conv_back_into(g_ref, sums_ref, 2, grad, s_before[...], 9, params_ref, keep)
            low = g_ref[...].astype(BF16)
            put_both(g_own, g_oth, low)
            dhid = both_nt(low, wd_a, wd_b).astype(BF16).astype(F32)
            dpre = (dhid * slope_ref[...]).astype(BF16)
            dpre_ref[...] = dpre
            part_ref[:, :half] = mm(dpre, wu_a[...], 1, 1).astype(BF16)
            part_ref[:, half:] = mm(dpre, wu_b[...], 1, 1).astype(BF16)

        (g1, g1_own, g1_oth, dpre1, back1, sums2) = kernel_call(
            mlp_back_body, "back_b",
            [g2, back2, far_back2, s4, s3, params, slope1,
             (w_down, 0), (wd_oth, 0), (w_up, 0), (wu_oth, 0)],
            [full, half_low, half_low, hid_low, full_low, sds((11, width))],
            flops=mlp_flops,
        )
        far_back1 = over_ha(back1)
        qkv_one, proj_one = attn_weights(dpk2, n2_own, n2_oth, g2_own, g2_oth, mixed2, "wgrad_c")

        def window_back_body(
            g_in, part_a, part_b, s_in, params_ref, qkv_ref, probs_ref, wp_a, wp_b,
            g_ref, g_own, g_oth, dpk_ref, sums_ref,
        ):
            grad = add_norm_back(g_in[...], part_a, part_b, s_in[...], params_ref, 1, sums_ref)
            g_ref[...] = grad
            low = grad.astype(BF16)
            put_both(g_own, g_oth, low)
            grad_mixed = both_nt(low, wp_a, wp_b).astype(BF16)
            attention_part_back(True, grad_mixed, None, qkv_ref, probs_ref, dpk_ref)

        (g0, g0_own, g0_oth, dpk0, sums1) = kernel_call(
            window_back_body, "back_a",
            [g1, back1, far_back1, s2, params, qkv0, probs0, (w_proj, 0), (wp_oth, 0)],
            [full, half_low, half_low, qkv_low, sds((2, width))],
            flops=attn_flops,
        )
        up_zero, down_zero = mlp_weights(dpre1, n1_own, n1_oth, g1_own, g1_oth, hid1, "wgrad_b")
        qkv_zero, proj_zero = attn_weights(dpk0, n0_own, n0_oth, g0_own, g0_oth, mixed0, "wgrad_a")

        def first_back_body(
            flag_ref, ha_ref, g_in, dpk_ref, s_in, x_ref, params_ref, wq_a, wq_b, compact_ref,
            kept, sent, crossed, sums_ref, scratch,
        ):
            keep = column_mask(rows)
            packed = [dpk_ref[part] for part in range(3)]
            upstream = jnp.concatenate(qkv_back(packed, wq_a, wq_b), axis=1)
            units, inv_std = norm_stats(s_in[...])
            sums_ref[0:1, :] = jnp.sum(upstream * units, axis=0, keepdims=True)
            sums_ref[1:2, :] = jnp.sum(upstream, axis=0, keepdims=True)
            grad = jnp.where(ha_ref[0] == 1, g_in[...], 0.0)
            grad = grad + norm_back(upstream, units, inv_std, row(params_ref, 18))
            conv_back_into(
                scratch, sums_ref, 2, grad, x_ref[...].astype(F32), 0, params_ref, keep
            )
            ship(flag_ref, scratch[...], compact_ref, kept, sent, crossed)

        *token_parts, sums0 = kernel_call(
            first_back_body, "back_0",
            [flag, first_ha, g0, dpk0, s1, x0, params, (wq_own, 0), (wq_oth, 0), compact],
            shipped + [sds((11, width))],
            scratch=[pltpu.VMEM((rows, width), F32)],
            flops=attn_flops * 3 // 4,
        )
        grad_tokens = deliver(*token_parts, "join_tokens")

        sums = jnp.concatenate([sums0, 0.5 * sums1, 0.5 * sums2, 0.5 * sums3], axis=0)
        total = sums[:, :half] + over_wa(sums[:, half:])
        total = total + over_ha(total)
        for bit in range(bits):
            total = total + over_dev(total, bit)
        gain_at, shift_at = (0, 11, 13, 24), (1, 12, 14, 25)
        grad_gain = jnp.stack([total[at] for at in gain_at])
        grad_shift = jnp.stack([total[at] for at in shift_at])
        grad_taps = jnp.stack([total[2:11], total[15:24]])

        grad_qkv = jnp.transpose(jnp.stack([qkv_zero, qkv_one]), (0, 3, 1, 2))
        grad_proj = jnp.transpose(jnp.stack([proj_zero, proj_one]), (0, 2, 1))
        grad_up = jnp.transpose(jnp.stack([up_zero, up_one]), (0, 2, 1))
        grad_down = jnp.transpose(jnp.stack([down_zero, down_one]), (0, 2, 1))
        return (
            output,
            grad_tokens,
            grad_taps,
            grad_gain,
            grad_shift,
            grad_qkv,
            grad_proj,
            grad_up,
            grad_down,
        )

    placed = (
        P(("dev", "ha"), "wa"),
        P(("dev", "ha"), "wa"),
        P(None, None, "wa"),
        P(None, "wa"),
        P(None, "wa"),
        P(None, "wa", None, "ha"),
        P(None, "ha", "wa"),
        P(None, "wa", "ha"),
        P(None, "ha", "wa"),
        P("dev", None),
    )
    return jax.shard_map(
        on_device,
        mesh=mesh,
        in_specs=placed,
        out_specs=(
            P(("dev", "ha"), "wa"),
            P(("dev", "ha"), "wa"),
            P(None, None, "wa"),
            P(None, "wa"),
            P(None, "wa"),
            P(None, "wa", None, ("ha", "dev")),
            P(None, "ha", ("wa", "dev")),
            P(None, "wa", ("ha", "dev")),
            P(None, "ha", ("wa", "dev")),
        ),
        check_vma=False,
    )
```

time: 843 us -> 285 us (0.34); the launches traced: 832 us -> 284 us
  blocking collectives: 290 us -> 0 us
  waiting for transfers between devices: 277 us -> 139 us
  local copies, waits for them, and re-layouts: 116 us -> 40 us
  matrix products: 53.4 us -> 0 us
  Pallas kernels: 0 us -> 44.1 us
  other arithmetic: 38.1 us -> 8.44 us
  between operations: 20.2 us -> 1.84 us
  starting transfers between devices: 37.7 us -> 50.7 us
    unnamed x19 -> x0, waiting for transfers between devices: 200 us -> none
    ppermute x0 -> x52, waiting for transfers between devices: none -> 139 us  [the longest x15 94.2 us: over_dev(): lax.ppermute(values, 'dev', [(i, i ^ 1 << bit) for i in range(n_dev)])]
    unnamed x14 -> x0, blocking collectives: 118 us -> none
    psum x9 -> x0, blocking collectives: 100 us -> none  [the longest x1 80.4 us: on_device(): lax.psum((jnp.stack([taps_zero, taps_one]), jnp.stack([gain_zero, gain_on...]
    reduce_scatter x1 -> x0, waiting for transfers between devices: 76.4 us -> none  [on_device(): lax.psum_scatter(qkv_local, 'dev', scatter_dimension=3, tiled=True)]
    all_gather x16 -> x0, blocking collectives: 71.1 us -> none  [the longest x8 49.1 us: head_rows(): return lax.all_gather(values, 'ha', axis=0, tiled=True)]
    dot_general x34 -> x0, matrix products: 51.3 us -> none  [the longest x24 45.1 us: contract(): lax.dot_general(left_mat, right_mat, (((left_dim,), (right_dim,)), ((), (...]
    ppermute x0 -> x52, starting transfers between devices: none -> 50.7 us  [the longest x15 22.2 us: over_dev(): lax.ppermute(values, 'dev', [(i, i ^ 1 << bit) for i in range(n_dev)])]
  transfers between devices with their start and end apart: 18 -> 52, of which waited for: 4 -> 19; matrix products, arithmetic and copies ran while one was open for 11% -> 4% of each run, Pallas kernels for 0% -> 10%
where the time goes in v1:
time: 285 us; the launch traced here: 284 us
  waiting for transfers between devices  139 us (49%)
  starting transfers between devices  50.7 us (18%)
  Pallas kernels  44.1 us (15%)
  local copies, waits for them, and re-layouts  40 us (14%)
  other arithmetic  8.44 us (3%)
    ppermute x15, waiting for transfers between devices, over_dev(): lax.ppermute(values, 'dev', [(i, i ^ 1 << bit) for i in range(n_dev)])  94.2 us
    pallas_call x16, Pallas kernels, kernel_call(): pl.pallas_call(body, grid=(1,), in_specs=specs, out_specs=[pl.BlockSpec(o...  44.1 us
    unnamed x204, local copies, waits for them, and re-layouts  37.6 us
    ppermute x7, waiting for transfers between devices, over_ha(): return lax.ppermute(values, 'ha', swap)  33.5 us
    ppermute x15, starting transfers between devices, over_dev(): lax.ppermute(values, 'dev', [(i, i ^ 1 << bit) for i in range(n_dev)])  22.2 us
    ppermute x7, starting transfers between devices, over_ha(): return lax.ppermute(values, 'ha', swap)  12.6 us
    ppermute x22, starting transfers between devices, over_wa(): return lax.ppermute(values, 'wa', swap)  8.26 us
  transfers between devices with their start and end apart: 52, of which 19 were waited for; matrix products, arithmetic and copies ran while one was open for 4% of the time, Pallas kernels for 10%

profile of v1, /device:TPU:0, one launch (start us, length us, event | category | flops | bytes accessed | tf_op | source)
XLA Modules:
  0.0 284.0 jit_solution(17711619912049412528)
XLA Ops:
  8.4 4.0 %collective-permute-done.near = bf16[147,384]{1,0:T(8,128)(2,1)S(1)} collective-permute-done((bf16[147,384]{1,0:T(8,128)(2,1)}, bf16[147,384]{1,0:T(8,128)(2,1)S(1)}, u32[]{:S(2)}, u32[]{:S(2)}) %collective-permute-start) | collective-permute-done | bytes 112928 | tf_op jit(solution)/shard_map/ppermute | solution.py:273
  21.0 3.8 %attn_a.1 = (bf16[168,768]{1,0:T(8,128)(2,1)S(1)}, f32[168,768]{1,0:T(8,128)S(1)}, bf16[168,384]{1,0:T(8,128)(2,1)S(1)}, bf16[168,384]{1,0:T(8,128)(2,1)S(1)}, b...) custom-call(s32[1]{0:T(128)} %bitcast.flag_ref, ...), custom_call_target="tpu_custom_call" | custom-call | flops 396361728 | bytes 7444468 | tf_op jit(solution)/shard_map/attn_a/pallas_call | solution.py:54
  28.9 7.5 %collective-permute-start.5 = (bf16[168,768]{1,0:T(8,128)(2,1)S(1)}, bf16[168,768]{1,0:T(8,128)(2,1)S(1)}, u32[]{:S(2)}, u32[]{:S(2)}) collective-permute-start(bf16[168,768]{1,0:T(8,128)(2,1)S(1)} %get-tuple-element.73.part_a), channel_id=1, source_target_pairs={{0,2},{2,0},{1,3},{3,1},{4,6},{6,4},{5,7},{7,5},{8,10},{10,8},{9,1... | collective-permute-start | bytes 774152 | tf_op jit(solution)/shard_map/ppermute | solution.py:233
  36.5 6.5 %collective-permute-done.5.part_b = bf16[168,768]{1,0:T(8,128)(2,1)S(1)} collective-permute-done((bf16[168,768]{1,0:T(8,128)(2,1)S(1)}, bf16[168,768]{1,0:T(8,128)(2,1)S(1)}, u32[]{:S(2)}, u32[]{:S(2)}) %collective-permute-start.5) | collective-permute-done | bytes 258080 | tf_op jit(solution)/shard_map/ppermute | solution.py:233
  43.0 4.6 %mlp_b.1 = (f32[168,768]{1,0:T(8,128)S(1)}, bf16[168,384]{1,0:T(8,128)(2,1)S(1)}, bf16[168,384]{1,0:T(8,128)(2,1)S(1)}, bf16[168,1536]{1,0:T(8,128)(2,1)S(1)}, f...) custom-call(f32[168,768]{1,0:T(8,128)S(1)} %get-tuple-element.72.s_in, bf16[168,768]{1,0:T(8,128)(2,1)S(1)} %get-tuple-element.73.part_a, ...), custom_call_target="tpu_custom_call" | custom-call | flops 792723456 | bytes 13129728 | tf_op jit(solution)/shard_map/mlp_b/pallas_call | solution.py:54
  54.6 5.7 %collective-permute-done.8.part_b = bf16[168,768]{1,0:T(8,128)(2,1)} collective-permute-done((bf16[168,768]{1,0:T(8,128)(2,1)}, bf16[168,768]{1,0:T(8,128)(2,1)}, u32[]{:S(2)}, u32[]{:S(2)}) %collective-permute-start.8) | collective-permute-done | bytes 258080 | tf_op jit(solution)/shard_map/ppermute | solution.py:233
  66.0 3.2 %attn_c.1 = (f32[168,768]{1,0:T(8,128)S(1)}, f32[168,768]{1,0:T(8,128)S(1)}, bf16[168,384]{1,0:T(8,128)(2,1)S(1)}, bf16[168,384]{1,0:T(8,128)(2,1)S(1)}, bf16[3,...) custom-call(f32[168,768]{1,0:T(8,128)S(1)} %copy-done.26, ...), custom_call_target="tpu_custom_call" | custom-call | flops 396361728 | bytes 8485536 | tf_op jit(solution)/shard_map/attn_c/pallas_call | solution.py:54
  74.9 4.3 %collective-permute-done.10.near = bf16[147,384]{1,0:T(8,128)(2,1)S(1)} collective-permute-done((bf16[147,384]{1,0:T(8,128)(2,1)S(1)}, bf16[147,384]{1,0:T(8,128)(2,1)S(1)}, u32[]{:S(2)}, u32[]{:S(2)}) %collective-permute-start.10) | collective-permute-done | bytes 112928 | tf_op jit(solution)/shard_map/ppermute | solution.py:278
  81.8 3.9 %mlp_d.1 = (f32[168,768]{1,0:T(8,128)S(1)}, bf16[168,384]{1,0:T(8,128)(2,1)S(1)}, bf16[168,384]{1,0:T(8,128)(2,1)S(1)}, bf16[168,1536]{1,0:T(8,128)(2,1)S(1)}, b...) custom-call(f32[168,768]{1,0:T(8,128)S(1)} %get-tuple-element.76.s_in, ...), custom_call_target="tpu_custom_call" | custom-call | flops 792723456 | bytes 8411136 | tf_op jit(solution)/shard_map/mlp_d/pallas_call | solution.py:54
  89.0 6.6 %collective-permute-done.14.part_b = bf16[168,768]{1,0:T(8,128)(2,1)S(1)} collective-permute-done((bf16[168,768]{1,0:T(8,128)(2,1)S(1)}, bf16[168,768]{1,0:T(8,128)(2,1)S(1)}, u32[]{:S(2)}, u32[]{:S(2)}) %collective-permute-start.14) | collective-permute-done | bytes 258080 | tf_op jit(solution)/shard_map/ppermute | solution.py:233
  95.6 3.6 %back_c.1 = (f32[168,768]{1,0:T(8,128)S(1)}, bf16[168,384]{1,0:T(8,128)(2,1)S(1)}, bf16[168,384]{1,0:T(8,128)(2,1)S(1)}, bf16[3,168,384]{2,1,0:T(8,128)(2,1)}, b...) custom-call(bf16[168,384]{1,0:T(8,128)(2,1)S(1)} %get-tuple-element.84.g_in_own.g_a, ...), custom_call_target="tpu_custom_call" | custom-call | flops 396361728 | bytes 8491680 | tf_op jit(solution)/shard_map/back_c/pallas_call | solution.py:54
  102.8 7.4 %collective-permute-done.15.part_b = bf16[168,768]{1,0:T(8,128)(2,1)} collective-permute-done((bf16[168,768]{1,0:T(8,128)(2,1)}, bf16[168,768]{1,0:T(8,128)(2,1)}, u32[]{:S(2)}, u32[]{:S(2)}) %collective-permute-start.15) | collective-permute-done | bytes 258080 | tf_op jit(solution)/shard_map/ppermute | solution.py:233
  117.1 4.9 %back_b.1 = (f32[168,768]{1,0:T(8,128)S(1)}, bf16[168,384]{1,0:T(8,128)(2,1)S(1)}, bf16[168,384]{1,0:T(8,128)(2,1)S(1)}, bf16[168,1536]{1,0:T(8,128)(2,1)S(1)}, ...) custom-call(f32[168,768]{1,0:T(8,128)S(1)} %copy-done.39, bf16[168,768]{1,0:T(8,128)(2,1)} %get-tuple-element.90.part_a, ...), custom_call_target="tpu_custom_call" | custom-call | flops 792723456 | bytes 14195712 | tf_op jit(solution)/shard_map/back_b/pallas_call | solution.py:54
  122.3 7.3 %collective-permute-done.16.part_b = bf16[168,768]{1,0:T(8,128)(2,1)S(1)} collective-permute-done((bf16[168,768]{1,0:T(8,128)(2,1)S(1)}, bf16[168,768]{1,0:T(8,128)(2,1)S(1)}, u32[]{:S(2)}, u32[]{:S(2)}) %collective-permute-start.16) | collective-permute-done | bytes 258080 | tf_op jit(solution)/shard_map/ppermute | solution.py:233
  145.6 3.1 %collective-permute-start.35 = (bf16[4,192,384]{2,1,0:T(8,128)(2,1)S(1)}, bf16[4,192,384]{2,1,0:T(8,128)(2,1)S(1)}, u32[]{:S(2)}, u32[]{:S(2)}) collective-permute-start(bf16[4,192,384]{2,1,0:T(8,128)(2,1)S(1)} %get-tuple-element.121), channel_id=1, source_target_pairs={{0,4},{4,0},{8,12},{12,8},{16,20},{20,16},{24,28},{28,24},{1,5},{5... | collective-permute-start | bytes 1769480 | tf_op jit(solution)/shard_map/ppermute | solution.py:239
  149.5 13.9 %collective-permute-done.21 = f32[26,384]{1,0:T(8,128)S(1)} collective-permute-done((f32[26,384]{1,0:T(8,128)S(1)}, f32[26,384]{1,0:T(8,128)S(1)}, u32[]{:S(2)}, u32[]{:S(2)}) %collective-permute-start.21) | collective-permute-done | bytes 39968 | tf_op jit(solution)/shard_map/ppermute | solution.py:239
  169.6 2.9 %collective-permute-start.25 = (bf16[168,384]{1,0:T(8,128)(2,1)S(1)}, bf16[168,384]{1,0:T(8,128)(2,1)S(1)}, u32[]{:S(2)}, u32[]{:S(2)}) collective-permute-start(bf16[168,384]{1,0:T(8,128)(2,1)S(1)} %copy-done.82), channel_id=1, source_target_pairs={{0,1},{1,0},{2,3},{3,2},{4,5},{5,4},{6,7},{7,6},{8,9},{9,8},{10,11... | collective-permute-start | bytes 387080 | tf_op jit(solution)/shard_map/ppermute | solution.py:236
  186.3 4.8 %collective-permute-done.36 = bf16[2,192,384]{2,1,0:T(8,128)(2,1)S(1)} collective-permute-done((bf16[2,192,384]{2,1,0:T(8,128)(2,1)S(1)}, bf16[2,192,384]{2,1,0:T(8,128)(2,1)S(1)}, u32[]{:S(2)}, u32[]{:S(2)}) %collective-permute-start.36) | collective-permute-done | bytes 294944 | tf_op jit(solution)/shard_map/ppermute | solution.py:239
  198.0 3.0 %collective-permute-done.37 = bf16[1,192,384]{2,1,0:T(8,128)(2,1)S(1)} collective-permute-done((bf16[1,192,384]{2,1,0:T(8,128)(2,1)S(1)}, bf16[1,192,384]{2,1,0:T(8,128)(2,1)S(1)}, u32[]{:S(2)}, u32[]{:S(2)}) %collective-permute-start.37) | collective-permute-done | bytes 147488 | tf_op jit(solution)/shard_map/ppermute | solution.py:239
  201.0 20.6 %collective-permute-done.28 = bf16[4,192,384]{2,1,0:T(8,128)(2,1)S(1)} collective-permute-done((bf16[4,192,384]{2,1,0:T(8,128)(2,1)S(1)}, bf16[4,192,384]{2,1,0:T(8,128)(2,1)S(1)}, u32[]{:S(2)}, u32[]{:S(2)}) %collective-permute-start.28) | collective-permute-done | bytes 589856 | tf_op jit(solution)/shard_map/ppermute | solution.py:239
  224.4 9.0 %collective-permute-done.29 = bf16[2,192,384]{2,1,0:T(8,128)(2,1)S(1)} collective-permute-done((bf16[2,192,384]{2,1,0:T(8,128)(2,1)S(1)}, bf16[2,192,384]{2,1,0:T(8,128)(2,1)S(1)}, u32[]{:S(2)}, u32[]{:S(2)}) %collective-permute-start.29) | collective-permute-done | bytes 294944 | tf_op jit(solution)/shard_map/ppermute | solution.py:239
  234.4 11.6 %collective-permute-done.42 = bf16[4,384,384]{2,1,0:T(8,128)(2,1)S(1)} collective-permute-done((bf16[4,384,384]{2,1,0:T(8,128)(2,1)S(1)}, bf16[4,384,384]{2,1,0:T(8,128)(2,1)S(1)}, u32[]{:S(2)}, u32[]{:S(2)}) %collective-permute-start.42) | collective-permute-done | bytes 1179680 | tf_op jit(solution)/shard_map/ppermute | solution.py:239
  251.6 15.7 %collective-permute-done.43 = bf16[2,384,384]{2,1,0:T(8,128)(2,1)S(1)} collective-permute-done((bf16[2,384,384]{2,1,0:T(8,128)(2,1)S(1)}, bf16[2,384,384]{2,1,0:T(8,128)(2,1)S(1)}, u32[]{:S(2)}, u32[]{:S(2)}) %collective-permute-start.43) | collective-permute-done | bytes 589856 | tf_op jit(solution)/shard_map/ppermute | solution.py:239
  268.6 13.3 %collective-permute-done.44 = bf16[1,384,384]{2,1,0:T(8,128)(2,1)S(1)} collective-permute-done((bf16[1,384,384]{2,1,0:T(8,128)(2,1)S(1)}, bf16[1,384,384]{2,1,0:T(8,128)(2,1)S(1)}, u32[]{:S(2)}, u32[]{:S(2)}) %collective-permute-start.44) | collective-permute-done | bytes 294944 | tf_op jit(solution)/shard_map/ppermute | solution.py:239
  (358 shorter events, 110.9 us)
Async XLA Ops:
  0.7 42.3 %collective-permute-start.6 = (bf16[2,384,1536]{2,1,0:T(8,128)(2,1)}, bf16[2,384,1536]{2,1,0:T(8,128)(2,1)}, u32[]{:S(2)}, u32[]{:S(2)}) collective-permute-start(bf16[2,384,1536]{2,1,0:T(8,128)(2,1)} %wu_a.5), channel_id=1, source_target_pairs={{0,1},{1,0},{2,3},{3,2},{4,5},{5,4},{6,7},{7,6},{8,9},{9,8},{10,11... | collective-permute-start | bytes 7077896 | tf_op jit(solution)/shard_map/ppermute | solution.py:236
  1.2 41.8 %collective-permute-start.7 = (bf16[2,1536,384]{2,1,0:T(8,128)(2,1)}, bf16[2,1536,384]{2,1,0:T(8,128)(2,1)}, u32[]{:S(2)}, u32[]{:S(2)}) collective-permute-start(bf16[2,1536,384]{2,1,0:T(8,128)(2,1)} %wd_a.7), channel_id=1, source_target_pairs={{0,1},{1,0},{2,3},{3,2},{4,5},{5,4},{6,7},{7,6},{8,9},{9,8},{10,11... | collective-permute-start | bytes 7077896 | tf_op jit(solution)/shard_map/ppermute | solution.py:236
  1.3 12.6 %collective-permute-start.3 = (bf16[2,3,384,384]{3,2,1,0:T(8,128)(2,1)}, bf16[2,3,384,384]{3,2,1,0:T(8,128)(2,1)S(1)}, u32[]{:S(2)}, u32[]{:S(2)}) collective-permute-start(bf16[2,3,384,384]{3,2,1,0:T(8,128)(2,1)} %bitcast.31), channel_id=1, source_target_pairs={{0,1},{1,0},{2,3},{3,2},{4,5},{5,4},{6,7},{7,6},{8,9},{9,8},{10,11... | collective-permute-start | bytes 5308424 | tf_op jit(solution)/shard_map/ppermute | solution.py:236
  1.7 12.2 %collective-permute-start.4 = (bf16[2,384,384]{2,1,0:T(8,128)(2,1)}, bf16[2,384,384]{2,1,0:T(8,128)(2,1)S(1)}, u32[]{:S(2)}, u32[]{:S(2)}) collective-permute-start(bf16[2,384,384]{2,1,0:T(8,128)(2,1)} %wp_a.7), channel_id=1, source_target_pairs={{0,1},{1,0},{2,3},{3,2},{4,5},{5,4},{6,7},{7,6},{8,9},{9,8},{10,11... | collective-permute-start | bytes 1769480 | tf_op jit(solution)/shard_map/ppermute | solution.py:236
  28.9 14.0 %collective-permute-start.5 = (bf16[168,768]{1,0:T(8,128)(2,1)S(1)}, bf16[168,768]{1,0:T(8,128)(2,1)S(1)}, u32[]{:S(2)}, u32[]{:S(2)}) collective-permute-start(bf16[168,768]{1,0:T(8,128)(2,1)S(1)} %get-tuple-element.73.part_a), channel_id=1, source_target_pairs={{0,2},{2,0},{1,3},{3,1},{4,6},{6,4},{5,7},{7,5},{8,10},{10,8},{9,1... | collective-permute-start | bytes 774152 | tf_op jit(solution)/shard_map/ppermute | solution.py:233
  102.8 34.6 %collective-permute-start.32 = (bf16[168,384]{1,0:T(8,128)(2,1)}, bf16[168,384]{1,0:T(8,128)(2,1)}, u32[]{:S(2)}, u32[]{:S(2)}) collective-permute-start(bf16[168,384]{1,0:T(8,128)(2,1)} %copy-done.93), channel_id=1, source_target_pairs={{0,1},{1,0},{2,3},{3,2},{4,5},{5,4},{6,7},{7,6},{8,9},{9,8},{10,11... | collective-permute-start | bytes 387080 | tf_op jit(solution)/shard_map/ppermute | solution.py:236
  122.3 20.7 %collective-permute-start.31 = (bf16[3,168,384]{2,1,0:T(8,128)(2,1)}, bf16[3,168,384]{2,1,0:T(8,128)(2,1)}, u32[]{:S(2)}, u32[]{:S(2)}) collective-permute-start(bf16[3,168,384]{2,1,0:T(8,128)(2,1)} %get-tuple-element.114.dpk_a), channel_id=1, source_target_pairs={{0,1},{1,0},{2,3},{3,2},{4,5},{5,4},{6,7},{7,6},{8,9},{9,8},{10,11... | collective-permute-start | bytes 1161224 | tf_op jit(solution)/shard_map/ppermute | solution.py:236
  137.3 32.3 %collective-permute-start.45 = (bf16[168,1536]{1,0:T(8,128)(2,1)}, bf16[168,1536]{1,0:T(8,128)(2,1)S(1)}, u32[]{:S(2)}, u32[]{:S(2)}) collective-permute-start(bf16[168,1536]{1,0:T(8,128)(2,1)} %copy-done.75), channel_id=1, source_target_pairs={{0,1},{1,0},{2,3},{3,2},{4,5},{5,4},{6,7},{7,6},{8,9},{9,8},{10,11... | collective-permute-start | bytes 1548296 | tf_op jit(solution)/shard_map/ppermute | solution.py:236
  137.4 35.2 %collective-permute-start.48 = (bf16[168,1536]{1,0:T(8,128)(2,1)S(1)}, bf16[168,1536]{1,0:T(8,128)(2,1)S(1)}, u32[]{:S(2)}, u32[]{:S(2)}) collective-permute-start(bf16[168,1536]{1,0:T(8,128)(2,1)S(1)} %copy-done.43), channel_id=1, source_target_pairs={{0,1},{1,0},{2,3},{3,2},{4,5},{5,4},{6,7},{7,6},{8,9},{9,8},{10,11... | collective-permute-start | bytes 1548296 | tf_op jit(solution)/shard_map/ppermute | solution.py:236
  145.6 33.7 %collective-permute-start.35 = (bf16[4,192,384]{2,1,0:T(8,128)(2,1)S(1)}, bf16[4,192,384]{2,1,0:T(8,128)(2,1)S(1)}, u32[]{:S(2)}, u32[]{:S(2)}) collective-permute-start(bf16[4,192,384]{2,1,0:T(8,128)(2,1)S(1)} %get-tuple-element.121), channel_id=1, source_target_pairs={{0,4},{4,0},{8,12},{12,8},{16,20},{20,16},{24,28},{28,24},{1,5},{5... | collective-permute-start | bytes 1769480 | tf_op jit(solution)/shard_map/ppermute | solution.py:239
  148.7 14.7 %collective-permute-start.21 = (f32[26,384]{1,0:T(8,128)S(1)}, f32[26,384]{1,0:T(8,128)S(1)}, u32[]{:S(2)}, u32[]{:S(2)}) collective-permute-start(f32[26,384]{1,0:T(8,128)S(1)} %add.58), channel_id=1, source_target_pairs={{0,4},{4,0},{8,12},{12,8},{16,20},{20,16},{24,28},{28,24},{1,5},{5... | collective-permute-start | bytes 119816 | tf_op jit(solution)/shard_map/ppermute | solution.py:239
  148.8 15.0 %collective-permute-start.13 = (bf16[147,384]{1,0:T(8,128)(2,1)S(1)}, bf16[147,384]{1,0:T(8,128)(2,1)S(1)}, u32[]{:S(2)}, u32[]{:S(2)}) collective-permute-start(bf16[147,384]{1,0:T(8,128)(2,1)S(1)} %get-tuple-element.83), channel_id=1, source_target_pairs={{1,2},{2,1},{5,6},{6,5},{9,10},{10,9},{13,14},{14,13},{17,18},{18,... | collective-permute-start | bytes 338696 | tf_op jit(solution)/shard_map/ppermute | solution.py:511
  166.0 11.9 %collective-permute-start.17 = (bf16[147,384]{1,0:T(8,128)(2,1)S(1)}, bf16[147,384]{1,0:T(8,128)(2,1)S(1)}, u32[]{:S(2)}, u32[]{:S(2)}) collective-permute-start(bf16[147,384]{1,0:T(8,128)(2,1)S(1)} %copy-done.98), channel_id=1, source_target_pairs={{2,0},{1,3},{0,1},{3,2},{6,4},{5,7},{4,5},{7,6},{10,8},{9,11},{8,9... | collective-permute-start | bytes 338696 | tf_op jit(solution)/shard_map/ppermute | solution.py:510
  178.0 13.9 %collective-permute-start.41 = (bf16[168,1536]{1,0:T(8,128)(2,1)S(1)}, bf16[168,1536]{1,0:T(8,128)(2,1)S(1)}, u32[]{:S(2)}, u32[]{:S(2)}) collective-permute-start(bf16[168,1536]{1,0:T(8,128)(2,1)S(1)} %copy-done.72), channel_id=1, source_target_pairs={{0,1},{1,0},{2,3},{3,2},{4,5},{5,4},{6,7},{7,6},{8,9},{9,8},{10,11... | collective-permute-start | bytes 1548296 | tf_op jit(solution)/shard_map/ppermute | solution.py:236
  180.1 43.3 %collective-permute-start.49 = (bf16[4,384,384]{2,1,0:T(8,128)(2,1)S(1)}, bf16[4,384,384]{2,1,0:T(8,128)(2,1)S(1)}, u32[]{:S(2)}, u32[]{:S(2)}) collective-permute-start(bf16[4,384,384]{2,1,0:T(8,128)(2,1)S(1)} %get-tuple-element.134), channel_id=1, source_target_pairs={{0,4},{4,0},{8,12},{12,8},{16,20},{20,16},{24,28},{28,24},{1,5},{5... | collective-permute-start | bytes 3538952 | tf_op jit(solution)/shard_map/ppermute | solution.py:239
  181.6 11.9 %collective-permute-start.38 = (bf16[168,1536]{1,0:T(8,128)(2,1)S(1)}, bf16[168,1536]{1,0:T(8,128)(2,1)S(1)}, u32[]{:S(2)}, u32[]{:S(2)}) collective-permute-start(bf16[168,1536]{1,0:T(8,128)(2,1)S(1)} %copy-done.74), channel_id=1, source_target_pairs={{0,1},{1,0},{2,3},{3,2},{4,5},{5,4},{6,7},{7,6},{8,9},{9,8},{10,11... | collective-permute-start | bytes 1548296 | tf_op jit(solution)/shard_map/ppermute | solution.py:236
  191.1 30.5 %collective-permute-start.28 = (bf16[4,192,384]{2,1,0:T(8,128)(2,1)S(1)}, bf16[4,192,384]{2,1,0:T(8,128)(2,1)S(1)}, u32[]{:S(2)}, u32[]{:S(2)}) collective-permute-start(bf16[4,192,384]{2,1,0:T(8,128)(2,1)S(1)} %get-tuple-element.113), channel_id=1, source_target_pairs={{0,4},{4,0},{8,12},{12,8},{16,20},{20,16},{24,28},{28,24},{1,5},{5... | collective-permute-start | bytes 1769480 | tf_op jit(solution)/shard_map/ppermute | solution.py:239
  196.0 50.0 %collective-permute-start.42 = (bf16[4,384,384]{2,1,0:T(8,128)(2,1)S(1)}, bf16[4,384,384]{2,1,0:T(8,128)(2,1)S(1)}, u32[]{:S(2)}, u32[]{:S(2)}) collective-permute-start(bf16[4,384,384]{2,1,0:T(8,128)(2,1)S(1)} %get-tuple-element.129), channel_id=1, source_target_pairs={{0,4},{4,0},{8,12},{12,8},{16,20},{20,16},{24,28},{28,24},{1,5},{5... | collective-permute-start | bytes 3538952 | tf_op jit(solution)/shard_map/ppermute | solution.py:239
  221.8 11.6 %collective-permute-start.29 = (bf16[2,192,384]{2,1,0:T(8,128)(2,1)S(1)}, bf16[2,192,384]{2,1,0:T(8,128)(2,1)S(1)}, u32[]{:S(2)}, u32[]{:S(2)}) collective-permute-start(bf16[2,192,384]{2,1,0:T(8,128)(2,1)S(1)} %slice.165), channel_id=1, source_target_pairs={{0,8},{4,12},{8,0},{12,4},{16,24},{20,28},{24,16},{28,20},{1,9},{5... | collective-permute-start | bytes 884744 | tf_op jit(solution)/shard_map/ppermute | solution.py:239
  223.8 25.1 %collective-permute-start.50 = (bf16[2,384,384]{2,1,0:T(8,128)(2,1)S(1)}, bf16[2,384,384]{2,1,0:T(8,128)(2,1)S(1)}, u32[]{:S(2)}, u32[]{:S(2)}) collective-permute-start(bf16[2,384,384]{2,1,0:T(8,128)(2,1)S(1)} %slice.182), channel_id=1, source_target_pairs={{0,8},{4,12},{8,0},{12,4},{16,24},{20,28},{24,16},{28,20},{1,9},{5... | collective-permute-start | bytes 1769480 | tf_op jit(solution)/shard_map/ppermute | solution.py:239
  233.5 14.5 %collective-permute-start.30 = (bf16[1,192,384]{2,1,0:T(8,128)(2,1)S(1)}, bf16[1,192,384]{2,1,0:T(8,128)(2,1)S(1)}, u32[]{:S(2)}, u32[]{:S(2)}) collective-permute-start(bf16[1,192,384]{2,1,0:T(8,128)(2,1)S(1)} %slice.167), channel_id=1, source_target_pairs={{0,16},{4,20},{8,24},{12,28},{16,0},{20,4},{24,8},{28,12},{1,17},{... | collective-permute-start | bytes 442376 | tf_op jit(solution)/shard_map/ppermute | solution.py:239
  246.4 20.9 %collective-permute-start.43 = (bf16[2,384,384]{2,1,0:T(8,128)(2,1)S(1)}, bf16[2,384,384]{2,1,0:T(8,128)(2,1)S(1)}, u32[]{:S(2)}, u32[]{:S(2)}) collective-permute-start(bf16[2,384,384]{2,1,0:T(8,128)(2,1)S(1)} %slice.177), channel_id=1, source_target_pairs={{0,8},{4,12},{8,0},{12,4},{16,24},{20,28},{24,16},{28,20},{1,9},{5... | collective-permute-start | bytes 1769480 | tf_op jit(solution)/shard_map/ppermute | solution.py:239
  249.1 19.2 %collective-permute-start.51 = (bf16[1,384,384]{2,1,0:T(8,128)(2,1)S(1)}, bf16[1,384,384]{2,1,0:T(8,128)(2,1)S(1)}, u32[]{:S(2)}, u32[]{:S(2)}) collective-permute-start(bf16[1,384,384]{2,1,0:T(8,128)(2,1)S(1)} %slice.184), channel_id=1, source_target_pairs={{0,16},{4,20},{8,24},{12,28},{16,0},{20,4},{24,8},{28,12},{1,17},{... | collective-permute-start | bytes 884744 | tf_op jit(solution)/shard_map/ppermute | solution.py:239
  267.5 14.5 %collective-permute-start.44 = (bf16[1,384,384]{2,1,0:T(8,128)(2,1)S(1)}, bf16[1,384,384]{2,1,0:T(8,128)(2,1)S(1)}, u32[]{:S(2)}, u32[]{:S(2)}) collective-permute-start(bf16[1,384,384]{2,1,0:T(8,128)(2,1)S(1)} %slice.179), channel_id=1, source_target_pairs={{0,16},{4,20},{8,24},{12,28},{16,0},{20,4},{24,8},{28,12},{1,17},{... | collective-permute-start | bytes 884744 | tf_op jit(solution)/shard_map/ppermute | solution.py:239
  (131 other events, 918.3 us)

commit v2 on v1

v2 whole, which is shorter than its diff:
```python
from functools import partial

import jax
import jax.numpy as jnp
import numpy as np
from jax import lax
from jax.experimental import pallas as pl
from jax.experimental.pallas import tpu as pltpu
from jax.sharding import PartitionSpec as P

WIN = 7
GRID_COLS = 8
PATCHES = 49
PADDED = WIN * GRID_COLS
HEAD_DIM = 32
LANES = 128
HEADS_TILE = LANES // HEAD_DIM
EPS = 1e-05
NEG = -1e30
BF16 = jnp.bfloat16
F32 = jnp.float32
VMEM_LIMIT = 16 * 2**20


def mm(left, right, left_dim, right_dim):
    return lax.dot_general(
        left, right, (((left_dim,), (right_dim,)), ((), ())), preferred_element_type=F32
    )


class Order:
    def __init__(self):
        self.last = None


def kernel_call(body, name, ins, outs, order, scratch=(), flops=0, hold=()):
    arrays = list(ins) + list(hold) + ([] if order.last is None else [order.last])
    specs = [
        pl.BlockSpec(
            memory_space=pltpu.SMEM if a.dtype == jnp.int32 and a.ndim == 1 else pltpu.VMEM
        )
        for a in arrays
    ]
    outs = list(outs) + [sds((8, LANES))]

    def wrapped(*refs):
        given = refs[: len(ins)] + refs[len(arrays) : len(arrays) + len(outs) - 1]
        body(*given, *refs[len(arrays) + len(outs) :])
        mark = refs[len(arrays) + len(outs) - 1]
        mark[...] = jnp.zeros_like(mark)

    moved = sum(int(np.prod(o.shape)) * o.dtype.itemsize for o in outs) + sum(
        int(np.prod(a.shape)) * a.dtype.itemsize for a in ins
    )
    *results, order.last = pl.pallas_call(
        wrapped,
        in_specs=specs,
        out_specs=[pl.BlockSpec(memory_space=pltpu.VMEM)] * len(outs),
        out_shape=outs,
        scratch_shapes=list(scratch),
        compiler_params=pltpu.CompilerParams(vmem_limit_bytes=VMEM_LIMIT),
        cost_estimate=pl.CostEstimate(flops=0, bytes_accessed=0, transcendentals=0),
        name=name,
    )(*arrays)
    return results


def sds(shape, dtype=F32):
    return jax.ShapeDtypeStruct(shape, dtype)


def column_mask(rows):
    return (lax.broadcasted_iota(jnp.int32, (rows, 1), 0) % GRID_COLS) < WIN


def placement(images, transposed):
    padded, plain = images * PADDED, images * PATCHES
    shape = (plain, padded) if transposed else (padded, plain)
    at = lax.broadcasted_iota(jnp.int32, shape, 1 if transposed else 0)
    image = sum((at >= i * PADDED).astype(jnp.int32) for i in range(1, images))
    inside = at - image * PADDED
    source = image * PATCHES + (inside >> 3) * WIN + (inside & 7)
    other = lax.broadcasted_iota(jnp.int32, shape, 0 if transposed else 1)
    return (((inside & 7) < WIN) & (source == other)).astype(F32).astype(BF16)


def side_shifts(values):
    rows = values.shape[0]
    return (pltpu.roll(values, 1, 0), values, pltpu.roll(values, rows - 1, 0))


def as_grid(values):
    return values.reshape(-1, WIN, GRID_COLS, values.shape[-1])


def move_rows(values, step):
    grid = as_grid(values)
    zeros = jnp.zeros_like(grid[:, :1])
    if step > 0:
        moved = jnp.concatenate([zeros, grid[:, :-1]], axis=1)
    else:
        moved = jnp.concatenate([grid[:, 1:], zeros], axis=1)
    return moved.reshape(values.shape)


def conv_cols(values, taps, keep):
    shifted = side_shifts(values)
    line = [
        sum(shifted[col] * taps[3 * row + col] for col in range(3)) for row in range(3)
    ]
    total = values + line[1] + move_rows(line[0], 1) + move_rows(line[2], -1)
    return jnp.where(keep, total, 0.0)


def tap_sums(grads, values):
    shifted = side_shifts(values)
    grad_grid = as_grid(grads)
    sums = []
    for row in range(3):
        for col in range(3):
            moved = as_grid(shifted[col])
            if row == 0:
                prod = grad_grid[:, 1:] * moved[:, :-1]
            elif row == 1:
                prod = grad_grid * moved
            else:
                prod = grad_grid[:, :-1] * moved[:, 1:]
            flat = prod.reshape(-1, GRID_COLS, prod.shape[-1])
            sums.append(jnp.sum(jnp.sum(flat, axis=0), axis=0, keepdims=True))
    return sums


def norm_stats(stream):
    width = stream.shape[1]
    center = jnp.sum(stream, axis=1, keepdims=True) * (1.0 / width)
    moved = stream - center
    inv_std = lax.rsqrt(jnp.sum(moved * moved, axis=1, keepdims=True) * (1.0 / width) + EPS)
    return moved * inv_std, inv_std


def norm_back(upstream, units, inv_std, gain):
    width = upstream.shape[1]
    scaled = upstream * gain
    first = jnp.sum(scaled, axis=1, keepdims=True) * (1.0 / width)
    second = jnp.sum(scaled * units, axis=1, keepdims=True) * (1.0 / width)
    return inv_std * (scaled - first - units * second)


def gelu_parts(values):
    z = jnp.abs(values) * (0.5**0.5)
    t = 1.0 / (1.0 + 0.3275911 * z)
    bell = jnp.exp(-z * z)
    poly = t * (
        0.254829592
        + t * (-0.284496736 + t * (1.421413741 + t * (-1.453152027 + t * 1.061405429)))
    )
    tail = 0.5 * poly * bell
    return jnp.where(values < 0, tail, 1.0 - tail), bell * float(1.0 / np.sqrt(2.0 * np.pi))


def head_mask(index):
    return (lax.broadcasted_iota(jnp.int32, (1, LANES), 1) // HEAD_DIM) == index


def spread_heads(tile):
    return jnp.concatenate(
        [jnp.where(head_mask(j), tile, 0.0) for j in range(HEADS_TILE)], axis=0
    ).astype(BF16)


def gather_heads(stacked):
    rows = stacked.shape[0] // HEADS_TILE
    total = jnp.where(head_mask(0), stacked[:rows], 0.0)
    for j in range(1, HEADS_TILE):
        total = jnp.where(head_mask(j), stacked[j * rows : (j + 1) * rows], total)
    return total


def softmax_rows(scores):
    top = jnp.max(scores, axis=0, keepdims=True)
    weights = jnp.exp(scores - top)
    return weights / jnp.sum(weights, axis=0, keepdims=True)


SCALE = HEAD_DIM**-0.5


def window_tile(q, k, v):
    keys_ok = column_mask(PADDED)
    scores = mm(k.astype(BF16), spread_heads(q), 1, 1) * SCALE
    probs = softmax_rows(jnp.where(keys_ok, scores, NEG))
    return probs, gather_heads(mm(probs.astype(BF16), v.astype(BF16), 0, 0))


def window_tile_back(q, k, v, probs, grad):
    low = probs.astype(BF16)
    q_big, g_big = spread_heads(q), spread_heads(grad)
    grad_probs = mm(v.astype(BF16), g_big, 1, 1)
    grad_v = mm(low, g_big, 1, 0)
    grad_scores = (
        probs * (grad_probs - jnp.sum(grad_probs * probs, axis=0, keepdims=True))
    ).astype(BF16)
    grad_k = mm(grad_scores, q_big, 1, 0) * SCALE
    grad_q = gather_heads(mm(grad_scores, k.astype(BF16), 0, 0)) * SCALE
    return grad_q, grad_k, grad_v


def same_head():
    first = lax.broadcasted_iota(jnp.int32, (LANES, LANES), 0) // HEAD_DIM
    second = lax.broadcasted_iota(jnp.int32, (LANES, LANES), 1) // HEAD_DIM
    return first == second


def channel_tile(q, k, v, mask):
    scores = mm(k.astype(BF16), (q * mask).astype(BF16), 0, 0) * SCALE
    probs = softmax_rows(jnp.where(same_head(), scores, NEG))
    return probs, mm(v.astype(BF16), probs.astype(BF16), 1, 0)


def channel_tile_back(q, k, v, probs, grad, mask):
    low = probs.astype(BF16)
    grad_low = grad.astype(BF16)
    grad_probs = mm(v.astype(BF16), grad_low, 0, 0)
    grad_v = mm(grad_low, low, 1, 1)
    grad_scores = (
        probs * (grad_probs - jnp.sum(grad_probs * probs, axis=0, keepdims=True))
    ).astype(BF16)
    grad_q = mm(k.astype(BF16), grad_scores, 1, 0) * SCALE * mask
    grad_k = mm((q * mask).astype(BF16), grad_scores, 1, 1) * SCALE
    return grad_q, grad_k, grad_v


def solution(mesh):
    n_dev = mesh.shape["dev"]
    bits = n_dev.bit_length() - 1
    assert n_dev == 1 << bits and mesh.shape["ha"] == 2 and mesh.shape["wa"] == 2

    swap = [(0, 1), (1, 0)]

    def over_ha(values):
        return lax.ppermute(values, "ha", swap)

    def over_wa(values):
        return lax.ppermute(values, "wa", swap)

    def over_dev(values, bit):
        return lax.ppermute(values, "dev", [(i, i ^ (1 << bit)) for i in range(n_dev)])

    def on_device(
        tokens, cotangent, conv_taps, norm_gain, norm_shift, w_qkv, w_proj, w_up, w_down, valid
    ):
        rows_in, half = tokens.shape
        images = rows_in // PATCHES
        rows = images * PADDED
        width = 2 * half
        heads_width = w_qkv.shape[3]
        hidden = w_up.shape[2]
        tiles = heads_width // LANES
        assert heads_width == half
        dev, ha, wa = (lax.axis_index(name) for name in ("dev", "ha", "wa"))
        orders = [list(range(bits)), [1, 0, *range(2, bits)]]

        def chunk_of(place, order):
            found = 0
            for step, bit in enumerate(order):
                found |= ((place >> (bits - 1 - step)) & 1) << bit
            return found ^ dev

        where = jnp.stack(
            [(ha == wa).astype(jnp.int32), (ha == 0).astype(jnp.int32), wa]
            + [chunk_of(place, order) for order in orders for place in range(n_dev)]
        ).astype(jnp.int32)

        order = Order()
        call = partial(kernel_call, order=order)

        def spread_rows(values):
            received = over_ha(values)
            oth = over_wa(jnp.where(ha == wa, received, values))
            return values, received, oth

        def later(values, event):
            return lax.optimization_barrier((values, event))[0]

        token_parts = spread_rows(tokens)
        small_own = jnp.concatenate([conv_taps.reshape(18, half), norm_gain, norm_shift], axis=0)
        small = (small_own, over_wa(small_own))

        def both_cores(values, event):
            return values, over_wa(later(values, event))

        wq_all = jnp.transpose(w_qkv, (0, 2, 1, 3))
        wq = [both_cores(wq_all[0], small[1])]
        wp = [both_cores(w_proj[0], small[1])]

        def unpack(where_ref, mine, received, oth):
            own = jnp.where(where_ref[0] == 1, mine[...], received[...])
            values = jnp.concatenate([own, oth[...]], axis=1)
            return mm(placement(images, False), values, 1, 0)

        def gain_row(refs, branch):
            return jnp.concatenate([ref[18 + branch : 19 + branch, :] for ref in refs], axis=1)

        def shift_row(refs, branch):
            return jnp.concatenate([ref[22 + branch : 23 + branch, :] for ref in refs], axis=1)

        def tap_rows(small_refs, section, col, flipped):
            ref = small_refs[col // half]
            at = col % half
            found = [
                ref[9 * section + t : 9 * section + t + 1, at : at + LANES] for t in range(9)
            ]
            return found[::-1] if flipped else found

        def project_in(normed, first, second):
            return mm(normed[:, :half], first, 1, 0) + mm(normed[:, half:], second, 1, 0)

        def project_back(values, first, second):
            return mm(values[:, :half], first, 1, 1) + mm(values[:, half:], second, 1, 1)

        def to_normed(stream, small_refs, branch):
            units, _ = norm_stats(stream)
            return (units * gain_row(small_refs, branch) + shift_row(small_refs, branch)).astype(
                BF16
            )

        def put_both(own_ref, oth_ref, values):
            own_ref[...] = values[:, :half]
            oth_ref[...] = values[:, half:]

        def add_parts(stream, part_a, part_b):
            return stream[...] + part_a[...].astype(F32) + part_b[...].astype(F32)

        def attention_part(window, normed, valid_rows, wq_a, wq_b, qkv_ref, probs_ref):
            packed = [
                project_in(normed, wq_a[part], wq_b[part]).astype(BF16)
                for part in range(3)
            ]
            for part in range(3):
                qkv_ref[part] = packed[part]
            wide = [part.astype(F32) for part in packed]
            mixed = []
            for image in range(images):
                line = []
                rows_at = slice(image * PADDED, (image + 1) * PADDED)
                for tile in range(tiles):
                    lanes_at = slice(tile * LANES, (tile + 1) * LANES)
                    q, k, v = (part[rows_at, lanes_at] for part in wide)
                    if window:
                        probs, out = window_tile(q, k, v)
                    else:
                        probs, out = channel_tile(q, k, v, valid_rows[image])
                    probs_ref[image * tiles + tile] = probs
                    line.append(out)
                mixed.append(jnp.concatenate(line, axis=1))
            return jnp.concatenate(mixed, axis=0).astype(BF16)

        def attention_part_back(window, grad_mixed, mask_ref, qkv_ref, probs_ref, dpk_ref):
            wide = [qkv_ref[part].astype(F32) for part in range(3)]
            grad = grad_mixed.astype(F32)
            found = [[], [], []]
            for image in range(images):
                lines = [[], [], []]
                for tile in range(tiles):
                    rows_at = slice(image * PADDED, (image + 1) * PADDED)
                    lanes_at = slice(tile * LANES, (tile + 1) * LANES)
                    q, k, v = (part[rows_at, lanes_at] for part in wide)
                    probs = probs_ref[image * tiles + tile]
                    if window:
                        parts = window_tile_back(q, k, v, probs, grad[rows_at, lanes_at])
                    else:
                        parts = channel_tile_back(
                            q, k, v, probs, grad[rows_at, lanes_at], mask_ref[rows_at, :]
                        )
                    for line, part in zip(lines, parts):
                        line.append(part)
                for part in range(3):
                    found[part].append(jnp.concatenate(lines[part], axis=1))
            packed = [jnp.concatenate(part, axis=0).astype(BF16) for part in found]
            for part in range(3):
                dpk_ref[part] = packed[part]
            return packed

        def mul_out(left, own_ref, oth_ref, out_ref):
            out_ref[:, :half] = mm(left, own_ref[...], 1, 0).astype(BF16)
            out_ref[:, half:] = mm(left, oth_ref[...], 1, 0).astype(BF16)

        def conv_into(out_ref, values, small_refs, section, keep):
            for col in range(0, width, LANES):
                taps = tap_rows(small_refs, section, col, False)
                out_ref[:, col : col + LANES] = conv_cols(values[:, col : col + LANES], taps, keep)

        def conv_back_into(out_ref, sums_ref, sums_at, grads, values, small_refs, section, keep):
            for col in range(0, width, LANES):
                lanes_at = slice(col, col + LANES)
                taps = tap_rows(small_refs, section, col, True)
                for t, total in enumerate(tap_sums(grads[:, lanes_at], values[:, lanes_at])):
                    sums_ref[sums_at + t : sums_at + t + 1, lanes_at] = total
                out_ref[:, lanes_at] = conv_cols(grads[:, lanes_at], taps, keep)

        window_probs = sds((images * tiles, PADDED, HEADS_TILE * PADDED))
        channel_probs = sds((images * tiles, LANES, LANES))
        full, full_low = sds((rows, width)), sds((rows, width), BF16)
        half_low = sds((rows, half), BF16)
        hid_low = sds((rows, hidden), BF16)
        qkv_low = sds((3, rows, heads_width), BF16)
        attn_flops = 2 * rows * (4 * width * heads_width)
        mlp_flops = 2 * rows * (2 * width * hidden)

        def first_body(
            where_ref, mine, received, far, small_a, small_b, wq_a, wq_b, wp_a, wp_b,
            x_ref, s_ref, n_own, n_oth, qkv_ref, probs_ref, mixed_ref, part_ref, keep_a, keep_b,
        ):
            keep_a[...], keep_b[...] = small_a[...], small_b[...]
            keep = column_mask(rows)
            stream = unpack(where_ref, mine, received, far)
            x_ref[...] = stream.astype(BF16)
            conv_into(s_ref, stream, (small_a, small_b), 0, keep)
            normed = to_normed(s_ref[...], (small_a, small_b), 0)
            put_both(n_own, n_oth, normed)
            mixed = attention_part(True, normed, None, wq_a, wq_b, qkv_ref, probs_ref)
            mixed_ref[...] = mixed
            mul_out(mixed, wp_a, wp_b, part_ref)

        (x0, s1, n0_own, n0_oth, qkv0, probs0, mixed0, part0, *small) = call(
            first_body, "attn_a",
            [where, *token_parts, *small, *wq[0], *wp[0]],
            [full_low, full, half_low, half_low, qkv_low, window_probs, half_low, full_low]
            + [sds((26, half))] * 2,
            flops=attn_flops,
        )
        far0 = over_ha(part0)
        wq.append(both_cores(later(wq_all[1], part0), part0))
        wp.append(both_cores(later(w_proj[1], part0), part0))
        wu = [both_cores(later(w_up[at], part0), part0) for at in range(2)]
        wd = [both_cores(later(w_down[at], part0), part0) for at in range(2)]
        cot_parts = spread_rows(later(cotangent, part0))
        keep_a = [x0, n0_own, n0_oth, qkv0, probs0, mixed0, s1]

        def mlp_body(
            s_in, part_a, part_b, small_a, small_b, wu_a, wu_b, wd_a, wd_b,
            s_ref, n_own, n_oth, hid_ref, slope_ref, part_ref,
        ):
            s_ref[...] = add_parts(s_in, part_a, part_b)
            normed = to_normed(s_ref[...], (small_a, small_b), 1)
            put_both(n_own, n_oth, normed)
            pre = project_in(normed, wu_a[...], wu_b[...])
            below, bell = gelu_parts(pre)
            hid = (pre * below).astype(BF16)
            hid_ref[...] = hid
            slope_ref[...] = below + pre * bell
            mul_out(hid, wd_a, wd_b, part_ref)

        (s2, n1_own, n1_oth, hid1, slope1, part1) = call(
            mlp_body, "mlp_b",
            [s1, part0, far0, *small, *wu[0], *wd[0]],
            [full, half_low, half_low, hid_low, sds((rows, hidden)), full_low],
            flops=mlp_flops, hold=[*keep_a, *wq[0], *wp[0]],
        )
        far1 = over_ha(part1)
        keep_b = [s2, n1_own, n1_oth, hid1, slope1]
        weights0 = [*wq[0], *wp[0], *wu[0], *wd[0]]

        def cot_body(where_ref, mine, received, far, wd_a, wd_b, g_own, g_oth, dhid_ref):
            grad = unpack(where_ref, mine, received, far).astype(BF16)
            put_both(g_own, g_oth, grad)
            dhid_ref[...] = project_back(grad, wd_a[...], wd_b[...]).astype(BF16)

        g3_own, g3_oth, dhid3 = call(
            cot_body, "cot_d",
            [where, *cot_parts, *wd[1]],
            [half_low, half_low, hid_low],
            flops=mlp_flops // 2, hold=[*keep_a, *keep_b, *small, *weights0],
        )

        def channel_body(
            where_ref, s_in, part_a, part_b, valid_ref, small_a, small_b,
            wq_a, wq_b, wp_a, wp_b,
            s_before, s_ref, n_own, n_oth, qkv_ref, probs_ref, mixed_ref, part_ref, mask_ref,
        ):
            keep = column_mask(rows)
            s_before[...] = jnp.where(keep, add_parts(s_in, part_a, part_b), 0.0)
            conv_into(s_ref, s_before, (small_a, small_b), 1, keep)
            normed = to_normed(s_ref[...], (small_a, small_b), 2)
            put_both(n_own, n_oth, normed)
            one_image = placement(1, False).astype(F32)
            valid_rows = []
            for image in range(images):
                line = jnp.where(
                    where_ref[2] == 0,
                    valid_ref[image : image + 1, :],
                    valid_ref[images + image : images + image + 1, :],
                ).astype(F32)
                valid_rows.append(jnp.sum(one_image * line, axis=1, keepdims=True))
                mask_ref[image * PADDED : (image + 1) * PADDED, :] = valid_rows[image]
            mixed = attention_part(False, normed, valid_rows, wq_a, wq_b, qkv_ref, probs_ref)
            mixed_ref[...] = mixed
            mul_out(mixed, wp_a, wp_b, part_ref)

        (s3, s4, n2_own, n2_oth, qkv2, probs2, mixed2, part2, mask) = call(
            channel_body, "attn_c",
            [where, s2, part1, far1, valid, *small, *wq[1], *wp[1]],
            [full, full, half_low, half_low, qkv_low, channel_probs, half_low, full_low,
             sds((rows, 1))],
            flops=attn_flops,
            hold=[*keep_a, *keep_b, g3_own, g3_oth, dhid3, *weights0, *wd[1]],
        )
        far2 = over_ha(part2)
        keep_c = [s3, s4, n2_own, n2_oth, qkv2, probs2, mixed2, mask]
        weights = [*weights0, *wq[1], *wp[1], *wu[1], *wd[1]]

        def last_body(
            s_in, part_a, part_b, small_a, small_b, dhid_ref, wu_a, wu_b,
            s_ref, n_own, n_oth, hid_ref, dpre_ref, part_ref,
        ):
            s_ref[...] = add_parts(s_in, part_a, part_b)
            normed = to_normed(s_ref[...], (small_a, small_b), 3)
            put_both(n_own, n_oth, normed)
            pre = project_in(normed, wu_a[...], wu_b[...])
            below, bell = gelu_parts(pre)
            hid_ref[...] = (pre * below).astype(BF16)
            dpre = (dhid_ref[...].astype(F32) * (below + pre * bell)).astype(BF16)
            dpre_ref[...] = dpre
            part_ref[:, :half] = mm(dpre, wu_a[...], 1, 1).astype(BF16)
            part_ref[:, half:] = mm(dpre, wu_b[...], 1, 1).astype(BF16)

        (s5, n3_own, n3_oth, hid3, dpre3, back3) = call(
            last_body, "mlp_d",
            [s4, part2, far2, *small, dhid3, *wu[1]],
            [full, half_low, half_low, hid_low, hid_low, full_low],
            flops=mlp_flops,
            hold=[*keep_a, *keep_b, *keep_c, g3_own, g3_oth, *weights0, *wq[1], *wp[1], *wd[1]],
        )
        far_back3 = over_ha(back3)

        def halve(kept, received, name, hold=()):
            cut = kept.shape[0] // 2

            def last_sum(kept_ref, received_ref, out_ref):
                out_ref[...] = kept_ref[0].astype(F32) + received_ref[0].astype(F32)

            def half_sum(kept_ref, received_ref, stay_ref, go_ref):
                for at in range(2 * cut):
                    total = (kept_ref[at].astype(F32) + received_ref[at].astype(F32)).astype(BF16)
                    (stay_ref if at < cut else go_ref)[at % cut] = total

            if cut == 0:
                return call(
                    last_sum, name, [kept, received], [sds(kept.shape[1:])], hold=hold
                )[0]
            return call(
                half_sum, name, [kept, received], [sds((cut,) + kept.shape[1:], BF16)] * 2, hold=hold
            )

        def scatter_chunks(scratch, where_ref, which, kept, sent):
            cut = n_dev // 2
            for at in range(n_dev):
                target = kept if at < cut else sent
                target[at % cut] = scratch[where_ref[3 + which * n_dev + at]].astype(BF16)

        up_rows, down_rows = hidden // n_dev, half // n_dev
        folds = hidden // half
        mlp_rows = up_rows + folds * down_rows

        def mlp_weights_body(
            where_ref, dpre_a, dpre_b, n_a, n_b, g_a, g_b, hid_a, hid_b, kept, sent, scratch
        ):
            up = mm(dpre_a[...], n_a[...], 0, 0) + mm(dpre_b[...], n_b[...], 0, 0)
            for chunk in range(n_dev):
                scratch[chunk, :up_rows, :] = up[chunk * up_rows : (chunk + 1) * up_rows]
            down = mm(g_a[...], hid_a[...], 0, 0) + mm(g_b[...], hid_b[...], 0, 0)
            for chunk in range(n_dev):
                for fold in range(folds):
                    at = up_rows + fold * down_rows
                    scratch[chunk, at : at + down_rows, :] = down[
                        chunk * down_rows : (chunk + 1) * down_rows,
                        fold * half : (fold + 1) * half,
                    ]
            scatter_chunks(scratch, where_ref, 0, kept, sent)

        def mlp_weights(dpre, n_own, n_oth, g_own, g_oth, hid, name, hold):
            return call(
                mlp_weights_body, name,
                [where, dpre, over_wa(dpre), n_own, over_wa(n_oth),
                 g_own, over_wa(g_oth), hid, over_wa(hid)],
                [sds((n_dev // 2, mlp_rows, half), BF16)] * 2,
                scratch=[pltpu.VMEM((n_dev, mlp_rows, half), F32)],
                flops=2 * 4 * rows * half * hidden, hold=hold,
            )

        qkv_rows, proj_rows = heads_width // n_dev, half // n_dev
        attn_rows = 3 * qkv_rows + proj_rows

        def attn_weights_body(
            where_ref, dpk_a, dpk_b, n_a, n_b, g_a, g_b, mix_a, mix_b, kept, sent, scratch
        ):
            for part in range(3):
                qkv = mm(dpk_a[part], n_a[...], 0, 0) + mm(dpk_b[part], n_b[...], 0, 0)
                for chunk in range(n_dev):
                    scratch[chunk, part * qkv_rows : (part + 1) * qkv_rows, :] = qkv[
                        chunk * qkv_rows : (chunk + 1) * qkv_rows
                    ]
            proj = mm(g_a[...], mix_a[...], 0, 0) + mm(g_b[...], mix_b[...], 0, 0)
            for chunk in range(n_dev):
                scratch[chunk, 3 * qkv_rows :, :] = proj[
                    chunk * proj_rows : (chunk + 1) * proj_rows
                ]
            scatter_chunks(scratch, where_ref, 1, kept, sent)

        def attn_weights(dpk, n_own, n_oth, g_own, g_oth, mixed, name, hold):
            return call(
                attn_weights_body, name,
                [where, dpk, over_wa(dpk), n_own, over_wa(n_oth),
                 g_own, over_wa(g_oth), mixed, over_wa(mixed)],
                [sds((n_dev // 2, attn_rows, half), BF16)] * 2,
                scratch=[pltpu.VMEM((n_dev, attn_rows, half), F32)],
                flops=2 * 2 * rows * half * 4 * heads_width, hold=hold,
            )

        def send(values, which, step):
            return over_dev(values, orders[which][step])

        def ship(total, kept, sent):
            packed = mm(placement(images, True), total.astype(BF16), 1, 0).astype(BF16)
            kept[...] = packed[:, :half]
            sent[...] = packed[:, half:]

        shipped = [sds((rows_in, half), BF16)] * 2

        def fold(where_ref, kept, received, stay, go):
            same = where_ref[0] == 1
            stay[...] = jnp.where(same, kept[...], received[...])
            go[...] = jnp.where(same, received[...], kept[...])

        def join(stay, received, out_ref):
            out_ref[...] = stay[...].astype(F32) + received[...].astype(F32)

        def out_body(where_ref, s_in, hid_ref, wd_a, wd_b, kept, sent):
            hid = hid_ref[...]
            base = jnp.where(where_ref[1] == 1, s_in[...], 0.0)
            branch = jnp.concatenate([mm(hid, wd_a[...], 1, 0), mm(hid, wd_b[...], 1, 0)], axis=1)
            ship(base + branch, kept, sent)

        kept_d, sent_d = mlp_weights(
            dpre3, n3_own, n3_oth, g3_own, g3_oth, hid3, "wgrad_d",
            [*keep_a, *keep_b, *keep_c, *small, *weights, s5],
        )
        got_d = send(sent_d, 0, 0)

        def add_norm_back(grad, part_a, part_b, stream, gain, sums_ref):
            upstream = part_a[...].astype(F32) + part_b[...].astype(F32)
            units, inv_std = norm_stats(stream)
            sums_ref[0:1, :] = jnp.sum(upstream * units, axis=0, keepdims=True)
            sums_ref[1:2, :] = jnp.sum(upstream, axis=0, keepdims=True)
            return grad + norm_back(upstream, units, inv_std, gain)

        def qkv_back(packed, wq_a, wq_b):
            return [
                sum(mm(packed[part], ref[part], 1, 1) for part in range(3)) for ref in (wq_a, wq_b)
            ]

        def channel_back_body(
            g_in_own, g_in_oth, part_a, part_b, s_in, small_a, small_b, mask_ref, qkv_ref,
            probs_ref, wp_a, wp_b, wq_a, wq_b, g_ref, g_own, g_oth, dpk_ref, part_ref, sums_ref,
        ):
            grad = jnp.concatenate([g_in_own[...], g_in_oth[...]], axis=1).astype(F32)
            gain = gain_row((small_a, small_b), 3)
            grad = add_norm_back(grad, part_a, part_b, s_in[...], gain, sums_ref)
            g_ref[...] = grad
            low = grad.astype(BF16)
            put_both(g_own, g_oth, low)
            grad_mixed = project_back(low, wp_a[...], wp_b[...]).astype(BF16)
            packed = attention_part_back(False, grad_mixed, mask_ref, qkv_ref, probs_ref, dpk_ref)
            own, oth = qkv_back(packed, wq_a, wq_b)
            part_ref[:, :half] = own.astype(BF16)
            part_ref[:, half:] = oth.astype(BF16)

        late = [hid3, *wd[1], s5]
        (g2, g2_own, g2_oth, dpk2, back2, sums3) = call(
            channel_back_body, "back_c",
            [g3_own, g3_oth, back3, far_back3, s5, *small, mask, qkv2, probs2, *wp[1], *wq[1]],
            [full, half_low, half_low, qkv_low, full_low, sds((2, width))],
            flops=attn_flops,
            hold=[*keep_a, *keep_b, s3, s4, n2_own, n2_oth, mixed2, *weights0, hid3, *wd[1]],
        )
        far_back2 = over_ha(back2)
        kept_c, sent_c = attn_weights(
            dpk2, n2_own, n2_oth, g2_own, g2_oth, mixed2, "wgrad_c",
            [*keep_a, *keep_b, s3, s4, *small, *weights0, g2, *late],
        )
        got_c = send(sent_c, 1, 0)

        def mlp_back_body(
            g_in, part_a, part_b, s_in, s_before, small_a, small_b, slope_ref,
            wd_a, wd_b, wu_a, wu_b, g_ref, g_own, g_oth, dpre_ref, part_ref, sums_ref,
        ):
            keep = column_mask(rows)
            gain = gain_row((small_a, small_b), 2)
            grad = add_norm_back(g_in[...], part_a, part_b, s_in[...], gain, sums_ref)
            conv_back_into(g_ref, sums_ref, 2, grad, s_before[...], (small_a, small_b), 1, keep)
            low = g_ref[...].astype(BF16)
            put_both(g_own, g_oth, low)
            dhid = project_back(low, wd_a[...], wd_b[...]).astype(BF16).astype(F32)
            dpre = (dhid * slope_ref[...]).astype(BF16)
            dpre_ref[...] = dpre
            part_ref[:, :half] = mm(dpre, wu_a[...], 1, 1).astype(BF16)
            part_ref[:, half:] = mm(dpre, wu_b[...], 1, 1).astype(BF16)

        (g1, g1_own, g1_oth, dpre1, back1, sums2) = call(
            mlp_back_body, "back_b",
            [g2, back2, far_back2, s4, s3, *small, slope1, *wd[0], *wu[0]],
            [full, half_low, half_low, hid_low, full_low, sds((11, width))],
            flops=mlp_flops, hold=[*keep_a, s2, n1_own, n1_oth, hid1, *wq[0], *wp[0], *late],
        )
        far_back1 = over_ha(back1)
        kept_b, sent_b = mlp_weights(
            dpre1, n1_own, n1_oth, g1_own, g1_oth, hid1, "wgrad_b",
            [*keep_a, s2, *small, *wq[0], *wp[0], g1, *late],
        )
        got_b = send(sent_b, 0, 0)

        def window_back_body(
            g_in, part_a, part_b, s_in, small_a, small_b, qkv_ref, probs_ref, wp_a, wp_b,
            g_ref, g_own, g_oth, dpk_ref, sums_ref,
        ):
            gain = gain_row((small_a, small_b), 1)
            grad = add_norm_back(g_in[...], part_a, part_b, s_in[...], gain, sums_ref)
            g_ref[...] = grad
            low = grad.astype(BF16)
            put_both(g_own, g_oth, low)
            grad_mixed = project_back(low, wp_a[...], wp_b[...]).astype(BF16)
            attention_part_back(True, grad_mixed, None, qkv_ref, probs_ref, dpk_ref)

        (g0, g0_own, g0_oth, dpk0, sums1) = call(
            window_back_body, "back_a",
            [g1, back1, far_back1, s2, *small, qkv0, probs0, *wp[0]],
            [full, half_low, half_low, qkv_low, sds((2, width))],
            flops=attn_flops, hold=[x0, n0_own, n0_oth, mixed0, s1, *wq[0], *late],
        )

        def first_back_body(
            where_ref, g_in, dpk_ref, s_in, x_ref, small_a, small_b, wq_a, wq_b,
            kept, sent, sums_ref, scratch,
        ):
            keep = column_mask(rows)
            packed = [dpk_ref[part] for part in range(3)]
            upstream = jnp.concatenate(qkv_back(packed, wq_a, wq_b), axis=1)
            units, inv_std = norm_stats(s_in[...])
            sums_ref[0:1, :] = jnp.sum(upstream * units, axis=0, keepdims=True)
            sums_ref[1:2, :] = jnp.sum(upstream, axis=0, keepdims=True)
            grad = jnp.where(where_ref[1] == 1, g_in[...], 0.0)
            grad = grad + norm_back(upstream, units, inv_std, gain_row((small_a, small_b), 0))
            conv_back_into(
                scratch, sums_ref, 2, grad, x_ref[...].astype(F32), (small_a, small_b), 0, keep
            )
            ship(scratch[...], kept, sent)

        token_kept, token_sent, sums0 = call(
            first_back_body, "back_0",
            [where, g0, dpk0, s1, x0, *small, *wq[0]],
            shipped + [sds((11, width))],
            scratch=[pltpu.VMEM((rows, width), F32)],
            flops=attn_flops * 3 // 4,
            hold=[n0_own, n0_oth, mixed0, g0_own, g0_oth, *late],
        )
        kept_a, sent_a = attn_weights(
            dpk0, n0_own, n0_oth, g0_own, g0_oth, mixed0, "wgrad_a", late
        )
        got_a = send(sent_a, 1, 0)
        token_stay, token_go = call(
            fold, "fold_tokens", [where, token_kept, over_wa(token_sent)], shipped, hold=late
        )
        token_got = over_ha(token_go)
        out_kept, out_sent = call(
            out_body, "out_d", [where, s5, hid3, *wd[1]], shipped, flops=mlp_flops // 2
        )
        out_stay, out_go = call(fold, "fold_out", [where, out_kept, over_wa(out_sent)], shipped)
        out_got = over_ha(out_go)

        sums = jnp.concatenate([sums0, 0.5 * sums1, 0.5 * sums2, 0.5 * sums3], axis=0)
        total = sums[:, :half] + over_wa(sums[:, half:])
        total = total + over_ha(total)

        kept_c, sent_c = halve(kept_c, got_c, "halve_c1")
        got_c = send(sent_c, 1, 1)
        kept_d, sent_d = halve(kept_d, got_d, "halve_d1")
        got_d = send(sent_d, 0, 1)
        owned = [sds((rows_in, half))]
        grad_tokens = call(join, "join_tokens", [token_stay, token_got], owned)[0]
        output = call(join, "join_out", [out_stay, out_got], owned)[0]
        kept_c, sent_c = halve(kept_c, got_c, "halve_c2")
        got_c = send(sent_c, 1, 2)
        kept_d, sent_d = halve(kept_d, got_d, "halve_d2")
        got_d = send(sent_d, 0, 2)
        kept_a, sent_a = halve(kept_a, got_a, "halve_a1")
        got_a = send(sent_a, 1, 1)
        kept_b, sent_b = halve(kept_b, got_b, "halve_b1")
        got_b = send(sent_b, 0, 1)
        kept_a, sent_a = halve(kept_a, got_a, "halve_a2")
        got_a = send(sent_a, 1, 2)
        kept_b, sent_b = halve(kept_b, got_b, "halve_b2")
        got_b = send(sent_b, 0, 2)
        for step in range(3, bits):
            kept_c, sent_c = halve(kept_c, got_c, f"halve_c{step}")
            got_c = send(sent_c, 1, step)
            kept_d, sent_d = halve(kept_d, got_d, f"halve_d{step}")
            got_d = send(sent_d, 0, step)
            kept_a, sent_a = halve(kept_a, got_a, f"halve_a{step}")
            got_a = send(sent_a, 1, step)
            kept_b, sent_b = halve(kept_b, got_b, f"halve_b{step}")
            got_b = send(sent_b, 0, step)
        sum_c = halve(kept_c, got_c, "halve_c")
        sum_d = halve(kept_d, got_d, "halve_d")
        sum_a = halve(kept_a, got_a, "halve_a")
        sum_b = halve(kept_b, got_b, "halve_b")

        for bit in range(bits):
            total = total + over_dev(total, bit)
        gain_at, shift_at = (0, 11, 13, 24), (1, 12, 14, 25)
        grad_gain = jnp.stack([total[at] for at in gain_at])
        grad_shift = jnp.stack([total[at] for at in shift_at])
        grad_taps = jnp.stack([total[2:11], total[15:24]])

        def down_of(total):
            down = total[up_rows:].reshape(folds, down_rows, half)
            return jnp.transpose(down, (1, 0, 2)).reshape(down_rows, hidden)

        def qkv_of(total):
            return total[: 3 * qkv_rows].reshape(3, qkv_rows, half)

        grad_qkv = jnp.transpose(jnp.stack([qkv_of(sum_a), qkv_of(sum_c)]), (0, 3, 1, 2))
        grad_proj = jnp.transpose(
            jnp.stack([sum_a[3 * qkv_rows :], sum_c[3 * qkv_rows :]]), (0, 2, 1)
        )
        grad_up = jnp.transpose(jnp.stack([sum_b[:up_rows], sum_d[:up_rows]]), (0, 2, 1))
        grad_down = jnp.transpose(jnp.stack([down_of(sum_b), down_of(sum_d)]), (0, 2, 1))
        return (
            output,
            grad_tokens,
            grad_taps,
            grad_gain,
            grad_shift,
            grad_qkv,
            grad_proj,
            grad_up,
            grad_down,
        )

    placed = (
        P(("dev", "ha"), "wa"),
        P(("dev", "ha"), "wa"),
        P(None, None, "wa"),
        P(None, "wa"),
        P(None, "wa"),
        P(None, "wa", None, "ha"),
        P(None, "ha", "wa"),
        P(None, "wa", "ha"),
        P(None, "ha", "wa"),
        P("dev", None),
    )
    return jax.shard_map(
        on_device,
        mesh=mesh,
        in_specs=placed,
        out_specs=(
            P(("dev", "ha"), "wa"),
            P(("dev", "ha"), "wa"),
            P(None, None, "wa"),
            P(None, "wa"),
            P(None, "wa"),
            P(None, "wa", None, ("ha", "dev")),
            P(None, "ha", ("wa", "dev")),
            P(None, "wa", ("ha", "dev")),
            P(None, "ha", ("wa", "dev")),
        ),
        check_vma=False,
    )
```

time: 285 us -> 196 us (0.69)
  waiting for transfers between devices: 139 us -> 89.4 us
  local copies, waits for them, and re-layouts: 40 us -> 13.7 us
  starting transfers between devices: 50.7 us -> 46 us
  Pallas kernels: 44.1 us -> 39.5 us
  other arithmetic: 8.44 us -> 5.29 us
    ppermute x15, waiting for transfers between devices: 94.2 us -> 48.9 us  [over_dev(): lax.ppermute(values, 'dev', [(i, i ^ 1 << bit) for i in range(n_dev)])]
    unnamed x204 -> x30, local copies, waits for them, and re-layouts: 37.6 us -> 4.9 us
    ppermute x8 -> x0, waiting for transfers between devices: 8.32 us -> none  [the longest x1 4.29 us: on_device(): near_cot = lax.ppermute(cotangent, pair, near_in)]
    squeeze x0 -> x4, local copies, waits for them, and re-layouts: none -> 8.03 us  [the longest x1 2.88 us: on_device(): wd = [both_cores(later(w_down[at], part0), part0) for at in range(2)]]
    ppermute x8 -> x0, starting transfers between devices: 7.55 us -> none  [the longest x1 2.89 us: on_device(): near_tokens = lax.ppermute(tokens, pair, near_in)]
    pallas_call x16 -> x30, Pallas kernels: 44.1 us -> 39.5 us  [kernel_call(): pl.pallas_call(wrapped, in_specs=specs, out_specs=[pl.BlockSpec(memory_sp...]
    ppermute x7 -> x11, starting transfers between devices: 12.6 us -> 17 us  [over_ha(): return lax.ppermute(values, 'ha', swap)]
    ppermute x22 -> x30, waiting for transfers between devices: 2.92 us -> 5.85 us  [over_wa(): return lax.ppermute(values, 'wa', swap)]
  transfers between devices with their start and end apart: 52 -> 56, of which waited for: 19 -> 22; matrix products, arithmetic and copies ran while one was open for 4% -> 6% of each run, Pallas kernels for 10% -> 15%
where the time goes in v2:
time: 196 us; the launch traced here: 195 us
  waiting for transfers between devices  89.4 us (46%)
  starting transfers between devices  46 us (23%)
  Pallas kernels  39.5 us (20%)
  local copies, waits for them, and re-layouts  13.7 us (7%)
  other arithmetic  5.29 us (3%)
    ppermute x15, waiting for transfers between devices, over_dev(): lax.ppermute(values, 'dev', [(i, i ^ 1 << bit) for i in range(n_dev)])  48.9 us
    pallas_call x30, Pallas kernels, kernel_call(): pl.pallas_call(wrapped, in_specs=specs, out_specs=[pl.BlockSpec(memory_sp...  39.5 us
    ppermute x11, waiting for transfers between devices, over_ha(): return lax.ppermute(values, 'ha', swap)  34.7 us
    ppermute x15, starting transfers between devices, over_dev(): lax.ppermute(values, 'dev', [(i, i ^ 1 << bit) for i in range(n_dev)])  21.1 us
    ppermute x11, starting transfers between devices, over_ha(): return lax.ppermute(values, 'ha', swap)  17 us
    ppermute x30, starting transfers between devices, over_wa(): return lax.ppermute(values, 'wa', swap)  7.9 us
    ppermute x30, waiting for transfers between devices, over_wa(): return lax.ppermute(values, 'wa', swap)  5.85 us
    unnamed x30, local copies, waits for them, and re-layouts  4.9 us
  transfers between devices with their start and end apart: 56, of which 22 were waited for; matrix products, arithmetic and copies ran while one was open for 6% of the time, Pallas kernels for 15%

profile of v2, /device:TPU:0, one launch (start us, length us, event | category | flops | bytes accessed | tf_op | source)
XLA Modules:
  0.0 195.1 jit_solution(9933508415852429710)
XLA Ops:
  2.7 2.6 %collective-permute-start = (bf16[147,384]{1,0:T(8,128)(2,1)}, bf16[147,384]{1,0:T(8,128)(2,1)S(1)}, u32[]{:S(2)}, u32[]{:S(2)}) collective-permute-start(bf16[147,384]{1,0:T(8,128)(2,1)} %refs_1_.1), channel_id=1, source_target_pairs={{0,2},{2,0},{1,3},{3,1},{4,6},{6,4},{5,7},{7,5},{8,10},{10,8},{9,1... | collective-permute-start | bytes 338696 | tf_op jit(solution)/shard_map/ppermute | solution.py:241
  5.3 2.6 %slice_bitcast_fusion.4 = (bf16[3,384,384]{2,1,0:T(8,128)(2,1)}, bf16[3,384,384]{2,1,0:T(8,128)(2,1)S(1)}) fusion(bf16[2,3,384,384]{3,2,1,0:T(8,128)(2,1)} %bitcast.56), kind=kLoop, calls=%fused_computation.4 | loop fusion | bytes 3538944 | tf_op jit(solution)/shard_map/squeeze | solution.py:433
  10.1 2.9 %slice_bitcast_fusion.1 = (bf16[1536,384]{1,0:T(8,128)(2,1)S(1)}, bf16[1536,384]{1,0:T(8,128)(2,1)}) fusion(bf16[2,1536,384]{2,1,0:T(8,128)(2,1)} %param.18), kind=kLoop, calls=%fused_computation.1 | loop fusion | bytes 4718592 | tf_op jit(solution)/shard_map/squeeze | solution.py:436
  16.6 4.7 %attn_a.1 = (bf16[168,768]{1,0:T(8,128)(2,1)S(1)}, f32[168,768]{1,0:T(8,128)S(1)}, bf16[168,384]{1,0:T(8,128)(2,1)S(1)}, bf16[168,384]{1,0:T(8,128)(2,1)S(1)}, b...) custom-call(s32[19]{0:T(128)S(1)} %stack.102.refs_0_, ...), custom_call_target="tpu_custom_call" | custom-call | tf_op jit(solution)/shard_map/attn_a/pallas_call | solution.py:55
  26.1 8.9 %collective-permute-done.11.refs_2_ = bf16[147,384]{1,0:T(8,128)(2,1)S(1)} collective-permute-done((bf16[147,384]{1,0:T(8,128)(2,1)S(1)}, bf16[147,384]{1,0:T(8,128)(2,1)S(1)}, u32[]{:S(2)}, u32[]{:S(2)}) %collective-permute-start.11) | collective-permute-done | bytes 112928 | tf_op jit(solution)/shard_map/ppermute | solution.py:241
  42.5 5.1 %collective-permute-done.8.refs_3_ = bf16[168,768]{1,0:T(8,128)(2,1)S(1)} collective-permute-done((bf16[168,768]{1,0:T(8,128)(2,1)S(1)}, bf16[168,768]{1,0:T(8,128)(2,1)S(1)}, u32[]{:S(2)}, u32[]{:S(2)}) %collective-permute-start.8) | collective-permute-done | bytes 258080 | tf_op jit(solution)/shard_map/ppermute | solution.py:241
  47.6 2.6 %attn_c.1 = (f32[168,768]{1,0:T(8,128)S(1)}, f32[168,768]{1,0:T(8,128)S(1)}, bf16[168,384]{1,0:T(8,128)(2,1)S(1)}, bf16[168,384]{1,0:T(8,128)(2,1)S(1)}, bf16[3,...) custom-call(s32[19]{0:T(128)S(1)} %stack.102.refs_0_, ...), custom_call_target="tpu_custom_call" | custom-call | tf_op jit(solution)/shard_map/attn_c/pallas_call | solution.py:55
  51.8 5.9 %collective-permute-done.14.refs_2_ = bf16[168,768]{1,0:T(8,128)(2,1)S(1)} collective-permute-done((bf16[168,768]{1,0:T(8,128)(2,1)S(1)}, bf16[168,768]{1,0:T(8,128)(2,1)S(1)}, u32[]{:S(2)}, u32[]{:S(2)}) %collective-permute-start.14) | collective-permute-done | bytes 258080 | tf_op jit(solution)/shard_map/ppermute | solution.py:241
  63.8 2.6 %wgrad_d.1 = (bf16[4,384,384]{2,1,0:T(8,128)(2,1)S(1)}, bf16[4,384,384]{2,1,0:T(8,128)(2,1)S(1)}, f32[8,128]{1,0:T(8,128)S(1)}) custom-call(s32[19]{0:T(128)S(1)} %stack.102.refs_0_, bf16[168,1536]{1,0:T(8,128)(2,1)S(1)} %get-tuple-element.193.refs_1_, bf16[168,1536]{1,0:T(8,128)(2,1)S(1)} %collective-permute-done.17.refs_2_, ...), custom_call_target="tpu_custom_call" | custom-call | tf_op jit(solution)/shard_map/wgrad_d/pallas_call | solution.py:55
  68.9 2.9 %back_c.1 = (f32[168,768]{1,0:T(8,128)S(1)}, bf16[168,384]{1,0:T(8,128)(2,1)S(1)}, bf16[168,384]{1,0:T(8,128)(2,1)S(1)}, bf16[3,168,384]{2,1,0:T(8,128)(2,1)S(1)...) custom-call(bf16[168,384]{1,0:T(8,128)(2,1)S(1)} %get-tuple-element.174.refs_23_.refs_28_.refs_5_.refs_0_, ...), custom_call_target="tpu_custom_call" | custom-call | tf_op jit(solution)/shard_map/back_c/pallas_call | solution.py:55
  80.6 2.8 %back_b.1 = (f32[168,768]{1,0:T(8,128)S(1)}, bf16[168,384]{1,0:T(8,128)(2,1)S(1)}, bf16[168,384]{1,0:T(8,128)(2,1)S(1)}, bf16[168,1536]{1,0:T(8,128)(2,1)S(1)}, ...) custom-call(f32[168,768]{1,0:T(8,128)S(1)} %get-tuple-element.198.refs_33_.refs_0_, ...), custom_call_target="tpu_custom_call" | custom-call | tf_op jit(solution)/shard_map/back_b/pallas_call | solution.py:55
  93.9 2.8 %back_a.1 = (f32[168,768]{1,0:T(8,128)S(1)}, bf16[168,384]{1,0:T(8,128)(2,1)S(1)}, bf16[168,384]{1,0:T(8,128)(2,1)S(1)}, bf16[3,168,384]{2,1,0:T(8,128)(2,1)S(1)...) custom-call(f32[168,768]{1,0:T(8,128)S(1)} %get-tuple-element.205.refs_23_.refs_0_, ...), custom_call_target="tpu_custom_call" | custom-call | tf_op jit(solution)/shard_map/back_a/pallas_call | solution.py:55
  98.9 2.7 %back_0.1 = (bf16[147,384]{1,0:T(8,128)(2,1)S(1)}, bf16[147,384]{1,0:T(8,128)(2,1)S(1)}, f32[11,768]{1,0:T(8,128)S(1)}, f32[8,128]{1,0:T(8,128)S(1)}) custom-call(s32[19]{0:T(128)S(1)} %stack.102.refs_0_, f32[168,768]{1,0:T(8,128)S(1)} %get-tuple-element.212.refs_1_, bf16[3,168,384]{2,1,0:T(8,128)(2,1)S(1)} %get-tuple-element.213.refs_2_.refs_1_, ...), custom_call_target="tpu_custom_call" | custom-call | tf_op jit(solution)/shard_map/back_0/pallas_call | solution.py:55
  111.7 2.6 %collective-permute-done.42 = f32[26,384]{1,0:T(8,128)S(1)} collective-permute-done((f32[26,384]{1,0:T(8,128)S(1)}, f32[26,384]{1,0:T(8,128)S(1)}, u32[]{:S(2)}, u32[]{:S(2)}) %collective-permute-start.42) | collective-permute-done | bytes 39968 | tf_op jit(solution)/shard_map/ppermute | solution.py:241
  114.9 15.5 %collective-permute-done.43 = f32[26,384]{1,0:T(8,128)S(1)} collective-permute-done((f32[26,384]{1,0:T(8,128)S(1)}, f32[26,384]{1,0:T(8,128)S(1)}, u32[]{:S(2)}, u32[]{:S(2)}) %collective-permute-start.43) | collective-permute-done | bytes 39968 | tf_op jit(solution)/shard_map/ppermute | solution.py:247
  133.6 2.7 %collective-permute-done.44 = f32[26,384]{1,0:T(8,128)S(1)} collective-permute-done((f32[26,384]{1,0:T(8,128)S(1)}, f32[26,384]{1,0:T(8,128)S(1)}, u32[]{:S(2)}, u32[]{:S(2)}) %collective-permute-start.44) | collective-permute-done | bytes 39968 | tf_op jit(solution)/shard_map/ppermute | solution.py:247
  136.2 2.7 %collective-permute-start.45 = (f32[26,384]{1,0:T(8,128)S(1)}, f32[26,384]{1,0:T(8,128)S(1)}, u32[]{:S(2)}, u32[]{:S(2)}) collective-permute-start(f32[26,384]{1,0:T(8,128)S(1)} %add.18), channel_id=1, source_target_pairs={{0,16},{4,20},{8,24},{12,28},{16,0},{20,4},{24,8},{28,12},{1,17},{... | collective-permute-start | bytes 119816 | tf_op jit(solution)/shard_map/ppermute | solution.py:247
  138.9 2.5 %collective-permute-done.45 = f32[26,384]{1,0:T(8,128)S(1)} collective-permute-done((f32[26,384]{1,0:T(8,128)S(1)}, f32[26,384]{1,0:T(8,128)S(1)}, u32[]{:S(2)}, u32[]{:S(2)}) %collective-permute-start.45) | collective-permute-done | bytes 39968 | tf_op jit(solution)/shard_map/ppermute | solution.py:247
  142.9 3.6 %collective-permute-done.38.refs_1_ = bf16[147,384]{1,0:T(8,128)(2,1)S(1)} collective-permute-done((bf16[147,384]{1,0:T(8,128)(2,1)S(1)}, bf16[147,384]{1,0:T(8,128)(2,1)S(1)}, u32[]{:S(2)}, u32[]{:S(2)}) %collective-permute-start.38) | collective-permute-done | bytes 112928 | tf_op jit(solution)/shard_map/ppermute | solution.py:241
  148.7 2.6 %collective-permute-done.37.refs_1_ = bf16[147,384]{1,0:T(8,128)(2,1)S(1)} collective-permute-done((bf16[147,384]{1,0:T(8,128)(2,1)S(1)}, bf16[147,384]{1,0:T(8,128)(2,1)S(1)}, u32[]{:S(2)}, u32[]{:S(2)}) %collective-permute-start.37) | collective-permute-done | bytes 112928 | tf_op jit(solution)/shard_map/ppermute | solution.py:241
  154.7 3.0 %collective-permute-start.52 = (bf16[1,384,384]{2,1,0:T(8,128)(2,1)S(1)}, bf16[1,384,384]{2,1,0:T(8,128)(2,1)S(1)}, u32[]{:S(2)}, u32[]{:S(2)}) collective-permute-start(bf16[1,384,384]{2,1,0:T(8,128)(2,1)S(1)} %get-tuple-element.261), channel_id=1, source_target_pairs={{0,16},{4,20},{8,24},{12,28},{16,0},{20,4},{24,8},{28,12},{1,17},{... | collective-permute-start | bytes 884744 | tf_op jit(solution)/shard_map/ppermute | solution.py:247
  163.0 13.7 %collective-permute-done.54.refs_1_ = bf16[2,384,384]{2,1,0:T(8,128)(2,1)S(1)} collective-permute-done((bf16[2,384,384]{2,1,0:T(8,128)(2,1)S(1)}, bf16[2,384,384]{2,1,0:T(8,128)(2,1)S(1)}, u32[]{:S(2)}, u32[]{:S(2)}) %collective-permute-start.54) | collective-permute-done | bytes 589856 | tf_op jit(solution)/shard_map/ppermute | solution.py:247
  177.5 8.5 %collective-permute-done.51.refs_1_ = bf16[1,192,384]{2,1,0:T(8,128)(2,1)S(1)} collective-permute-done((bf16[1,192,384]{2,1,0:T(8,128)(2,1)S(1)}, bf16[1,192,384]{2,1,0:T(8,128)(2,1)S(1)}, u32[]{:S(2)}, u32[]{:S(2)}) %collective-permute-start.51) | collective-permute-done | bytes 147488 | tf_op jit(solution)/shard_map/ppermute | solution.py:247
  187.6 4.6 %collective-permute-done.55.refs_1_ = bf16[1,384,384]{2,1,0:T(8,128)(2,1)S(1)} collective-permute-done((bf16[1,384,384]{2,1,0:T(8,128)(2,1)S(1)}, bf16[1,384,384]{2,1,0:T(8,128)(2,1)S(1)}, u32[]{:S(2)}, u32[]{:S(2)}) %collective-permute-start.55) | collective-permute-done | bytes 294944 | tf_op jit(solution)/shard_map/ppermute | solution.py:247
  (183 shorter events, 82.7 us)
Async XLA Ops:
  21.3 14.2 %collective-permute-start.7 = (bf16[1536,384]{1,0:T(8,128)(2,1)S(1)}, bf16[1536,384]{1,0:T(8,128)(2,1)S(1)}, u32[]{:S(2)}, u32[]{:S(2)}) collective-permute-start(bf16[1536,384]{1,0:T(8,128)(2,1)S(1)} %copy-done), channel_id=1, source_target_pairs={{0,1},{1,0},{2,3},{3,2},{4,5},{5,4},{6,7},{7,6},{8,9},{9,8},{10,11... | collective-permute-start | bytes 3538952 | tf_op jit(solution)/shard_map/ppermute | solution.py:244
  23.5 12.2 %collective-permute-start.6 = (bf16[384,1536]{1,0:T(8,128)(2,1)S(1)}, bf16[384,1536]{1,0:T(8,128)(2,1)S(1)}, u32[]{:S(2)}, u32[]{:S(2)}) collective-permute-start(bf16[384,1536]{1,0:T(8,128)(2,1)S(1)} %get-tuple-element.150.refs_5_.refs_24_.refs_30_.refs_34_.refs_35_.refs_29_.refs_10_), channel_id=1, source_target_pairs={{0,1},{1,0},{2,3},{3,2},{4,5},{5,4},{6,7},{7,6},{8,9},{9,8},{10,11... | collective-permute-start | bytes 3538952 | tf_op jit(solution)/shard_map/ppermute | solution.py:244
  23.9 17.0 %collective-permute-start.13 = (bf16[1536,384]{1,0:T(8,128)(2,1)S(1)}, bf16[1536,384]{1,0:T(8,128)(2,1)S(1)}, u32[]{:S(2)}, u32[]{:S(2)}) collective-permute-start(bf16[1536,384]{1,0:T(8,128)(2,1)S(1)} %get-tuple-element.172.refs_4_.refs_34_.refs_42_.refs_45_.refs_40_.refs_35_.refs_28_.refs_25_.refs_18_.refs_, ...), channel_id=1, source_target_pairs={{0,1},{1,0},{2,3},{3,2},{4,5},{5,4},{6,7},{7,6},{8,9},{9,8},{10,11... | collective-permute-start | bytes 3538952 | tf_op jit(solution)/shard_map/ppermute | solution.py:244
  24.1 10.9 %collective-permute-start.5 = (bf16[168,768]{1,0:T(8,128)(2,1)S(1)}, bf16[168,768]{1,0:T(8,128)(2,1)S(1)}, u32[]{:S(2)}, u32[]{:S(2)}) collective-permute-start(bf16[168,768]{1,0:T(8,128)(2,1)S(1)} %get-tuple-element.146.refs_1_), channel_id=1, source_target_pairs={{0,2},{2,0},{1,3},{3,1},{4,6},{6,4},{5,7},{7,5},{8,10},{10,8},{9,1... | collective-permute-start | bytes 774152 | tf_op jit(solution)/shard_map/ppermute | solution.py:241
  25.8 9.2 %collective-permute-start.11 = (bf16[147,384]{1,0:T(8,128)(2,1)S(1)}, bf16[147,384]{1,0:T(8,128)(2,1)S(1)}, u32[]{:S(2)}, u32[]{:S(2)}) collective-permute-start(bf16[147,384]{1,0:T(8,128)(2,1)S(1)} %copy-done.7), channel_id=1, source_target_pairs={{0,2},{2,0},{1,3},{3,1},{4,6},{6,4},{5,7},{7,5},{8,10},{10,8},{9,1... | collective-permute-start | bytes 338696 | tf_op jit(solution)/shard_map/ppermute | solution.py:241
  35.0 16.8 %collective-permute-start.15 = (bf16[384,1536]{1,0:T(8,128)(2,1)S(1)}, bf16[384,1536]{1,0:T(8,128)(2,1)S(1)}, u32[]{:S(2)}, u32[]{:S(2)}) collective-permute-start(bf16[384,1536]{1,0:T(8,128)(2,1)S(1)} %get-tuple-element.181.refs_6_.refs_43_), channel_id=1, source_target_pairs={{0,1},{1,0},{2,3},{3,2},{4,5},{5,4},{6,7},{7,6},{8,9},{9,8},{10,11... | collective-permute-start | bytes 3538952 | tf_op jit(solution)/shard_map/ppermute | solution.py:244
  39.3 8.3 %collective-permute-start.8 = (bf16[168,768]{1,0:T(8,128)(2,1)S(1)}, bf16[168,768]{1,0:T(8,128)(2,1)S(1)}, u32[]{:S(2)}, u32[]{:S(2)}) collective-permute-start(bf16[168,768]{1,0:T(8,128)(2,1)S(1)} %get-tuple-element.161.refs_2_), channel_id=1, source_target_pairs={{0,2},{2,0},{1,3},{3,1},{4,6},{6,4},{5,7},{7,5},{8,10},{10,8},{9,1... | collective-permute-start | bytes 774152 | tf_op jit(solution)/shard_map/ppermute | solution.py:241
  60.7 8.2 %collective-permute-start.16 = (bf16[168,768]{1,0:T(8,128)(2,1)S(1)}, bf16[168,768]{1,0:T(8,128)(2,1)S(1)}, u32[]{:S(2)}, u32[]{:S(2)}) collective-permute-start(bf16[168,768]{1,0:T(8,128)(2,1)S(1)} %get-tuple-element.192.refs_2_), channel_id=1, source_target_pairs={{0,2},{2,0},{1,3},{3,1},{4,6},{6,4},{5,7},{7,5},{8,10},{10,8},{9,1... | collective-permute-start | bytes 774152 | tf_op jit(solution)/shard_map/ppermute | solution.py:241
  74.0 13.2 %collective-permute-start.30 = (bf16[168,1536]{1,0:T(8,128)(2,1)S(1)}, bf16[168,1536]{1,0:T(8,128)(2,1)S(1)}, u32[]{:S(2)}, u32[]{:S(2)}) collective-permute-start(bf16[168,1536]{1,0:T(8,128)(2,1)S(1)} %get-tuple-element.168.refs_16_.refs_21_.refs_18_.refs_19_.refs_24_.refs_22_.refs_7_), channel_id=1, source_target_pairs={{0,1},{1,0},{2,3},{3,2},{4,5},{5,4},{6,7},{7,6},{8,9},{9,8},{10,11... | collective-permute-start | bytes 1548296 | tf_op jit(solution)/shard_map/ppermute | solution.py:244
  76.1 33.2 %collective-permute-start.39 = (bf16[4,384,384]{2,1,0:T(8,128)(2,1)S(1)}, bf16[4,384,384]{2,1,0:T(8,128)(2,1)S(1)}, u32[]{:S(2)}, u32[]{:S(2)}) collective-permute-start(bf16[4,384,384]{2,1,0:T(8,128)(2,1)S(1)} %get-tuple-element.230), channel_id=1, source_target_pairs={{0,4},{4,0},{8,12},{12,8},{16,20},{20,16},{24,28},{28,24},{1,5},{5... | collective-permute-start | bytes 3538952 | tf_op jit(solution)/shard_map/ppermute | solution.py:247
  85.6 8.3 %collective-permute-start.26 = (bf16[168,768]{1,0:T(8,128)(2,1)S(1)}, bf16[168,768]{1,0:T(8,128)(2,1)S(1)}, u32[]{:S(2)}, u32[]{:S(2)}) collective-permute-start(bf16[168,768]{1,0:T(8,128)(2,1)S(1)} %get-tuple-element.206.refs_1_), channel_id=1, source_target_pairs={{0,2},{2,0},{1,3},{3,1},{4,6},{6,4},{5,7},{7,5},{8,10},{10,8},{9,1... | collective-permute-start | bytes 774152 | tf_op jit(solution)/shard_map/ppermute | solution.py:241
  87.2 9.6 %collective-permute-start.35 = (bf16[168,384]{1,0:T(8,128)(2,1)S(1)}, bf16[168,384]{1,0:T(8,128)(2,1)S(1)}, u32[]{:S(2)}, u32[]{:S(2)}) collective-permute-start(bf16[168,384]{1,0:T(8,128)(2,1)S(1)} %get-tuple-element.158.refs_14_.refs_11_.refs_16_.refs_13_.refs_19_.refs_17_.refs_7_), channel_id=1, source_target_pairs={{0,1},{1,0},{2,3},{3,2},{4,5},{5,4},{6,7},{7,6},{8,9},{9,8},{10,11... | collective-permute-start | bytes 387080 | tf_op jit(solution)/shard_map/ppermute | solution.py:244
  87.2 10.1 %collective-permute-start.33 = (bf16[168,384]{1,0:T(8,128)(2,1)S(1)}, bf16[168,384]{1,0:T(8,128)(2,1)S(1)}, u32[]{:S(2)}, u32[]{:S(2)}) collective-permute-start(bf16[168,384]{1,0:T(8,128)(2,1)S(1)} %get-tuple-element.155.refs_11_.refs_8_.refs_13_.refs_10_.refs_16_.refs_14_.refs_12_), channel_id=1, source_target_pairs={{0,1},{1,0},{2,3},{3,2},{4,5},{5,4},{6,7},{7,6},{8,9},{9,8},{10,11... | collective-permute-start | bytes 387080 | tf_op jit(solution)/shard_map/ppermute | solution.py:244
  87.7 21.4 %collective-permute-start.40 = (bf16[4,192,384]{2,1,0:T(8,128)(2,1)S(1)}, bf16[4,192,384]{2,1,0:T(8,128)(2,1)S(1)}, u32[]{:S(2)}, u32[]{:S(2)}) collective-permute-start(bf16[4,192,384]{2,1,0:T(8,128)(2,1)S(1)} %get-tuple-element.232), channel_id=1, source_target_pairs={{0,8},{4,12},{8,0},{12,4},{16,24},{20,28},{24,16},{28,20},{1,9},{5... | collective-permute-start | bytes 1769480 | tf_op jit(solution)/shard_map/ppermute | solution.py:247
  97.3 55.7 %collective-permute-start.50 = (bf16[4,384,384]{2,1,0:T(8,128)(2,1)S(1)}, bf16[4,384,384]{2,1,0:T(8,128)(2,1)S(1)}, u32[]{:S(2)}, u32[]{:S(2)}) collective-permute-start(bf16[4,384,384]{2,1,0:T(8,128)(2,1)S(1)} %get-tuple-element.255), channel_id=1, source_target_pairs={{0,4},{4,0},{8,12},{12,8},{16,20},{20,16},{24,28},{28,24},{1,5},{5... | collective-permute-start | bytes 3538952 | tf_op jit(solution)/shard_map/ppermute | solution.py:247
  106.9 45.4 %collective-permute-start.46 = (bf16[4,192,384]{2,1,0:T(8,128)(2,1)S(1)}, bf16[4,192,384]{2,1,0:T(8,128)(2,1)S(1)}, u32[]{:S(2)}, u32[]{:S(2)}) collective-permute-start(bf16[4,192,384]{2,1,0:T(8,128)(2,1)S(1)} %get-tuple-element.244), channel_id=1, source_target_pairs={{0,8},{4,12},{8,0},{12,4},{16,24},{20,28},{24,16},{28,20},{1,9},{5... | collective-permute-start | bytes 1769480 | tf_op jit(solution)/shard_map/ppermute | solution.py:247
  109.6 42.5 %collective-permute-start.47 = (bf16[2,384,384]{2,1,0:T(8,128)(2,1)S(1)}, bf16[2,384,384]{2,1,0:T(8,128)(2,1)S(1)}, u32[]{:S(2)}, u32[]{:S(2)}) collective-permute-start(bf16[2,384,384]{2,1,0:T(8,128)(2,1)S(1)} %get-tuple-element.246), channel_id=1, source_target_pairs={{0,8},{4,12},{8,0},{12,4},{16,24},{20,28},{24,16},{28,20},{1,9},{5... | collective-permute-start | bytes 1769480 | tf_op jit(solution)/shard_map/ppermute | solution.py:247
  114.3 16.1 %collective-permute-start.43 = (f32[26,384]{1,0:T(8,128)S(1)}, f32[26,384]{1,0:T(8,128)S(1)}, u32[]{:S(2)}, u32[]{:S(2)}) collective-permute-start(f32[26,384]{1,0:T(8,128)S(1)} %add.16), channel_id=1, source_target_pairs={{0,4},{4,0},{8,12},{12,8},{16,20},{20,16},{24,28},{28,24},{1,5},{5... | collective-permute-start | bytes 119816 | tf_op jit(solution)/shard_map/ppermute | solution.py:247
  132.1 20.0 %collective-permute-start.48 = (bf16[2,192,384]{2,1,0:T(8,128)(2,1)S(1)}, bf16[2,192,384]{2,1,0:T(8,128)(2,1)S(1)}, u32[]{:S(2)}, u32[]{:S(2)}) collective-permute-start(bf16[2,192,384]{2,1,0:T(8,128)(2,1)S(1)} %get-tuple-element.248), channel_id=1, source_target_pairs={{0,4},{4,0},{8,12},{12,8},{16,20},{20,16},{24,28},{28,24},{1,5},{5... | collective-permute-start | bytes 884744 | tf_op jit(solution)/shard_map/ppermute | solution.py:247
  153.4 23.4 %collective-permute-start.54 = (bf16[2,384,384]{2,1,0:T(8,128)(2,1)S(1)}, bf16[2,384,384]{2,1,0:T(8,128)(2,1)S(1)}, u32[]{:S(2)}, u32[]{:S(2)}) collective-permute-start(bf16[2,384,384]{2,1,0:T(8,128)(2,1)S(1)} %get-tuple-element.265), channel_id=1, source_target_pairs={{0,8},{4,12},{8,0},{12,4},{16,24},{20,28},{24,16},{28,20},{1,9},{5... | collective-permute-start | bytes 1769480 | tf_op jit(solution)/shard_map/ppermute | solution.py:247
  154.7 22.7 %collective-permute-start.52 = (bf16[1,384,384]{2,1,0:T(8,128)(2,1)S(1)}, bf16[1,384,384]{2,1,0:T(8,128)(2,1)S(1)}, u32[]{:S(2)}, u32[]{:S(2)}) collective-permute-start(bf16[1,384,384]{2,1,0:T(8,128)(2,1)S(1)} %get-tuple-element.261), channel_id=1, source_target_pairs={{0,16},{4,20},{8,24},{12,28},{16,0},{20,4},{24,8},{28,12},{1,17},{... | collective-permute-start | bytes 884744 | tf_op jit(solution)/shard_map/ppermute | solution.py:247
  157.8 19.6 %collective-permute-start.53 = (bf16[1,192,384]{2,1,0:T(8,128)(2,1)S(1)}, bf16[1,192,384]{2,1,0:T(8,128)(2,1)S(1)}, u32[]{:S(2)}, u32[]{:S(2)}) collective-permute-start(bf16[1,192,384]{2,1,0:T(8,128)(2,1)S(1)} %get-tuple-element.263), channel_id=1, source_target_pairs={{0,16},{4,20},{8,24},{12,28},{16,0},{20,4},{24,8},{28,12},{1,17},{... | collective-permute-start | bytes 442376 | tf_op jit(solution)/shard_map/ppermute | solution.py:247
  159.3 26.7 %collective-permute-start.51 = (bf16[1,192,384]{2,1,0:T(8,128)(2,1)S(1)}, bf16[1,192,384]{2,1,0:T(8,128)(2,1)S(1)}, u32[]{:S(2)}, u32[]{:S(2)}) collective-permute-start(bf16[1,192,384]{2,1,0:T(8,128)(2,1)S(1)} %get-tuple-element.259), channel_id=1, source_target_pairs={{0,16},{4,20},{8,24},{12,28},{16,0},{20,4},{24,8},{28,12},{1,17},{... | collective-permute-start | bytes 442376 | tf_op jit(solution)/shard_map/ppermute | solution.py:247
  176.9 15.2 %collective-permute-start.55 = (bf16[1,384,384]{2,1,0:T(8,128)(2,1)S(1)}, bf16[1,384,384]{2,1,0:T(8,128)(2,1)S(1)}, u32[]{:S(2)}, u32[]{:S(2)}) collective-permute-start(bf16[1,384,384]{2,1,0:T(8,128)(2,1)S(1)} %get-tuple-element.273), channel_id=1, source_target_pairs={{0,16},{4,20},{8,24},{12,28},{16,0},{20,4},{24,8},{28,12},{1,17},{... | collective-permute-start | bytes 884744 | tf_op jit(solution)/shard_map/ppermute | solution.py:247
  (46 other events, 204.3 us)

commit v3 on v2

v3 whole, which is shorter than its diff:
```python
from functools import partial

import jax
import jax.numpy as jnp
import numpy as np
from jax import lax
from jax.experimental import pallas as pl
from jax.experimental.pallas import tpu as pltpu
from jax.sharding import PartitionSpec as P

WIN = 7
GRID_COLS = 8
PATCHES = 49
PADDED = WIN * GRID_COLS
HEAD_DIM = 32
LANES = 128
HEADS_TILE = LANES // HEAD_DIM
EPS = 1e-05
NEG = -1e30
SPLIT_D, SPLIT_C, SPLIT_B, SPLIT_A = 0, 2, 1, 3
BF16 = jnp.bfloat16
F32 = jnp.float32
VMEM_LIMIT = 16 * 2**20


def mm(left, right, left_dim, right_dim):
    return lax.dot_general(
        left, right, (((left_dim,), (right_dim,)), ((), ())), preferred_element_type=F32
    )


class Order:
    def __init__(self):
        self.last = None


def kernel_call(body, name, ins, outs, order, scratch=(), flops=0, hold=(), far=0):
    arrays = list(ins) + list(hold) + ([] if order.last is None else [order.last])
    specs = [
        pl.BlockSpec(
            memory_space=pltpu.SMEM if a.dtype == jnp.int32 and a.ndim == 1 else pltpu.VMEM
        )
        for a in arrays
    ]
    for at in range(len(ins) - far, len(ins)):
        specs[at] = pl.BlockSpec(memory_space=pltpu.HBM)
    outs = list(outs) + [sds((8, LANES))]

    def wrapped(*refs):
        given = refs[: len(ins)] + refs[len(arrays) : len(arrays) + len(outs) - 1]
        body(*given, *refs[len(arrays) + len(outs) :])
        mark = refs[len(arrays) + len(outs) - 1]
        mark[...] = jnp.zeros_like(mark)

    moved = sum(int(np.prod(o.shape)) * o.dtype.itemsize for o in outs) + sum(
        int(np.prod(a.shape)) * a.dtype.itemsize for a in ins
    )
    *results, order.last = pl.pallas_call(
        wrapped,
        in_specs=specs,
        out_specs=[pl.BlockSpec(memory_space=pltpu.VMEM)] * len(outs),
        out_shape=outs,
        scratch_shapes=list(scratch),
        compiler_params=pltpu.CompilerParams(vmem_limit_bytes=VMEM_LIMIT),
        cost_estimate=pl.CostEstimate(flops=0, bytes_accessed=0, transcendentals=0),
        name=name,
    )(*arrays)
    return results


def sds(shape, dtype=F32):
    return jax.ShapeDtypeStruct(shape, dtype)


def column_mask(rows):
    return (lax.broadcasted_iota(jnp.int32, (rows, 1), 0) % GRID_COLS) < WIN


def placement(images, transposed):
    padded, plain = images * PADDED, images * PATCHES
    shape = (plain, padded) if transposed else (padded, plain)
    at = lax.broadcasted_iota(jnp.int32, shape, 1 if transposed else 0)
    image = sum((at >= i * PADDED).astype(jnp.int32) for i in range(1, images))
    inside = at - image * PADDED
    source = image * PATCHES + (inside >> 3) * WIN + (inside & 7)
    other = lax.broadcasted_iota(jnp.int32, shape, 0 if transposed else 1)
    return (((inside & 7) < WIN) & (source == other)).astype(F32).astype(BF16)


def side_shifts(values):
    rows = values.shape[0]
    return (pltpu.roll(values, 1, 0), values, pltpu.roll(values, rows - 1, 0))


def as_grid(values):
    return values.reshape(-1, WIN, GRID_COLS, values.shape[-1])


def move_rows(values, step):
    grid = as_grid(values)
    zeros = jnp.zeros_like(grid[:, :1])
    if step > 0:
        moved = jnp.concatenate([zeros, grid[:, :-1]], axis=1)
    else:
        moved = jnp.concatenate([grid[:, 1:], zeros], axis=1)
    return moved.reshape(values.shape)


def conv_cols(values, taps, keep):
    shifted = side_shifts(values)
    line = [
        sum(shifted[col] * taps[3 * row + col] for col in range(3)) for row in range(3)
    ]
    total = values + line[1] + move_rows(line[0], 1) + move_rows(line[2], -1)
    return jnp.where(keep, total, 0.0)


def tap_sums(grads, values):
    shifted = side_shifts(values)
    grad_grid = as_grid(grads)
    sums = []
    for row in range(3):
        for col in range(3):
            moved = as_grid(shifted[col])
            if row == 0:
                prod = grad_grid[:, 1:] * moved[:, :-1]
            elif row == 1:
                prod = grad_grid * moved
            else:
                prod = grad_grid[:, :-1] * moved[:, 1:]
            flat = prod.reshape(-1, GRID_COLS, prod.shape[-1])
            sums.append(jnp.sum(jnp.sum(flat, axis=0), axis=0, keepdims=True))
    return sums


def norm_stats(stream):
    width = stream.shape[1]
    center = jnp.sum(stream, axis=1, keepdims=True) * (1.0 / width)
    moved = stream - center
    inv_std = lax.rsqrt(jnp.sum(moved * moved, axis=1, keepdims=True) * (1.0 / width) + EPS)
    return moved * inv_std, inv_std


def norm_back(upstream, units, inv_std, gain):
    width = upstream.shape[1]
    scaled = upstream * gain
    first = jnp.sum(scaled, axis=1, keepdims=True) * (1.0 / width)
    second = jnp.sum(scaled * units, axis=1, keepdims=True) * (1.0 / width)
    return inv_std * (scaled - first - units * second)


def gelu_parts(values):
    z = jnp.abs(values) * (0.5**0.5)
    t = 1.0 / (1.0 + 0.3275911 * z)
    bell = jnp.exp(-z * z)
    poly = t * (
        0.254829592
        + t * (-0.284496736 + t * (1.421413741 + t * (-1.453152027 + t * 1.061405429)))
    )
    tail = 0.5 * poly * bell
    return jnp.where(values < 0, tail, 1.0 - tail), bell * float(1.0 / np.sqrt(2.0 * np.pi))


def head_mask(index):
    return (lax.broadcasted_iota(jnp.int32, (1, LANES), 1) // HEAD_DIM) == index


def spread_heads(tile):
    return jnp.concatenate(
        [jnp.where(head_mask(j), tile, 0.0) for j in range(HEADS_TILE)], axis=0
    ).astype(BF16)


def gather_heads(stacked):
    rows = stacked.shape[0] // HEADS_TILE
    total = jnp.where(head_mask(0), stacked[:rows], 0.0)
    for j in range(1, HEADS_TILE):
        total = jnp.where(head_mask(j), stacked[j * rows : (j + 1) * rows], total)
    return total


def softmax_rows(scores):
    top = jnp.max(scores, axis=0, keepdims=True)
    weights = jnp.exp(scores - top)
    return weights / jnp.sum(weights, axis=0, keepdims=True)


SCALE = HEAD_DIM**-0.5


def window_tile(q, k, v):
    keys_ok = column_mask(PADDED)
    scores = mm(k.astype(BF16), spread_heads(q), 1, 1) * SCALE
    probs = softmax_rows(jnp.where(keys_ok, scores, NEG))
    return probs, gather_heads(mm(probs.astype(BF16), v.astype(BF16), 0, 0))


def window_tile_back(q, k, v, probs, grad):
    low = probs.astype(BF16)
    q_big, g_big = spread_heads(q), spread_heads(grad)
    grad_probs = mm(v.astype(BF16), g_big, 1, 1)
    grad_v = mm(low, g_big, 1, 0)
    grad_scores = (
        probs * (grad_probs - jnp.sum(grad_probs * probs, axis=0, keepdims=True))
    ).astype(BF16)
    grad_k = mm(grad_scores, q_big, 1, 0) * SCALE
    grad_q = gather_heads(mm(grad_scores, k.astype(BF16), 0, 0)) * SCALE
    return grad_q, grad_k, grad_v


def same_head():
    first = lax.broadcasted_iota(jnp.int32, (LANES, LANES), 0) // HEAD_DIM
    second = lax.broadcasted_iota(jnp.int32, (LANES, LANES), 1) // HEAD_DIM
    return first == second


def channel_tile(q, k, v, mask):
    scores = mm(k.astype(BF16), (q * mask).astype(BF16), 0, 0) * SCALE
    probs = softmax_rows(jnp.where(same_head(), scores, NEG))
    return probs, mm(v.astype(BF16), probs.astype(BF16), 1, 0)


def channel_tile_back(q, k, v, probs, grad, mask):
    low = probs.astype(BF16)
    grad_low = grad.astype(BF16)
    grad_probs = mm(v.astype(BF16), grad_low, 0, 0)
    grad_v = mm(grad_low, low, 1, 1)
    grad_scores = (
        probs * (grad_probs - jnp.sum(grad_probs * probs, axis=0, keepdims=True))
    ).astype(BF16)
    grad_q = mm(k.astype(BF16), grad_scores, 1, 0) * SCALE * mask
    grad_k = mm((q * mask).astype(BF16), grad_scores, 1, 1) * SCALE
    return grad_q, grad_k, grad_v


def solution(mesh):
    n_dev = mesh.shape["dev"]
    bits = n_dev.bit_length() - 1
    assert n_dev == 1 << bits and mesh.shape["ha"] == 2 and mesh.shape["wa"] == 2

    swap = [(0, 1), (1, 0)]

    def over_ha(values):
        return lax.ppermute(values, "ha", swap)

    def over_wa(values):
        return lax.ppermute(values, "wa", swap)

    def over_dev(values, bit):
        return lax.ppermute(values, "dev", [(i, i ^ (1 << bit)) for i in range(n_dev)])

    def on_device(
        tokens, cotangent, conv_taps, norm_gain, norm_shift, w_qkv, w_proj, w_up, w_down, valid
    ):
        rows_in, half = tokens.shape
        images = rows_in // PATCHES
        rows = images * PADDED
        width = 2 * half
        heads_width = w_qkv.shape[3]
        hidden = w_up.shape[2]
        tiles = heads_width // LANES
        assert heads_width == half
        orders = [list(range(bits)), [1, 0, *range(2, bits)]]

        def here(name):
            return lax.axis_index(name)

        def chunk_at(place, which):
            found = 0
            for step, bit in enumerate(orders[which]):
                found |= ((place >> (bits - 1 - step)) & 1) << bit
            return found ^ here("dev")

        order = Order()
        call = partial(kernel_call, order=order)

        def later(values, event):
            return lax.optimization_barrier((values, event))[0]

        def pack_small(taps_ref, gain_ref, shift_ref, out_ref):
            for section in range(2):
                for t in range(9):
                    at = 9 * section + t
                    out_ref[at : at + 1, :] = taps_ref[t, section : section + 1, :]
            out_ref[18:22, :] = gain_ref[...]
            out_ref[22:26, :] = shift_ref[...]

        def choose(mine, received, own, other):
            same = here("ha") == here("wa")
            own[...] = jnp.where(same, mine[...], received[...])
            other[...] = jnp.where(same, received[...], mine[...])

        wq_own = jnp.transpose(w_qkv, (0, 2, 1, 3))
        wq, wp = (wq_own, over_wa(wq_own)), (w_proj, over_wa(w_proj))
        tokens_in = over_ha(tokens)
        small_own = call(
            pack_small, "pack_small",
            [jnp.transpose(conv_taps, (1, 0, 2)), norm_gain, norm_shift], [sds((26, half))],
            hold=[wq_own, w_proj, tokens],
        )[0]
        small = (small_own, over_wa(small_own))
        chosen = [sds((rows_in, half), BF16)] * 2
        tokens_own, tokens_oth = call(
            choose, "choose_tokens", [tokens, tokens_in], chosen, hold=[*wq, *wp, small_own]
        )
        token_parts = (tokens_own, over_wa(tokens_oth))
        arrived = (token_parts[1], small[1])
        wu, wd = ((values, over_wa(later(values, arrived))) for values in (w_up, w_down))

        def unpack(own, oth):
            values = jnp.concatenate([own[...], oth[...]], axis=1)
            return mm(placement(images, False), values, 1, 0)

        def gain_row(refs, branch):
            return jnp.concatenate([ref[18 + branch : 19 + branch, :] for ref in refs], axis=1)

        def shift_row(refs, branch):
            return jnp.concatenate([ref[22 + branch : 23 + branch, :] for ref in refs], axis=1)

        def tap_rows(small_refs, section, col, flipped):
            ref = small_refs[col // half]
            at = col % half
            found = [
                ref[9 * section + t : 9 * section + t + 1, at : at + LANES] for t in range(9)
            ]
            return found[::-1] if flipped else found

        def project_in(normed, first, second):
            return mm(normed[:, :half], first, 1, 0) + mm(normed[:, half:], second, 1, 0)

        def project_back(values, first, second):
            return mm(values[:, :half], first, 1, 1) + mm(values[:, half:], second, 1, 1)

        def to_normed(stream, small_refs, branch):
            units, _ = norm_stats(stream)
            return (units * gain_row(small_refs, branch) + shift_row(small_refs, branch)).astype(
                BF16
            )

        def put_both(own_ref, oth_ref, values):
            own_ref[...] = values[:, :half]
            oth_ref[...] = values[:, half:]

        def add_parts(stream, part_a, part_b):
            return stream[...] + part_a[...].astype(F32) + part_b[...].astype(F32)

        def attention_part(window, section, normed, valid_rows, wq_a, wq_b, qkv_ref, probs_ref):
            packed = [
                project_in(normed, wq_a[section, part], wq_b[section, part]).astype(BF16)
                for part in range(3)
            ]
            for part in range(3):
                qkv_ref[part] = packed[part]
            wide = [part.astype(F32) for part in packed]
            mixed = []
            for image in range(images):
                line = []
                rows_at = slice(image * PADDED, (image + 1) * PADDED)
                for tile in range(tiles):
                    lanes_at = slice(tile * LANES, (tile + 1) * LANES)
                    q, k, v = (part[rows_at, lanes_at] for part in wide)
                    if window:
                        probs, out = window_tile(q, k, v)
                    else:
                        probs, out = channel_tile(q, k, v, valid_rows[image])
                    probs_ref[image * tiles + tile] = probs
                    line.append(out)
                mixed.append(jnp.concatenate(line, axis=1))
            return jnp.concatenate(mixed, axis=0).astype(BF16)

        def attention_part_back(window, grad_mixed, mask_ref, qkv_ref, probs_ref, dpk_ref):
            wide = [qkv_ref[part].astype(F32) for part in range(3)]
            grad = grad_mixed.astype(F32)
            found = [[], [], []]
            for image in range(images):
                lines = [[], [], []]
                for tile in range(tiles):
                    rows_at = slice(image * PADDED, (image + 1) * PADDED)
                    lanes_at = slice(tile * LANES, (tile + 1) * LANES)
                    q, k, v = (part[rows_at, lanes_at] for part in wide)
                    probs = probs_ref[image * tiles + tile]
                    if window:
                        parts = window_tile_back(q, k, v, probs, grad[rows_at, lanes_at])
                    else:
                        parts = channel_tile_back(
                            q, k, v, probs, grad[rows_at, lanes_at], mask_ref[rows_at, :]
                        )
                    for line, part in zip(lines, parts):
                        line.append(part)
                for part in range(3):
                    found[part].append(jnp.concatenate(lines[part], axis=1))
            packed = [jnp.concatenate(part, axis=0).astype(BF16) for part in found]
            for part in range(3):
                dpk_ref[part] = packed[part]
            return packed

        def mul_out(left, section, own_ref, oth_ref, out_ref):
            out_ref[:, :half] = mm(left, own_ref[section], 1, 0).astype(BF16)
            out_ref[:, half:] = mm(left, oth_ref[section], 1, 0).astype(BF16)

        def conv_into(out_ref, values, small_refs, section, keep):
            for col in range(0, width, LANES):
                taps = tap_rows(small_refs, section, col, False)
                out_ref[:, col : col + LANES] = conv_cols(values[:, col : col + LANES], taps, keep)

        def conv_back_into(out_ref, sums_ref, sums_at, grads, values, small_refs, section, keep):
            for col in range(0, width, LANES):
                lanes_at = slice(col, col + LANES)
                taps = tap_rows(small_refs, section, col, True)
                for t, total in enumerate(tap_sums(grads[:, lanes_at], values[:, lanes_at])):
                    sums_ref[sums_at + t : sums_at + t + 1, lanes_at] = total
                out_ref[:, lanes_at] = conv_cols(grads[:, lanes_at], taps, keep)

        window_probs = sds((images * tiles, PADDED, HEADS_TILE * PADDED))
        channel_probs = sds((images * tiles, LANES, LANES))
        full, full_low = sds((rows, width)), sds((rows, width), BF16)
        half_low = sds((rows, half), BF16)
        hid_low = sds((rows, hidden), BF16)
        qkv_low = sds((3, rows, heads_width), BF16)
        attn_flops = 2 * rows * (4 * width * heads_width)
        mlp_flops = 2 * rows * (2 * width * hidden)

        def first_body(
            tokens_a, tokens_b, small_a, small_b, wq_a, wq_b, wp_a, wp_b,
            x_ref, s_ref, n_own, n_oth, qkv_ref, probs_ref, mixed_ref, part_ref, keep_a, keep_b,
        ):
            keep_a[...], keep_b[...] = small_a[...], small_b[...]
            keep = column_mask(rows)
            stream = unpack(tokens_a, tokens_b)
            x_ref[...] = stream.astype(BF16)
            conv_into(s_ref, stream, (small_a, small_b), 0, keep)
            normed = to_normed(s_ref[...], (small_a, small_b), 0)
            put_both(n_own, n_oth, normed)
            mixed = attention_part(True, 0, normed, None, wq_a, wq_b, qkv_ref, probs_ref)
            mixed_ref[...] = mixed
            mul_out(mixed, 0, wp_a, wp_b, part_ref)

        (x0, s1, n0_own, n0_oth, qkv0, probs0, mixed0, part0, *small) = call(
            first_body, "attn_a",
            [*token_parts, *small, *wq, *wp],
            [full_low, full, half_low, half_low, qkv_low, window_probs, half_low, full_low]
            + [sds((26, half))] * 2,
            flops=attn_flops,
        )
        far0 = over_ha(part0)
        keep_a = [x0, n0_own, n0_oth, qkv0, probs0, mixed0, s1]

        def mlp_body(
            s_in, part_a, part_b, small_a, small_b, wu_a, wu_b, wd_a, wd_b,
            s_ref, n_own, n_oth, hid_ref, slope_ref, part_ref,
        ):
            s_ref[...] = add_parts(s_in, part_a, part_b)
            normed = to_normed(s_ref[...], (small_a, small_b), 1)
            put_both(n_own, n_oth, normed)
            pre = project_in(normed, wu_a[0], wu_b[0])
            below, bell = gelu_parts(pre)
            hid = (pre * below).astype(BF16)
            hid_ref[...] = hid
            slope_ref[...] = below + pre * bell
            mul_out(hid, 0, wd_a, wd_b, part_ref)

        (s2, n1_own, n1_oth, hid1, slope1, part1) = call(
            mlp_body, "mlp_b",
            [s1, part0, far0, *small, *wu, *wd],
            [full, half_low, half_low, hid_low, sds((rows, hidden)), full_low],
            flops=mlp_flops, hold=[*keep_a, *wq, *wp],
        )
        far1 = over_ha(part1)
        keep_b = [s2, n1_own, n1_oth, hid1, slope1]
        weights = [*wq, *wp, *wu, *wd]


        cot_in = over_ha(later(cotangent, part1))

        def channel_body(
            s_in, part_a, part_b, valid_ref, small_a, small_b,
            wq_a, wq_b, wp_a, wp_b,
            s_before, s_ref, n_own, n_oth, qkv_ref, probs_ref, mixed_ref, part_ref, mask_ref,
        ):
            keep = column_mask(rows)
            s_before[...] = jnp.where(keep, add_parts(s_in, part_a, part_b), 0.0)
            conv_into(s_ref, s_before, (small_a, small_b), 1, keep)
            normed = to_normed(s_ref[...], (small_a, small_b), 2)
            put_both(n_own, n_oth, normed)
            one_image = placement(1, False).astype(F32)
            valid_rows = []
            for image in range(images):
                line = jnp.where(
                    here("wa") == 0,
                    valid_ref[image : image + 1, :],
                    valid_ref[images + image : images + image + 1, :],
                ).astype(F32)
                valid_rows.append(jnp.sum(one_image * line, axis=1, keepdims=True))
                mask_ref[image * PADDED : (image + 1) * PADDED, :] = valid_rows[image]
            mixed = attention_part(False, 1, normed, valid_rows, wq_a, wq_b, qkv_ref, probs_ref)
            mixed_ref[...] = mixed
            mul_out(mixed, 1, wp_a, wp_b, part_ref)

        (s3, s4, n2_own, n2_oth, qkv2, probs2, mixed2, part2, mask) = call(
            channel_body, "attn_c",
            [s2, part1, far1, valid, *small, *wq, *wp],
            [full, full, half_low, half_low, qkv_low, channel_probs, half_low, full_low,
             sds((rows, 1))],
            flops=attn_flops,
            hold=[*keep_a, *keep_b, *wu, *wd, cot_in],
        )
        far2 = over_ha(part2)
        keep_c = [s3, s4, n2_own, n2_oth, qkv2, probs2, mixed2, mask]

        cot_own, cot_oth = call(
            choose, "choose_cot", [cotangent, cot_in], chosen,
            hold=[*keep_a, *keep_b, *keep_c, *small, *wq, *wp, *wu, *wd],
        )
        cot_parts = (cot_own, over_wa(cot_oth))

        def cot_body(cot_a, cot_b, wd_a, wd_b, g_own, g_oth, dhid_ref):
            grad = unpack(cot_a, cot_b).astype(BF16)
            put_both(g_own, g_oth, grad)
            dhid_ref[...] = project_back(grad, wd_a[1], wd_b[1]).astype(BF16)

        g3_own, g3_oth, dhid3 = call(
            cot_body, "cot_d",
            [*cot_parts, *wd],
            [half_low, half_low, hid_low],
            flops=mlp_flops // 2, hold=[*keep_a, *keep_b, *keep_c, *small, *wq, *wp, *wu],
        )

        def last_body(
            s_in, part_a, part_b, small_a, small_b, dhid_ref, wu_a, wu_b,
            s_ref, n_own, n_oth, hid_ref, dpre_ref, part_ref,
        ):
            s_ref[...] = add_parts(s_in, part_a, part_b)
            normed = to_normed(s_ref[...], (small_a, small_b), 3)
            put_both(n_own, n_oth, normed)
            pre = project_in(normed, wu_a[1], wu_b[1])
            below, bell = gelu_parts(pre)
            hid_ref[...] = (pre * below).astype(BF16)
            dpre = (dhid_ref[...].astype(F32) * (below + pre * bell)).astype(BF16)
            dpre_ref[...] = dpre
            part_ref[:, :half] = mm(dpre, wu_a[1], 1, 1).astype(BF16)
            part_ref[:, half:] = mm(dpre, wu_b[1], 1, 1).astype(BF16)

        (s5, n3_own, n3_oth, hid3, dpre3, back3) = call(
            last_body, "mlp_d",
            [s4, part2, far2, *small, dhid3, *wu],
            [full, half_low, half_low, hid_low, hid_low, full_low],
            flops=mlp_flops,
            hold=[*keep_a, *keep_b, *keep_c, g3_own, g3_oth, *wq, *wp, *wd],
        )
        far_back3 = over_ha(back3)

        up_rows, down_rows = hidden // n_dev, half // n_dev
        qkv_rows, proj_rows = heads_width // n_dev, half // n_dev
        folds = hidden // half
        cut = n_dev // 2
        sum_rows = 32

        class Stream:
            def __init__(self, which, pieces):
                self.bits, self.which, self.pieces = orders[which], which, pieces
                self.chunk_rows = sum(piece_rows(piece) for piece in pieces)
                self.step, self.kept, self.got, self.at, self.final = 0, None, None, 0, None

        def piece_rows(piece):
            return {"up": up_rows, "q": qkv_rows, "k": qkv_rows, "v": qkv_rows}.get(
                piece, down_rows
            )

        downs = [("down", fold) for fold in range(folds)]

        def mlp_streams(first):
            return [Stream(0, ["up", *downs[:first]]), Stream(1, downs[first:])]

        def attn_streams(first):
            parts = ["q", "k", "v", "proj"]
            return [Stream(0, parts[:first]), Stream(1, parts[first:])]

        def write_pieces(values, streams, scratches):
            for stream, scratch in zip(streams, scratches):
                at = 0
                for piece in stream.pieces:
                    size = piece_rows(piece)
                    for chunk in range(n_dev):
                        rows_at = slice(chunk * size, (chunk + 1) * size)
                        if isinstance(piece, tuple):
                            columns = slice(piece[1] * half, (piece[1] + 1) * half)
                            part = values["down"][rows_at, columns]
                        else:
                            part = values[piece][rows_at]
                        scratch[chunk, at : at + size, :] = part
                    at += size

        def write_mlp(refs, streams, scratches):
            dpre_a, dpre_b, n_a, n_b, g_a, g_b, hid_a, hid_b = refs
            up = mm(dpre_a[...], n_a[...], 0, 0) + mm(dpre_b[...], n_b[...], 0, 0)
            down = mm(g_a[...], hid_a[...], 0, 0) + mm(g_b[...], hid_b[...], 0, 0)
            write_pieces({"up": up, "down": down}, streams, scratches)

        def write_attn(refs, streams, scratches):
            dpk_a, dpk_b, n_a, n_b, g_a, g_b, mix_a, mix_b = refs
            values = {
                name: mm(dpk_a[part], n_a[...], 0, 0) + mm(dpk_b[part], n_b[...], 0, 0)
                for part, name in enumerate(("q", "k", "v"))
            }
            values["proj"] = mm(g_a[...], mix_a[...], 0, 0) + mm(g_b[...], mix_b[...], 0, 0)
            write_pieces(values, streams, scratches)

        def split_low(values):
            high = values.astype(BF16)
            return high, (values - high.astype(F32)).astype(BF16)

        def joined(ref, at):
            high = ref[at : at + sum_rows, :].astype(F32)
            return high + ref[at + sum_rows : at + 2 * sum_rows, :].astype(F32)

        def last_sum(stream, kept, got):
            return kept[...].astype(F32) + got[
                stream.at : stream.at + stream.chunk_rows, :
            ].astype(F32)

        def slot(
            name, write=None, fresh=(), sources=(), moving=(), ending=(), sums=None, hold=()
        ):
            ins, outs, sizes = list(sources), [], {}
            plan_fresh, plan_moving = [], []

            def room(bit, size):
                at = sizes.get(bit, 0)
                sizes[bit] = at + size
                return at

            for stream in fresh:
                size = cut * stream.chunk_rows
                plan_fresh.append((len(outs), stream.bits[0], room(stream.bits[0], size)))
                outs.append(sds((size, half), BF16))
            got_places = {}

            def place_of(array):
                for at, known in enumerate(ins):
                    if known is array:
                        return at
                ins.append(array)
                return len(ins) - 1

            for stream in moving:
                size = stream.kept.shape[0] // 2
                bit = stream.bits[stream.step]
                plan_moving.append(
                    (place_of(stream.kept), place_of(stream.got), stream.at, size,
                     len(outs), bit, room(bit, size))
                )
                outs.append(sds((size, half), BF16))
            plan_ending = []
            for stream in ending:
                plan_ending.append(
                    (stream, place_of(stream.kept), place_of(stream.got), len(outs))
                )
                outs.append(sds((stream.chunk_rows, half)))
            if sums is not None:
                total_at = place_of(sums[0])
                sums_got = None if sums[1] is None else place_of(sums[1])
                sums_room = room(sums[3], 2 * sum_rows)
                sums_out = len(outs)
                outs.append(sds((sum_rows, half)))
            bits_used = sorted(sizes)
            buffer_at = {bit: len(outs) + at for at, bit in enumerate(bits_used)}
            outs += [sds((sizes[bit], half), BF16) for bit in bits_used]
            scratch = [pltpu.VMEM((n_dev, stream.chunk_rows, half), F32) for stream in fresh]

            def body(*refs):
                in_refs, out_refs = refs[: len(ins)], refs[len(ins) : len(ins) + len(outs)]
                scratches = refs[len(ins) + len(outs) :]
                if fresh:
                    write(in_refs[: len(sources)], fresh, scratches)
                for stream, held, (kept_at, bit, at) in zip(fresh, scratches, plan_fresh):
                    size = stream.chunk_rows
                    for place in range(n_dev):
                        chunk = held[chunk_at(place, stream.which)].astype(BF16)
                        if place < cut:
                            out_refs[kept_at][place * size : (place + 1) * size, :] = chunk
                        else:
                            to = at + (place - cut) * size
                            out_refs[buffer_at[bit]][to : to + size, :] = chunk
                for kept_in, got_in, got_row, size, kept_at, bit, at in plan_moving:
                    kept, got = in_refs[kept_in], in_refs[got_in]
                    out_refs[kept_at][...] = (
                        kept[:size, :].astype(F32) + got[got_row : got_row + size, :].astype(F32)
                    ).astype(BF16)
                    out_refs[buffer_at[bit]][at : at + size, :] = (
                        kept[size:, :].astype(F32)
                        + got[got_row + size : got_row + 2 * size, :].astype(F32)
                    ).astype(BF16)
                for stream, kept_in, got_in, out_at in plan_ending:
                    out_refs[out_at][...] = last_sum(stream, in_refs[kept_in], in_refs[got_in])
                if sums is not None:
                    total = in_refs[total_at][...]
                    if sums_got is not None:
                        total = total + joined(in_refs[sums_got], sums[2])
                    high, low = split_low(total)
                    out_refs[sums_out][...] = high.astype(F32) + low.astype(F32)
                    buffer = out_refs[buffer_at[sums[3]]]
                    buffer[sums_room : sums_room + sum_rows, :] = high
                    buffer[sums_room + sum_rows : sums_room + 2 * sum_rows, :] = low

            results = call(body, name, ins, outs, scratch=scratch, hold=hold)
            received = {bit: over_dev(results[buffer_at[bit]], bit) for bit in bits_used}
            for stream, (kept_at, bit, at) in zip(fresh, plan_fresh):
                stream.kept, stream.got, stream.at = results[kept_at], received[bit], at
                stream.step = 1
            for stream, _, _, out_at in plan_ending:
                stream.final = results[out_at]
            for stream, (_, _, _, _, kept_at, bit, at) in zip(moving, plan_moving):
                stream.kept, stream.got, stream.at = results[kept_at], received[bit], at
                stream.step += 1
            if sums is not None:
                sums[:3] = results[sums_out], received[sums[3]], sums_room

        def gradient_sources(left, n_own, n_oth, g_own, g_oth, right):
            return [left, over_wa(left), n_own, over_wa(n_oth),
                    g_own, over_wa(g_oth), right, over_wa(right)]

        def ship(total, kept, sent):
            packed = mm(placement(images, True), total.astype(BF16), 1, 0).astype(BF16)
            kept[...] = packed[:, :half]
            sent[...] = packed[:, half:]

        shipped = [sds((rows_in, half), BF16)] * 2

        def fold(kept, received, stay, go):
            same = here("ha") == here("wa")
            stay[...] = jnp.where(same, kept[...], received[...])
            go[:rows_in, :] = jnp.where(same, received[...], kept[...])

        def join(stay, received, out_ref):
            out_ref[...] = stay[...].astype(F32) + received[:rows_in, :].astype(F32)

        def out_body(s_in, hid_ref, wd_a, wd_b, kept, sent):
            hid = hid_ref[...]
            base = jnp.where(here("ha") == 0, s_in[...], 0.0)
            branch = jnp.concatenate([mm(hid, wd_a[1], 1, 0), mm(hid, wd_b[1], 1, 0)], axis=1)
            ship(base + branch, kept, sent)

        streams_d = mlp_streams(SPLIT_D)
        slot(
            "wgrad_d", write_mlp, streams_d,
            gradient_sources(dpre3, n3_own, n3_oth, g3_own, g3_oth, hid3),
            hold=[*keep_a, *keep_b, *keep_c, *small, *weights, s5],
        )

        def add_norm_back(grad, part_a, part_b, stream, gain, sums_ref):
            upstream = part_a[...].astype(F32) + part_b[...].astype(F32)
            units, inv_std = norm_stats(stream)
            sums_ref[0:1, :] = jnp.sum(upstream * units, axis=0, keepdims=True)
            sums_ref[1:2, :] = jnp.sum(upstream, axis=0, keepdims=True)
            return grad + norm_back(upstream, units, inv_std, gain)

        def qkv_back(packed, section, wq_a, wq_b):
            return [
                sum(mm(packed[part], ref[section, part], 1, 1) for part in range(3))
                for ref in (wq_a, wq_b)
            ]

        def channel_back_body(
            g_in_own, g_in_oth, part_a, part_b, s_in, small_a, small_b, mask_ref, qkv_ref,
            probs_ref, wp_a, wp_b, wq_a, wq_b, g_ref, g_own, g_oth, dpk_ref, part_ref, sums_ref,
        ):
            grad = jnp.concatenate([g_in_own[...], g_in_oth[...]], axis=1).astype(F32)
            gain = gain_row((small_a, small_b), 3)
            grad = add_norm_back(grad, part_a, part_b, s_in[...], gain, sums_ref)
            g_ref[...] = grad
            low = grad.astype(BF16)
            put_both(g_own, g_oth, low)
            grad_mixed = project_back(low, wp_a[1], wp_b[1]).astype(BF16)
            packed = attention_part_back(False, grad_mixed, mask_ref, qkv_ref, probs_ref, dpk_ref)
            own, oth = qkv_back(packed, 1, wq_a, wq_b)
            part_ref[:, :half] = own.astype(BF16)
            part_ref[:, half:] = oth.astype(BF16)

        late = [hid3, *wd, s5]
        (g2, g2_own, g2_oth, dpk2, back2, sums3) = call(
            channel_back_body, "back_c",
            [g3_own, g3_oth, back3, far_back3, s5, *small, mask, qkv2, probs2, *wp, *wq],
            [full, half_low, half_low, qkv_low, full_low, sds((2, width))],
            flops=attn_flops,
            hold=[*keep_a, *keep_b, s3, s4, n2_own, n2_oth, mixed2, *wu, *wd, hid3],
        )
        far_back2 = over_ha(back2)
        streams_c = attn_streams(SPLIT_C)
        slot(
            "wgrad_c", write_attn, streams_c,
            gradient_sources(dpk2, n2_own, n2_oth, g2_own, g2_oth, mixed2),
            moving=streams_d,
            hold=[*keep_a, *keep_b, s3, s4, *small, *weights, g2, *late, sums3, back2, far_back2],
        )

        def mlp_back_body(
            g_in, part_a, part_b, s_in, s_before, small_a, small_b, slope_ref,
            wd_a, wd_b, wu_a, wu_b, g_ref, g_own, g_oth, dpre_ref, part_ref, sums_ref,
        ):
            keep = column_mask(rows)
            gain = gain_row((small_a, small_b), 2)
            grad = add_norm_back(g_in[...], part_a, part_b, s_in[...], gain, sums_ref)
            conv_back_into(g_ref, sums_ref, 2, grad, s_before[...], (small_a, small_b), 1, keep)
            low = g_ref[...].astype(BF16)
            put_both(g_own, g_oth, low)
            dhid = project_back(low, wd_a[0], wd_b[0]).astype(BF16).astype(F32)
            dpre = (dhid * slope_ref[...]).astype(BF16)
            dpre_ref[...] = dpre
            part_ref[:, :half] = mm(dpre, wu_a[0], 1, 1).astype(BF16)
            part_ref[:, half:] = mm(dpre, wu_b[0], 1, 1).astype(BF16)

        (g1, g1_own, g1_oth, dpre1, back1, sums2) = call(
            mlp_back_body, "back_b",
            [g2, back2, far_back2, s4, s3, *small, slope1, *wd, *wu],
            [full, half_low, half_low, hid_low, full_low, sds((11, width))],
            flops=mlp_flops, hold=[*keep_a, s2, n1_own, n1_oth, hid1, *wq, *wp, hid3, s5, sums3],
        )
        far_back1 = over_ha(back1)
        streams_b = mlp_streams(SPLIT_B)
        slot(
            "wgrad_b", write_mlp, streams_b,
            gradient_sources(dpre1, n1_own, n1_oth, g1_own, g1_oth, hid1),
            moving=[*streams_d, *streams_c],
            hold=[*keep_a, s2, *small, *wq, *wp, g1, *late, sums3, sums2, back1, far_back1],
        )

        def window_back_body(
            g_in, part_a, part_b, s_in, small_a, small_b, qkv_ref, probs_ref, wp_a, wp_b,
            g_ref, g_own, g_oth, dpk_ref, sums_ref,
        ):
            gain = gain_row((small_a, small_b), 1)
            grad = add_norm_back(g_in[...], part_a, part_b, s_in[...], gain, sums_ref)
            g_ref[...] = grad
            low = grad.astype(BF16)
            put_both(g_own, g_oth, low)
            grad_mixed = project_back(low, wp_a[0], wp_b[0]).astype(BF16)
            attention_part_back(True, grad_mixed, None, qkv_ref, probs_ref, dpk_ref)

        (g0, g0_own, g0_oth, dpk0, sums1) = call(
            window_back_body, "back_a",
            [g1, back1, far_back1, s2, *small, qkv0, probs0, *wp],
            [full, half_low, half_low, qkv_low, sds((2, width))],
            flops=attn_flops, hold=[x0, n0_own, n0_oth, mixed0, s1, *wq, *late, sums3, sums2],
        )

        def first_back_body(
            g_in, dpk_ref, s_in, x_ref, small_a, small_b, wq_a, wq_b,
            sums_one, sums_two, sums_three, kept, sent, sums_own, sums_oth, scratch, sums_ref,
        ):
            keep = column_mask(rows)
            packed = [dpk_ref[part] for part in range(3)]
            upstream = jnp.concatenate(qkv_back(packed, 0, wq_a, wq_b), axis=1)
            units, inv_std = norm_stats(s_in[...])
            sums_ref[0:1, :] = jnp.sum(upstream * units, axis=0, keepdims=True)
            sums_ref[1:2, :] = jnp.sum(upstream, axis=0, keepdims=True)
            grad = jnp.where(here("ha") == 0, g_in[...], 0.0)
            grad = grad + norm_back(upstream, units, inv_std, gain_row((small_a, small_b), 0))
            conv_back_into(
                scratch, sums_ref, 2, grad, x_ref[...].astype(F32), (small_a, small_b), 0, keep
            )
            ship(scratch[...], kept, sent)
            sums_ref[11:13, :] = 0.5 * sums_one[...]
            sums_ref[13:24, :] = 0.5 * sums_two[...]
            sums_ref[24:26, :] = 0.5 * sums_three[...]
            sums_ref[26:, :] = jnp.zeros((sum_rows - 26, width), F32)
            put_both(sums_own, sums_oth, sums_ref[...])

        sums_half = sds((sum_rows, half))
        token_kept, token_sent, sums_own, sums_oth = call(
            first_back_body, "back_0",
            [g0, dpk0, s1, x0, *small, *wq, sums1, sums2, sums3],
            shipped + [sums_half] * 2,
            scratch=[pltpu.VMEM((rows, width), F32), pltpu.VMEM((sum_rows, width), F32)],
            flops=attn_flops * 3 // 4,
            hold=[n0_own, n0_oth, mixed0, g0_own, g0_oth, *late],
        )
        keep_wgrad = [dpk0, n0_own, n0_oth, g0_own, g0_oth, mixed0]

        sums_at = -(-rows_in // 16) * 16

        def fold_tokens(kept, received, sums_a, sums_b, stay, go, sums_ref):
            fold(kept, received, stay, go)
            high, low = split_low(sums_a[...] + sums_b[...])
            sums_ref[...] = high.astype(F32) + low.astype(F32)
            go[sums_at : sums_at + sum_rows, :] = high
            go[sums_at + sum_rows :, :] = low

        token_stay, token_go, sums_chip = call(
            fold_tokens, "fold_tokens",
            [token_kept, over_wa(token_sent), sums_own, over_wa(sums_oth)],
            [shipped[0], sds((sums_at + 2 * sum_rows, half), BF16), sums_half],
            hold=[*late, *keep_wgrad],
        )
        token_got = over_ha(token_go)
        out_kept, out_sent = call(
            out_body, "out_d", [s5, hid3, *wd], shipped, flops=mlp_flops // 2,
            hold=[*keep_wgrad, token_stay, sums_chip],
        )
        out_stay, out_go = call(
            fold, "fold_out", [out_kept, over_wa(out_sent)], shipped,
            hold=[*keep_wgrad, token_stay, sums_chip],
        )
        out_got = over_ha(out_go)

        def join_tokens(stay, received, sums_chip, out_ref, sums_ref):
            join(stay, received, out_ref)
            sums_ref[...] = sums_chip[...] + joined(received, sums_at)

        earlier = [*streams_d, *streams_c, *streams_b]
        slot(
            "halve_bc", moving=[s for s in earlier if s.step < bits],
            ending=[s for s in earlier if s.step == bits],
            hold=[*keep_wgrad, token_stay, sums_chip, out_stay],
        )
        streams_a = attn_streams(SPLIT_A)
        slot(
            "wgrad_a", write_attn, streams_a,
            gradient_sources(dpk0, n0_own, n0_oth, g0_own, g0_oth, mixed0),
            hold=[token_stay, sums_chip, out_stay],
        )
        owned = sds((rows_in, half))
        grad_tokens, sums_ha = call(
            join_tokens, "join_tokens", [token_stay, token_got, sums_chip], [owned, sums_half],
            hold=[out_stay],
        )
        left_bits = list(range(bits))
        sums = [sums_ha, None, 0, left_bits.pop(0)]
        turn = 0
        while left_bits or any(stream.step < bits for stream in [*earlier, *streams_a]):
            turn += 1
            moving = [s for s in earlier if s.step < bits]
            arrived = [s for s in earlier if s.step == bits and s.final is None]
            if moving:
                slot(f"halve_{turn}", moving=moving, sums=sums if turn == 1 else None)
            if turn == 1:
                output = call(join, "join_out", [out_stay, out_got], [owned])[0]
            now = None
            if left_bits:
                sums[3] = left_bits.pop(0)
                now = sums
            slot(
                f"halve_a{turn}", moving=[s for s in streams_a if s.step < bits],
                ending=arrived, sums=now,
            )

        def finish_body(*refs):
            (up, down, qkv, proj, taps_ref, gain_ref, shift_ref) = refs[-7:]
            at = iter(refs)
            total = next(at)[...] + joined(next(at), sums[2])
            for branch, row in enumerate((0, 11, 13, 24)):
                gain_ref[branch : branch + 1, :] = total[row : row + 1]
                shift_ref[branch : branch + 1, :] = total[row + 1 : row + 2]
            for section, row in enumerate((2, 15)):
                for t in range(9):
                    taps_ref[t, section : section + 1, :] = total[row + t : row + t + 1]

            def finished(stream):
                if stream.final is not None:
                    return next(at)[...]
                return last_sum(stream, next(at), next(at))

            for section, streams in enumerate(
                ((*streams_a, *streams_b), (*streams_c, *streams_d))
            ):
                for stream in streams:
                    values, row = finished(stream), 0
                    for piece in stream.pieces:
                        part = values[row : row + piece_rows(piece)]
                        row += piece_rows(piece)
                        if piece == "up":
                            up[section] = part
                        elif piece == "proj":
                            proj[section] = part
                        elif isinstance(piece, tuple):
                            down[section, :, piece[1] * half : (piece[1] + 1) * half] = part
                        else:
                            qkv[section, ("q", "k", "v").index(piece)] = part

        ends = []
        for stream in (*streams_a, *streams_b, *streams_c, *streams_d):
            ends += [stream.kept, stream.got] if stream.final is None else [stream.final]
        up, down, qkv, proj, grad_taps, grad_gain, grad_shift = call(
            finish_body, "finish", [*sums[:2], *ends],
            [sds((2, up_rows, half)), sds((2, down_rows, hidden)), sds((2, 3, qkv_rows, half)),
             sds((2, proj_rows, half)), sds((9, 2, half)), sds((4, half)), sds((4, half))],
        )
        grad_taps = jnp.transpose(grad_taps, (1, 0, 2))
        grad_qkv = jnp.transpose(qkv, (0, 3, 1, 2))
        grad_proj, grad_up, grad_down = (
            jnp.transpose(values, (0, 2, 1)) for values in (proj, up, down)
        )
        return (
            output,
            grad_tokens,
            grad_taps,
            grad_gain,
            grad_shift,
            grad_qkv,
            grad_proj,
            grad_up,
            grad_down,
        )

    placed = (
        P(("dev", "ha"), "wa"),
        P(("dev", "ha"), "wa"),
        P(None, None, "wa"),
        P(None, "wa"),
        P(None, "wa"),
        P(None, "wa", None, "ha"),
        P(None, "ha", "wa"),
        P(None, "wa", "ha"),
        P(None, "ha", "wa"),
        P("dev", None),
    )
    return jax.shard_map(
        on_device,
        mesh=mesh,
        in_specs=placed,
        out_specs=(
            P(("dev", "ha"), "wa"),
            P(("dev", "ha"), "wa"),
            P(None, None, "wa"),
            P(None, "wa"),
            P(None, "wa"),
            P(None, "wa", None, ("ha", "dev")),
            P(None, "ha", ("wa", "dev")),
            P(None, "wa", ("ha", "dev")),
            P(None, "ha", ("wa", "dev")),
        ),
        check_vma=False,
    )
```

time: 196 us -> 164 us (0.84)
  starting transfers between devices: 46 us -> 35.7 us
  local copies, waits for them, and re-layouts: 13.7 us -> 7.81 us
  Pallas kernels: 39.5 us -> 34.2 us
  other arithmetic: 5.29 us -> 0 us
  waiting for transfers between devices: 89.4 us -> 85.3 us
    ppermute x15 -> x17, waiting for transfers between devices: 48.9 us -> 31.3 us  [over_dev(): lax.ppermute(values, 'dev', [(i, i ^ 1 << bit) for i in range(n_dev)])]
    ppermute x11 -> x10, starting transfers between devices: 17 us -> 8.34 us  [over_ha(): return lax.ppermute(values, 'ha', swap)]
    squeeze x4 -> x0, local copies, waits for them, and re-layouts: 8.03 us -> none  [the longest x1 2.88 us: on_device(): wd = [both_cores(later(w_down[at], part0), part0) for at in range(2)]]
    ppermute x11 -> x10, waiting for transfers between devices: 34.7 us -> 41.4 us  [over_ha(): return lax.ppermute(values, 'ha', swap)]
    ppermute x30 -> x26, waiting for transfers between devices: 5.85 us -> 12.5 us  [over_wa(): return lax.ppermute(values, 'wa', swap)]
    pallas_call x30 -> x26, Pallas kernels: 39.5 us -> 34.2 us  [kernel_call(): pl.pallas_call(wrapped, in_specs=specs, out_specs=[pl.BlockSpec(memory_sp...]
    transpose x4 -> x0, other arithmetic: 3.17 us -> none  [the longest x1 0.86 us: on_device(): jnp.transpose(jnp.stack([down_of(sum_b), down_of(sum_d)]), (0, 2, 1))]
    unnamed x30 -> x26, local copies, waits for them, and re-layouts: 4.9 us -> 7.81 us
  transfers between devices with their start and end apart: 56 -> 53, of which waited for: 22 -> 27; matrix products, arithmetic and copies ran while one was open for 6% -> 0% of each run, Pallas kernels for 15% -> 14%
where the time goes in v3:
time: 164 us
  waiting for transfers between devices  85.3 us (52%)
  starting transfers between devices  35.7 us (22%)
  Pallas kernels  34.2 us (21%)
  local copies, waits for them, and re-layouts  7.81 us (5%)
    ppermute x10, waiting for transfers between devices, over_ha(): return lax.ppermute(values, 'ha', swap)  41.4 us
    pallas_call x26, Pallas kernels, kernel_call(): pl.pallas_call(wrapped, in_specs=specs, out_specs=[pl.BlockSpec(memory_sp...  34.2 us
    ppermute x17, waiting for transfers between devices, over_dev(): lax.ppermute(values, 'dev', [(i, i ^ 1 << bit) for i in range(n_dev)])  31.3 us
    ppermute x17, starting transfers between devices, over_dev(): lax.ppermute(values, 'dev', [(i, i ^ 1 << bit) for i in range(n_dev)])  22.3 us
    ppermute x26, waiting for transfers between devices, over_wa(): return lax.ppermute(values, 'wa', swap)  12.5 us
    ppermute x10, starting transfers between devices, over_ha(): return lax.ppermute(values, 'ha', swap)  8.34 us
    unnamed x26, local copies, waits for them, and re-layouts  7.81 us
    ppermute x26, starting transfers between devices, over_wa(): return lax.ppermute(values, 'wa', swap)  5.05 us
  transfers between devices with their start and end apart: 53, of which 27 were waited for; matrix products, arithmetic and copies ran while one was open for 0% of the time, Pallas kernels for 14%

profile of v3, /device:TPU:0, one launch (start us, length us, event | category | flops | bytes accessed | tf_op | source)
XLA Modules:
  0.0 163.9 jit_solution(7957460979301535001)
XLA Ops:
  1.2 2.9 %collective-permute-start = (bf16[147,384]{1,0:T(8,128)(2,1)}, bf16[147,384]{1,0:T(8,128)(2,1)S(1)}, u32[]{:S(2)}, u32[]{:S(2)}) collective-permute-start(bf16[147,384]{1,0:T(8,128)(2,1)} %refs_0_.2), channel_id=1, source_target_pairs={{0,2},{2,0},{1,3},{3,1},{4,6},{6,4},{5,7},{7,5},{8,10},{10,8},{9,1... | collective-permute-start | bytes 338696 | tf_op jit(solution)/shard_map/ppermute | solution.py:244
  13.7 3.7 %attn_a.1 = (bf16[168,768]{1,0:T(8,128)(2,1)S(1)}, f32[168,768]{1,0:T(8,128)S(1)}, bf16[168,384]{1,0:T(8,128)(2,1)S(1)}, bf16[168,384]{1,0:T(8,128)(2,1)S(1)}, b...) custom-call(bf16[147,384]{1,0:T(8,128)(2,1)S(1)} %get-tuple-element., ...), custom_call_target="tpu_custom_call" | custom-call | tf_op jit(solution)/shard_map/attn_a/pallas_call | solution.py:58
  17.6 8.6 %collective-permute-done.5.refs_2_ = bf16[168,768]{1,0:T(8,128)(2,1)S(1)} collective-permute-done((bf16[168,768]{1,0:T(8,128)(2,1)S(1)}, bf16[168,768]{1,0:T(8,128)(2,1)S(1)}, u32[]{:S(2)}, u32[]{:S(2)}) %collective-permute-start.5) | collective-permute-done | bytes 258080 | tf_op jit(solution)/shard_map/ppermute | solution.py:244
  26.2 2.2 %mlp_b.1 = (f32[168,768]{1,0:T(8,128)S(1)}, bf16[168,384]{1,0:T(8,128)(2,1)S(1)}, bf16[168,384]{1,0:T(8,128)(2,1)S(1)}, bf16[168,1536]{1,0:T(8,128)(2,1)S(1)}, f...) custom-call(f32[168,768]{1,0:T(8,128)S(1)} %get-tuple-element.169.refs_0_.refs_15_.refs_16_.refs_8_.refs_1, ...), custom_call_target="tpu_custom_call" | custom-call | tf_op jit(solution)/shard_map/mlp_b/pallas_call | solution.py:58
  30.5 8.3 %collective-permute-done.9.refs_26_.refs_1_ = bf16[147,384]{1,0:T(8,128)(2,1)S(1)} collective-permute-done((bf16[147,384]{1,0:T(8,128)(2,1)S(1)}, bf16[147,384]{1,0:T(8,128)(2,1)S(1)}, u32[]{:S(2)}, u32[]{:S(2)}) %collective-permute-start.9) | collective-permute-done | bytes 112928 | tf_op jit(solution)/shard_map/ppermute | solution.py:244
  43.9 4.0 %collective-permute-done.10.refs_2_ = bf16[168,768]{1,0:T(8,128)(2,1)S(1)} collective-permute-done((bf16[168,768]{1,0:T(8,128)(2,1)S(1)}, bf16[168,768]{1,0:T(8,128)(2,1)S(1)}, u32[]{:S(2)}, u32[]{:S(2)}) %collective-permute-start.10) | collective-permute-done | bytes 258080 | tf_op jit(solution)/shard_map/ppermute | solution.py:244
  47.9 2.5 %mlp_d.1 = (f32[168,768]{1,0:T(8,128)S(1)}, bf16[168,384]{1,0:T(8,128)(2,1)S(1)}, bf16[168,384]{1,0:T(8,128)(2,1)S(1)}, bf16[168,1536]{1,0:T(8,128)(2,1)S(1)}, b...) custom-call(f32[168,768]{1,0:T(8,128)S(1)} %get-tuple-element.190.refs_15_.refs_17_.refs_0_.refs_21_, ...), custom_call_target="tpu_custom_call" | custom-call | tf_op jit(solution)/shard_map/mlp_d/pallas_call | solution.py:58
  59.7 2.9 %back_c.1 = (f32[168,768]{1,0:T(8,128)S(1)}, bf16[168,384]{1,0:T(8,128)(2,1)S(1)}, bf16[168,384]{1,0:T(8,128)(2,1)S(1)}, bf16[3,168,384]{2,1,0:T(8,128)(2,1)S(1)...) custom-call(bf16[168,384]{1,0:T(8,128)(2,1)S(1)} %get-tuple-element.204.refs_28_.refs_4_.refs_0_, ...), custom_call_target="tpu_custom_call" | custom-call | tf_op jit(solution)/shard_map/back_c/pallas_call | solution.py:58
  66.1 5.3 %collective-permute-done.17.refs_43_.refs_2_ = bf16[168,768]{1,0:T(8,128)(2,1)S(1)} collective-permute-done((bf16[168,768]{1,0:T(8,128)(2,1)S(1)}, bf16[168,768]{1,0:T(8,128)(2,1)S(1)}, u32[]{:S(2)}, u32[]{:S(2)}) %collective-permute-start.17) | collective-permute-done | bytes 258080 | tf_op jit(solution)/shard_map/ppermute | solution.py:244
  76.2 2.8 %back_b.1 = (f32[168,768]{1,0:T(8,128)S(1)}, bf16[168,384]{1,0:T(8,128)(2,1)S(1)}, bf16[168,384]{1,0:T(8,128)(2,1)S(1)}, bf16[168,1536]{1,0:T(8,128)(2,1)S(1)}, ...) custom-call(f32[168,768]{1,0:T(8,128)S(1)} %get-tuple-element.215.refs_36_.refs_0_, ...), custom_call_target="tpu_custom_call" | custom-call | tf_op jit(solution)/shard_map/back_b/pallas_call | solution.py:58
  83.1 6.4 %collective-permute-done.24.refs_36_.refs_2_ = bf16[168,768]{1,0:T(8,128)(2,1)S(1)} collective-permute-done((bf16[168,768]{1,0:T(8,128)(2,1)S(1)}, bf16[168,768]{1,0:T(8,128)(2,1)S(1)}, u32[]{:S(2)}, u32[]{:S(2)}) %collective-permute-start.24) | collective-permute-done | bytes 258080 | tf_op jit(solution)/shard_map/ppermute | solution.py:244
  89.5 2.2 %wgrad_b.1 = (bf16[960,384]{1,0:T(8,128)(2,1)S(1)}, bf16[576,384]{1,0:T(8,128)(2,1)S(1)}, bf16[192,384]{1,0:T(8,128)(2,1)S(1)}, bf16[192,384]{1,0:T(8,128)(2,1)S...) custom-call(bf16[168,1536]{1,0:T(8,128)(2,1)S(1)} %get-tuple-element, ...), custom_call_target="tpu_custom_call" | custom-call | tf_op jit(solution)/shard_map/wgrad_b/pallas_call | solution.py:58
  93.5 2.5 %collective-permute-start.37 = (bf16[384,384]{1,0:T(8,128)(2,1)S(1)}, bf16[384,384]{1,0:T(8,128)(2,1)S(1)}, u32[]{:S(2)}, u32[]{:S(2)}) collective-permute-start(bf16[384,384]{1,0:T(8,128)(2,1)S(1)} %get-tuple-element.267), channel_id=1, source_target_pairs={{0,16},{4,20},{8,24},{12,28},{16,0},{20,4},{24,8},{28,12},{1,17},{... | collective-permute-start | bytes 884744 | tf_op jit(solution)/shard_map/ppermute | solution.py:250
  96.0 2.9 %back_a.1 = (f32[168,768]{1,0:T(8,128)S(1)}, bf16[168,384]{1,0:T(8,128)(2,1)S(1)}, bf16[168,384]{1,0:T(8,128)(2,1)S(1)}, bf16[3,168,384]{2,1,0:T(8,128)(2,1)S(1)...) custom-call(f32[168,768]{1,0:T(8,128)S(1)} %get-tuple-element.227.refs_28_.refs_0_, ...), custom_call_target="tpu_custom_call" | custom-call | tf_op jit(solution)/shard_map/back_a/pallas_call | solution.py:58
  98.9 2.2 %back_0.1 = (bf16[147,384]{1,0:T(8,128)(2,1)S(1)}, bf16[147,384]{1,0:T(8,128)(2,1)S(1)}, f32[32,384]{1,0:T(8,128)S(1)}, f32[32,384]{1,0:T(8,128)S(1)}, f32[8,128]{1,0:T(8,128)S(1)}) custom-call(f32[168,768]{1,0:T(8,128)S(1)} %get-tuple-element.244.refs_0_, bf16[3,168,384]{2,1,0:T(8,128)(2,1)S(1)} %get-tuple-element.241.refs_1_.refs_8_.refs_4_.refs_2_.refs_9_.refs_0_, ...), custom_call_target="tpu_custom_call" | custom-call | tf_op jit(solution)/shard_map/back_0/pallas_call | solution.py:58
  106.3 5.3 %collective-permute-done.37.refs_7_ = bf16[384,384]{1,0:T(8,128)(2,1)S(1)} collective-permute-done((bf16[384,384]{1,0:T(8,128)(2,1)S(1)}, bf16[384,384]{1,0:T(8,128)(2,1)S(1)}, u32[]{:S(2)}, u32[]{:S(2)}) %collective-permute-start.37) | collective-permute-done | bytes 294944 | tf_op jit(solution)/shard_map/ppermute | solution.py:250
  117.0 2.7 %collective-permute-start.38 = (bf16[480,384]{1,0:T(8,128)(2,1)S(1)}, bf16[480,384]{1,0:T(8,128)(2,1)S(1)}, u32[]{:S(2)}, u32[]{:S(2)}) collective-permute-start(bf16[480,384]{1,0:T(8,128)(2,1)S(1)} %get-tuple-element.271), channel_id=1, source_target_pairs={{0,8},{4,12},{8,0},{12,4},{16,24},{20,28},{24,16},{28,20},{1,9},{5... | collective-permute-start | bytes 1105928 | tf_op jit(solution)/shard_map/ppermute | solution.py:250
  121.5 5.3 %collective-permute-done.40.refs_1_ = bf16[224,384]{1,0:T(8,128)(2,1)S(1)} collective-permute-done((bf16[224,384]{1,0:T(8,128)(2,1)S(1)}, bf16[224,384]{1,0:T(8,128)(2,1)S(1)}, u32[]{:S(2)}, u32[]{:S(2)}) %collective-permute-start.40) | collective-permute-done | bytes 172064 | tf_op jit(solution)/shard_map/ppermute | solution.py:244
  126.8 6.3 %collective-permute-done.39.refs_3_ = bf16[288,384]{1,0:T(8,128)(2,1)S(1)} collective-permute-done((bf16[288,384]{1,0:T(8,128)(2,1)S(1)}, bf16[288,384]{1,0:T(8,128)(2,1)S(1)}, u32[]{:S(2)}, u32[]{:S(2)}) %collective-permute-start.39) | collective-permute-done | bytes 221216 | tf_op jit(solution)/shard_map/ppermute | solution.py:250
  135.4 2.6 %collective-permute-done.34.refs_1_ = bf16[147,384]{1,0:T(8,128)(2,1)S(1)} collective-permute-done((bf16[147,384]{1,0:T(8,128)(2,1)S(1)}, bf16[147,384]{1,0:T(8,128)(2,1)S(1)}, u32[]{:S(2)}, u32[]{:S(2)}) %collective-permute-start.34) | collective-permute-done | bytes 112928 | tf_op jit(solution)/shard_map/ppermute | solution.py:244
  142.8 3.6 %collective-permute-done.50.refs_3_ = bf16[96,384]{1,0:T(8,128)(2,1)S(1)} collective-permute-done((bf16[96,384]{1,0:T(8,128)(2,1)S(1)}, bf16[96,384]{1,0:T(8,128)(2,1)S(1)}, u32[]{:S(2)}, u32[]{:S(2)}) %collective-permute-start.50) | collective-permute-done | bytes 73760 | tf_op jit(solution)/shard_map/ppermute | solution.py:250
  146.3 5.9 %collective-permute-done.51.refs_5_ = bf16[384,384]{1,0:T(8,128)(2,1)S(1)} collective-permute-done((bf16[384,384]{1,0:T(8,128)(2,1)S(1)}, bf16[384,384]{1,0:T(8,128)(2,1)S(1)}, u32[]{:S(2)}, u32[]{:S(2)}) %collective-permute-start.51) | collective-permute-done | bytes 294944 | tf_op jit(solution)/shard_map/ppermute | solution.py:250
  152.4 2.8 %collective-permute-start.52 = (bf16[256,384]{1,0:T(8,128)(2,1)S(1)}, bf16[256,384]{1,0:T(8,128)(2,1)S(1)}, u32[]{:S(2)}, u32[]{:S(2)}) collective-permute-start(bf16[256,384]{1,0:T(8,128)(2,1)S(1)} %get-tuple-element.302), channel_id=1, source_target_pairs={{0,16},{4,20},{8,24},{12,28},{16,0},{20,4},{24,8},{28,12},{1,17},{... | collective-permute-start | bytes 589832 | tf_op jit(solution)/shard_map/ppermute | solution.py:250
  155.3 7.3 %collective-permute-done.52.refs_1_.refs_3_.refs_5_ = bf16[256,384]{1,0:T(8,128)(2,1)S(1)} collective-permute-done((bf16[256,384]{1,0:T(8,128)(2,1)S(1)}, bf16[256,384]{1,0:T(8,128)(2,1)S(1)}, u32[]{:S(2)}, u32[]{:S(2)}) %collective-permute-start.52) | collective-permute-done | bytes 196640 | tf_op jit(solution)/shard_map/ppermute | solution.py:250
  (134 shorter events, 61.5 us)
Async XLA Ops:
  0.6 9.2 %collective-permute-start.1 = (bf16[2,3,384,384]{3,2,1,0:T(8,128)(2,1)}, bf16[2,3,384,384]{3,2,1,0:T(8,128)(2,1)S(1)}, u32[]{:S(2)}, u32[]{:S(2)}) collective-permute-start(bf16[2,3,384,384]{3,2,1,0:T(8,128)(2,1)} %bitcast.7), channel_id=1, source_target_pairs={{0,1},{1,0},{2,3},{3,2},{4,5},{5,4},{6,7},{7,6},{8,9},{9,8},{10,11... | collective-permute-start | bytes 5308424 | tf_op jit(solution)/shard_map/ppermute | solution.py:247
  13.0 13.1 %collective-permute-start.7 = (bf16[2,1536,384]{2,1,0:T(8,128)(2,1)S(1)}, bf16[2,1536,384]{2,1,0:T(8,128)(2,1)S(1)}, u32[]{:S(2)}, u32[]{:S(2)}) collective-permute-start(bf16[2,1536,384]{2,1,0:T(8,128)(2,1)S(1)} %copy-done), channel_id=1, source_target_pairs={{0,1},{1,0},{2,3},{3,2},{4,5},{5,4},{6,7},{7,6},{8,9},{9,8},{10,11... | collective-permute-start | bytes 7077896 | tf_op jit(solution)/shard_map/ppermute | solution.py:247
  13.7 12.4 %collective-permute-start.6 = (bf16[2,384,1536]{2,1,0:T(8,128)(2,1)S(1)}, bf16[2,384,1536]{2,1,0:T(8,128)(2,1)S(1)}, u32[]{:S(2)}, u32[]{:S(2)}) collective-permute-start(bf16[2,384,1536]{2,1,0:T(8,128)(2,1)S(1)} %copy-done.3), channel_id=1, source_target_pairs={{0,1},{1,0},{2,3},{3,2},{4,5},{5,4},{6,7},{7,6},{8,9},{9,8},{10,11... | collective-permute-start | bytes 7077896 | tf_op jit(solution)/shard_map/ppermute | solution.py:247
  28.4 10.4 %collective-permute-start.8 = (bf16[168,768]{1,0:T(8,128)(2,1)S(1)}, bf16[168,768]{1,0:T(8,128)(2,1)S(1)}, u32[]{:S(2)}, u32[]{:S(2)}) collective-permute-start(bf16[168,768]{1,0:T(8,128)(2,1)S(1)} %get-tuple-element.183.refs_1_), channel_id=1, source_target_pairs={{0,2},{2,0},{1,3},{3,1},{4,6},{6,4},{5,7},{7,5},{8,10},{10,8},{9,1... | collective-permute-start | bytes 774152 | tf_op jit(solution)/shard_map/ppermute | solution.py:244
  28.8 10.1 %collective-permute-start.9 = (bf16[147,384]{1,0:T(8,128)(2,1)S(1)}, bf16[147,384]{1,0:T(8,128)(2,1)S(1)}, u32[]{:S(2)}, u32[]{:S(2)}) collective-permute-start(bf16[147,384]{1,0:T(8,128)(2,1)S(1)} %copy-done.8), channel_id=1, source_target_pairs={{0,2},{2,0},{1,3},{3,1},{4,6},{6,4},{5,7},{7,5},{8,10},{10,8},{9,1... | collective-permute-start | bytes 338696 | tf_op jit(solution)/shard_map/ppermute | solution.py:244
  55.5 15.9 %collective-permute-start.22 = (bf16[768,384]{1,0:T(8,128)(2,1)S(1)}, bf16[768,384]{1,0:T(8,128)(2,1)S(1)}, u32[]{:S(2)}, u32[]{:S(2)}) collective-permute-start(bf16[768,384]{1,0:T(8,128)(2,1)S(1)} %get-tuple-element.222), channel_id=1, source_target_pairs={{0,4},{4,0},{8,12},{12,8},{16,20},{20,16},{24,28},{28,24},{1,5},{5... | collective-permute-start | bytes 1769480 | tf_op jit(solution)/shard_map/ppermute | solution.py:250
  57.1 15.1 %collective-permute-start.23 = (bf16[768,384]{1,0:T(8,128)(2,1)S(1)}, bf16[768,384]{1,0:T(8,128)(2,1)S(1)}, u32[]{:S(2)}, u32[]{:S(2)}) collective-permute-start(bf16[768,384]{1,0:T(8,128)(2,1)S(1)} %get-tuple-element.224), channel_id=1, source_target_pairs={{0,8},{4,12},{8,0},{12,4},{16,24},{20,28},{24,16},{28,20},{1,9},{5... | collective-permute-start | bytes 1769480 | tf_op jit(solution)/shard_map/ppermute | solution.py:250
  62.6 8.8 %collective-permute-start.18 = (bf16[3,168,384]{2,1,0:T(8,128)(2,1)S(1)}, bf16[3,168,384]{2,1,0:T(8,128)(2,1)S(1)}, u32[]{:S(2)}, u32[]{:S(2)}) collective-permute-start(bf16[3,168,384]{2,1,0:T(8,128)(2,1)S(1)} %get-tuple-element.218.refs_0_), channel_id=1, source_target_pairs={{0,1},{1,0},{2,3},{3,2},{4,5},{5,4},{6,7},{7,6},{8,9},{9,8},{10,11... | collective-permute-start | bytes 1161224 | tf_op jit(solution)/shard_map/ppermute | solution.py:247
  66.0 15.8 %collective-permute-start.28 = (bf16[168,1536]{1,0:T(8,128)(2,1)S(1)}, bf16[168,1536]{1,0:T(8,128)(2,1)S(1)}, u32[]{:S(2)}, u32[]{:S(2)}) collective-permute-start(bf16[168,1536]{1,0:T(8,128)(2,1)S(1)} %get-tuple-element.186.refs_20_.refs_12_.refs_14_.refs_18_.refs_24_.refs_22_.refs_6_), channel_id=1, source_target_pairs={{0,1},{1,0},{2,3},{3,2},{4,5},{5,4},{6,7},{7,6},{8,9},{9,8},{10,11... | collective-permute-start | bytes 1548296 | tf_op jit(solution)/shard_map/ppermute | solution.py:247
  73.8 15.7 %collective-permute-start.29 = (bf16[768,384]{1,0:T(8,128)(2,1)S(1)}, bf16[768,384]{1,0:T(8,128)(2,1)S(1)}, u32[]{:S(2)}, u32[]{:S(2)}) collective-permute-start(bf16[768,384]{1,0:T(8,128)(2,1)S(1)} %get-tuple-element.234), channel_id=1, source_target_pairs={{0,8},{4,12},{8,0},{12,4},{16,24},{20,28},{24,16},{28,20},{1,9},{5... | collective-permute-start | bytes 1769480 | tf_op jit(solution)/shard_map/ppermute | solution.py:250
  75.5 14.0 %collective-permute-start.30 = (bf16[768,384]{1,0:T(8,128)(2,1)S(1)}, bf16[768,384]{1,0:T(8,128)(2,1)S(1)}, u32[]{:S(2)}, u32[]{:S(2)}) collective-permute-start(bf16[768,384]{1,0:T(8,128)(2,1)S(1)} %get-tuple-element.236), channel_id=1, source_target_pairs={{0,4},{4,0},{8,12},{12,8},{16,20},{20,16},{24,28},{28,24},{1,5},{5... | collective-permute-start | bytes 1769480 | tf_op jit(solution)/shard_map/ppermute | solution.py:250
  79.1 10.4 %collective-permute-start.25 = (bf16[168,1536]{1,0:T(8,128)(2,1)S(1)}, bf16[168,1536]{1,0:T(8,128)(2,1)S(1)}, u32[]{:S(2)}, u32[]{:S(2)}) collective-permute-start(bf16[168,1536]{1,0:T(8,128)(2,1)S(1)} %get-tuple-element.230.refs_0_), channel_id=1, source_target_pairs={{0,1},{1,0},{2,3},{3,2},{4,5},{5,4},{6,7},{7,6},{8,9},{9,8},{10,11... | collective-permute-start | bytes 1548296 | tf_op jit(solution)/shard_map/ppermute | solution.py:247
  91.7 21.9 %collective-permute-start.36 = (bf16[1152,384]{1,0:T(8,128)(2,1)S(1)}, bf16[1152,384]{1,0:T(8,128)(2,1)S(1)}, u32[]{:S(2)}, u32[]{:S(2)}) collective-permute-start(bf16[1152,384]{1,0:T(8,128)(2,1)S(1)} %get-tuple-element.263), channel_id=1, source_target_pairs={{0,4},{4,0},{8,12},{12,8},{16,20},{20,16},{24,28},{28,24},{1,5},{5... | collective-permute-start | bytes 2654216 | tf_op jit(solution)/shard_map/ppermute | solution.py:250
  93.1 20.6 %collective-permute-start.35 = (bf16[768,384]{1,0:T(8,128)(2,1)S(1)}, bf16[768,384]{1,0:T(8,128)(2,1)S(1)}, u32[]{:S(2)}, u32[]{:S(2)}) collective-permute-start(bf16[768,384]{1,0:T(8,128)(2,1)S(1)} %get-tuple-element.261), channel_id=1, source_target_pairs={{0,8},{4,12},{8,0},{12,4},{16,24},{20,28},{24,16},{28,20},{1,9},{5... | collective-permute-start | bytes 1769480 | tf_op jit(solution)/shard_map/ppermute | solution.py:250
  93.5 18.1 %collective-permute-start.37 = (bf16[384,384]{1,0:T(8,128)(2,1)S(1)}, bf16[384,384]{1,0:T(8,128)(2,1)S(1)}, u32[]{:S(2)}, u32[]{:S(2)}) collective-permute-start(bf16[384,384]{1,0:T(8,128)(2,1)S(1)} %get-tuple-element.267), channel_id=1, source_target_pairs={{0,16},{4,20},{8,24},{12,28},{16,0},{20,4},{24,8},{28,12},{1,17},{... | collective-permute-start | bytes 884744 | tf_op jit(solution)/shard_map/ppermute | solution.py:250
  101.2 13.8 %collective-permute-start.41 = (bf16[3,168,384]{2,1,0:T(8,128)(2,1)S(1)}, bf16[3,168,384]{2,1,0:T(8,128)(2,1)S(1)}, u32[]{:S(2)}, u32[]{:S(2)}) collective-permute-start(bf16[3,168,384]{2,1,0:T(8,128)(2,1)S(1)} %get-tuple-element.241.refs_1_.refs_8_.refs_4_.refs_2_.refs_9_.refs_0_), channel_id=1, source_target_pairs={{0,1},{1,0},{2,3},{3,2},{4,5},{5,4},{6,7},{7,6},{8,9},{9,8},{10,11... | collective-permute-start | bytes 1161224 | tf_op jit(solution)/shard_map/ppermute | solution.py:247
  116.1 24.3 %collective-permute-start.45 = (bf16[576,384]{1,0:T(8,128)(2,1)S(1)}, bf16[576,384]{1,0:T(8,128)(2,1)S(1)}, u32[]{:S(2)}, u32[]{:S(2)}) collective-permute-start(bf16[576,384]{1,0:T(8,128)(2,1)S(1)} %get-tuple-element.283), channel_id=1, source_target_pairs={{0,4},{4,0},{8,12},{12,8},{16,20},{20,16},{24,28},{28,24},{1,5},{5... | collective-permute-start | bytes 1327112 | tf_op jit(solution)/shard_map/ppermute | solution.py:250
  117.0 17.4 %collective-permute-start.38 = (bf16[480,384]{1,0:T(8,128)(2,1)S(1)}, bf16[480,384]{1,0:T(8,128)(2,1)S(1)}, u32[]{:S(2)}, u32[]{:S(2)}) collective-permute-start(bf16[480,384]{1,0:T(8,128)(2,1)S(1)} %get-tuple-element.271), channel_id=1, source_target_pairs={{0,8},{4,12},{8,0},{12,4},{16,24},{20,28},{24,16},{28,20},{1,9},{5... | collective-permute-start | bytes 1105928 | tf_op jit(solution)/shard_map/ppermute | solution.py:250
  119.7 13.5 %collective-permute-start.39 = (bf16[288,384]{1,0:T(8,128)(2,1)S(1)}, bf16[288,384]{1,0:T(8,128)(2,1)S(1)}, u32[]{:S(2)}, u32[]{:S(2)}) collective-permute-start(bf16[288,384]{1,0:T(8,128)(2,1)S(1)} %get-tuple-element.273), channel_id=1, source_target_pairs={{0,4},{4,0},{8,12},{12,8},{16,20},{20,16},{24,28},{28,24},{1,5},{5... | collective-permute-start | bytes 663560 | tf_op jit(solution)/shard_map/ppermute | solution.py:250
  121.5 18.9 %collective-permute-start.46 = (bf16[192,384]{1,0:T(8,128)(2,1)S(1)}, bf16[192,384]{1,0:T(8,128)(2,1)S(1)}, u32[]{:S(2)}, u32[]{:S(2)}) collective-permute-start(bf16[192,384]{1,0:T(8,128)(2,1)S(1)} %get-tuple-element.285), channel_id=1, source_target_pairs={{0,8},{4,12},{8,0},{12,4},{16,24},{20,28},{24,16},{28,20},{1,9},{5... | collective-permute-start | bytes 442376 | tf_op jit(solution)/shard_map/ppermute | solution.py:250
  126.7 13.7 %collective-permute-start.47 = (bf16[192,384]{1,0:T(8,128)(2,1)S(1)}, bf16[192,384]{1,0:T(8,128)(2,1)S(1)}, u32[]{:S(2)}, u32[]{:S(2)}) collective-permute-start(bf16[192,384]{1,0:T(8,128)(2,1)S(1)} %get-tuple-element.287), channel_id=1, source_target_pairs={{0,16},{4,20},{8,24},{12,28},{16,0},{20,4},{24,8},{28,12},{1,17},{... | collective-permute-start | bytes 442376 | tf_op jit(solution)/shard_map/ppermute | solution.py:250
  138.0 14.3 %collective-permute-start.51 = (bf16[384,384]{1,0:T(8,128)(2,1)S(1)}, bf16[384,384]{1,0:T(8,128)(2,1)S(1)}, u32[]{:S(2)}, u32[]{:S(2)}) collective-permute-start(bf16[384,384]{1,0:T(8,128)(2,1)S(1)} %get-tuple-element.297), channel_id=1, source_target_pairs={{0,16},{4,20},{8,24},{12,28},{16,0},{20,4},{24,8},{28,12},{1,17},{... | collective-permute-start | bytes 884744 | tf_op jit(solution)/shard_map/ppermute | solution.py:250
  140.6 11.6 %collective-permute-start.49 = (bf16[352,384]{1,0:T(8,128)(2,1)S(1)}, bf16[352,384]{1,0:T(8,128)(2,1)S(1)}, u32[]{:S(2)}, u32[]{:S(2)}) collective-permute-start(bf16[352,384]{1,0:T(8,128)(2,1)S(1)} %get-tuple-element.293), channel_id=1, source_target_pairs={{0,8},{4,12},{8,0},{12,4},{16,24},{20,28},{24,16},{28,20},{1,9},{5... | collective-permute-start | bytes 811016 | tf_op jit(solution)/shard_map/ppermute | solution.py:250
  152.4 10.1 %collective-permute-start.52 = (bf16[256,384]{1,0:T(8,128)(2,1)S(1)}, bf16[256,384]{1,0:T(8,128)(2,1)S(1)}, u32[]{:S(2)}, u32[]{:S(2)}) collective-permute-start(bf16[256,384]{1,0:T(8,128)(2,1)S(1)} %get-tuple-element.302), channel_id=1, source_target_pairs={{0,16},{4,20},{8,24},{12,28},{16,0},{20,4},{24,8},{28,12},{1,17},{... | collective-permute-start | bytes 589832 | tf_op jit(solution)/shard_map/ppermute | solution.py:250
  (42 other events, 149.9 us)

commit v4 on v3

--- a/solution.py
+++ b/solution.py
@@ -17,10 +17,11 @@
 HEADS_TILE = LANES // HEAD_DIM
 EPS = 1e-05
 NEG = -1e30
-SPLIT_D, SPLIT_C, SPLIT_B, SPLIT_A = 0, 2, 1, 3
+SPLIT_D, SPLIT_C, SPLIT_B, SPLIT_A = 0, 2, 0, 4
 BF16 = jnp.bfloat16
 F32 = jnp.float32
 VMEM_LIMIT = 16 * 2**20
+TIMES = {"pack_small": 5.0, "choose": 5.0}
 
 
 def mm(left, right, left_dim, right_dim):
@@ -62,7 +63,9 @@
         out_shape=outs,
         scratch_shapes=list(scratch),
         compiler_params=pltpu.CompilerParams(vmem_limit_bytes=VMEM_LIMIT),
-        cost_estimate=pl.CostEstimate(flops=0, bytes_accessed=0, transcendentals=0),
+        cost_estimate=pl.CostEstimate(
+            flops=int(TIMES.get(name, 0) * 1.15e9), bytes_accessed=0, transcendentals=0
+        ),
         name=name,
     )(*arrays)
     return results
@@ -260,7 +263,8 @@
         hidden = w_up.shape[2]
         tiles = heads_width // LANES
         assert heads_width == half
-        orders = [list(range(bits)), [1, 0, *range(2, bits)]]
+        rest = list(range(3, bits))
+        orders = [[0, 1, 2, *rest], [1, 0, 2, *rest], [0, 2, 1, *rest], [1, 2, 0, *rest]]
 
         def here(name):
             return lax.axis_index(name)
@@ -285,26 +289,29 @@
             out_ref[18:22, :] = gain_ref[...]
             out_ref[22:26, :] = shift_ref[...]
 
-        def choose(mine, received, own, other):
+        def choose(mine, received, cot, cot_received, own, other, cot_own, cot_other):
             same = here("ha") == here("wa")
             own[...] = jnp.where(same, mine[...], received[...])
             other[...] = jnp.where(same, received[...], mine[...])
+            cot_own[...] = jnp.where(same, cot[...], cot_received[...])
+            cot_other[...] = jnp.where(same, cot_received[...], cot[...])
 
         wq_own = jnp.transpose(w_qkv, (0, 2, 1, 3))
         wq, wp = (wq_own, over_wa(wq_own)), (w_proj, over_wa(w_proj))
-        tokens_in = over_ha(tokens)
+        tokens_in, cot_in = over_ha(tokens), over_ha(cotangent)
         small_own = call(
             pack_small, "pack_small",
             [jnp.transpose(conv_taps, (1, 0, 2)), norm_gain, norm_shift], [sds((26, half))],
-            hold=[wq_own, w_proj, tokens],
+            hold=[tokens],
         )[0]
         small = (small_own, over_wa(small_own))
-        chosen = [sds((rows_in, half), BF16)] * 2
-        tokens_own, tokens_oth = call(
-            choose, "choose_tokens", [tokens, tokens_in], chosen, hold=[*wq, *wp, small_own]
+        tokens_own, tokens_oth, cot_own, cot_oth = call(
+            choose, "choose", [tokens, tokens_in, cotangent, cot_in],
+            [sds((rows_in, half), BF16)] * 4, hold=[wq[1], wp[1], small_own],
         )
         token_parts = (tokens_own, over_wa(tokens_oth))
         arrived = (token_parts[1], small[1])
+        cot_parts = (cot_own, over_wa(later(cot_oth, arrived)))
         wu, wd = ((values, over_wa(later(values, arrived))) for values in (w_up, w_down))
 
         def unpack(own, oth):
@@ -337,9 +344,12 @@
                 BF16
             )
 
+        def both_rear(pieces):
+            return pieces, [over_wa(piece) for piece in pieces]
+
         def put_both(own_ref, oth_ref, values):
             own_ref[...] = values[:, :half]
-            oth_ref[...] = values[:, half:]
+            oth_ref[:, :half] = values[:, half:]
 
         def add_parts(stream, part_a, part_b):
             return stream[...] + part_a[...].astype(F32) + part_b[...].astype(F32)
@@ -368,7 +378,7 @@
                 mixed.append(jnp.concatenate(line, axis=1))
             return jnp.concatenate(mixed, axis=0).astype(BF16)
 
-        def attention_part_back(window, grad_mixed, mask_ref, qkv_ref, probs_ref, dpk_ref):
+        def attention_part_back(window, grad_mixed, mask_ref, qkv_ref, probs_ref, rear_refs):
             wide = [qkv_ref[part].astype(F32) for part in range(3)]
             grad = grad_mixed.astype(F32)
             found = [[], [], []]
@@ -391,7 +401,7 @@
                     found[part].append(jnp.concatenate(lines[part], axis=1))
             packed = [jnp.concatenate(part, axis=0).astype(BF16) for part in found]
             for part in range(3):
-                dpk_ref[part] = packed[part]
+                put_rear(rear_refs, half + part * heads_width, packed[part])
             return packed
 
         def mul_out(left, section, own_ref, oth_ref, out_ref):
@@ -417,12 +427,42 @@
         half_low = sds((rows, half), BF16)
         hid_low = sds((rows, hidden), BF16)
         qkv_low = sds((3, rows, heads_width), BF16)
+        fore_attn, fore_mlp = (
+            sds((rows, half + heads_width), BF16),
+            sds((rows, half + hidden), BF16),
+        )
+        def cuts(total, count):
+            tiles_all = total // LANES
+            return [LANES * (-(-tiles_all * (at + 1) // count)) for at in range(count)]
+
+        def rear_shapes(total, count):
+            ends = cuts(total, count)
+            return [sds((rows, e - b), BF16) for b, e in zip([0, *ends], ends)]
+
+        def rear_ranges(refs, at, size):
+            begin = 0
+            for ref in refs:
+                end = begin + ref.shape[1]
+                low, high = max(begin, at), min(end, at + size)
+                if low < high:
+                    yield ref, low - begin, high - begin, low - at
+                begin = end
+
+        def put_rear(refs, at, values):
+            for ref, low, high, source in rear_ranges(refs, at, values.shape[1]):
+                ref[:, low:high] = values[:, source : source + high - low]
+
+        def get_rear(refs, at, size):
+            parts = [ref[:, low:high] for ref, low, high, _ in rear_ranges(refs, at, size)]
+            return parts[0] if len(parts) == 1 else jnp.concatenate(parts, axis=1)
+
+        rear_width_attn, rear_width_mlp = half + 3 * heads_width, half + hidden
         attn_flops = 2 * rows * (4 * width * heads_width)
         mlp_flops = 2 * rows * (2 * width * hidden)
 
         def first_body(
             tokens_a, tokens_b, small_a, small_b, wq_a, wq_b, wp_a, wp_b,
-            x_ref, s_ref, n_own, n_oth, qkv_ref, probs_ref, mixed_ref, part_ref, keep_a, keep_b,
+            x_ref, s_ref, n_own, fore_ref, qkv_ref, probs_ref, part_ref, keep_a, keep_b,
         ):
             keep_a[...], keep_b[...] = small_a[...], small_b[...]
             keep = column_mask(rows)
@@ -430,58 +470,70 @@
             x_ref[...] = stream.astype(BF16)
             conv_into(s_ref, stream, (small_a, small_b), 0, keep)
             normed = to_normed(s_ref[...], (small_a, small_b), 0)
-            put_both(n_own, n_oth, normed)
+            put_both(n_own, fore_ref, normed)
             mixed = attention_part(True, 0, normed, None, wq_a, wq_b, qkv_ref, probs_ref)
-            mixed_ref[...] = mixed
+            fore_ref[:, half:] = mixed
             mul_out(mixed, 0, wp_a, wp_b, part_ref)
 
-        (x0, s1, n0_own, n0_oth, qkv0, probs0, mixed0, part0, *small) = call(
+        (x0, s1, n0_own, fore0, qkv0, probs0, part0, *small) = call(
             first_body, "attn_a",
             [*token_parts, *small, *wq, *wp],
-            [full_low, full, half_low, half_low, qkv_low, window_probs, half_low, full_low]
+            [full_low, full, half_low, fore_attn, qkv_low, window_probs, full_low]
             + [sds((26, half))] * 2,
-            flops=attn_flops,
+            flops=attn_flops, hold=[cot_own],
         )
         far0 = over_ha(part0)
-        keep_a = [x0, n0_own, n0_oth, qkv0, probs0, mixed0, s1]
+        fore0 = (fore0, over_wa(fore0))
+        keep_a = [x0, n0_own, *fore0, qkv0, probs0, s1]
 
         def mlp_body(
             s_in, part_a, part_b, small_a, small_b, wu_a, wu_b, wd_a, wd_b,
-            s_ref, n_own, n_oth, hid_ref, slope_ref, part_ref,
+            s_ref, n_own, fore_ref, slope_ref, part_ref,
         ):
             s_ref[...] = add_parts(s_in, part_a, part_b)
             normed = to_normed(s_ref[...], (small_a, small_b), 1)
-            put_both(n_own, n_oth, normed)
+            put_both(n_own, fore_ref, normed)
             pre = project_in(normed, wu_a[0], wu_b[0])
             below, bell = gelu_parts(pre)
             hid = (pre * below).astype(BF16)
-            hid_ref[...] = hid
+            fore_ref[:, half:] = hid
             slope_ref[...] = below + pre * bell
             mul_out(hid, 0, wd_a, wd_b, part_ref)
 
-        (s2, n1_own, n1_oth, hid1, slope1, part1) = call(
+        (s2, n1_own, fore1, slope1, part1) = call(
             mlp_body, "mlp_b",
             [s1, part0, far0, *small, *wu, *wd],
-            [full, half_low, half_low, hid_low, sds((rows, hidden)), full_low],
-            flops=mlp_flops, hold=[*keep_a, *wq, *wp],
+            [full, half_low, fore_mlp, sds((rows, hidden)), full_low],
+            flops=mlp_flops, hold=[*keep_a, *wq, *wp, *cot_parts],
         )
         far1 = over_ha(part1)
-        keep_b = [s2, n1_own, n1_oth, hid1, slope1]
+        fore1 = (fore1, over_wa(fore1))
+        keep_b = [s2, n1_own, *fore1, slope1]
         weights = [*wq, *wp, *wu, *wd]
 
 
-        cot_in = over_ha(later(cotangent, part1))
+        def cot_body(cot_a, cot_b, wd_a, wd_b, g_own, g_oth, dhid_ref):
+            grad = unpack(cot_a, cot_b).astype(BF16)
+            put_both(g_own, g_oth, grad)
+            dhid_ref[...] = project_back(grad, wd_a[1], wd_b[1]).astype(BF16)
+
+        g3_own, g3_oth, dhid3 = call(
+            cot_body, "cot_d",
+            [*cot_parts, *wd],
+            [half_low, half_low, hid_low],
+            flops=mlp_flops // 2, hold=[*keep_a, *keep_b, *small, *wq, *wp, *wu],
+        )
 
         def channel_body(
             s_in, part_a, part_b, valid_ref, small_a, small_b,
             wq_a, wq_b, wp_a, wp_b,
-            s_before, s_ref, n_own, n_oth, qkv_ref, probs_ref, mixed_ref, part_ref, mask_ref,
+            s_before, s_ref, n_own, fore_ref, qkv_ref, probs_ref, part_ref, mask_ref,
         ):
             keep = column_mask(rows)
             s_before[...] = jnp.where(keep, add_parts(s_in, part_a, part_b), 0.0)
             conv_into(s_ref, s_before, (small_a, small_b), 1, keep)
             normed = to_normed(s_ref[...], (small_a, small_b), 2)
-            put_both(n_own, n_oth, normed)
+            put_both(n_own, fore_ref, normed)
             one_image = placement(1, False).astype(F32)
             valid_rows = []
             for image in range(images):
@@ -493,61 +545,47 @@
                 valid_rows.append(jnp.sum(one_image * line, axis=1, keepdims=True))
                 mask_ref[image * PADDED : (image + 1) * PADDED, :] = valid_rows[image]
             mixed = attention_part(False, 1, normed, valid_rows, wq_a, wq_b, qkv_ref, probs_ref)
-            mixed_ref[...] = mixed
+            fore_ref[:, half:] = mixed
             mul_out(mixed, 1, wp_a, wp_b, part_ref)
 
-        (s3, s4, n2_own, n2_oth, qkv2, probs2, mixed2, part2, mask) = call(
+        (s3, s4, n2_own, fore2, qkv2, probs2, part2, mask) = call(
             channel_body, "attn_c",
             [s2, part1, far1, valid, *small, *wq, *wp],
-            [full, full, half_low, half_low, qkv_low, channel_probs, half_low, full_low,
+            [full, full, half_low, fore_attn, qkv_low, channel_probs, full_low,
              sds((rows, 1))],
             flops=attn_flops,
-            hold=[*keep_a, *keep_b, *wu, *wd, cot_in],
+            hold=[*keep_a, *keep_b, *wu, *wd, g3_own, g3_oth, dhid3],
         )
         far2 = over_ha(part2)
-        keep_c = [s3, s4, n2_own, n2_oth, qkv2, probs2, mixed2, mask]
-
-        cot_own, cot_oth = call(
-            choose, "choose_cot", [cotangent, cot_in], chosen,
-            hold=[*keep_a, *keep_b, *keep_c, *small, *wq, *wp, *wu, *wd],
-        )
-        cot_parts = (cot_own, over_wa(cot_oth))
-
-        def cot_body(cot_a, cot_b, wd_a, wd_b, g_own, g_oth, dhid_ref):
-            grad = unpack(cot_a, cot_b).astype(BF16)
-            put_both(g_own, g_oth, grad)
-            dhid_ref[...] = project_back(grad, wd_a[1], wd_b[1]).astype(BF16)
-
-        g3_own, g3_oth, dhid3 = call(
-            cot_body, "cot_d",
-            [*cot_parts, *wd],
-            [half_low, half_low, hid_low],
-            flops=mlp_flops // 2, hold=[*keep_a, *keep_b, *keep_c, *small, *wq, *wp, *wu],
-        )
+        fore2 = (fore2, over_wa(fore2))
+        keep_c = [s3, s4, n2_own, *fore2, qkv2, probs2, mask]
 
         def last_body(
-            s_in, part_a, part_b, small_a, small_b, dhid_ref, wu_a, wu_b,
-            s_ref, n_own, n_oth, hid_ref, dpre_ref, part_ref,
+            s_in, part_a, part_b, small_a, small_b, dhid_ref, g_oth, wu_a, wu_b,
+            s_ref, n_own, fore_ref, part_ref, *rear_refs,
         ):
             s_ref[...] = add_parts(s_in, part_a, part_b)
             normed = to_normed(s_ref[...], (small_a, small_b), 3)
-            put_both(n_own, n_oth, normed)
+            put_both(n_own, fore_ref, normed)
             pre = project_in(normed, wu_a[1], wu_b[1])
             below, bell = gelu_parts(pre)
-            hid_ref[...] = (pre * below).astype(BF16)
+            fore_ref[:, half:] = (pre * below).astype(BF16)
             dpre = (dhid_ref[...].astype(F32) * (below + pre * bell)).astype(BF16)
-            dpre_ref[...] = dpre
+            put_rear(rear_refs, 0, g_oth[...])
+            put_rear(rear_refs, half, dpre)
             part_ref[:, :half] = mm(dpre, wu_a[1], 1, 1).astype(BF16)
             part_ref[:, half:] = mm(dpre, wu_b[1], 1, 1).astype(BF16)
 
-        (s5, n3_own, n3_oth, hid3, dpre3, back3) = call(
+        (s5, n3_own, fore3, back3, *rear3) = call(
             last_body, "mlp_d",
-            [s4, part2, far2, *small, dhid3, *wu],
-            [full, half_low, half_low, hid_low, hid_low, full_low],
+            [s4, part2, far2, *small, dhid3, g3_oth, *wu],
+            [full, half_low, fore_mlp, full_low, *rear_shapes(rear_width_mlp, 2)],
             flops=mlp_flops,
             hold=[*keep_a, *keep_b, *keep_c, g3_own, g3_oth, *wq, *wp, *wd],
         )
         far_back3 = over_ha(back3)
+        fore3 = (fore3, over_wa(fore3))
+        rear3 = both_rear(rear3)
 
         up_rows, down_rows = hidden // n_dev, half // n_dev
         qkv_rows, proj_rows = heads_width // n_dev, half // n_dev
@@ -568,12 +606,15 @@
 
         downs = [("down", fold) for fold in range(folds)]
 
-        def mlp_streams(first):
-            return [Stream(0, ["up", *downs[:first]]), Stream(1, downs[first:])]
-
-        def attn_streams(first):
-            parts = ["q", "k", "v", "proj"]
-            return [Stream(0, parts[:first]), Stream(1, parts[first:])]
+        def two_streams(parts, first, which):
+            streams = [Stream(which, parts[:first]), Stream(which + 1, parts[first:])]
+            return [stream for stream in streams if stream.pieces]
+
+        def mlp_streams(first, which):
+            return two_streams(["up", *downs], 1 + first, which)
+
+        def attn_streams(first, which):
+            return two_streams(["q", "k", "v", "proj"], first, which)
 
         def write_pieces(values, streams, scratches):
             for stream, scratch in zip(streams, scratches):
@@ -590,20 +631,55 @@
                         scratch[chunk, at : at + size, :] = part
                     at += size
 
-        def write_mlp(refs, streams, scratches):
-            dpre_a, dpre_b, n_a, n_b, g_a, g_b, hid_a, hid_b = refs
-            up = mm(dpre_a[...], n_a[...], 0, 0) + mm(dpre_b[...], n_b[...], 0, 0)
-            down = mm(g_a[...], hid_a[...], 0, 0) + mm(g_b[...], hid_b[...], 0, 0)
-            write_pieces({"up": up, "down": down}, streams, scratches)
-
-        def write_attn(refs, streams, scratches):
-            dpk_a, dpk_b, n_a, n_b, g_a, g_b, mix_a, mix_b = refs
+        def both_sums(n_own, g_own, fore_a, fore_b, rear_a, rear_b):
+            def left(at, size):
+                return mm(get_rear(rear_a, at, size), n_own[...], 0, 0) + mm(
+                    get_rear(rear_b, at, size), fore_b[:, :half], 0, 0
+                )
+
+            right = mm(g_own[...], fore_a[:, half:], 0, 0) + mm(
+                get_rear(rear_b, 0, half), fore_b[:, half:], 0, 0
+            )
+            return left, right
+
+        def write_mlp(*refs):
+            left, right = both_sums(*refs)
+            return {"up": left(half, hidden), "down": right}
+
+        def write_attn(*refs):
+            left, right = both_sums(*refs)
             values = {
-                name: mm(dpk_a[part], n_a[...], 0, 0) + mm(dpk_b[part], n_b[...], 0, 0)
+                name: left(half + part * heads_width, heads_width)
                 for part, name in enumerate(("q", "k", "v"))
             }
-            values["proj"] = mm(g_a[...], mix_a[...], 0, 0) + mm(g_b[...], mix_b[...], 0, 0)
-            write_pieces(values, streams, scratches)
+            return {**values, "proj": right}
+
+        def make(name, write, streams, n_own, g_own, fore, rear, hold):
+            outs = [sds((cut * s.chunk_rows, half), BF16) for s in streams for _ in range(2)]
+            count = len(rear[0])
+
+            def body(n_ref, g_ref, fore_a, fore_b, *refs):
+                rear_a, rear_b, refs = refs[:count], refs[count : 2 * count], refs[2 * count :]
+                out_refs, scratches = refs[: len(outs)], refs[len(outs) :]
+                values = write(n_ref, g_ref, fore_a, fore_b, rear_a, rear_b)
+                write_pieces(values, streams, scratches)
+                for at, (stream, scratch) in enumerate(zip(streams, scratches)):
+                    size = stream.chunk_rows
+                    for place in range(n_dev):
+                        chunk = scratch[chunk_at(place, stream.which)].astype(BF16)
+                        to = (place % cut) * size
+                        out_refs[2 * at + place // cut][to : to + size, :] = chunk
+
+            results = call(
+                body, name, [n_own, g_own, *fore, *rear[0], *rear[1]], outs, hold=hold,
+                scratch=[pltpu.VMEM((n_dev, s.chunk_rows, half), F32) for s in streams],
+            )
+            for at, stream in enumerate(streams):
+                stream.kept, stream.sent = results[2 * at], results[2 * at + 1]
+
+        def send_first(streams):
+            for stream in streams:
+                stream.got, stream.step = over_dev(stream.sent, stream.bits[0]), 1
 
         def split_low(values):
             high = values.astype(BF16)
@@ -618,22 +694,14 @@
                 stream.at : stream.at + stream.chunk_rows, :
             ].astype(F32)
 
-        def slot(
-            name, write=None, fresh=(), sources=(), moving=(), ending=(), sums=None, hold=()
-        ):
-            ins, outs, sizes = list(sources), [], {}
+        def slot(name, fresh=(), moving=(), ending=(), sums=None, hold=()):
+            ins, outs, sizes = [], [], {}
             plan_fresh, plan_moving = [], []
 
             def room(bit, size):
                 at = sizes.get(bit, 0)
                 sizes[bit] = at + size
                 return at
-
-            for stream in fresh:
-                size = cut * stream.chunk_rows
-                plan_fresh.append((len(outs), stream.bits[0], room(stream.bits[0], size)))
-                outs.append(sds((size, half), BF16))
-            got_places = {}
 
             def place_of(array):
                 for at, known in enumerate(ins):
@@ -642,6 +710,9 @@
                 ins.append(array)
                 return len(ins) - 1
 
+            for stream in fresh:
+                size, bit = stream.sent.shape[0], stream.bits[0]
+                plan_fresh.append((place_of(stream.sent), size, bit, room(bit, size)))
             for stream in moving:
                 size = stream.kept.shape[0] // 2
                 bit = stream.bits[stream.step]
@@ -665,22 +736,11 @@
             bits_used = sorted(sizes)
             buffer_at = {bit: len(outs) + at for at, bit in enumerate(bits_used)}
             outs += [sds((sizes[bit], half), BF16) for bit in bits_used]
-            scratch = [pltpu.VMEM((n_dev, stream.chunk_rows, half), F32) for stream in fresh]
 
             def body(*refs):
-                in_refs, out_refs = refs[: len(ins)], refs[len(ins) : len(ins) + len(outs)]
-                scratches = refs[len(ins) + len(outs) :]
-                if fresh:
-                    write(in_refs[: len(sources)], fresh, scratches)
-                for stream, held, (kept_at, bit, at) in zip(fresh, scratches, plan_fresh):
-                    size = stream.chunk_rows
-                    for place in range(n_dev):
-                        chunk = held[chunk_at(place, stream.which)].astype(BF16)
-                        if place < cut:
-                            out_refs[kept_at][place * size : (place + 1) * size, :] = chunk
-                        else:
-                            to = at + (place - cut) * size
-                            out_refs[buffer_at[bit]][to : to + size, :] = chunk
+                in_refs, out_refs = refs[: len(ins)], refs[len(ins) :]
+                for sent_in, size, bit, at in plan_fresh:
+                    out_refs[buffer_at[bit]][at : at + size, :] = in_refs[sent_in][...]
                 for kept_in, got_in, got_row, size, kept_at, bit, at in plan_moving:
                     kept, got = in_refs[kept_in], in_refs[got_in]
                     out_refs[kept_at][...] = (
@@ -702,11 +762,10 @@
                     buffer[sums_room : sums_room + sum_rows, :] = high
                     buffer[sums_room + sum_rows : sums_room + 2 * sum_rows, :] = low
 
-            results = call(body, name, ins, outs, scratch=scratch, hold=hold)
+            results = call(body, name, ins, outs, hold=hold)
             received = {bit: over_dev(results[buffer_at[bit]], bit) for bit in bits_used}
-            for stream, (kept_at, bit, at) in zip(fresh, plan_fresh):
-                stream.kept, stream.got, stream.at = results[kept_at], received[bit], at
-                stream.step = 1
+            for stream, (_, _, bit, at) in zip(fresh, plan_fresh):
+                stream.got, stream.at, stream.step = received[bit], at, 1
             for stream, _, _, out_at in plan_ending:
                 stream.final = results[out_at]
             for stream, (_, _, _, _, kept_at, bit, at) in zip(moving, plan_moving):
@@ -715,10 +774,6 @@
             if sums is not None:
                 sums[:3] = results[sums_out], received[sums[3]], sums_room
 
-        def gradient_sources(left, n_own, n_oth, g_own, g_oth, right):
-            return [left, over_wa(left), n_own, over_wa(n_oth),
-                    g_own, over_wa(g_oth), right, over_wa(right)]
-
         def ship(total, kept, sent):
             packed = mm(placement(images, True), total.astype(BF16), 1, 0).astype(BF16)
             kept[...] = packed[:, :half]
@@ -734,18 +789,18 @@
         def join(stay, received, out_ref):
             out_ref[...] = stay[...].astype(F32) + received[:rows_in, :].astype(F32)
 
-        def out_body(s_in, hid_ref, wd_a, wd_b, kept, sent):
-            hid = hid_ref[...]
+        def out_body(s_in, fore_ref, wd_a, wd_b, kept, sent):
+            hid = fore_ref[:, half:]
             base = jnp.where(here("ha") == 0, s_in[...], 0.0)
             branch = jnp.concatenate([mm(hid, wd_a[1], 1, 0), mm(hid, wd_b[1], 1, 0)], axis=1)
             ship(base + branch, kept, sent)
 
-        streams_d = mlp_streams(SPLIT_D)
-        slot(
-            "wgrad_d", write_mlp, streams_d,
-            gradient_sources(dpre3, n3_own, n3_oth, g3_own, g3_oth, hid3),
-            hold=[*keep_a, *keep_b, *keep_c, *small, *weights, s5],
-        )
+        streams_d = mlp_streams(SPLIT_D, 0)
+        make(
+            "wgrad_d", write_mlp, streams_d, n3_own, g3_own, fore3, rear3,
+            [*keep_a, *keep_b, *keep_c, *small, *weights, s5],
+        )
+        send_first(streams_d)
 
         def add_norm_back(grad, part_a, part_b, stream, gain, sums_ref):
             upstream = part_a[...].astype(F32) + part_b[...].astype(F32)
@@ -762,93 +817,111 @@
 
         def channel_back_body(
             g_in_own, g_in_oth, part_a, part_b, s_in, small_a, small_b, mask_ref, qkv_ref,
-            probs_ref, wp_a, wp_b, wq_a, wq_b, g_ref, g_own, g_oth, dpk_ref, part_ref, sums_ref,
+            probs_ref, wp_a, wp_b, wq_a, wq_b,
+            g_ref, g_own, part_ref, sums_ref, *rear_refs,
         ):
             grad = jnp.concatenate([g_in_own[...], g_in_oth[...]], axis=1).astype(F32)
             gain = gain_row((small_a, small_b), 3)
             grad = add_norm_back(grad, part_a, part_b, s_in[...], gain, sums_ref)
             g_ref[...] = grad
             low = grad.astype(BF16)
-            put_both(g_own, g_oth, low)
+            g_own[...] = low[:, :half]
+            put_rear(rear_refs, 0, low[:, half:])
             grad_mixed = project_back(low, wp_a[1], wp_b[1]).astype(BF16)
-            packed = attention_part_back(False, grad_mixed, mask_ref, qkv_ref, probs_ref, dpk_ref)
+            packed = attention_part_back(
+                False, grad_mixed, mask_ref, qkv_ref, probs_ref, rear_refs
+            )
             own, oth = qkv_back(packed, 1, wq_a, wq_b)
             part_ref[:, :half] = own.astype(BF16)
             part_ref[:, half:] = oth.astype(BF16)
 
-        late = [hid3, *wd, s5]
-        (g2, g2_own, g2_oth, dpk2, back2, sums3) = call(
+        late = [fore3[0], *wd, s5]
+        (g2, g2_own, back2, sums3, *rear2) = call(
             channel_back_body, "back_c",
             [g3_own, g3_oth, back3, far_back3, s5, *small, mask, qkv2, probs2, *wp, *wq],
-            [full, half_low, half_low, qkv_low, full_low, sds((2, width))],
+            [full, half_low, full_low, sds((2, width)), *rear_shapes(rear_width_attn, 1)],
             flops=attn_flops,
-            hold=[*keep_a, *keep_b, s3, s4, n2_own, n2_oth, mixed2, *wu, *wd, hid3],
+            hold=[*keep_a, *keep_b, s3, s4, n2_own, *fore2, *wu, *wd, fore3[0]],
         )
         far_back2 = over_ha(back2)
-        streams_c = attn_streams(SPLIT_C)
+        rear2 = both_rear(rear2)
+        streams_c = attn_streams(SPLIT_C, 2)
+        kept_c = [*keep_a, *keep_b, s3, s4, *small, *weights, g2, *late, sums3]
+        make("wgrad_c", write_attn, streams_c, n2_own, g2_own, fore2, rear2, kept_c)
         slot(
-            "wgrad_c", write_attn, streams_c,
-            gradient_sources(dpk2, n2_own, n2_oth, g2_own, g2_oth, mixed2),
-            moving=streams_d,
-            hold=[*keep_a, *keep_b, s3, s4, *small, *weights, g2, *late, sums3, back2, far_back2],
+            "slot_c", fresh=streams_c, moving=streams_d, hold=[*kept_c, back2, far_back2],
         )
 
         def mlp_back_body(
             g_in, part_a, part_b, s_in, s_before, small_a, small_b, slope_ref,
-            wd_a, wd_b, wu_a, wu_b, g_ref, g_own, g_oth, dpre_ref, part_ref, sums_ref,
+            wd_a, wd_b, wu_a, wu_b, g_ref, g_own, part_ref, sums_ref, *rear_refs,
         ):
             keep = column_mask(rows)
             gain = gain_row((small_a, small_b), 2)
             grad = add_norm_back(g_in[...], part_a, part_b, s_in[...], gain, sums_ref)
             conv_back_into(g_ref, sums_ref, 2, grad, s_before[...], (small_a, small_b), 1, keep)
             low = g_ref[...].astype(BF16)
-            put_both(g_own, g_oth, low)
+            g_own[...] = low[:, :half]
+            put_rear(rear_refs, 0, low[:, half:])
             dhid = project_back(low, wd_a[0], wd_b[0]).astype(BF16).astype(F32)
             dpre = (dhid * slope_ref[...]).astype(BF16)
-            dpre_ref[...] = dpre
+            put_rear(rear_refs, half, dpre)
             part_ref[:, :half] = mm(dpre, wu_a[0], 1, 1).astype(BF16)
             part_ref[:, half:] = mm(dpre, wu_b[0], 1, 1).astype(BF16)
 
-        (g1, g1_own, g1_oth, dpre1, back1, sums2) = call(
+        (g1, g1_own, back1, sums2, *rear1) = call(
             mlp_back_body, "back_b",
             [g2, back2, far_back2, s4, s3, *small, slope1, *wd, *wu],
-            [full, half_low, half_low, hid_low, full_low, sds((11, width))],
-            flops=mlp_flops, hold=[*keep_a, s2, n1_own, n1_oth, hid1, *wq, *wp, hid3, s5, sums3],
+            [full, half_low, full_low, sds((11, width)), *rear_shapes(rear_width_mlp, 2)],
+            flops=mlp_flops,
+            hold=[*keep_a, s2, n1_own, *fore1, *wq, *wp, fore3[0], s5, sums3],
         )
         far_back1 = over_ha(back1)
-        streams_b = mlp_streams(SPLIT_B)
-        slot(
-            "wgrad_b", write_mlp, streams_b,
-            gradient_sources(dpre1, n1_own, n1_oth, g1_own, g1_oth, hid1),
-            moving=[*streams_d, *streams_c],
-            hold=[*keep_a, s2, *small, *wq, *wp, g1, *late, sums3, sums2, back1, far_back1],
+        rear1 = both_rear(rear1)
+        streams_b = mlp_streams(SPLIT_B, 0)
+        make(
+            "wgrad_b", write_mlp, streams_b, n1_own, g1_own, fore1, rear1,
+            [*keep_a, s2, *small, *wq, *wp, g1, *late, sums3, sums2],
         )
 
         def window_back_body(
             g_in, part_a, part_b, s_in, small_a, small_b, qkv_ref, probs_ref, wp_a, wp_b,
-            g_ref, g_own, g_oth, dpk_ref, sums_ref,
+            g_ref, g_own, sums_ref, *rear_refs,
         ):
             gain = gain_row((small_a, small_b), 1)
             grad = add_norm_back(g_in[...], part_a, part_b, s_in[...], gain, sums_ref)
             g_ref[...] = grad
             low = grad.astype(BF16)
-            put_both(g_own, g_oth, low)
+            g_own[...] = low[:, :half]
+            put_rear(rear_refs, 0, low[:, half:])
             grad_mixed = project_back(low, wp_a[0], wp_b[0]).astype(BF16)
-            attention_part_back(True, grad_mixed, None, qkv_ref, probs_ref, dpk_ref)
-
-        (g0, g0_own, g0_oth, dpk0, sums1) = call(
+            attention_part_back(True, grad_mixed, None, qkv_ref, probs_ref, rear_refs)
+
+        (g0, g0_own, sums1, *rear0) = call(
             window_back_body, "back_a",
             [g1, back1, far_back1, s2, *small, qkv0, probs0, *wp],
-            [full, half_low, half_low, qkv_low, sds((2, width))],
-            flops=attn_flops, hold=[x0, n0_own, n0_oth, mixed0, s1, *wq, *late, sums3, sums2],
+            [full, half_low, sds((2, width)), *rear_shapes(rear_width_attn, 3)],
+            flops=attn_flops, hold=[x0, n0_own, *fore0, s1, *wq, *late, sums3, sums2],
+        )
+        rear0 = both_rear(rear0)
+
+        keep_0 = [g0, s1, x0, *small, *wq, sums1, sums2, sums3, *rear0[0]]
+        streams_a = attn_streams(SPLIT_A, 2)
+        make("wgrad_a", write_attn, streams_a, n0_own, g0_own, fore0, rear0, [*late, *keep_0])
+        every = [*streams_d, *streams_c, *streams_b, *streams_a]
+        slot(
+            "slot_ab", fresh=[*streams_b, *streams_a], moving=[*streams_d, *streams_c],
+            hold=[*late, *keep_0],
         )
 
         def first_back_body(
-            g_in, dpk_ref, s_in, x_ref, small_a, small_b, wq_a, wq_b,
-            sums_one, sums_two, sums_three, kept, sent, sums_own, sums_oth, scratch, sums_ref,
+            g_in, s_in, x_ref, small_a, small_b, wq_a, wq_b, sums_one, sums_two, sums_three, *refs
         ):
+            rear_refs, (kept, sent, sums_own, sums_oth, scratch, sums_ref) = refs[:-6], refs[-6:]
             keep = column_mask(rows)
-            packed = [dpk_ref[part] for part in range(3)]
+            packed = [
+                get_rear(rear_refs, half + part * heads_width, heads_width) for part in range(3)
+            ]
             upstream = jnp.concatenate(qkv_back(packed, 0, wq_a, wq_b), axis=1)
             units, inv_std = norm_stats(s_in[...])
             sums_ref[0:1, :] = jnp.sum(upstream * units, axis=0, keepdims=True)
@@ -868,15 +941,13 @@
         sums_half = sds((sum_rows, half))
         token_kept, token_sent, sums_own, sums_oth = call(
             first_back_body, "back_0",
-            [g0, dpk0, s1, x0, *small, *wq, sums1, sums2, sums3],
-            shipped + [sums_half] * 2,
+            [g0, s1, x0, *small, *wq, sums1, sums2, sums3, *rear0[0]],
+            shipped + [sds((sum_rows, half))] * 2,
             scratch=[pltpu.VMEM((rows, width), F32), pltpu.VMEM((sum_rows, width), F32)],
-            flops=attn_flops * 3 // 4,
-            hold=[n0_own, n0_oth, mixed0, g0_own, g0_oth, *late],
-        )
-        keep_wgrad = [dpk0, n0_own, n0_oth, g0_own, g0_oth, mixed0]
-
+            flops=attn_flops * 3 // 4, hold=late,
+        )
         sums_at = -(-rows_in // 16) * 16
+        sums_half = sds((sum_rows, half))
 
         def fold_tokens(kept, received, sums_a, sums_b, stay, go, sums_ref):
             fold(kept, received, stay, go)
@@ -888,60 +959,41 @@
         token_stay, token_go, sums_chip = call(
             fold_tokens, "fold_tokens",
             [token_kept, over_wa(token_sent), sums_own, over_wa(sums_oth)],
-            [shipped[0], sds((sums_at + 2 * sum_rows, half), BF16), sums_half],
-            hold=[*late, *keep_wgrad],
+            [shipped[0], sds((sums_at + 2 * sum_rows, half), BF16), sums_half], hold=late,
         )
         token_got = over_ha(token_go)
-        out_kept, out_sent = call(
-            out_body, "out_d", [s5, hid3, *wd], shipped, flops=mlp_flops // 2,
-            hold=[*keep_wgrad, token_stay, sums_chip],
-        )
-        out_stay, out_go = call(
-            fold, "fold_out", [out_kept, over_wa(out_sent)], shipped,
-            hold=[*keep_wgrad, token_stay, sums_chip],
-        )
-        out_got = over_ha(out_go)
 
         def join_tokens(stay, received, sums_chip, out_ref, sums_ref):
             join(stay, received, out_ref)
             sums_ref[...] = sums_chip[...] + joined(received, sums_at)
 
-        earlier = [*streams_d, *streams_c, *streams_b]
-        slot(
-            "halve_bc", moving=[s for s in earlier if s.step < bits],
-            ending=[s for s in earlier if s.step == bits],
-            hold=[*keep_wgrad, token_stay, sums_chip, out_stay],
-        )
-        streams_a = attn_streams(SPLIT_A)
-        slot(
-            "wgrad_a", write_attn, streams_a,
-            gradient_sources(dpk0, n0_own, n0_oth, g0_own, g0_oth, mixed0),
-            hold=[token_stay, sums_chip, out_stay],
-        )
         owned = sds((rows_in, half))
         grad_tokens, sums_ha = call(
             join_tokens, "join_tokens", [token_stay, token_got, sums_chip], [owned, sums_half],
-            hold=[out_stay],
-        )
-        left_bits = list(range(bits))
+            hold=late,
+        )
+        left_bits = [2, 0, 1, *range(3, bits)]
         sums = [sums_ha, None, 0, left_bits.pop(0)]
+        slot("sums_z", sums=sums, hold=late)
         turn = 0
-        while left_bits or any(stream.step < bits for stream in [*earlier, *streams_a]):
+        while left_bits or any(stream.step < bits for stream in every):
             turn += 1
-            moving = [s for s in earlier if s.step < bits]
-            arrived = [s for s in earlier if s.step == bits and s.final is None]
-            if moving:
-                slot(f"halve_{turn}", moving=moving, sums=sums if turn == 1 else None)
-            if turn == 1:
-                output = call(join, "join_out", [out_stay, out_got], [owned])[0]
             now = None
             if left_bits:
                 sums[3] = left_bits.pop(0)
                 now = sums
             slot(
-                f"halve_a{turn}", moving=[s for s in streams_a if s.step < bits],
-                ending=arrived, sums=now,
+                f"slot_{turn}", moving=[s for s in every if s.step < bits], sums=now,
+                ending=[s for s in every if s.step == bits and s.final is None],
+                hold=late if turn == 1 else [],
             )
+            if turn == 1:
+                out_kept, out_sent = call(
+                    out_body, "out_d", [s5, fore3[0], *wd], shipped, flops=mlp_flops // 2
+                )
+                out_stay, out_go = call(fold, "fold_out", [out_kept, over_wa(out_sent)], shipped)
+                out_got = over_ha(out_go)
+        output = call(join, "join_out", [out_stay, out_got], [owned])[0]
 
         def finish_body(*refs):
             (up, down, qkv, proj, taps_ref, gain_ref, shift_ref) = refs[-7:]

time: 164 us -> 158 us (0.963)
  local copies, waits for them, and re-layouts: 7.81 us -> 4.17 us
  waiting for transfers between devices: 85.3 us -> 82.8 us
    ppermute x10, starting transfers between devices: 8.34 us -> 16.6 us  [over_ha(): return lax.ppermute(values, 'ha', swap)]
    ppermute x17 -> x13, starting transfers between devices: 22.3 us -> 14.8 us  [over_dev(): lax.ppermute(values, 'dev', [(i, i ^ 1 << bit) for i in range(n_dev)])]
    ppermute x26 -> x22, waiting for transfers between devices: 12.5 us -> 6.83 us  [over_wa(): return lax.ppermute(values, 'wa', swap)]
    ppermute x17 -> x13, waiting for transfers between devices: 31.3 us -> 36.6 us  [over_dev(): lax.ppermute(values, 'dev', [(i, i ^ 1 << bit) for i in range(n_dev)])]
    unnamed x26 -> x20, local copies, waits for them, and re-layouts: 7.81 us -> 4.17 us
    ppermute x10, waiting for transfers between devices: 41.4 us -> 39.3 us  [over_ha(): return lax.ppermute(values, 'ha', swap)]
    ppermute x26 -> x22, starting transfers between devices: 5.05 us -> 4.32 us  [over_wa(): return lax.ppermute(values, 'wa', swap)]
  transfers between devices with their start and end apart: 53 -> 45, of which waited for: 27 -> 27; matrix products, arithmetic and copies ran while one was open for 0% -> 0% of each run, Pallas kernels for 14% -> 15%
where the time goes in v4:
time: 158 us
  waiting for transfers between devices  82.8 us (52%)
  starting transfers between devices  35.7 us (23%)
  Pallas kernels  34.2 us (22%)
  local copies, waits for them, and re-layouts  4.17 us (3%)
    ppermute x10, waiting for transfers between devices, over_ha(): return lax.ppermute(values, 'ha', swap)  39.3 us
    ppermute x13, waiting for transfers between devices, over_dev(): lax.ppermute(values, 'dev', [(i, i ^ 1 << bit) for i in range(n_dev)])  36.6 us
    pallas_call x26, Pallas kernels, kernel_call(): pl.pallas_call(wrapped, in_specs=specs, out_specs=[pl.BlockSpec(memory_sp...  34.2 us
    ppermute x10, starting transfers between devices, over_ha(): return lax.ppermute(values, 'ha', swap)  16.6 us
    ppermute x13, starting transfers between devices, over_dev(): lax.ppermute(values, 'dev', [(i, i ^ 1 << bit) for i in range(n_dev)])  14.8 us
    ppermute x22, waiting for transfers between devices, over_wa(): return lax.ppermute(values, 'wa', swap)  6.83 us
    ppermute x22, starting transfers between devices, over_wa(): return lax.ppermute(values, 'wa', swap)  4.32 us
    unnamed x20, local copies, waits for them, and re-layouts  4.17 us
  transfers between devices with their start and end apart: 45, of which 27 were waited for; matrix products, arithmetic and copies ran while one was open for 0% of the time, Pallas kernels for 15%

profile of v4, /device:TPU:0, one launch (start us, length us, event | category | flops | bytes accessed | tf_op | source)
XLA Modules:
  0.0 157.8 jit_solution(7634256330724813195)
XLA Ops:
  1.2 2.9 %collective-permute-start = (bf16[147,384]{1,0:T(8,128)(2,1)}, bf16[147,384]{1,0:T(8,128)(2,1)S(1)}, u32[]{:S(2)}, u32[]{:S(2)}) collective-permute-start(bf16[147,384]{1,0:T(8,128)(2,1)} %refs_0_.1), channel_id=1, source_target_pairs={{0,2},{2,0},{1,3},{3,1},{4,6},{6,4},{5,7},{7,5},{8,10},{10,8},{9,1... | collective-permute-start | bytes 338696 | tf_op jit(solution)/shard_map/ppermute | solution.py:247
  13.3 3.7 %attn_a.1 = (bf16[168,768]{1,0:T(8,128)(2,1)S(1)}, f32[168,768]{1,0:T(8,128)S(1)}, bf16[168,384]{1,0:T(8,128)(2,1)S(1)}, bf16[168,768]{1,0:T(8,128)(2,1)S(1)}, b...) custom-call(bf16[147,384]{1,0:T(8,128)(2,1)S(1)} %get-tuple-element., ...), custom_call_target="tpu_custom_call" | custom-call | tf_op jit(solution)/shard_map/attn_a/pallas_call | solution.py:59
  20.5 5.3 %collective-permute-done.6.refs_2_ = bf16[168,768]{1,0:T(8,128)(2,1)S(1)} collective-permute-done((bf16[168,768]{1,0:T(8,128)(2,1)S(1)}, bf16[168,768]{1,0:T(8,128)(2,1)S(1)}, u32[]{:S(2)}, u32[]{:S(2)}) %collective-permute-start.6) | collective-permute-done | bytes 258080 | tf_op jit(solution)/shard_map/ppermute | solution.py:247
  25.8 2.2 %mlp_b.1 = (f32[168,768]{1,0:T(8,128)S(1)}, bf16[168,384]{1,0:T(8,128)(2,1)S(1)}, bf16[168,1920]{1,0:T(8,128)(2,1)S(1)}, f32[168,1536]{1,0:T(8,128)S(1)}, bf16[1...) custom-call(f32[168,768]{1,0:T(8,128)S(1)} %get-tuple-element.163.refs_0_.refs_15_.refs_10_.refs_16_.refs_14_.refs_20_.refs_12_.refs_18_.refs_1_, ...), custom_call_target="tpu_custom_call" | custom-call | tf_op jit(solution)/shard_map/mlp_b/pallas_call | solution.py:59
  31.2 5.5 %collective-permute-done.11.refs_2_ = bf16[168,768]{1,0:T(8,128)(2,1)S(1)} collective-permute-done((bf16[168,768]{1,0:T(8,128)(2,1)S(1)}, bf16[168,768]{1,0:T(8,128)(2,1)S(1)}, u32[]{:S(2)}, u32[]{:S(2)}) %collective-permute-start.11) | collective-permute-done | bytes 258080 | tf_op jit(solution)/shard_map/ppermute | solution.py:247
  36.7 2.1 %attn_c.1 = (f32[168,768]{1,0:T(8,128)S(1)}, f32[168,768]{1,0:T(8,128)S(1)}, bf16[168,384]{1,0:T(8,128)(2,1)S(1)}, bf16[168,768]{1,0:T(8,128)(2,1)S(1)}, bf16[3,...) custom-call(f32[168,768]{1,0:T(8,128)S(1)} %get-tuple-element.177.re, ...), custom_call_target="tpu_custom_call" | custom-call | tf_op jit(solution)/shard_map/attn_c/pallas_call | solution.py:59
  40.6 6.0 %collective-permute-done.13.refs_2_ = bf16[168,768]{1,0:T(8,128)(2,1)S(1)} collective-permute-done((bf16[168,768]{1,0:T(8,128)(2,1)S(1)}, bf16[168,768]{1,0:T(8,128)(2,1)S(1)}, u32[]{:S(2)}, u32[]{:S(2)}) %collective-permute-start.13) | collective-permute-done | bytes 258080 | tf_op jit(solution)/shard_map/ppermute | solution.py:247
  46.7 2.5 %mlp_d.1 = (f32[168,768]{1,0:T(8,128)S(1)}, bf16[168,384]{1,0:T(8,128)(2,1)S(1)}, bf16[168,1920]{1,0:T(8,128)(2,1)S(1)}, bf16[168,768]{1,0:T(8,128)(2,1)S(1)}, b...) custom-call(f32[168,768]{1,0:T(8,128)S(1)} %get-tuple-element.187.refs_0_.refs_22_.refs_21_.refs_27_, ...), custom_call_target="tpu_custom_call" | custom-call | tf_op jit(solution)/shard_map/mlp_d/pallas_call | solution.py:59
  52.2 2.1 %wgrad_d.1 = (bf16[768,384]{1,0:T(8,128)(2,1)S(1)}, bf16[768,384]{1,0:T(8,128)(2,1)S(1)}, bf16[768,384]{1,0:T(8,128)(2,1)S(1)}, bf16[768,384]{1,0:T(8,128)(2,1)S(1)}, f32[8,128]{1,0:T(8,128)S(1)}) custom-call(bf16[168,384]{1,0:T(8,128)(2,1)S(1)} %get-tuple-element.199.refs_0_, bf16[168,384]{1,0:T(8,128)(2,1)S(1)} %get-tuple-element.183.refs_26_.refs_29_.refs_1_.refs_0_, ...), custom_call_target="tpu_custom_call" | custom-call | tf_op jit(solution)/shard_map/wgrad_d/pallas_call | solution.py:59
  58.4 2.9 %back_c.1 = (f32[168,768]{1,0:T(8,128)S(1)}, bf16[168,384]{1,0:T(8,128)(2,1)S(1)}, bf16[168,768]{1,0:T(8,128)(2,1)S(1)}, f32[2,768]{1,0:T(2,128)S(1)}, bf16[168,...) custom-call(bf16[168,384]{1,0:T(8,128)(2,1)S(1)} %get-tuple-element.183.refs_26_.refs_29_.refs_1_.refs_0_, ...), custom_call_target="tpu_custom_call" | custom-call | tf_op jit(solution)/shard_map/back_c/pallas_call | solution.py:59
  64.4 5.7 %collective-permute-done.19.refs_37_.refs_2_ = bf16[168,768]{1,0:T(8,128)(2,1)S(1)} collective-permute-done((bf16[168,768]{1,0:T(8,128)(2,1)S(1)}, bf16[168,768]{1,0:T(8,128)(2,1)S(1)}, u32[]{:S(2)}, u32[]{:S(2)}) %collective-permute-start.19) | collective-permute-done | bytes 258080 | tf_op jit(solution)/shard_map/ppermute | solution.py:247
  73.7 2.8 %back_b.1 = (f32[168,768]{1,0:T(8,128)S(1)}, bf16[168,384]{1,0:T(8,128)(2,1)S(1)}, bf16[168,768]{1,0:T(8,128)(2,1)S(1)}, f32[11,768]{1,0:T(8,128)S(1)}, bf16[168...) custom-call(f32[168,768]{1,0:T(8,128)S(1)} %get-tuple-element.204.refs_30_.refs_0_, ...), custom_call_target="tpu_custom_call" | custom-call | tf_op jit(solution)/shard_map/back_b/pallas_call | solution.py:59
  80.6 4.7 %collective-permute-done.25.refs_2_ = bf16[168,768]{1,0:T(8,128)(2,1)S(1)} collective-permute-done((bf16[168,768]{1,0:T(8,128)(2,1)S(1)}, bf16[168,768]{1,0:T(8,128)(2,1)S(1)}, u32[]{:S(2)}, u32[]{:S(2)}) %collective-permute-start.25) | collective-permute-done | bytes 258080 | tf_op jit(solution)/shard_map/ppermute | solution.py:247
  85.3 2.9 %back_a.1 = (f32[168,768]{1,0:T(8,128)S(1)}, bf16[168,384]{1,0:T(8,128)(2,1)S(1)}, f32[2,768]{1,0:T(2,128)S(1)}, bf16[168,512]{1,0:T(8,128)(2,1)S(1)}, bf16[168,...) custom-call(f32[168,768]{1,0:T(8,128)S(1)} %get-tuple-element.221.refs_22_.refs_0_, ...), custom_call_target="tpu_custom_call" | custom-call | tf_op jit(solution)/shard_map/back_a/pallas_call | solution.py:59
  93.4 2.6 %collective-permute-start.31 = (bf16[768,384]{1,0:T(8,128)(2,1)S(1)}, bf16[768,384]{1,0:T(8,128)(2,1)S(1)}, u32[]{:S(2)}, u32[]{:S(2)}) collective-permute-start(bf16[768,384]{1,0:T(8,128)(2,1)S(1)} %get-tuple-element.244), channel_id=1, source_target_pairs={{0,16},{4,20},{8,24},{12,28},{16,0},{20,4},{24,8},{28,12},{1,17},{... | collective-permute-start | bytes 1769480 | tf_op jit(solution)/shard_map/ppermute | solution.py:253
  96.4 2.2 %back_0.1 = (bf16[147,384]{1,0:T(8,128)(2,1)S(1)}, bf16[147,384]{1,0:T(8,128)(2,1)S(1)}, f32[32,384]{1,0:T(8,128)S(1)}, f32[32,384]{1,0:T(8,128)S(1)}, f32[8,128]{1,0:T(8,128)S(1)}) custom-call(f32[168,768]{1,0:T(8,128)S(1)} %get-tuple-element.232.refs_14_.refs_13_.refs_0_, ...), custom_call_target="tpu_custom_call" | custom-call | tf_op jit(solution)/shard_map/back_0/pallas_call | solution.py:59
  101.7 5.1 %collective-permute-done.36.refs_1_ = bf16[224,384]{1,0:T(8,128)(2,1)S(1)} collective-permute-done((bf16[224,384]{1,0:T(8,128)(2,1)S(1)}, bf16[224,384]{1,0:T(8,128)(2,1)S(1)}, u32[]{:S(2)}, u32[]{:S(2)}) %collective-permute-start.36) | collective-permute-done | bytes 172064 | tf_op jit(solution)/shard_map/ppermute | solution.py:247
  108.0 16.3 %collective-permute-done.37.refs_11_ = bf16[64,384]{1,0:T(8,128)(2,1)S(1)} collective-permute-done((bf16[64,384]{1,0:T(8,128)(2,1)S(1)}, bf16[64,384]{1,0:T(8,128)(2,1)S(1)}, u32[]{:S(2)}, u32[]{:S(2)}) %collective-permute-start.37) | collective-permute-done | bytes 49184 | tf_op jit(solution)/shard_map/ppermute | solution.py:253
  125.7 2.3 %collective-permute-start.42 = (bf16[384,384]{1,0:T(8,128)(2,1)S(1)}, bf16[384,384]{1,0:T(8,128)(2,1)S(1)}, u32[]{:S(2)}, u32[]{:S(2)}) collective-permute-start(bf16[384,384]{1,0:T(8,128)(2,1)S(1)} %get-tuple-element.279), channel_id=1, source_target_pairs={{0,16},{4,20},{8,24},{12,28},{16,0},{20,4},{24,8},{28,12},{1,17},{... | collective-permute-start | bytes 884744 | tf_op jit(solution)/shard_map/ppermute | solution.py:253
  130.3 9.4 %collective-permute-done.42.refs_5_ = bf16[384,384]{1,0:T(8,128)(2,1)S(1)} collective-permute-done((bf16[384,384]{1,0:T(8,128)(2,1)S(1)}, bf16[384,384]{1,0:T(8,128)(2,1)S(1)}, u32[]{:S(2)}, u32[]{:S(2)}) %collective-permute-start.42) | collective-permute-done | bytes 294944 | tf_op jit(solution)/shard_map/ppermute | solution.py:253
  139.7 2.2 %collective-permute-done.40.refs_1_ = bf16[480,384]{1,0:T(8,128)(2,1)S(1)} collective-permute-done((bf16[480,384]{1,0:T(8,128)(2,1)S(1)}, bf16[480,384]{1,0:T(8,128)(2,1)S(1)}, u32[]{:S(2)}, u32[]{:S(2)}) %collective-permute-start.40) | collective-permute-done | bytes 368672 | tf_op jit(solution)/shard_map/ppermute | solution.py:253
  145.1 3.3 %collective-permute-done.39.refs_1_ = bf16[147,384]{1,0:T(8,128)(2,1)S(1)} collective-permute-done((bf16[147,384]{1,0:T(8,128)(2,1)S(1)}, bf16[147,384]{1,0:T(8,128)(2,1)S(1)}, u32[]{:S(2)}, u32[]{:S(2)}) %collective-permute-start.39) | collective-permute-done | bytes 112928 | tf_op jit(solution)/shard_map/ppermute | solution.py:247
  149.1 3.9 %collective-permute-done.43.refs_1_.refs_3_ = bf16[256,384]{1,0:T(8,128)(2,1)S(1)} collective-permute-done((bf16[256,384]{1,0:T(8,128)(2,1)S(1)}, bf16[256,384]{1,0:T(8,128)(2,1)S(1)}, u32[]{:S(2)}, u32[]{:S(2)}) %collective-permute-start.43) | collective-permute-done | bytes 196640 | tf_op jit(solution)/shard_map/ppermute | solution.py:253
  153.0 3.5 %collective-permute-done.44.refs_5_.refs_7_ = bf16[384,384]{1,0:T(8,128)(2,1)S(1)} collective-permute-done((bf16[384,384]{1,0:T(8,128)(2,1)S(1)}, bf16[384,384]{1,0:T(8,128)(2,1)S(1)}, u32[]{:S(2)}, u32[]{:S(2)}) %collective-permute-start.44) | collective-permute-done | bytes 294944 | tf_op jit(solution)/shard_map/ppermute | solution.py:253
  (112 shorter events, 54.7 us)
Async XLA Ops:
  0.6 9.7 %collective-permute-start.2 = (bf16[2,3,384,384]{3,2,1,0:T(8,128)(2,1)}, bf16[2,3,384,384]{3,2,1,0:T(8,128)(2,1)S(1)}, u32[]{:S(2)}, u32[]{:S(2)}) collective-permute-start(bf16[2,3,384,384]{3,2,1,0:T(8,128)(2,1)} %bitcast.7), channel_id=1, source_target_pairs={{0,1},{1,0},{2,3},{3,2},{4,5},{5,4},{6,7},{7,6},{8,9},{9,8},{10,11... | collective-permute-start | bytes 5308424 | tf_op jit(solution)/shard_map/ppermute | solution.py:250
  1.2 9.2 %collective-permute-start.3 = (bf16[2,384,384]{2,1,0:T(8,128)(2,1)}, bf16[2,384,384]{2,1,0:T(8,128)(2,1)S(1)}, u32[]{:S(2)}, u32[]{:S(2)}) collective-permute-start(bf16[2,384,384]{2,1,0:T(8,128)(2,1)} %refs_8_.5), channel_id=1, source_target_pairs={{0,1},{1,0},{2,3},{3,2},{4,5},{5,4},{6,7},{7,6},{8,9},{9,8},{10,11... | collective-permute-start | bytes 1769480 | tf_op jit(solution)/shard_map/ppermute | solution.py:250
  1.2 7.1 %collective-permute-start = (bf16[147,384]{1,0:T(8,128)(2,1)}, bf16[147,384]{1,0:T(8,128)(2,1)S(1)}, u32[]{:S(2)}, u32[]{:S(2)}) collective-permute-start(bf16[147,384]{1,0:T(8,128)(2,1)} %refs_0_.1), channel_id=1, source_target_pairs={{0,2},{2,0},{1,3},{3,1},{4,6},{6,4},{5,7},{7,5},{8,10},{10,8},{9,1... | collective-permute-start | bytes 338696 | tf_op jit(solution)/shard_map/ppermute | solution.py:247
  12.0 13.8 %collective-permute-start.8 = (bf16[2,1536,384]{2,1,0:T(8,128)(2,1)S(1)}, bf16[2,1536,384]{2,1,0:T(8,128)(2,1)S(1)}, u32[]{:S(2)}, u32[]{:S(2)}) collective-permute-start(bf16[2,1536,384]{2,1,0:T(8,128)(2,1)S(1)} %copy-done), channel_id=1, source_target_pairs={{0,1},{1,0},{2,3},{3,2},{4,5},{5,4},{6,7},{7,6},{8,9},{9,8},{10,11... | collective-permute-start | bytes 7077896 | tf_op jit(solution)/shard_map/ppermute | solution.py:250
  12.7 13.1 %collective-permute-start.7 = (bf16[2,384,1536]{2,1,0:T(8,128)(2,1)S(1)}, bf16[2,384,1536]{2,1,0:T(8,128)(2,1)S(1)}, u32[]{:S(2)}, u32[]{:S(2)}) collective-permute-start(bf16[2,384,1536]{2,1,0:T(8,128)(2,1)S(1)} %copy-done.2), channel_id=1, source_target_pairs={{0,1},{1,0},{2,3},{3,2},{4,5},{5,4},{6,7},{7,6},{8,9},{9,8},{10,11... | collective-permute-start | bytes 7077896 | tf_op jit(solution)/shard_map/ppermute | solution.py:250
  17.2 8.6 %collective-permute-start.6 = (bf16[168,768]{1,0:T(8,128)(2,1)S(1)}, bf16[168,768]{1,0:T(8,128)(2,1)S(1)}, u32[]{:S(2)}, u32[]{:S(2)}) collective-permute-start(bf16[168,768]{1,0:T(8,128)(2,1)S(1)} %get-tuple-element.164.refs_1_), channel_id=1, source_target_pairs={{0,2},{2,0},{1,3},{3,1},{4,6},{6,4},{5,7},{7,5},{8,10},{10,8},{9,1... | collective-permute-start | bytes 774152 | tf_op jit(solution)/shard_map/ppermute | solution.py:247
  28.1 8.6 %collective-permute-start.11 = (bf16[168,768]{1,0:T(8,128)(2,1)S(1)}, bf16[168,768]{1,0:T(8,128)(2,1)S(1)}, u32[]{:S(2)}, u32[]{:S(2)}) collective-permute-start(bf16[168,768]{1,0:T(8,128)(2,1)S(1)} %get-tuple-element.178.refs_1_), channel_id=1, source_target_pairs={{0,2},{2,0},{1,3},{3,1},{4,6},{6,4},{5,7},{7,5},{8,10},{10,8},{9,1... | collective-permute-start | bytes 774152 | tf_op jit(solution)/shard_map/ppermute | solution.py:247
  38.8 7.8 %collective-permute-start.13 = (bf16[168,768]{1,0:T(8,128)(2,1)S(1)}, bf16[168,768]{1,0:T(8,128)(2,1)S(1)}, u32[]{:S(2)}, u32[]{:S(2)}) collective-permute-start(bf16[168,768]{1,0:T(8,128)(2,1)S(1)} %get-tuple-element.188.refs_1_), channel_id=1, source_target_pairs={{0,2},{2,0},{1,3},{3,1},{4,6},{6,4},{5,7},{7,5},{8,10},{10,8},{9,1... | collective-permute-start | bytes 774152 | tf_op jit(solution)/shard_map/ppermute | solution.py:247
  49.8 8.6 %collective-permute-start.15 = (bf16[168,768]{1,0:T(8,128)(2,1)S(1)}, bf16[168,768]{1,0:T(8,128)(2,1)S(1)}, u32[]{:S(2)}, u32[]{:S(2)}) collective-permute-start(bf16[168,768]{1,0:T(8,128)(2,1)S(1)} %get-tuple-element.198.refs_2_), channel_id=1, source_target_pairs={{0,2},{2,0},{1,3},{3,1},{4,6},{6,4},{5,7},{7,5},{8,10},{10,8},{9,1... | collective-permute-start | bytes 774152 | tf_op jit(solution)/shard_map/ppermute | solution.py:247
  54.3 15.7 %collective-permute-start.21 = (bf16[768,384]{1,0:T(8,128)(2,1)S(1)}, bf16[768,384]{1,0:T(8,128)(2,1)S(1)}, u32[]{:S(2)}, u32[]{:S(2)}) collective-permute-start(bf16[768,384]{1,0:T(8,128)(2,1)S(1)} %get-tuple-element.213), channel_id=1, source_target_pairs={{0,4},{4,0},{8,12},{12,8},{16,20},{20,16},{24,28},{28,24},{1,5},{5... | collective-permute-start | bytes 1769480 | tf_op jit(solution)/shard_map/ppermute | solution.py:253
  56.1 15.1 %collective-permute-start.22 = (bf16[768,384]{1,0:T(8,128)(2,1)S(1)}, bf16[768,384]{1,0:T(8,128)(2,1)S(1)}, u32[]{:S(2)}, u32[]{:S(2)}) collective-permute-start(bf16[768,384]{1,0:T(8,128)(2,1)S(1)} %get-tuple-element.215), channel_id=1, source_target_pairs={{0,8},{4,12},{8,0},{12,4},{16,24},{20,28},{24,16},{28,20},{1,9},{5... | collective-permute-start | bytes 1769480 | tf_op jit(solution)/shard_map/ppermute | solution.py:253
  61.4 8.6 %collective-permute-start.19 = (bf16[168,768]{1,0:T(8,128)(2,1)S(1)}, bf16[168,768]{1,0:T(8,128)(2,1)S(1)}, u32[]{:S(2)}, u32[]{:S(2)}) collective-permute-start(bf16[168,768]{1,0:T(8,128)(2,1)S(1)} %get-tuple-element.205.refs_36_.refs_1_), channel_id=1, source_target_pairs={{0,2},{2,0},{1,3},{3,1},{4,6},{6,4},{5,7},{7,5},{8,10},{10,8},{9,1... | collective-permute-start | bytes 774152 | tf_op jit(solution)/shard_map/ppermute | solution.py:247
  71.5 19.8 %collective-permute-start.29 = (bf16[768,384]{1,0:T(8,128)(2,1)S(1)}, bf16[768,384]{1,0:T(8,128)(2,1)S(1)}, u32[]{:S(2)}, u32[]{:S(2)}) collective-permute-start(bf16[768,384]{1,0:T(8,128)(2,1)S(1)} %get-tuple-element.237), channel_id=1, source_target_pairs={{0,8},{4,12},{8,0},{12,4},{16,24},{20,28},{24,16},{28,20},{1,9},{5... | collective-permute-start | bytes 1769480 | tf_op jit(solution)/shard_map/ppermute | solution.py:253
  73.2 18.2 %collective-permute-start.30 = (bf16[768,384]{1,0:T(8,128)(2,1)S(1)}, bf16[768,384]{1,0:T(8,128)(2,1)S(1)}, u32[]{:S(2)}, u32[]{:S(2)}) collective-permute-start(bf16[768,384]{1,0:T(8,128)(2,1)S(1)} %get-tuple-element.239), channel_id=1, source_target_pairs={{0,4},{4,0},{8,12},{12,8},{16,20},{20,16},{24,28},{28,24},{1,5},{5... | collective-permute-start | bytes 1769480 | tf_op jit(solution)/shard_map/ppermute | solution.py:253
  77.1 8.2 %collective-permute-start.25 = (bf16[168,768]{1,0:T(8,128)(2,1)S(1)}, bf16[168,768]{1,0:T(8,128)(2,1)S(1)}, u32[]{:S(2)}, u32[]{:S(2)}) collective-permute-start(bf16[168,768]{1,0:T(8,128)(2,1)S(1)} %get-tuple-element.226.refs_1_), channel_id=1, source_target_pairs={{0,2},{2,0},{1,3},{3,1},{4,6},{6,4},{5,7},{7,5},{8,10},{10,8},{9,1... | collective-permute-start | bytes 774152 | tf_op jit(solution)/shard_map/ppermute | solution.py:247
  91.8 32.7 %collective-permute-start.32 = (bf16[1536,384]{1,0:T(8,128)(2,1)S(1)}, bf16[1536,384]{1,0:T(8,128)(2,1)S(1)}, u32[]{:S(2)}, u32[]{:S(2)}) collective-permute-start(bf16[1536,384]{1,0:T(8,128)(2,1)S(1)} %get-tuple-element.247), channel_id=1, source_target_pairs={{0,4},{4,0},{8,12},{12,8},{16,20},{20,16},{24,28},{28,24},{1,5},{5... | collective-permute-start | bytes 3538952 | tf_op jit(solution)/shard_map/ppermute | solution.py:253
  93.4 30.9 %collective-permute-start.31 = (bf16[768,384]{1,0:T(8,128)(2,1)S(1)}, bf16[768,384]{1,0:T(8,128)(2,1)S(1)}, u32[]{:S(2)}, u32[]{:S(2)}) collective-permute-start(bf16[768,384]{1,0:T(8,128)(2,1)S(1)} %get-tuple-element.244), channel_id=1, source_target_pairs={{0,16},{4,20},{8,24},{12,28},{16,0},{20,4},{24,8},{28,12},{1,17},{... | collective-permute-start | bytes 1769480 | tf_op jit(solution)/shard_map/ppermute | solution.py:253
  96.0 28.5 %collective-permute-start.33 = (bf16[768,384]{1,0:T(8,128)(2,1)S(1)}, bf16[768,384]{1,0:T(8,128)(2,1)S(1)}, u32[]{:S(2)}, u32[]{:S(2)}) collective-permute-start(bf16[768,384]{1,0:T(8,128)(2,1)S(1)} %get-tuple-element.249), channel_id=1, source_target_pairs={{0,8},{4,12},{8,0},{12,4},{16,24},{20,28},{24,16},{28,20},{1,9},{5... | collective-permute-start | bytes 1769480 | tf_op jit(solution)/shard_map/ppermute | solution.py:253
  107.6 16.6 %collective-permute-start.37 = (bf16[64,384]{1,0:T(8,128)(2,1)S(1)}, bf16[64,384]{1,0:T(8,128)(2,1)S(1)}, u32[]{:S(2)}, u32[]{:S(2)}) collective-permute-start(bf16[64,384]{1,0:T(8,128)(2,1)S(1)} %get-tuple-element.266), channel_id=1, source_target_pairs={{0,16},{4,20},{8,24},{12,28},{16,0},{20,4},{24,8},{28,12},{1,17},{... | collective-permute-start | bytes 147464 | tf_op jit(solution)/shard_map/ppermute | solution.py:253
  125.1 16.8 %collective-permute-start.41 = (bf16[544,384]{1,0:T(8,128)(2,1)S(1)}, bf16[544,384]{1,0:T(8,128)(2,1)S(1)}, u32[]{:S(2)}, u32[]{:S(2)}) collective-permute-start(bf16[544,384]{1,0:T(8,128)(2,1)S(1)} %get-tuple-element.277), channel_id=1, source_target_pairs={{0,4},{4,0},{8,12},{12,8},{16,20},{20,16},{24,28},{28,24},{1,5},{5... | collective-permute-start | bytes 1253384 | tf_op jit(solution)/shard_map/ppermute | solution.py:253
  125.7 16.3 %collective-permute-start.40 = (bf16[480,384]{1,0:T(8,128)(2,1)S(1)}, bf16[480,384]{1,0:T(8,128)(2,1)S(1)}, u32[]{:S(2)}, u32[]{:S(2)}) collective-permute-start(bf16[480,384]{1,0:T(8,128)(2,1)S(1)} %get-tuple-element.275), channel_id=1, source_target_pairs={{0,8},{4,12},{8,0},{12,4},{16,24},{20,28},{24,16},{28,20},{1,9},{5... | collective-permute-start | bytes 1105928 | tf_op jit(solution)/shard_map/ppermute | solution.py:253
  125.7 14.1 %collective-permute-start.42 = (bf16[384,384]{1,0:T(8,128)(2,1)S(1)}, bf16[384,384]{1,0:T(8,128)(2,1)S(1)}, u32[]{:S(2)}, u32[]{:S(2)}) collective-permute-start(bf16[384,384]{1,0:T(8,128)(2,1)S(1)} %get-tuple-element.279), channel_id=1, source_target_pairs={{0,16},{4,20},{8,24},{12,28},{16,0},{20,4},{24,8},{28,12},{1,17},{... | collective-permute-start | bytes 884744 | tf_op jit(solution)/shard_map/ppermute | solution.py:253
  142.2 14.2 %collective-permute-start.44 = (bf16[384,384]{1,0:T(8,128)(2,1)S(1)}, bf16[384,384]{1,0:T(8,128)(2,1)S(1)}, u32[]{:S(2)}, u32[]{:S(2)}) collective-permute-start(bf16[384,384]{1,0:T(8,128)(2,1)S(1)} %get-tuple-element.291), channel_id=1, source_target_pairs={{0,16},{4,20},{8,24},{12,28},{16,0},{20,4},{24,8},{28,12},{1,17},{... | collective-permute-start | bytes 884744 | tf_op jit(solution)/shard_map/ppermute | solution.py:253
  143.5 9.5 %collective-permute-start.43 = (bf16[256,384]{1,0:T(8,128)(2,1)S(1)}, bf16[256,384]{1,0:T(8,128)(2,1)S(1)}, u32[]{:S(2)}, u32[]{:S(2)}) collective-permute-start(bf16[256,384]{1,0:T(8,128)(2,1)S(1)} %get-tuple-element.288), channel_id=1, source_target_pairs={{0,8},{4,12},{8,0},{12,4},{16,24},{20,28},{24,16},{28,20},{1,9},{5... | collective-permute-start | bytes 589832 | tf_op jit(solution)/shard_map/ppermute | solution.py:253
  (31 other events, 79.6 us)

commit v5 on v4

--- a/solution.py
+++ b/solution.py
@@ -344,8 +344,14 @@
                 BF16
             )
 
-        def both_rear(pieces):
+        def both_rear(pieces, gather=True):
+            pieces = list(pieces)
+            if gather:
+                return pieces, [lax.all_gather(piece, "wa") for piece in pieces]
             return pieces, [over_wa(piece) for piece in pieces]
+
+        def other_core(ref):
+            return ref.at[1 - here("wa")] if len(ref.shape) == 3 else ref
 
         def put_both(own_ref, oth_ref, values):
             own_ref[...] = values[:, :half]
@@ -585,7 +591,7 @@
         )
         far_back3 = over_ha(back3)
         fore3 = (fore3, over_wa(fore3))
-        rear3 = both_rear(rear3)
+        rear3 = both_rear(rear3, False)
 
         up_rows, down_rows = hidden // n_dev, half // n_dev
         qkv_rows, proj_rows = heads_width // n_dev, half // n_dev
@@ -660,6 +666,7 @@
 
             def body(n_ref, g_ref, fore_a, fore_b, *refs):
                 rear_a, rear_b, refs = refs[:count], refs[count : 2 * count], refs[2 * count :]
+                rear_b = [other_core(ref) for ref in rear_b]
                 out_refs, scratches = refs[: len(outs)], refs[len(outs) :]
                 values = write(n_ref, g_ref, fore_a, fore_b, rear_a, rear_b)
                 write_pieces(values, streams, scratches)
@@ -777,14 +784,15 @@
         def ship(total, kept, sent):
             packed = mm(placement(images, True), total.astype(BF16), 1, 0).astype(BF16)
             kept[...] = packed[:, :half]
-            sent[...] = packed[:, half:]
+            sent[:rows_in, :] = packed[:, half:]
 
         shipped = [sds((rows_in, half), BF16)] * 2
 
         def fold(kept, received, stay, go):
             same = here("ha") == here("wa")
-            stay[...] = jnp.where(same, kept[...], received[...])
-            go[:rows_in, :] = jnp.where(same, received[...], kept[...])
+            theirs = received[:rows_in, :]
+            stay[...] = jnp.where(same, kept[...], theirs)
+            go[:rows_in, :] = jnp.where(same, theirs, kept[...])
 
         def join(stay, received, out_ref):
             out_ref[...] = stay[...].astype(F32) + received[:rows_in, :].astype(F32)
@@ -844,7 +852,7 @@
             hold=[*keep_a, *keep_b, s3, s4, n2_own, *fore2, *wu, *wd, fore3[0]],
         )
         far_back2 = over_ha(back2)
-        rear2 = both_rear(rear2)
+        rear2 = both_rear(rear2, False)
         streams_c = attn_streams(SPLIT_C, 2)
         kept_c = [*keep_a, *keep_b, s3, s4, *small, *weights, g2, *late, sums3]
         make("wgrad_c", write_attn, streams_c, n2_own, g2_own, fore2, rear2, kept_c)
@@ -883,6 +891,7 @@
             "wgrad_b", write_mlp, streams_b, n1_own, g1_own, fore1, rear1,
             [*keep_a, s2, *small, *wq, *wp, g1, *late, sums3, sums2],
         )
+        send_first(streams_b)
 
         def window_back_body(
             g_in, part_a, part_b, s_in, small_a, small_b, qkv_ref, probs_ref, wp_a, wp_b,
@@ -900,24 +909,33 @@
         (g0, g0_own, sums1, *rear0) = call(
             window_back_body, "back_a",
             [g1, back1, far_back1, s2, *small, qkv0, probs0, *wp],
-            [full, half_low, sds((2, width)), *rear_shapes(rear_width_attn, 3)],
+            [full, half_low, sds((2, width)), *rear_shapes(rear_width_attn, 1)],
             flops=attn_flops, hold=[x0, n0_own, *fore0, s1, *wq, *late, sums3, sums2],
         )
         rear0 = both_rear(rear0)
 
         keep_0 = [g0, s1, x0, *small, *wq, sums1, sums2, sums3, *rear0[0]]
-        streams_a = attn_streams(SPLIT_A, 2)
+        streams_a = attn_streams(SPLIT_A, 0)
         make("wgrad_a", write_attn, streams_a, n0_own, g0_own, fore0, rear0, [*late, *keep_0])
         every = [*streams_d, *streams_c, *streams_b, *streams_a]
         slot(
-            "slot_ab", fresh=[*streams_b, *streams_a], moving=[*streams_d, *streams_c],
+            "slot_a", fresh=streams_a, moving=[*streams_d, *streams_c],
             hold=[*late, *keep_0],
         )
+
+        sums_at = -(-rows_in // 16) * 16
+        sums_half = sds((sum_rows, half))
+        with_sums = sds((sums_at + 2 * sum_rows, half), BF16)
+
+        def put_sums(ref, total):
+            high, low = split_low(total)
+            ref[sums_at : sums_at + sum_rows, :] = high
+            ref[sums_at + sum_rows :, :] = low
 
         def first_back_body(
             g_in, s_in, x_ref, small_a, small_b, wq_a, wq_b, sums_one, sums_two, sums_three, *refs
         ):
-            rear_refs, (kept, sent, sums_own, sums_oth, scratch, sums_ref) = refs[:-6], refs[-6:]
+            rear_refs, (kept, sent, sums_own, scratch, sums_ref) = refs[:-5], refs[-5:]
             keep = column_mask(rows)
             packed = [
                 get_rear(rear_refs, half + part * heads_width, heads_width) for part in range(3)
@@ -936,30 +954,28 @@
             sums_ref[13:24, :] = 0.5 * sums_two[...]
             sums_ref[24:26, :] = 0.5 * sums_three[...]
             sums_ref[26:, :] = jnp.zeros((sum_rows - 26, width), F32)
-            put_both(sums_own, sums_oth, sums_ref[...])
-
-        sums_half = sds((sum_rows, half))
-        token_kept, token_sent, sums_own, sums_oth = call(
+            sums_own[...] = sums_ref[:, :half]
+            put_sums(sent, sums_ref[:, half:])
+
+        token_kept, token_sent, sums_own = call(
             first_back_body, "back_0",
             [g0, s1, x0, *small, *wq, sums1, sums2, sums3, *rear0[0]],
-            shipped + [sds((sum_rows, half))] * 2,
+            [shipped[0], with_sums, sums_half],
             scratch=[pltpu.VMEM((rows, width), F32), pltpu.VMEM((sum_rows, width), F32)],
             flops=attn_flops * 3 // 4, hold=late,
         )
-        sums_at = -(-rows_in // 16) * 16
-        sums_half = sds((sum_rows, half))
-
-        def fold_tokens(kept, received, sums_a, sums_b, stay, go, sums_ref):
+
+        def fold_tokens(kept, both, sums_a, stay, go, sums_ref):
+            received = other_core(both)
             fold(kept, received, stay, go)
-            high, low = split_low(sums_a[...] + sums_b[...])
-            sums_ref[...] = high.astype(F32) + low.astype(F32)
-            go[sums_at : sums_at + sum_rows, :] = high
-            go[sums_at + sum_rows :, :] = low
+            total = sums_a[...] + joined(received, sums_at)
+            put_sums(go, total)
+            sums_ref[...] = joined(go, sums_at)
 
         token_stay, token_go, sums_chip = call(
             fold_tokens, "fold_tokens",
-            [token_kept, over_wa(token_sent), sums_own, over_wa(sums_oth)],
-            [shipped[0], sds((sums_at + 2 * sum_rows, half), BF16), sums_half], hold=late,
+            [token_kept, lax.all_gather(token_sent, "wa"), sums_own],
+            [shipped[0], with_sums, sums_half], hold=late,
         )
         token_got = over_ha(token_go)
 
@@ -972,26 +988,37 @@
             join_tokens, "join_tokens", [token_stay, token_got, sums_chip], [owned, sums_half],
             hold=late,
         )
-        left_bits = [2, 0, 1, *range(3, bits)]
+        left_bits = list(range(bits))
         sums = [sums_ha, None, 0, left_bits.pop(0)]
-        slot("sums_z", sums=sums, hold=late)
+        slot("sums_x", sums=sums, hold=late)
+        out_kept, out_sent = call(
+            out_body, "out_d", [s5, fore3[0], *wd], shipped, flops=mlp_flops // 2
+        )
+        out_both = lax.all_gather(out_sent, "wa")
+
+        def hop():
+            if not left_bits:
+                return None
+            sums[3] = left_bits.pop(0)
+            return sums
+
         turn = 0
         while left_bits or any(stream.step < bits for stream in every):
             turn += 1
-            now = None
-            if left_bits:
-                sums[3] = left_bits.pop(0)
-                now = sums
+            arrived = [s for s in every if s.step == bits and s.final is None]
+            first = [*streams_b, streams_c[1]] if turn > 1 else streams_b
+            slot(f"slot_b{turn}", moving=[s for s in first if s.step < bits])
+            second = [s for s in every if s.step < bits and s not in (*streams_b, streams_c[1])]
             slot(
-                f"slot_{turn}", moving=[s for s in every if s.step < bits], sums=now,
-                ending=[s for s in every if s.step == bits and s.final is None],
-                hold=late if turn == 1 else [],
+                f"slot_ac{turn}", moving=second, ending=arrived, sums=hop() if turn == 1 else None
             )
+            if turn > 1 and left_bits:
+                slot(f"sums_{turn}", sums=hop())
             if turn == 1:
-                out_kept, out_sent = call(
-                    out_body, "out_d", [s5, fore3[0], *wd], shipped, flops=mlp_flops // 2
+                out_stay, out_go = call(
+                    lambda kept, both, *refs: fold(kept, other_core(both), *refs),
+                    "fold_out", [out_kept, out_both], shipped,
                 )
-                out_stay, out_go = call(fold, "fold_out", [out_kept, over_wa(out_sent)], shipped)
                 out_got = over_ha(out_go)
         output = call(join, "join_out", [out_stay, out_got], [owned])[0]
 

time: 158 us -> 153 us (0.968)
  waiting for transfers between devices: 82.8 us -> 63 us
  blocking collectives: 0 us -> 11.3 us
  starting transfers between devices: 35.7 us -> 40 us
    ppermute x13 -> x16, waiting for transfers between devices: 36.6 us -> 24 us  [over_dev(): lax.ppermute(values, 'dev', [(i, i ^ 1 << bit) for i in range(n_dev)])]
    all_gather x0 -> x5, blocking collectives: none -> 11.3 us  [the longest x3 7.28 us: both_rear(): return (pieces, [lax.all_gather(piece, 'wa') for piece in pieces])]
    ppermute x13 -> x16, starting transfers between devices: 14.8 us -> 22.9 us  [over_dev(): lax.ppermute(values, 'dev', [(i, i ^ 1 << bit) for i in range(n_dev)])]
    ppermute x22 -> x14, waiting for transfers between devices: 6.83 us -> 3.25 us  [over_wa(): return lax.ppermute(values, 'wa', swap)]
    ppermute x10, waiting for transfers between devices: 39.3 us -> 35.8 us  [over_ha(): return lax.ppermute(values, 'ha', swap)]
    ppermute x10, starting transfers between devices: 16.6 us -> 14.6 us  [over_ha(): return lax.ppermute(values, 'ha', swap)]
    ppermute x22 -> x14, starting transfers between devices: 4.32 us -> 2.47 us  [over_wa(): return lax.ppermute(values, 'wa', swap)]
    pallas_call x26 -> x29, Pallas kernels: 34.2 us -> 33.7 us  [kernel_call(): pl.pallas_call(wrapped, in_specs=specs, out_specs=[pl.BlockSpec(memory_sp...]
  transfers between devices with their start and end apart: 45 -> 40, of which waited for: 27 -> 20; matrix products, arithmetic and copies ran while one was open for 0% -> 0% of each run, Pallas kernels for 15% -> 17%
where the time goes in v5:
time: 153 us
  waiting for transfers between devices  63 us (41%)
  starting transfers between devices  40 us (26%)
  Pallas kernels  33.7 us (22%)
  blocking collectives  11.3 us (7%)
  local copies, waits for them, and re-layouts  4.18 us (3%)
    ppermute x10, waiting for transfers between devices, over_ha(): return lax.ppermute(values, 'ha', swap)  35.8 us
    pallas_call x29, Pallas kernels, kernel_call(): pl.pallas_call(wrapped, in_specs=specs, out_specs=[pl.BlockSpec(memory_sp...  33.7 us
    ppermute x16, waiting for transfers between devices, over_dev(): lax.ppermute(values, 'dev', [(i, i ^ 1 << bit) for i in range(n_dev)])  24 us
    ppermute x16, starting transfers between devices, over_dev(): lax.ppermute(values, 'dev', [(i, i ^ 1 << bit) for i in range(n_dev)])  22.9 us
    ppermute x10, starting transfers between devices, over_ha(): return lax.ppermute(values, 'ha', swap)  14.6 us
    all_gather x3, blocking collectives, both_rear(): return (pieces, [lax.all_gather(piece, 'wa') for piece in pieces])  7.28 us
    unnamed x20, local copies, waits for them, and re-layouts  4.18 us
    ppermute x14, waiting for transfers between devices, over_wa(): return lax.ppermute(values, 'wa', swap)  3.25 us
  transfers between devices with their start and end apart: 40, of which 20 were waited for; matrix products, arithmetic and copies ran while one was open for 0% of the time, Pallas kernels for 17%

profile of v5, /device:TPU:0, one launch (start us, length us, event | category | flops | bytes accessed | tf_op | source)
XLA Modules:
  0.0 153.1 jit_solution(7867044336635396958)
XLA Ops:
  1.2 2.9 %collective-permute-start = (bf16[147,384]{1,0:T(8,128)(2,1)}, bf16[147,384]{1,0:T(8,128)(2,1)S(1)}, u32[]{:S(2)}, u32[]{:S(2)}) collective-permute-start(bf16[147,384]{1,0:T(8,128)(2,1)} %refs_0_.1), channel_id=1, source_target_pairs={{0,2},{2,0},{1,3},{3,1},{4,6},{6,4},{5,7},{7,5},{8,10},{10,8},{9,1... | collective-permute-start | bytes 338696 | tf_op jit(solution)/shard_map/ppermute | solution.py:247
  13.3 3.7 %attn_a.1 = (bf16[168,768]{1,0:T(8,128)(2,1)S(1)}, f32[168,768]{1,0:T(8,128)S(1)}, bf16[168,384]{1,0:T(8,128)(2,1)S(1)}, bf16[168,768]{1,0:T(8,128)(2,1)S(1)}, b...) custom-call(bf16[147,384]{1,0:T(8,128)(2,1)S(1)} %get-tuple-element., ...), custom_call_target="tpu_custom_call" | custom-call | tf_op jit(solution)/shard_map/attn_a/pallas_call | solution.py:59
  20.5 5.3 %collective-permute-done.6.refs_2_ = bf16[168,768]{1,0:T(8,128)(2,1)S(1)} collective-permute-done((bf16[168,768]{1,0:T(8,128)(2,1)S(1)}, bf16[168,768]{1,0:T(8,128)(2,1)S(1)}, u32[]{:S(2)}, u32[]{:S(2)}) %collective-permute-start.6) | collective-permute-done | bytes 258080 | tf_op jit(solution)/shard_map/ppermute | solution.py:247
  25.8 2.2 %mlp_b.1 = (f32[168,768]{1,0:T(8,128)S(1)}, bf16[168,384]{1,0:T(8,128)(2,1)S(1)}, bf16[168,1920]{1,0:T(8,128)(2,1)S(1)}, f32[168,1536]{1,0:T(8,128)S(1)}, bf16[1...) custom-call(f32[168,768]{1,0:T(8,128)S(1)} %get-tuple-element.163.refs_0_.refs_15_.refs_10_.refs_16_.refs_14_.refs_20_.refs_12_.refs_18_.refs_11, ...), custom_call_target="tpu_custom_call" | custom-call | tf_op jit(solution)/shard_map/mlp_b/pallas_call | solution.py:59
  31.2 5.5 %collective-permute-done.11.refs_2_ = bf16[168,768]{1,0:T(8,128)(2,1)S(1)} collective-permute-done((bf16[168,768]{1,0:T(8,128)(2,1)S(1)}, bf16[168,768]{1,0:T(8,128)(2,1)S(1)}, u32[]{:S(2)}, u32[]{:S(2)}) %collective-permute-start.11) | collective-permute-done | bytes 258080 | tf_op jit(solution)/shard_map/ppermute | solution.py:247
  36.7 2.1 %attn_c.1 = (f32[168,768]{1,0:T(8,128)S(1)}, f32[168,768]{1,0:T(8,128)S(1)}, bf16[168,384]{1,0:T(8,128)(2,1)S(1)}, bf16[168,768]{1,0:T(8,128)(2,1)S(1)}, bf16[3,...) custom-call(f32[168,768]{1,0:T(8,128)S(1)} %get-tuple-element.177.re, ...), custom_call_target="tpu_custom_call" | custom-call | tf_op jit(solution)/shard_map/attn_c/pallas_call | solution.py:59
  40.6 6.0 %collective-permute-done.13.refs_2_ = bf16[168,768]{1,0:T(8,128)(2,1)S(1)} collective-permute-done((bf16[168,768]{1,0:T(8,128)(2,1)S(1)}, bf16[168,768]{1,0:T(8,128)(2,1)S(1)}, u32[]{:S(2)}, u32[]{:S(2)}) %collective-permute-start.13) | collective-permute-done | bytes 258080 | tf_op jit(solution)/shard_map/ppermute | solution.py:247
  46.7 2.5 %mlp_d.1 = (f32[168,768]{1,0:T(8,128)S(1)}, bf16[168,384]{1,0:T(8,128)(2,1)S(1)}, bf16[168,1920]{1,0:T(8,128)(2,1)S(1)}, bf16[168,768]{1,0:T(8,128)(2,1)S(1)}, b...) custom-call(f32[168,768]{1,0:T(8,128)S(1)} %get-tuple-element.187.refs_0_.refs_22_.refs_21_.refs_27_, ...), custom_call_target="tpu_custom_call" | custom-call | tf_op jit(solution)/shard_map/mlp_d/pallas_call | solution.py:59
  52.2 2.1 %wgrad_d.1 = (bf16[768,384]{1,0:T(8,128)(2,1)S(1)}, bf16[768,384]{1,0:T(8,128)(2,1)S(1)}, bf16[768,384]{1,0:T(8,128)(2,1)S(1)}, bf16[768,384]{1,0:T(8,128)(2,1)S(1)}, f32[8,128]{1,0:T(8,128)S(1)}) custom-call(bf16[168,384]{1,0:T(8,128)(2,1)S(1)} %get-tuple-element.199.refs_0_, bf16[168,384]{1,0:T(8,128)(2,1)S(1)} %get-tuple-element.183.refs_26_.refs_29_.refs_1_.refs_0_, ...), custom_call_target="tpu_custom_call" | custom-call | tf_op jit(solution)/shard_map/wgrad_d/pallas_call | solution.py:59
  58.4 2.9 %back_c.1 = (f32[168,768]{1,0:T(8,128)S(1)}, bf16[168,384]{1,0:T(8,128)(2,1)S(1)}, bf16[168,768]{1,0:T(8,128)(2,1)S(1)}, f32[2,768]{1,0:T(2,128)S(1)}, bf16[168,...) custom-call(bf16[168,384]{1,0:T(8,128)(2,1)S(1)} %get-tuple-element.183.refs_26_.refs_29_.refs_1_.refs_0_, ...), custom_call_target="tpu_custom_call" | custom-call | tf_op jit(solution)/shard_map/back_c/pallas_call | solution.py:59
  64.3 5.7 %collective-permute-done.19.refs_37_.refs_2_ = bf16[168,768]{1,0:T(8,128)(2,1)S(1)} collective-permute-done((bf16[168,768]{1,0:T(8,128)(2,1)S(1)}, bf16[168,768]{1,0:T(8,128)(2,1)S(1)}, u32[]{:S(2)}, u32[]{:S(2)}) %collective-permute-start.19) | collective-permute-done | bytes 258080 | tf_op jit(solution)/shard_map/ppermute | solution.py:247
  73.7 2.8 %back_b.1 = (f32[168,768]{1,0:T(8,128)S(1)}, bf16[168,384]{1,0:T(8,128)(2,1)S(1)}, bf16[168,768]{1,0:T(8,128)(2,1)S(1)}, f32[11,768]{1,0:T(8,128)S(1)}, bf16[168...) custom-call(f32[168,768]{1,0:T(8,128)S(1)} %get-tuple-element.204.refs_30_.refs_0_, ...), custom_call_target="tpu_custom_call" | custom-call | tf_op jit(solution)/shard_map/back_b/pallas_call | solution.py:59
  78.2 2.2 %all-gather.1 = bf16[336,896]{1,0:T(8,128)(2,1)S(1)} all-gather(bf16[168,896]{1,0:T(8,128)(2,1)S(1)} %get-tuple-element.223.refs_5_), channel_id=3, replica_groups=mesh['dev'=8,'ha'=2,'wa'=2] {'wa'}, dimensions={0}, use_global_device_ids=true | all-gather | bytes 903168 | tf_op jit(solution)/shard_map/all_gather | solution.py:350
  80.4 2.3 %all-gather = bf16[336,1024]{1,0:T(8,128)(2,1)S(1)} all-gather(bf16[168,1024]{1,0:T(8,128)(2,1)S(1)} %get-tuple-element.222.refs_4_), channel_id=2, replica_groups=mesh['dev'=8,'ha'=2,'wa'=2] {'wa'}, dimensions={0}, use_global_device_ids=true | all-gather | bytes 1032192 | tf_op jit(solution)/shard_map/all_gather | solution.py:350
  86.6 2.8 %back_a.1 = (f32[168,768]{1,0:T(8,128)S(1)}, bf16[168,384]{1,0:T(8,128)(2,1)S(1)}, f32[2,768]{1,0:T(2,128)S(1)}, bf16[168,1536]{1,0:T(8,128)(2,1)S(1)}, f32[8,128]{1,0:T(8,128)S(1)}) custom-call(f32[168,768]{1,0:T(8,128)S(1)} %get-tuple-element.218.refs_22_.refs_0_, bf16[168,768]{1,0:T(8,128)(2,1)S(1)} %get-tuple-element.219.refs_1_, ...), custom_call_target="tpu_custom_call" | custom-call | tf_op jit(solution)/shard_map/back_a/pallas_call | solution.py:59
  89.5 2.8 %all-gather.2 = bf16[336,1536]{1,0:T(8,128)(2,1)S(1)} all-gather(bf16[168,1536]{1,0:T(8,128)(2,1)S(1)} %get-tuple-element.228.refs_4_.refs_20_.refs_21_.refs_10_), channel_id=4, replica_groups=mesh['dev'=8,'ha'=2,'wa'=2] {'wa'}, dimensions={0}, use_global_device_ids=true | all-gather | bytes 1548288 | tf_op jit(solution)/shard_map/all_gather | solution.py:350
  93.8 2.7 %collective-permute-start.27 = (bf16[768,384]{1,0:T(8,128)(2,1)S(1)}, bf16[768,384]{1,0:T(8,128)(2,1)S(1)}, u32[]{:S(2)}, u32[]{:S(2)}) collective-permute-start(bf16[768,384]{1,0:T(8,128)(2,1)S(1)} %get-tuple-element.254), channel_id=1, source_target_pairs={{0,16},{4,20},{8,24},{12,28},{16,0},{20,4},{24,8},{28,12},{1,17},{... | collective-permute-start | bytes 1769480 | tf_op jit(solution)/shard_map/ppermute | solution.py:253
  101.6 5.9 %collective-permute-done.26.refs_1_ = bf16[224,384]{1,0:T(8,128)(2,1)S(1)} collective-permute-done((bf16[224,384]{1,0:T(8,128)(2,1)S(1)}, bf16[224,384]{1,0:T(8,128)(2,1)S(1)}, u32[]{:S(2)}, u32[]{:S(2)}) %collective-permute-start.26) | collective-permute-done | bytes 172064 | tf_op jit(solution)/shard_map/ppermute | solution.py:247
  113.7 9.1 %collective-permute-done.27.refs_1_.refs_5_ = bf16[768,384]{1,0:T(8,128)(2,1)S(1)} collective-permute-done((bf16[768,384]{1,0:T(8,128)(2,1)S(1)}, bf16[768,384]{1,0:T(8,128)(2,1)S(1)}, u32[]{:S(2)}, u32[]{:S(2)}) %collective-permute-start.27) | collective-permute-done | bytes 589856 | tf_op jit(solution)/shard_map/ppermute | solution.py:253
  126.7 4.0 %collective-permute-start.38 = (bf16[384,384]{1,0:T(8,128)(2,1)S(1)}, bf16[384,384]{1,0:T(8,128)(2,1)S(1)}, u32[]{:S(2)}, u32[]{:S(2)}) collective-permute-start(bf16[384,384]{1,0:T(8,128)(2,1)S(1)} %get-tuple-element.290), channel_id=1, source_target_pairs={{0,16},{4,20},{8,24},{12,28},{16,0},{20,4},{24,8},{28,12},{1,17},{... | collective-permute-start | bytes 884744 | tf_op jit(solution)/shard_map/ppermute | solution.py:253
  130.7 9.3 %collective-permute-done.33.refs_1_ = bf16[544,384]{1,0:T(8,128)(2,1)S(1)} collective-permute-done((bf16[544,384]{1,0:T(8,128)(2,1)S(1)}, bf16[544,384]{1,0:T(8,128)(2,1)S(1)}, u32[]{:S(2)}, u32[]{:S(2)}) %collective-permute-start.33) | collective-permute-done | bytes 417824 | tf_op jit(solution)/shard_map/ppermute | solution.py:253
  140.1 2.9 %collective-permute-start.37 = (bf16[192,384]{1,0:T(8,128)(2,1)S(1)}, bf16[192,384]{1,0:T(8,128)(2,1)S(1)}, u32[]{:S(2)}, u32[]{:S(2)}) collective-permute-start(bf16[192,384]{1,0:T(8,128)(2,1)S(1)} %get-tuple-element.288), channel_id=1, source_target_pairs={{0,16},{4,20},{8,24},{12,28},{16,0},{20,4},{24,8},{28,12},{1,17},{... | collective-permute-start | bytes 442376 | tf_op jit(solution)/shard_map/ppermute | solution.py:253
  144.2 3.6 %collective-permute-done.32.refs_1_ = bf16[147,384]{1,0:T(8,128)(2,1)S(1)} collective-permute-done((bf16[147,384]{1,0:T(8,128)(2,1)S(1)}, bf16[147,384]{1,0:T(8,128)(2,1)S(1)}, u32[]{:S(2)}, u32[]{:S(2)}) %collective-permute-start.32) | collective-permute-done | bytes 112928 | tf_op jit(solution)/shard_map/ppermute | solution.py:247
  148.6 3.2 %collective-permute-done.36.refs_1_ = bf16[64,384]{1,0:T(8,128)(2,1)S(1)} collective-permute-done((bf16[64,384]{1,0:T(8,128)(2,1)S(1)}, bf16[64,384]{1,0:T(8,128)(2,1)S(1)}, u32[]{:S(2)}, u32[]{:S(2)}) %collective-permute-start.36) | collective-permute-done | bytes 49184 | tf_op jit(solution)/shard_map/ppermute | solution.py:253
  (110 shorter events, 57.4 us)
Async XLA Ops:
  0.6 9.7 %collective-permute-start.2 = (bf16[2,3,384,384]{3,2,1,0:T(8,128)(2,1)}, bf16[2,3,384,384]{3,2,1,0:T(8,128)(2,1)S(1)}, u32[]{:S(2)}, u32[]{:S(2)}) collective-permute-start(bf16[2,3,384,384]{3,2,1,0:T(8,128)(2,1)} %bitcast.12), channel_id=1, source_target_pairs={{0,1},{1,0},{2,3},{3,2},{4,5},{5,4},{6,7},{7,6},{8,9},{9,8},{10,11... | collective-permute-start | bytes 5308424 | tf_op jit(solution)/shard_map/ppermute | solution.py:250
  1.2 9.2 %collective-permute-start.3 = (bf16[2,384,384]{2,1,0:T(8,128)(2,1)}, bf16[2,384,384]{2,1,0:T(8,128)(2,1)S(1)}, u32[]{:S(2)}, u32[]{:S(2)}) collective-permute-start(bf16[2,384,384]{2,1,0:T(8,128)(2,1)} %refs_8_.6), channel_id=1, source_target_pairs={{0,1},{1,0},{2,3},{3,2},{4,5},{5,4},{6,7},{7,6},{8,9},{9,8},{10,11... | collective-permute-start | bytes 1769480 | tf_op jit(solution)/shard_map/ppermute | solution.py:250
  12.0 13.8 %collective-permute-start.8 = (bf16[2,1536,384]{2,1,0:T(8,128)(2,1)S(1)}, bf16[2,1536,384]{2,1,0:T(8,128)(2,1)S(1)}, u32[]{:S(2)}, u32[]{:S(2)}) collective-permute-start(bf16[2,1536,384]{2,1,0:T(8,128)(2,1)S(1)} %copy-done), channel_id=1, source_target_pairs={{0,1},{1,0},{2,3},{3,2},{4,5},{5,4},{6,7},{7,6},{8,9},{9,8},{10,11... | collective-permute-start | bytes 7077896 | tf_op jit(solution)/shard_map/ppermute | solution.py:250
  12.7 13.1 %collective-permute-start.7 = (bf16[2,384,1536]{2,1,0:T(8,128)(2,1)S(1)}, bf16[2,384,1536]{2,1,0:T(8,128)(2,1)S(1)}, u32[]{:S(2)}, u32[]{:S(2)}) collective-permute-start(bf16[2,384,1536]{2,1,0:T(8,128)(2,1)S(1)} %copy-done.2), channel_id=1, source_target_pairs={{0,1},{1,0},{2,3},{3,2},{4,5},{5,4},{6,7},{7,6},{8,9},{9,8},{10,11... | collective-permute-start | bytes 7077896 | tf_op jit(solution)/shard_map/ppermute | solution.py:250
  17.2 8.6 %collective-permute-start.6 = (bf16[168,768]{1,0:T(8,128)(2,1)S(1)}, bf16[168,768]{1,0:T(8,128)(2,1)S(1)}, u32[]{:S(2)}, u32[]{:S(2)}) collective-permute-start(bf16[168,768]{1,0:T(8,128)(2,1)S(1)} %get-tuple-element.164.refs_1_), channel_id=1, source_target_pairs={{0,2},{2,0},{1,3},{3,1},{4,6},{6,4},{5,7},{7,5},{8,10},{10,8},{9,1... | collective-permute-start | bytes 774152 | tf_op jit(solution)/shard_map/ppermute | solution.py:247
  28.1 8.6 %collective-permute-start.11 = (bf16[168,768]{1,0:T(8,128)(2,1)S(1)}, bf16[168,768]{1,0:T(8,128)(2,1)S(1)}, u32[]{:S(2)}, u32[]{:S(2)}) collective-permute-start(bf16[168,768]{1,0:T(8,128)(2,1)S(1)} %get-tuple-element.178.refs_1_), channel_id=1, source_target_pairs={{0,2},{2,0},{1,3},{3,1},{4,6},{6,4},{5,7},{7,5},{8,10},{10,8},{9,1... | collective-permute-start | bytes 774152 | tf_op jit(solution)/shard_map/ppermute | solution.py:247
  38.8 7.9 %collective-permute-start.13 = (bf16[168,768]{1,0:T(8,128)(2,1)S(1)}, bf16[168,768]{1,0:T(8,128)(2,1)S(1)}, u32[]{:S(2)}, u32[]{:S(2)}) collective-permute-start(bf16[168,768]{1,0:T(8,128)(2,1)S(1)} %get-tuple-element.188.refs_1_), channel_id=1, source_target_pairs={{0,2},{2,0},{1,3},{3,1},{4,6},{6,4},{5,7},{7,5},{8,10},{10,8},{9,1... | collective-permute-start | bytes 774152 | tf_op jit(solution)/shard_map/ppermute | solution.py:247
  49.8 8.6 %collective-permute-start.15 = (bf16[168,768]{1,0:T(8,128)(2,1)S(1)}, bf16[168,768]{1,0:T(8,128)(2,1)S(1)}, u32[]{:S(2)}, u32[]{:S(2)}) collective-permute-start(bf16[168,768]{1,0:T(8,128)(2,1)S(1)} %get-tuple-element.198.refs_2_), channel_id=1, source_target_pairs={{0,2},{2,0},{1,3},{3,1},{4,6},{6,4},{5,7},{7,5},{8,10},{10,8},{9,1... | collective-permute-start | bytes 774152 | tf_op jit(solution)/shard_map/ppermute | solution.py:247
  54.3 15.7 %collective-permute-start.21 = (bf16[768,384]{1,0:T(8,128)(2,1)S(1)}, bf16[768,384]{1,0:T(8,128)(2,1)S(1)}, u32[]{:S(2)}, u32[]{:S(2)}) collective-permute-start(bf16[768,384]{1,0:T(8,128)(2,1)S(1)} %get-tuple-element.213), channel_id=1, source_target_pairs={{0,4},{4,0},{8,12},{12,8},{16,20},{20,16},{24,28},{28,24},{1,5},{5... | collective-permute-start | bytes 1769480 | tf_op jit(solution)/shard_map/ppermute | solution.py:253
  56.1 15.1 %collective-permute-start.22 = (bf16[768,384]{1,0:T(8,128)(2,1)S(1)}, bf16[768,384]{1,0:T(8,128)(2,1)S(1)}, u32[]{:S(2)}, u32[]{:S(2)}) collective-permute-start(bf16[768,384]{1,0:T(8,128)(2,1)S(1)} %get-tuple-element.215), channel_id=1, source_target_pairs={{0,8},{4,12},{8,0},{12,4},{16,24},{20,28},{24,16},{28,20},{1,9},{5... | collective-permute-start | bytes 1769480 | tf_op jit(solution)/shard_map/ppermute | solution.py:253
  61.4 8.6 %collective-permute-start.19 = (bf16[168,768]{1,0:T(8,128)(2,1)S(1)}, bf16[168,768]{1,0:T(8,128)(2,1)S(1)}, u32[]{:S(2)}, u32[]{:S(2)}) collective-permute-start(bf16[168,768]{1,0:T(8,128)(2,1)S(1)} %get-tuple-element.205.refs_36_.refs_1_), channel_id=1, source_target_pairs={{0,2},{2,0},{1,3},{3,1},{4,6},{6,4},{5,7},{7,5},{8,10},{10,8},{9,1... | collective-permute-start | bytes 774152 | tf_op jit(solution)/shard_map/ppermute | solution.py:247
  71.5 21.8 %collective-permute-start.24 = (bf16[768,384]{1,0:T(8,128)(2,1)S(1)}, bf16[768,384]{1,0:T(8,128)(2,1)S(1)}, u32[]{:S(2)}, u32[]{:S(2)}) collective-permute-start(bf16[768,384]{1,0:T(8,128)(2,1)S(1)} %get-tuple-element.233), channel_id=1, source_target_pairs={{0,8},{4,12},{8,0},{12,4},{16,24},{20,28},{24,16},{28,20},{1,9},{5... | collective-permute-start | bytes 1769480 | tf_op jit(solution)/shard_map/ppermute | solution.py:253
  73.2 20.2 %collective-permute-start.25 = (bf16[768,384]{1,0:T(8,128)(2,1)S(1)}, bf16[768,384]{1,0:T(8,128)(2,1)S(1)}, u32[]{:S(2)}, u32[]{:S(2)}) collective-permute-start(bf16[768,384]{1,0:T(8,128)(2,1)S(1)} %get-tuple-element.235), channel_id=1, source_target_pairs={{0,4},{4,0},{8,12},{12,8},{16,20},{20,16},{24,28},{28,24},{1,5},{5... | collective-permute-start | bytes 1769480 | tf_op jit(solution)/shard_map/ppermute | solution.py:253
  76.6 10.1 %collective-permute-start.23 = (bf16[168,768]{1,0:T(8,128)(2,1)S(1)}, bf16[168,768]{1,0:T(8,128)(2,1)S(1)}, u32[]{:S(2)}, u32[]{:S(2)}) collective-permute-start(bf16[168,768]{1,0:T(8,128)(2,1)S(1)} %get-tuple-element.219.refs_1_), channel_id=1, source_target_pairs={{0,2},{2,0},{1,3},{3,1},{4,6},{6,4},{5,7},{7,5},{8,10},{10,8},{9,1... | collective-permute-start | bytes 774152 | tf_op jit(solution)/shard_map/ppermute | solution.py:247
  84.6 26.1 %collective-permute-start.30 = (bf16[768,384]{1,0:T(8,128)(2,1)S(1)}, bf16[768,384]{1,0:T(8,128)(2,1)S(1)}, u32[]{:S(2)}, u32[]{:S(2)}) collective-permute-start(bf16[768,384]{1,0:T(8,128)(2,1)S(1)} %get-tuple-element.262), channel_id=1, source_target_pairs={{0,4},{4,0},{8,12},{12,8},{16,20},{20,16},{24,28},{28,24},{1,5},{5... | collective-permute-start | bytes 1769480 | tf_op jit(solution)/shard_map/ppermute | solution.py:253
  86.2 24.6 %collective-permute-start.31 = (bf16[768,384]{1,0:T(8,128)(2,1)S(1)}, bf16[768,384]{1,0:T(8,128)(2,1)S(1)}, u32[]{:S(2)}, u32[]{:S(2)}) collective-permute-start(bf16[768,384]{1,0:T(8,128)(2,1)S(1)} %get-tuple-element.264), channel_id=1, source_target_pairs={{0,8},{4,12},{8,0},{12,4},{16,24},{20,28},{24,16},{28,20},{1,9},{5... | collective-permute-start | bytes 1769480 | tf_op jit(solution)/shard_map/ppermute | solution.py:253
  93.8 29.1 %collective-permute-start.27 = (bf16[768,384]{1,0:T(8,128)(2,1)S(1)}, bf16[768,384]{1,0:T(8,128)(2,1)S(1)}, u32[]{:S(2)}, u32[]{:S(2)}) collective-permute-start(bf16[768,384]{1,0:T(8,128)(2,1)S(1)} %get-tuple-element.254), channel_id=1, source_target_pairs={{0,16},{4,20},{8,24},{12,28},{16,0},{20,4},{24,8},{28,12},{1,17},{... | collective-permute-start | bytes 1769480 | tf_op jit(solution)/shard_map/ppermute | solution.py:253
  96.4 26.5 %collective-permute-start.28 = (bf16[768,384]{1,0:T(8,128)(2,1)S(1)}, bf16[768,384]{1,0:T(8,128)(2,1)S(1)}, u32[]{:S(2)}, u32[]{:S(2)}) collective-permute-start(bf16[768,384]{1,0:T(8,128)(2,1)S(1)} %get-tuple-element.256), channel_id=1, source_target_pairs={{0,4},{4,0},{8,12},{12,8},{16,20},{20,16},{24,28},{28,24},{1,5},{5... | collective-permute-start | bytes 1769480 | tf_op jit(solution)/shard_map/ppermute | solution.py:253
  111.0 15.4 %collective-permute-start.34 = (bf16[384,384]{1,0:T(8,128)(2,1)S(1)}, bf16[384,384]{1,0:T(8,128)(2,1)S(1)}, u32[]{:S(2)}, u32[]{:S(2)}) collective-permute-start(bf16[384,384]{1,0:T(8,128)(2,1)S(1)} %get-tuple-element.275), channel_id=1, source_target_pairs={{0,8},{4,12},{8,0},{12,4},{16,24},{20,28},{24,16},{28,20},{1,9},{5... | collective-permute-start | bytes 884744 | tf_op jit(solution)/shard_map/ppermute | solution.py:253
  112.7 13.8 %collective-permute-start.35 = (bf16[384,384]{1,0:T(8,128)(2,1)S(1)}, bf16[384,384]{1,0:T(8,128)(2,1)S(1)}, u32[]{:S(2)}, u32[]{:S(2)}) collective-permute-start(bf16[384,384]{1,0:T(8,128)(2,1)S(1)} %get-tuple-element.277), channel_id=1, source_target_pairs={{0,4},{4,0},{8,12},{12,8},{16,20},{20,16},{24,28},{28,24},{1,5},{5... | collective-permute-start | bytes 884744 | tf_op jit(solution)/shard_map/ppermute | solution.py:253
  123.2 16.9 %collective-permute-start.33 = (bf16[544,384]{1,0:T(8,128)(2,1)S(1)}, bf16[544,384]{1,0:T(8,128)(2,1)S(1)}, u32[]{:S(2)}, u32[]{:S(2)}) collective-permute-start(bf16[544,384]{1,0:T(8,128)(2,1)S(1)} %get-tuple-element.271), channel_id=1, source_target_pairs={{0,8},{4,12},{8,0},{12,4},{16,24},{20,28},{24,16},{28,20},{1,9},{5... | collective-permute-start | bytes 1253384 | tf_op jit(solution)/shard_map/ppermute | solution.py:253
  126.7 21.9 %collective-permute-start.38 = (bf16[384,384]{1,0:T(8,128)(2,1)S(1)}, bf16[384,384]{1,0:T(8,128)(2,1)S(1)}, u32[]{:S(2)}, u32[]{:S(2)}) collective-permute-start(bf16[384,384]{1,0:T(8,128)(2,1)S(1)} %get-tuple-element.290), channel_id=1, source_target_pairs={{0,16},{4,20},{8,24},{12,28},{16,0},{20,4},{24,8},{28,12},{1,17},{... | collective-permute-start | bytes 884744 | tf_op jit(solution)/shard_map/ppermute | solution.py:253
  140.1 11.7 %collective-permute-start.37 = (bf16[192,384]{1,0:T(8,128)(2,1)S(1)}, bf16[192,384]{1,0:T(8,128)(2,1)S(1)}, u32[]{:S(2)}, u32[]{:S(2)}) collective-permute-start(bf16[192,384]{1,0:T(8,128)(2,1)S(1)} %get-tuple-element.288), channel_id=1, source_target_pairs={{0,16},{4,20},{8,24},{12,28},{16,0},{20,4},{24,8},{28,12},{1,17},{... | collective-permute-start | bytes 442376 | tf_op jit(solution)/shard_map/ppermute | solution.py:253
  144.1 7.7 %collective-permute-start.36 = (bf16[64,384]{1,0:T(8,128)(2,1)S(1)}, bf16[64,384]{1,0:T(8,128)(2,1)S(1)}, u32[]{:S(2)}, u32[]{:S(2)}) collective-permute-start(bf16[64,384]{1,0:T(8,128)(2,1)S(1)} %get-tuple-element.286), channel_id=1, source_target_pairs={{0,16},{4,20},{8,24},{12,28},{16,0},{20,4},{24,8},{28,12},{1,17},{... | collective-permute-start | bytes 147464 | tf_op jit(solution)/shard_map/ppermute | solution.py:253
  (26 other events, 84.1 us)

commit v6 on v5

--- a/solution.py
+++ b/solution.py
@@ -35,33 +35,30 @@
         self.last = None
 
 
-def kernel_call(body, name, ins, outs, order, scratch=(), flops=0, hold=(), far=0):
+def kernel_call(
+    body, name, ins, outs, order, scratch=(), flops=0, hold=(), reuse=None, carry=None
+):
+    reuse = reuse or {}
     arrays = list(ins) + list(hold) + ([] if order.last is None else [order.last])
-    specs = [
-        pl.BlockSpec(
-            memory_space=pltpu.SMEM if a.dtype == jnp.int32 and a.ndim == 1 else pltpu.VMEM
-        )
-        for a in arrays
-    ]
-    for at in range(len(ins) - far, len(ins)):
-        specs[at] = pl.BlockSpec(memory_space=pltpu.HBM)
+    first_reused = len(arrays)
+    aliases = {first_reused + at: out for at, out in enumerate(reuse)}
+    arrays += list(reuse.values())
     outs = list(outs) + [sds((8, LANES))]
 
     def wrapped(*refs):
-        given = refs[: len(ins)] + refs[len(arrays) : len(arrays) + len(outs) - 1]
-        body(*given, *refs[len(arrays) + len(outs) :])
-        mark = refs[len(arrays) + len(outs) - 1]
-        mark[...] = jnp.zeros_like(mark)
-
-    moved = sum(int(np.prod(o.shape)) * o.dtype.itemsize for o in outs) + sum(
-        int(np.prod(a.shape)) * a.dtype.itemsize for a in ins
-    )
+        out_refs = refs[len(arrays) : len(arrays) + len(outs)]
+        for at, out in aliases.items():
+            carry(refs[at], out_refs[out])
+        body(*refs[: len(ins)], *out_refs[:-1], *refs[len(arrays) + len(outs) :])
+        out_refs[-1][...] = jnp.zeros_like(out_refs[-1])
+
     *results, order.last = pl.pallas_call(
         wrapped,
-        in_specs=specs,
+        in_specs=[pl.BlockSpec(memory_space=pltpu.VMEM)] * len(arrays),
         out_specs=[pl.BlockSpec(memory_space=pltpu.VMEM)] * len(outs),
         out_shape=outs,
         scratch_shapes=list(scratch),
+        input_output_aliases=aliases,
         compiler_params=pltpu.CompilerParams(vmem_limit_bytes=VMEM_LIMIT),
         cost_estimate=pl.CostEstimate(
             flops=int(TIMES.get(name, 0) * 1.15e9), bytes_accessed=0, transcendentals=0
@@ -79,10 +76,10 @@
     return (lax.broadcasted_iota(jnp.int32, (rows, 1), 0) % GRID_COLS) < WIN
 
 
-def placement(images, transposed):
-    padded, plain = images * PADDED, images * PATCHES
+def placement(images, transposed, begin=0, count=None):
+    padded, plain = count or images * PADDED, images * PATCHES
     shape = (plain, padded) if transposed else (padded, plain)
-    at = lax.broadcasted_iota(jnp.int32, shape, 1 if transposed else 0)
+    at = lax.broadcasted_iota(jnp.int32, shape, 1 if transposed else 0) + begin
     image = sum((at >= i * PADDED).astype(jnp.int32) for i in range(1, images))
     inside = at - image * PADDED
     source = image * PATCHES + (inside >> 3) * WIN + (inside & 7)
@@ -153,15 +150,9 @@
 
 
 def gelu_parts(values):
-    z = jnp.abs(values) * (0.5**0.5)
-    t = 1.0 / (1.0 + 0.3275911 * z)
-    bell = jnp.exp(-z * z)
-    poly = t * (
-        0.254829592
-        + t * (-0.284496736 + t * (1.421413741 + t * (-1.453152027 + t * 1.061405429)))
-    )
-    tail = 0.5 * poly * bell
-    return jnp.where(values < 0, tail, 1.0 - tail), bell * float(1.0 / np.sqrt(2.0 * np.pi))
+    below = 0.5 + 0.5 * lax.erf(values * float(0.5**0.5))
+    bell = jnp.exp2(values * values * float(-0.5 * np.log2(np.e)))
+    return below, bell * float(1.0 / np.sqrt(2.0 * np.pi))
 
 
 def head_mask(index):
@@ -185,30 +176,41 @@
 def softmax_rows(scores):
     top = jnp.max(scores, axis=0, keepdims=True)
     weights = jnp.exp(scores - top)
-    return weights / jnp.sum(weights, axis=0, keepdims=True)
+    return weights * (1.0 / jnp.sum(weights, axis=0, keepdims=True))
 
 
 SCALE = HEAD_DIM**-0.5
 
 
-def window_tile(q, k, v):
+def low(tiles):
+    return [tile.astype(BF16) for tile in tiles]
+
+
+def minus_row_sums(probs, grads):
+    return [
+        (p * (g - jnp.sum(g * p, axis=0, keepdims=True))).astype(BF16)
+        for p, g in zip(probs, grads)
+    ]
+
+
+def window_tiles(queries, keys, values):
     keys_ok = column_mask(PADDED)
-    scores = mm(k.astype(BF16), spread_heads(q), 1, 1) * SCALE
-    probs = softmax_rows(jnp.where(keys_ok, scores, NEG))
-    return probs, gather_heads(mm(probs.astype(BF16), v.astype(BF16), 0, 0))
-
-
-def window_tile_back(q, k, v, probs, grad):
-    low = probs.astype(BF16)
-    q_big, g_big = spread_heads(q), spread_heads(grad)
-    grad_probs = mm(v.astype(BF16), g_big, 1, 1)
-    grad_v = mm(low, g_big, 1, 0)
-    grad_scores = (
-        probs * (grad_probs - jnp.sum(grad_probs * probs, axis=0, keepdims=True))
-    ).astype(BF16)
-    grad_k = mm(grad_scores, q_big, 1, 0) * SCALE
-    grad_q = gather_heads(mm(grad_scores, k.astype(BF16), 0, 0)) * SCALE
-    return grad_q, grad_k, grad_v
+    scores = [
+        mm(k, spread_heads(q), 1, 1) * SCALE for q, k in zip(queries, low(keys))
+    ]
+    probs = [softmax_rows(jnp.where(keys_ok, score, NEG)) for score in scores]
+    mixed = [mm(p, v, 0, 0) for p, v in zip(low(probs), low(values))]
+    return probs, [gather_heads(tile) for tile in mixed]
+
+
+def window_tiles_back(queries, keys, values, probs, grads):
+    q_big, g_big = ([spread_heads(tile) for tile in tiles] for tiles in (queries, grads))
+    grad_probs = [mm(v, g, 1, 1) for v, g in zip(low(values), g_big)]
+    grad_v = [mm(p, g, 1, 0) for p, g in zip(low(probs), g_big)]
+    grad_scores = minus_row_sums(probs, grad_probs)
+    grad_k = [mm(d, q, 1, 0) * SCALE for d, q in zip(grad_scores, q_big)]
+    grad_q = [mm(d, k, 0, 0) for d, k in zip(grad_scores, low(keys))]
+    return [gather_heads(tile) * SCALE for tile in grad_q], grad_k, grad_v
 
 
 def same_head():
@@ -217,23 +219,39 @@
     return first == second
 
 
-def channel_tile(q, k, v, mask):
-    scores = mm(k.astype(BF16), (q * mask).astype(BF16), 0, 0) * SCALE
-    probs = softmax_rows(jnp.where(same_head(), scores, NEG))
-    return probs, mm(v.astype(BF16), probs.astype(BF16), 1, 0)
-
-
-def channel_tile_back(q, k, v, probs, grad, mask):
-    low = probs.astype(BF16)
-    grad_low = grad.astype(BF16)
-    grad_probs = mm(v.astype(BF16), grad_low, 0, 0)
-    grad_v = mm(grad_low, low, 1, 1)
-    grad_scores = (
-        probs * (grad_probs - jnp.sum(grad_probs * probs, axis=0, keepdims=True))
-    ).astype(BF16)
-    grad_q = mm(k.astype(BF16), grad_scores, 1, 0) * SCALE * mask
-    grad_k = mm((q * mask).astype(BF16), grad_scores, 1, 1) * SCALE
+def channel_tiles(queries, keys, values, masks):
+    own_head = same_head()
+    masked = low([q * mask for q, mask in zip(queries, masks)])
+    scores = [mm(k, q, 0, 0) * SCALE for q, k in zip(masked, low(keys))]
+    probs = [softmax_rows(jnp.where(own_head, score, NEG)) for score in scores]
+    return probs, [mm(v, p, 1, 0) for p, v in zip(low(probs), low(values))]
+
+
+def channel_tiles_back(queries, keys, values, probs, grads, masks):
+    masked = low([q * mask for q, mask in zip(queries, masks)])
+    grads = low(grads)
+    grad_probs = [mm(v, g, 0, 0) for v, g in zip(low(values), grads)]
+    grad_v = [mm(g, p, 1, 1) for g, p in zip(grads, low(probs))]
+    grad_scores = minus_row_sums(probs, grad_probs)
+    grad_q = [mm(k, d, 1, 0) * SCALE * m for k, d, m in zip(low(keys), grad_scores, masks)]
+    grad_k = [mm(q, d, 1, 1) * SCALE for q, d in zip(masked, grad_scores)]
     return grad_q, grad_k, grad_v
+
+
+def cut_tiles(values, images, tiles):
+    return [
+        values[image * PADDED : (image + 1) * PADDED, tile * LANES : (tile + 1) * LANES]
+        for image in range(images)
+        for tile in range(tiles)
+    ]
+
+
+def paste_tiles(parts, images, tiles):
+    lines = [
+        jnp.concatenate(parts[image * tiles : (image + 1) * tiles], axis=1)
+        for image in range(images)
+    ]
+    return jnp.concatenate(lines, axis=0).astype(BF16)
 
 
 def solution(mesh):
@@ -289,12 +307,13 @@
             out_ref[18:22, :] = gain_ref[...]
             out_ref[22:26, :] = shift_ref[...]
 
-        def choose(mine, received, cot, cot_received, own, other, cot_own, cot_other):
+        def choose(mine, received, own, *others):
             same = here("ha") == here("wa")
             own[...] = jnp.where(same, mine[...], received[...])
-            other[...] = jnp.where(same, received[...], mine[...])
-            cot_own[...] = jnp.where(same, cot[...], cot_received[...])
-            cot_other[...] = jnp.where(same, cot_received[...], cot[...])
+            other, at = jnp.where(same, received[...], mine[...]), 0
+            for ref in others:
+                ref[...] = other[:, at : at + ref.shape[1]]
+                at += ref.shape[1]
 
         wq_own = jnp.transpose(w_qkv, (0, 2, 1, 3))
         wq, wp = (wq_own, over_wa(wq_own)), (w_proj, over_wa(w_proj))
@@ -305,18 +324,24 @@
             hold=[tokens],
         )[0]
         small = (small_own, over_wa(small_own))
-        tokens_own, tokens_oth, cot_own, cot_oth = call(
-            choose, "choose", [tokens, tokens_in, cotangent, cot_in],
-            [sds((rows_in, half), BF16)] * 4, hold=[wq[1], wp[1], small_own],
-        )
-        token_parts = (tokens_own, over_wa(tokens_oth))
-        arrived = (token_parts[1], small[1])
-        cot_parts = (cot_own, over_wa(later(cot_oth, arrived)))
+        chosen = [sds((rows_in, columns), BF16) for columns in (half, LANES, half - LANES)]
+        tokens_own, *tokens_oth = call(
+            choose, "choose", [tokens, tokens_in], chosen, hold=[wq[1], wp[1], small_own]
+        )
+        token_parts = (tokens_own, *[over_wa(values) for values in tokens_oth])
+
+        def arrive(out_ref):
+            out_ref[...] = jnp.zeros_like(out_ref)
+
+        arrived = call(
+            arrive, "arrive", [], [sds((8, LANES))],
+            hold=[*token_parts, small[1], cot_in, small_own, wq[1], wp[1]],
+        )[0]
         wu, wd = ((values, over_wa(later(values, arrived))) for values in (w_up, w_down))
 
-        def unpack(own, oth):
-            values = jnp.concatenate([own[...], oth[...]], axis=1)
-            return mm(placement(images, False), values, 1, 0)
+        def unpack(parts, begin=0, count=None):
+            values = jnp.concatenate([part[...] for part in parts], axis=1)
+            return mm(placement(images, False, begin, count), values, 1, 0)
 
         def gain_row(refs, branch):
             return jnp.concatenate([ref[18 + branch : 19 + branch, :] for ref in refs], axis=1)
@@ -358,54 +383,45 @@
             oth_ref[:, :half] = values[:, half:]
 
         def add_parts(stream, part_a, part_b):
-            return stream[...] + part_a[...].astype(F32) + part_b[...].astype(F32)
-
-        def attention_part(window, section, normed, valid_rows, wq_a, wq_b, qkv_ref, probs_ref):
+            return stream + part_a[...].astype(F32) + part_b[...].astype(F32)
+
+        def attention_part(
+            window, section, normed, valid_rows, wq_a, wq_b, qkv_ref, probs_ref, first_image
+        ):
+            count = normed.shape[0] // PADDED
             packed = [
                 project_in(normed, wq_a[section, part], wq_b[section, part]).astype(BF16)
                 for part in range(3)
             ]
+            begin = first_image * PADDED
             for part in range(3):
-                qkv_ref[part] = packed[part]
-            wide = [part.astype(F32) for part in packed]
-            mixed = []
-            for image in range(images):
-                line = []
-                rows_at = slice(image * PADDED, (image + 1) * PADDED)
-                for tile in range(tiles):
-                    lanes_at = slice(tile * LANES, (tile + 1) * LANES)
-                    q, k, v = (part[rows_at, lanes_at] for part in wide)
-                    if window:
-                        probs, out = window_tile(q, k, v)
-                    else:
-                        probs, out = channel_tile(q, k, v, valid_rows[image])
-                    probs_ref[image * tiles + tile] = probs
-                    line.append(out)
-                mixed.append(jnp.concatenate(line, axis=1))
-            return jnp.concatenate(mixed, axis=0).astype(BF16)
+                qkv_ref[part, begin : begin + count * PADDED, :] = packed[part]
+            q, k, v = (cut_tiles(part.astype(F32), count, tiles) for part in packed)
+            if window:
+                probs, mixed = window_tiles(q, k, v)
+            else:
+                masks = [mask for mask in valid_rows for _ in range(tiles)]
+                probs, mixed = channel_tiles(q, k, v, masks)
+            for at, tile in enumerate(probs):
+                probs_ref[first_image * tiles + at] = tile
+            return paste_tiles(mixed, count, tiles)
 
         def attention_part_back(window, grad_mixed, mask_ref, qkv_ref, probs_ref, rear_refs):
-            wide = [qkv_ref[part].astype(F32) for part in range(3)]
-            grad = grad_mixed.astype(F32)
-            found = [[], [], []]
-            for image in range(images):
-                lines = [[], [], []]
-                for tile in range(tiles):
-                    rows_at = slice(image * PADDED, (image + 1) * PADDED)
-                    lanes_at = slice(tile * LANES, (tile + 1) * LANES)
-                    q, k, v = (part[rows_at, lanes_at] for part in wide)
-                    probs = probs_ref[image * tiles + tile]
-                    if window:
-                        parts = window_tile_back(q, k, v, probs, grad[rows_at, lanes_at])
-                    else:
-                        parts = channel_tile_back(
-                            q, k, v, probs, grad[rows_at, lanes_at], mask_ref[rows_at, :]
-                        )
-                    for line, part in zip(lines, parts):
-                        line.append(part)
-                for part in range(3):
-                    found[part].append(jnp.concatenate(lines[part], axis=1))
-            packed = [jnp.concatenate(part, axis=0).astype(BF16) for part in found]
+            q, k, v = (
+                cut_tiles(qkv_ref[part].astype(F32), images, tiles) for part in range(3)
+            )
+            grads = cut_tiles(grad_mixed.astype(F32), images, tiles)
+            probs = [probs_ref[at] for at in range(images * tiles)]
+            if window:
+                found = window_tiles_back(q, k, v, probs, grads)
+            else:
+                masks = [
+                    mask_ref[image * PADDED : (image + 1) * PADDED, :]
+                    for image in range(images)
+                    for _ in range(tiles)
+                ]
+                found = channel_tiles_back(q, k, v, probs, grads, masks)
+            packed = [paste_tiles(part, images, tiles) for part in found]
             for part in range(3):
                 put_rear(rear_refs, half + part * heads_width, packed[part])
             return packed
@@ -414,10 +430,12 @@
             out_ref[:, :half] = mm(left, own_ref[section], 1, 0).astype(BF16)
             out_ref[:, half:] = mm(left, oth_ref[section], 1, 0).astype(BF16)
 
-        def conv_into(out_ref, values, small_refs, section, keep):
+        def conv_into(out_ref, rows_at, values, small_refs, section, keep):
             for col in range(0, width, LANES):
                 taps = tap_rows(small_refs, section, col, False)
-                out_ref[:, col : col + LANES] = conv_cols(values[:, col : col + LANES], taps, keep)
+                out_ref[rows_at, col : col + LANES] = conv_cols(
+                    values[:, col : col + LANES], taps, keep
+                )
 
         def conv_back_into(out_ref, sums_ref, sums_at, grads, values, small_refs, section, keep):
             for col in range(0, width, LANES):
@@ -433,10 +451,7 @@
         half_low = sds((rows, half), BF16)
         hid_low = sds((rows, hidden), BF16)
         qkv_low = sds((3, rows, heads_width), BF16)
-        fore_attn, fore_mlp = (
-            sds((rows, half + heads_width), BF16),
-            sds((rows, half + hidden), BF16),
-        )
+        fore_attn = sds((rows, half + heads_width), BF16)
         def cuts(total, count):
             tiles_all = total // LANES
             return [LANES * (-(-tiles_all * (at + 1) // count)) for at in range(count)]
@@ -454,72 +469,171 @@
                     yield ref, low - begin, high - begin, low - at
                 begin = end
 
-        def put_rear(refs, at, values):
+        def put_rear(refs, at, values, span=slice(None)):
             for ref, low, high, source in rear_ranges(refs, at, values.shape[1]):
-                ref[:, low:high] = values[:, source : source + high - low]
+                ref[span, low:high] = values[:, source : source + high - low]
 
         def get_rear(refs, at, size):
             parts = [ref[:, low:high] for ref, low, high, _ in rear_ranges(refs, at, size)]
             return parts[0] if len(parts) == 1 else jnp.concatenate(parts, axis=1)
 
         rear_width_attn, rear_width_mlp = half + 3 * heads_width, half + hidden
+        fore_mlp = sds((rows, rear_width_mlp), BF16)
         attn_flops = 2 * rows * (4 * width * heads_width)
         mlp_flops = 2 * rows * (2 * width * hidden)
 
-        def first_body(
-            tokens_a, tokens_b, small_a, small_b, wq_a, wq_b, wp_a, wp_b,
-            x_ref, s_ref, n_own, fore_ref, qkv_ref, probs_ref, part_ref, keep_a, keep_b,
-        ):
-            keep_a[...], keep_b[...] = small_a[...], small_b[...]
-            keep = column_mask(rows)
-            stream = unpack(tokens_a, tokens_b)
-            x_ref[...] = stream.astype(BF16)
-            conv_into(s_ref, stream, (small_a, small_b), 0, keep)
-            normed = to_normed(s_ref[...], (small_a, small_b), 0)
-            put_both(n_own, fore_ref, normed)
-            mixed = attention_part(True, 0, normed, None, wq_a, wq_b, qkv_ref, probs_ref)
-            fore_ref[:, half:] = mixed
-            mul_out(mixed, 0, wp_a, wp_b, part_ref)
-
-        (x0, s1, n0_own, fore0, qkv0, probs0, part0, *small) = call(
-            first_body, "attn_a",
-            [*token_parts, *small, *wq, *wp],
-            [full_low, full, half_low, fore_attn, qkv_low, window_probs, full_low]
-            + [sds((26, half))] * 2,
-            flops=attn_flops, hold=[cot_own],
-        )
-        far0 = over_ha(part0)
-        fore0 = (fore0, over_wa(fore0))
-        keep_a = [x0, n0_own, *fore0, qkv0, probs0, s1]
-
-        def mlp_body(
-            s_in, part_a, part_b, small_a, small_b, wu_a, wu_b, wd_a, wd_b,
-            s_ref, n_own, fore_ref, slope_ref, part_ref,
-        ):
-            s_ref[...] = add_parts(s_in, part_a, part_b)
-            normed = to_normed(s_ref[...], (small_a, small_b), 1)
-            put_both(n_own, fore_ref, normed)
-            pre = project_in(normed, wu_a[0], wu_b[0])
-            below, bell = gelu_parts(pre)
-            hid = (pre * below).astype(BF16)
-            fore_ref[:, half:] = hid
-            slope_ref[...] = below + pre * bell
-            mul_out(hid, 0, wd_a, wd_b, part_ref)
-
-        (s2, n1_own, fore1, slope1, part1) = call(
-            mlp_body, "mlp_b",
-            [s1, part0, far0, *small, *wu, *wd],
-            [full, half_low, fore_mlp, sds((rows, hidden)), full_low],
-            flops=mlp_flops, hold=[*keep_a, *wq, *wp, *cot_parts],
-        )
-        far1 = over_ha(part1)
-        fore1 = (fore1, over_wa(fore1))
-        keep_b = [s2, n1_own, *fore1, slope1]
+        split = (images + 1) // 2
+        chunks = [(0, split), (split, images)] if split < images else [(0, images)]
+        spans = [slice(begin * PADDED, end * PADDED) for begin, end in chunks]
+
+        def chunk_rows(span):
+            return span.stop - span.start
+
+        def part_shape(span):
+            return sds((chunk_rows(span), width), BF16)
+
+        def put_normed(own_ref, fore_refs, span, normed):
+            own_ref[span, :] = normed[:, :half]
+            put_rear(fore_refs, 0, normed[:, half:], span)
+
+        def first_body(chunk, span):
+            def body(
+                tokens_a, tokens_b, tokens_c, small_a, small_b, wq_a, wq_b, wp_a, wp_b,
+                x_ref, s_ref, n_own, fore_ref, qkv_ref, probs_ref, part_ref, *copies,
+            ):
+                if copies:
+                    copies[0][...], copies[1][...] = small_a[...], small_b[...]
+                keep = column_mask(chunk_rows(span))
+                stream = unpack((tokens_a, tokens_b, tokens_c), span.start, chunk_rows(span))
+                x_ref[span, :] = stream.astype(BF16)
+                conv_into(s_ref, span, stream, (small_a, small_b), 0, keep)
+                normed = to_normed(s_ref[span, :], (small_a, small_b), 0)
+                put_normed(n_own, [fore_ref], span, normed)
+                mixed = attention_part(
+                    True, 0, normed, None, wq_a, wq_b, qkv_ref, probs_ref, chunk[0]
+                )
+                fore_ref[span, half:] = mixed
+                mul_out(mixed, 0, wp_a, wp_b, part_ref)
+
+            return body
+
+        def carry_spans(upto):
+            def carry(old, new):
+                for chunk, span in zip(chunks[:upto], spans[:upto]):
+                    if old.shape[0] == rows:
+                        new[span, :] = old[span, :]
+                    elif old.shape[1] == rows:
+                        new[:, span, :] = old[:, span, :]
+                    else:
+                        per_image = old.shape[0] // images
+                        held = slice(chunk[0] * per_image, chunk[1] * per_image)
+                        new[held] = old[held]
+
+            return carry
+
+        def in_chunks(name, make_body, ins, shapes, hold, extra=(), between=None):
+            arrays, parts, fars, more = None, [], [], []
+            for at, (chunk, span) in enumerate(zip(chunks, spans)):
+                results = call(
+                    make_body(chunk, span), f"{name}{at}", ins(at),
+                    [*shapes, part_shape(span), *(extra if at == 0 else ())],
+                    hold=[*hold, *more, *parts],
+                    reuse=None if arrays is None else dict(enumerate(arrays)),
+                    carry=carry_spans(at),
+                )
+                arrays, part = results[: len(shapes)], results[len(shapes)]
+                more = more or results[len(shapes) + 1 :]
+                parts.append(part)
+                fars.append(over_ha(part))
+                if at == 0 and between is not None:
+                    between(arrays, more)
+            return arrays, parts, fars, more
+
+        small_in, cot_parts = small, []
+
+        def choose_cot(arrays, more):
+            own, *others = call(
+                choose, "choose_cot", [cotangent, cot_in], chosen,
+                hold=[*arrays, *more, *wq, *wp],
+            )
+            cot_parts.extend([own, *others])
+
+        (x0, s1, n0_own, fore0, qkv0, probs0), part0, far0, small = in_chunks(
+            "attn_a", first_body, lambda at: [*token_parts, *small_in, *wq, *wp],
+            [full_low, full, half_low, fore_attn, qkv_low, window_probs], [cot_in, arrived],
+            [sds((26, half))] * 2, choose_cot,
+        )
+        keep_a = [x0, n0_own, fore0, qkv0, probs0, s1]
+
+        def mlp_body(chunk, span):
+            def body(
+                s_in, part_a, part_b, small_a, small_b, wu_a, wu_b, wd_a, wd_b,
+                s_ref, n_own, slope_ref, *refs,
+            ):
+                *fore_refs, part_ref = refs
+                s_ref[span, :] = add_parts(s_in[span, :], part_a, part_b)
+                normed = to_normed(s_ref[span, :], (small_a, small_b), 1)
+                put_normed(n_own, fore_refs, span, normed)
+                pre = project_in(normed, wu_a[0], wu_b[0])
+                below, bell = gelu_parts(pre)
+                hid = (pre * below).astype(BF16)
+                put_rear(fore_refs, half, hid, span)
+                slope_ref[span, :] = below + pre * bell
+                mul_out(hid, 0, wd_a, wd_b, part_ref)
+
+            return body
+
+        (s2, n1_own, slope1, *fore1), part1, far1, _ = in_chunks(
+            "mlp_b", mlp_body, lambda at: [s1, part0[at], far0[at], *small, *wu, *wd],
+            [full, half_low, sds((rows, hidden)), half_low, hid_low],
+            [*keep_a, *wq, *wp, *cot_parts],
+        )
+        n1_got = over_wa(fore1[0])
+        cot_parts[1:] = [over_wa(later(values, part1[0])) for values in cot_parts[1:]]
+        keep_b = [s2, n1_own, *fore1, slope1, n1_got]
         weights = [*wq, *wp, *wu, *wd]
 
-
-        def cot_body(cot_a, cot_b, wd_a, wd_b, g_own, g_oth, dhid_ref):
-            grad = unpack(cot_a, cot_b).astype(BF16)
+        def channel_body(chunk, span):
+            def body(
+                s_in, part_a, part_b, valid_ref, small_a, small_b, wq_a, wq_b, wp_a, wp_b,
+                s_before, s_ref, n_own, qkv_ref, probs_ref, mask_ref, *refs,
+            ):
+                *fore_refs, part_ref = refs
+                keep = column_mask(chunk_rows(span))
+                stream = jnp.where(keep, add_parts(s_in[span, :], part_a, part_b), 0.0)
+                s_before[span, :] = stream
+                conv_into(s_ref, span, stream, (small_a, small_b), 1, keep)
+                normed = to_normed(s_ref[span, :], (small_a, small_b), 2)
+                put_normed(n_own, fore_refs, span, normed)
+                one_image = placement(1, False).astype(F32)
+                valid_rows = []
+                for image in range(*chunk):
+                    line = jnp.where(
+                        here("wa") == 0,
+                        valid_ref[image : image + 1, :],
+                        valid_ref[images + image : images + image + 1, :],
+                    ).astype(F32)
+                    valid_rows.append(jnp.sum(one_image * line, axis=1, keepdims=True))
+                    mask_ref[image * PADDED : (image + 1) * PADDED, :] = valid_rows[-1]
+                mixed = attention_part(
+                    False, 1, normed, valid_rows, wq_a, wq_b, qkv_ref, probs_ref, chunk[0]
+                )
+                put_rear(fore_refs, half, mixed, span)
+                mul_out(mixed, 1, wp_a, wp_b, part_ref)
+
+            return body
+
+        (s3, s4, n2_own, qkv2, probs2, mask, *fore2), part2, far2, _ = in_chunks(
+            "attn_c", channel_body,
+            lambda at: [s2, part1[at], far1[at], valid, *small, *wq, *wp],
+            [full, full, half_low, qkv_low, channel_probs, sds((rows, 1)), half_low, half_low],
+            [*keep_a, *keep_b, *wu, *wd, *cot_parts],
+        )
+        fore2 = both_rear(fore2, False)
+        keep_c = [s3, s4, n2_own, *fore2[0], qkv2, probs2, mask]
+
+        def cot_body(cot_a, cot_b, cot_c, wd_a, wd_b, g_own, g_oth, dhid_ref):
+            grad = unpack((cot_a, cot_b, cot_c)).astype(BF16)
             put_both(g_own, g_oth, grad)
             dhid_ref[...] = project_back(grad, wd_a[1], wd_b[1]).astype(BF16)
 
@@ -527,70 +641,39 @@
             cot_body, "cot_d",
             [*cot_parts, *wd],
             [half_low, half_low, hid_low],
-            flops=mlp_flops // 2, hold=[*keep_a, *keep_b, *small, *wq, *wp, *wu],
-        )
-
-        def channel_body(
-            s_in, part_a, part_b, valid_ref, small_a, small_b,
-            wq_a, wq_b, wp_a, wp_b,
-            s_before, s_ref, n_own, fore_ref, qkv_ref, probs_ref, part_ref, mask_ref,
-        ):
-            keep = column_mask(rows)
-            s_before[...] = jnp.where(keep, add_parts(s_in, part_a, part_b), 0.0)
-            conv_into(s_ref, s_before, (small_a, small_b), 1, keep)
-            normed = to_normed(s_ref[...], (small_a, small_b), 2)
-            put_both(n_own, fore_ref, normed)
-            one_image = placement(1, False).astype(F32)
-            valid_rows = []
-            for image in range(images):
-                line = jnp.where(
-                    here("wa") == 0,
-                    valid_ref[image : image + 1, :],
-                    valid_ref[images + image : images + image + 1, :],
-                ).astype(F32)
-                valid_rows.append(jnp.sum(one_image * line, axis=1, keepdims=True))
-                mask_ref[image * PADDED : (image + 1) * PADDED, :] = valid_rows[image]
-            mixed = attention_part(False, 1, normed, valid_rows, wq_a, wq_b, qkv_ref, probs_ref)
-            fore_ref[:, half:] = mixed
-            mul_out(mixed, 1, wp_a, wp_b, part_ref)
-
-        (s3, s4, n2_own, fore2, qkv2, probs2, part2, mask) = call(
-            channel_body, "attn_c",
-            [s2, part1, far1, valid, *small, *wq, *wp],
-            [full, full, half_low, fore_attn, qkv_low, channel_probs, full_low,
-             sds((rows, 1))],
-            flops=attn_flops,
-            hold=[*keep_a, *keep_b, *wu, *wd, g3_own, g3_oth, dhid3],
-        )
-        far2 = over_ha(part2)
-        fore2 = (fore2, over_wa(fore2))
-        keep_c = [s3, s4, n2_own, *fore2, qkv2, probs2, mask]
-
-        def last_body(
-            s_in, part_a, part_b, small_a, small_b, dhid_ref, g_oth, wu_a, wu_b,
-            s_ref, n_own, fore_ref, part_ref, *rear_refs,
-        ):
-            s_ref[...] = add_parts(s_in, part_a, part_b)
-            normed = to_normed(s_ref[...], (small_a, small_b), 3)
-            put_both(n_own, fore_ref, normed)
-            pre = project_in(normed, wu_a[1], wu_b[1])
-            below, bell = gelu_parts(pre)
-            fore_ref[:, half:] = (pre * below).astype(BF16)
-            dpre = (dhid_ref[...].astype(F32) * (below + pre * bell)).astype(BF16)
-            put_rear(rear_refs, 0, g_oth[...])
-            put_rear(rear_refs, half, dpre)
-            part_ref[:, :half] = mm(dpre, wu_a[1], 1, 1).astype(BF16)
-            part_ref[:, half:] = mm(dpre, wu_b[1], 1, 1).astype(BF16)
-
-        (s5, n3_own, fore3, back3, *rear3) = call(
-            last_body, "mlp_d",
-            [s4, part2, far2, *small, dhid3, g3_oth, *wu],
-            [full, half_low, fore_mlp, full_low, *rear_shapes(rear_width_mlp, 2)],
-            flops=mlp_flops,
-            hold=[*keep_a, *keep_b, *keep_c, g3_own, g3_oth, *wq, *wp, *wd],
-        )
-        far_back3 = over_ha(back3)
-        fore3 = (fore3, over_wa(fore3))
+            flops=mlp_flops // 2,
+            hold=[*keep_a, *keep_b, *keep_c, *small, *wq, *wp, *wu],
+        )
+
+
+        def last_body(chunk, span):
+            def body(
+                s_in, part_a, part_b, small_a, small_b, dhid_ref, g_oth, wu_a, wu_b,
+                s_ref, n_own, fore_ref, *refs,
+            ):
+                *rear_refs, part_ref = refs
+                s_ref[span, :] = add_parts(s_in[span, :], part_a, part_b)
+                normed = to_normed(s_ref[span, :], (small_a, small_b), 3)
+                put_normed(n_own, [fore_ref], span, normed)
+                pre = project_in(normed, wu_a[1], wu_b[1])
+                below, bell = gelu_parts(pre)
+                fore_ref[span, half:] = (pre * below).astype(BF16)
+                dpre = (dhid_ref[span, :].astype(F32) * (below + pre * bell)).astype(BF16)
+                put_rear(rear_refs, 0, g_oth[span, :], span)
+                put_rear(rear_refs, half, dpre, span)
+                part_ref[:, :half] = mm(dpre, wu_a[1], 1, 1).astype(BF16)
+                part_ref[:, half:] = mm(dpre, wu_b[1], 1, 1).astype(BF16)
+
+            return body
+
+        (s5, n3_own, fore3, *rear3), back3, far_back3, _ = in_chunks(
+            "mlp_d", last_body,
+            lambda at: [s4, part2[at], far2[at], *small, dhid3, g3_oth, *wu],
+            [full, half_low, fore_mlp, *rear_shapes(rear_width_mlp, 2)],
+            [*keep_a, *keep_b, *keep_c, *fore2[1], g3_own, *wq, *wp, *wd],
+        )
+        fore3 = both_rear([fore3], False)
+        keep_c += fore2[1]
         rear3 = both_rear(rear3, False)
 
         up_rows, down_rows = hidden // n_dev, half // n_dev
@@ -634,17 +717,18 @@
                             part = values["down"][rows_at, columns]
                         else:
                             part = values[piece][rows_at]
-                        scratch[chunk, at : at + size, :] = part
+                        scratch[chunk, at : at + size, :] = part.astype(BF16)
                     at += size
 
         def both_sums(n_own, g_own, fore_a, fore_b, rear_a, rear_b):
             def left(at, size):
                 return mm(get_rear(rear_a, at, size), n_own[...], 0, 0) + mm(
-                    get_rear(rear_b, at, size), fore_b[:, :half], 0, 0
+                    get_rear(rear_b, at, size), get_rear(fore_b, 0, half), 0, 0
                 )
 
-            right = mm(g_own[...], fore_a[:, half:], 0, 0) + mm(
-                get_rear(rear_b, 0, half), fore_b[:, half:], 0, 0
+            size = sum(ref.shape[1] for ref in fore_a) - half
+            right = mm(g_own[...], get_rear(fore_a, half, size), 0, 0) + mm(
+                get_rear(rear_b, 0, half), get_rear(fore_b, half, size), 0, 0
             )
             return left, right
 
@@ -664,7 +748,11 @@
             outs = [sds((cut * s.chunk_rows, half), BF16) for s in streams for _ in range(2)]
             count = len(rear[0])
 
-            def body(n_ref, g_ref, fore_a, fore_b, *refs):
+            pieces = len(fore[0])
+
+            def body(n_ref, g_ref, *refs):
+                fore_a, fore_b, refs = refs[:pieces], refs[pieces : 2 * pieces], refs[2 * pieces :]
+                fore_b = [other_core(ref) for ref in fore_b]
                 rear_a, rear_b, refs = refs[:count], refs[count : 2 * count], refs[2 * count :]
                 rear_b = [other_core(ref) for ref in rear_b]
                 out_refs, scratches = refs[: len(outs)], refs[len(outs) :]
@@ -673,13 +761,13 @@
                 for at, (stream, scratch) in enumerate(zip(streams, scratches)):
                     size = stream.chunk_rows
                     for place in range(n_dev):
-                        chunk = scratch[chunk_at(place, stream.which)].astype(BF16)
+                        chunk = scratch[chunk_at(place, stream.which)]
                         to = (place % cut) * size
                         out_refs[2 * at + place // cut][to : to + size, :] = chunk
 
             results = call(
-                body, name, [n_own, g_own, *fore, *rear[0], *rear[1]], outs, hold=hold,
-                scratch=[pltpu.VMEM((n_dev, s.chunk_rows, half), F32) for s in streams],
+                body, name, [n_own, g_own, *fore[0], *fore[1], *rear[0], *rear[1]], outs, hold=hold,
+                scratch=[pltpu.VMEM((n_dev, s.chunk_rows, half), BF16) for s in streams],
             )
             for at, stream in enumerate(streams):
                 stream.kept, stream.sent = results[2 * at], results[2 * at + 1]
@@ -701,7 +789,12 @@
                 stream.at : stream.at + stream.chunk_rows, :
             ].astype(F32)
 
-        def slot(name, fresh=(), moving=(), ending=(), sums=None, hold=()):
+        def slot(*args, **kwargs):
+            prepare_slot(*args, **kwargs)()
+
+        def prepare_slot(
+            name, fresh=(), moving=(), ending=(), sums=None, hold=(), spare=None
+        ):
             ins, outs, sizes = [], [], {}
             plan_fresh, plan_moving = [], []
 
@@ -740,6 +833,8 @@
                 sums_room = room(sums[3], 2 * sum_rows)
                 sums_out = len(outs)
                 outs.append(sds((sum_rows, half)))
+            if spare is not None:
+                spare_at = room(spare, 16)
             bits_used = sorted(sizes)
             buffer_at = {bit: len(outs) + at for at, bit in enumerate(bits_used)}
             outs += [sds((sizes[bit], half), BF16) for bit in bits_used]
@@ -757,6 +852,8 @@
                         kept[size:, :].astype(F32)
                         + got[got_row + size : got_row + 2 * size, :].astype(F32)
                     ).astype(BF16)
+                if spare is not None:
+                    out_refs[buffer_at[spare]][spare_at:, :] = jnp.zeros((16, half), BF16)
                 for stream, kept_in, got_in, out_at in plan_ending:
                     out_refs[out_at][...] = last_sum(stream, in_refs[kept_in], in_refs[got_in])
                 if sums is not None:
@@ -770,16 +867,22 @@
                     buffer[sums_room + sum_rows : sums_room + 2 * sum_rows, :] = low
 
             results = call(body, name, ins, outs, hold=hold)
-            received = {bit: over_dev(results[buffer_at[bit]], bit) for bit in bits_used}
-            for stream, (_, _, bit, at) in zip(fresh, plan_fresh):
-                stream.got, stream.at, stream.step = received[bit], at, 1
             for stream, _, _, out_at in plan_ending:
                 stream.final = results[out_at]
-            for stream, (_, _, _, _, kept_at, bit, at) in zip(moving, plan_moving):
-                stream.kept, stream.got, stream.at = results[kept_at], received[bit], at
-                stream.step += 1
-            if sums is not None:
-                sums[:3] = results[sums_out], received[sums[3]], sums_room
+            for stream, (_, _, _, _, kept_at, _, _) in zip(moving, plan_moving):
+                stream.kept = results[kept_at]
+
+            def depart():
+                received = {bit: over_dev(results[buffer_at[bit]], bit) for bit in bits_used}
+                for stream, (_, _, bit, at) in zip(fresh, plan_fresh):
+                    stream.got, stream.at, stream.step = received[bit], at, 1
+                for stream, (_, _, _, _, _, bit, at) in zip(moving, plan_moving):
+                    stream.got, stream.at = received[bit], at
+                    stream.step += 1
+                if sums is not None:
+                    sums[:3] = results[sums_out], received[sums[3]], sums_room
+
+            return depart
 
         def ship(total, kept, sent):
             packed = mm(placement(images, True), total.astype(BF16), 1, 0).astype(BF16)
@@ -824,10 +927,15 @@
             ]
 
         def channel_back_body(
-            g_in_own, g_in_oth, part_a, part_b, s_in, small_a, small_b, mask_ref, qkv_ref,
-            probs_ref, wp_a, wp_b, wq_a, wq_b,
-            g_ref, g_own, part_ref, sums_ref, *rear_refs,
+            g_in_own, g_in_oth, s_in, small_a, small_b, mask_ref, qkv_ref, probs_ref,
+            wp_a, wp_b, wq_a, wq_b, *refs,
         ):
+            count = len(chunks)
+            part_a, part_b = (
+                jnp.concatenate([ref[...] for ref in refs[at : at + count]], axis=0)
+                for at in (0, count)
+            )
+            g_ref, g_own, part_ref, sums_ref, *rear_refs = refs[2 * count :]
             grad = jnp.concatenate([g_in_own[...], g_in_oth[...]], axis=1).astype(F32)
             gain = gain_row((small_a, small_b), 3)
             grad = add_norm_back(grad, part_a, part_b, s_in[...], gain, sums_ref)
@@ -843,16 +951,22 @@
             part_ref[:, :half] = own.astype(BF16)
             part_ref[:, half:] = oth.astype(BF16)
 
-        late = [fore3[0], *wd, s5]
+        late = [*fore3[0], *wd, s5]
         (g2, g2_own, back2, sums3, *rear2) = call(
             channel_back_body, "back_c",
-            [g3_own, g3_oth, back3, far_back3, s5, *small, mask, qkv2, probs2, *wp, *wq],
+            [g3_own, g3_oth, s5, *small, mask, qkv2, probs2, *wp, *wq, *back3, *far_back3],
             [full, half_low, full_low, sds((2, width)), *rear_shapes(rear_width_attn, 1)],
             flops=attn_flops,
-            hold=[*keep_a, *keep_b, s3, s4, n2_own, *fore2, *wu, *wd, fore3[0]],
+            hold=[*keep_a, *keep_b, s3, s4, n2_own, *fore2[0], *fore2[1], *wu, *wd, *fore3[0]],
         )
         far_back2 = over_ha(back2)
         rear2 = both_rear(rear2, False)
+        hid_got, fore0_got = (
+            lax.all_gather(later(values, g2), "wa") for values in (fore1[1], fore0)
+        )
+        fore1, fore0 = (fore1, [n1_got, hid_got]), ([fore0], [fore0_got])
+        keep_a.append(fore0_got)
+        keep_b.append(hid_got)
         streams_c = attn_streams(SPLIT_C, 2)
         kept_c = [*keep_a, *keep_b, s3, s4, *small, *weights, g2, *late, sums3]
         make("wgrad_c", write_attn, streams_c, n2_own, g2_own, fore2, rear2, kept_c)
@@ -882,7 +996,7 @@
             [g2, back2, far_back2, s4, s3, *small, slope1, *wd, *wu],
             [full, half_low, full_low, sds((11, width)), *rear_shapes(rear_width_mlp, 2)],
             flops=mlp_flops,
-            hold=[*keep_a, s2, n1_own, *fore1, *wq, *wp, fore3[0], s5, sums3],
+            hold=[*keep_a, s2, n1_own, *fore1[0], *fore1[1], *wq, *wp, *fore3[0], s5, sums3],
         )
         far_back1 = over_ha(back1)
         rear1 = both_rear(rear1)
@@ -910,18 +1024,22 @@
             window_back_body, "back_a",
             [g1, back1, far_back1, s2, *small, qkv0, probs0, *wp],
             [full, half_low, sds((2, width)), *rear_shapes(rear_width_attn, 1)],
-            flops=attn_flops, hold=[x0, n0_own, *fore0, s1, *wq, *late, sums3, sums2],
-        )
-        rear0 = both_rear(rear0)
+            flops=attn_flops, hold=[x0, n0_own, *fore0[0], *fore0[1], s1, *wq, *late, sums3, sums2],
+        )
+        every = [*streams_d, *streams_c]
+        depart = prepare_slot(
+            "slot_cd", moving=every, spare=2,
+            hold=[x0, n0_own, *fore0[0], *fore0[1], s1, *small, *wq, *late, sums1, sums2, sums3,
+                  g0, g0_own, *rear0],
+        )
+        rear0 = both_rear(later(rear0, streams_d[0].kept))
 
         keep_0 = [g0, s1, x0, *small, *wq, sums1, sums2, sums3, *rear0[0]]
         streams_a = attn_streams(SPLIT_A, 0)
         make("wgrad_a", write_attn, streams_a, n0_own, g0_own, fore0, rear0, [*late, *keep_0])
         every = [*streams_d, *streams_c, *streams_b, *streams_a]
-        slot(
-            "slot_a", fresh=streams_a, moving=[*streams_d, *streams_c],
-            hold=[*late, *keep_0],
-        )
+        send_first(streams_a)
+        depart()
 
         sums_at = -(-rows_in // 16) * 16
         sums_half = sds((sum_rows, half))
@@ -992,7 +1110,7 @@
         sums = [sums_ha, None, 0, left_bits.pop(0)]
         slot("sums_x", sums=sums, hold=late)
         out_kept, out_sent = call(
-            out_body, "out_d", [s5, fore3[0], *wd], shipped, flops=mlp_flops // 2
+            out_body, "out_d", [s5, *fore3[0], *wd], shipped, flops=mlp_flops // 2
         )
         out_both = lax.all_gather(out_sent, "wa")
 
@@ -1006,14 +1124,10 @@
         while left_bits or any(stream.step < bits for stream in every):
             turn += 1
             arrived = [s for s in every if s.step == bits and s.final is None]
-            first = [*streams_b, streams_c[1]] if turn > 1 else streams_b
+            first = [*streams_b, *streams_c] if turn > 1 else streams_b
             slot(f"slot_b{turn}", moving=[s for s in first if s.step < bits])
-            second = [s for s in every if s.step < bits and s not in (*streams_b, streams_c[1])]
-            slot(
-                f"slot_ac{turn}", moving=second, ending=arrived, sums=hop() if turn == 1 else None
-            )
-            if turn > 1 and left_bits:
-                slot(f"sums_{turn}", sums=hop())
+            second = [s for s in [*streams_d, *streams_a] if s.step < bits]
+            slot(f"slot_a{turn}", moving=second, ending=arrived, sums=hop())
             if turn == 1:
                 out_stay, out_go = call(
                     lambda kept, both, *refs: fold(kept, other_core(both), *refs),

time: 153 us -> 138 us (0.902)
  waiting for transfers between devices: 63 us -> 47.9 us
  blocking collectives: 11.3 us -> 16 us
  starting transfers between devices: 40 us -> 36.3 us
    ppermute x10 -> x14, waiting for transfers between devices: 35.8 us -> 18.2 us  [over_ha(): return lax.ppermute(values, 'ha', swap)]
    ppermute x16, starting transfers between devices: 22.9 us -> 16.6 us  [over_dev(): lax.ppermute(values, 'dev', [(i, i ^ 1 << bit) for i in range(n_dev)])]
    all_gather x0 -> x2, blocking collectives: none -> 4.69 us  [on_device(): lax.all_gather(later(values, g2), 'wa')]
    ppermute x16, waiting for transfers between devices: 24 us -> 27.3 us  [over_dev(): lax.ppermute(values, 'dev', [(i, i ^ 1 << bit) for i in range(n_dev)])]
    ppermute x10 -> x14, starting transfers between devices: 14.6 us -> 16.1 us  [over_ha(): return lax.ppermute(values, 'ha', swap)]
    ppermute x14 -> x16, starting transfers between devices: 2.47 us -> 3.64 us  [over_wa(): return lax.ppermute(values, 'wa', swap)]
    pallas_call x29 -> x34, Pallas kernels: 33.7 us -> 32.9 us  [kernel_call(): pl.pallas_call(wrapped, in_specs=[pl.BlockSpec(memory_space=pltpu.VMEM)]...]
    ppermute x14 -> x16, waiting for transfers between devices: 3.25 us -> 2.41 us  [over_wa(): return lax.ppermute(values, 'wa', swap)]
  transfers between devices with their start and end apart: 40 -> 46, of which waited for: 20 -> 22; matrix products, arithmetic and copies ran while one was open for 0% -> 0% of each run, Pallas kernels for 17% -> 22%
where the time goes in v6:
time: 138 us
  waiting for transfers between devices  47.9 us (35%)
  starting transfers between devices  36.3 us (26%)
  Pallas kernels  32.9 us (24%)
  blocking collectives  16 us (12%)
  local copies, waits for them, and re-layouts  3.6 us (3%)
    pallas_call x34, Pallas kernels, kernel_call(): pl.pallas_call(wrapped, in_specs=[pl.BlockSpec(memory_space=pltpu.VMEM)]...  32.9 us
    ppermute x16, waiting for transfers between devices, over_dev(): lax.ppermute(values, 'dev', [(i, i ^ 1 << bit) for i in range(n_dev)])  27.3 us
    ppermute x14, waiting for transfers between devices, over_ha(): return lax.ppermute(values, 'ha', swap)  18.2 us
    ppermute x16, starting transfers between devices, over_dev(): lax.ppermute(values, 'dev', [(i, i ^ 1 << bit) for i in range(n_dev)])  16.6 us
    ppermute x14, starting transfers between devices, over_ha(): return lax.ppermute(values, 'ha', swap)  16.1 us
    all_gather x3, blocking collectives, both_rear(): return (pieces, [lax.all_gather(piece, 'wa') for piece in pieces])  7.26 us
    all_gather x2, blocking collectives, on_device(): lax.all_gather(later(values, g2), 'wa')  4.69 us
    ppermute x16, starting transfers between devices, over_wa(): return lax.ppermute(values, 'wa', swap)  3.64 us
  transfers between devices with their start and end apart: 46, of which 22 were waited for; matrix products, arithmetic and copies ran while one was open for 0% of the time, Pallas kernels for 22%

profile of v6, /device:TPU:0, one launch (start us, length us, event | category | flops | bytes accessed | tf_op | source)
XLA Modules:
  0.0 137.7 jit_solution(17171911218617612787)
XLA Ops:
  1.2 2.9 %collective-permute-start = (bf16[147,384]{1,0:T(8,128)(2,1)}, bf16[147,384]{1,0:T(8,128)(2,1)S(1)}, u32[]{:S(2)}, u32[]{:S(2)}) collective-permute-start(bf16[147,384]{1,0:T(8,128)(2,1)} %refs_0_.2), channel_id=1, source_target_pairs={{0,2},{2,0},{1,3},{3,1},{4,6},{6,4},{5,7},{7,5},{8,10},{10,8},{9,1... | collective-permute-start | bytes 338696 | tf_op jit(solution)/shard_map/ppermute | solution.py:265
  13.2 2.1 %collective-permute-start.10 = (bf16[112,768]{1,0:T(8,128)(2,1)S(1)}, bf16[112,768]{1,0:T(8,128)(2,1)S(1)}, u32[]{:S(2)}, u32[]{:S(2)}) collective-permute-start(bf16[112,768]{1,0:T(8,128)(2,1)S(1)} %get-tuple-element.207.refs_13_.refs_1_), channel_id=1, source_target_pairs={{0,2},{2,0},{1,3},{3,1},{4,6},{6,4},{5,7},{7,5},{8,10},{10,8},{9,1... | collective-permute-start | bytes 516104 | tf_op jit(solution)/shard_map/ppermute | solution.py:265
  16.9 3.4 %collective-permute-done.10.refs_2_ = bf16[112,768]{1,0:T(8,128)(2,1)S(1)} collective-permute-done((bf16[112,768]{1,0:T(8,128)(2,1)S(1)}, bf16[112,768]{1,0:T(8,128)(2,1)S(1)}, u32[]{:S(2)}, u32[]{:S(2)}) %collective-permute-start.10) | collective-permute-done | bytes 172064 | tf_op jit(solution)/shard_map/ppermute | solution.py:265
  21.7 2.1 %collective-permute-start.15 = (bf16[112,768]{1,0:T(8,128)(2,1)S(1)}, bf16[112,768]{1,0:T(8,128)(2,1)S(1)}, u32[]{:S(2)}, u32[]{:S(2)}) collective-permute-start(bf16[112,768]{1,0:T(8,128)(2,1)S(1)} %get-tuple-element.229.refs_22_.refs_1_), channel_id=1, source_target_pairs={{0,2},{2,0},{1,3},{3,1},{4,6},{6,4},{5,7},{7,5},{8,10},{10,8},{9,1... | collective-permute-start | bytes 516104 | tf_op jit(solution)/shard_map/ppermute | solution.py:265
  28.9 2.5 %collective-permute-start.19 = (bf16[112,768]{1,0:T(8,128)(2,1)S(1)}, bf16[112,768]{1,0:T(8,128)(2,1)S(1)}, u32[]{:S(2)}, u32[]{:S(2)}) collective-permute-start(bf16[112,768]{1,0:T(8,128)(2,1)S(1)} %get-tuple-element.245.refs_29_.refs_1_), channel_id=1, source_target_pairs={{0,2},{2,0},{1,3},{3,1},{4,6},{6,4},{5,7},{7,5},{8,10},{10,8},{9,1... | collective-permute-start | bytes 516104 | tf_op jit(solution)/shard_map/ppermute | solution.py:265
  42.5 2.1 %wgrad_d.1 = (bf16[768,384]{1,0:T(8,128)(2,1)S(1)}, bf16[768,384]{1,0:T(8,128)(2,1)S(1)}, bf16[768,384]{1,0:T(8,128)(2,1)S(1)}, bf16[768,384]{1,0:T(8,128)(2,1)S(1)}, f32[8,128]{1,0:T(8,128)S(1)}) custom-call(bf16[168,384]{1,0:T(8,128)(2,1)S(1)} %get-tuple-element.279.refs_0_, bf16[168,384]{1,0:T(8,128)(2,1)S(1)} %get-tuple-element.267.refs_31_.refs_1_.refs_0_, ...), custom_call_target="tpu_custom_call" | custom-call | tf_op jit(solution)/shard_map/wgrad_d/pallas_call | solution.py:55
  48.6 2.1 %back_c.1 = (f32[168,768]{1,0:T(8,128)S(1)}, bf16[168,384]{1,0:T(8,128)(2,1)S(1)}, bf16[168,768]{1,0:T(8,128)(2,1)S(1)}, f32[2,768]{1,0:T(2,128)S(1)}, bf16[168,...) custom-call(bf16[168,384]{1,0:T(8,128)(2,1)S(1)} %get-tuple-element.267.refs_31_.refs_1_.refs_0_, ...), custom_call_target="tpu_custom_call" | custom-call | tf_op jit(solution)/shard_map/back_c/pallas_call | solution.py:55
  52.2 2.2 %all-gather = bf16[336,768]{1,0:T(8,128)(2,1)S(1)} all-gather(bf16[168,768]{1,0:T(8,128)(2,1)S(1)} %get-tuple-element.286.refs_11_.refs_12_.refs_7_.refs_10_.refs_18_.refs_8_.refs_14_.refs_2_), channel_id=2, replica_groups=mesh['dev'=8,'ha'=2,'wa'=2] {'wa'}, dimensions={0}, use_global_device_ids=true | all-gather | bytes 774144 | tf_op jit(solution)/shard_map/all_gather | solution.py:965
  54.3 2.5 %all-gather.1 = bf16[336,1536]{1,0:T(8,128)(2,1)S(1)} all-gather(bf16[168,1536]{1,0:T(8,128)(2,1)S(1)} %get-tuple-element.287.refs_19_.refs_14_.refs_18_.refs_17_.refs_25_.refs_16_.refs_22_.refs_3_), channel_id=3, replica_groups=mesh['dev'=8,'ha'=2,'wa'=2] {'wa'}, dimensions={0}, use_global_device_ids=true | all-gather | bytes 1548288 | tf_op jit(solution)/shard_map/all_gather | solution.py:965
  63.5 2.8 %back_b.1 = (f32[168,768]{1,0:T(8,128)S(1)}, bf16[168,384]{1,0:T(8,128)(2,1)S(1)}, bf16[168,768]{1,0:T(8,128)(2,1)S(1)}, f32[11,768]{1,0:T(8,128)S(1)}, bf16[168...) custom-call(f32[168,768]{1,0:T(8,128)S(1)} %get-tuple-element.284.refs_34_.refs_32_.refs_0_, ...), custom_call_target="tpu_custom_call" | custom-call | tf_op jit(solution)/shard_map/back_b/pallas_call | solution.py:55
  67.9 2.2 %all-gather.3 = bf16[336,896]{1,0:T(8,128)(2,1)S(1)} all-gather(bf16[168,896]{1,0:T(8,128)(2,1)S(1)} %get-tuple-element.305.refs_7_), channel_id=5, replica_groups=mesh['dev'=8,'ha'=2,'wa'=2] {'wa'}, dimensions={0}, use_global_device_ids=true | all-gather | bytes 903168 | tf_op jit(solution)/shard_map/all_gather | solution.py:375
  70.1 2.3 %all-gather.2 = bf16[336,1024]{1,0:T(8,128)(2,1)S(1)} all-gather(bf16[168,1024]{1,0:T(8,128)(2,1)S(1)} %get-tuple-element.304.refs_6_), channel_id=4, replica_groups=mesh['dev'=8,'ha'=2,'wa'=2] {'wa'}, dimensions={0}, use_global_device_ids=true | all-gather | bytes 1032192 | tf_op jit(solution)/shard_map/all_gather | solution.py:375
  78.4 2.7 %collective-permute-start.34 = (bf16[784,384]{1,0:T(8,128)(2,1)S(1)}, bf16[784,384]{1,0:T(8,128)(2,1)S(1)}, u32[]{:S(2)}, u32[]{:S(2)}) collective-permute-start(bf16[784,384]{1,0:T(8,128)(2,1)S(1)} %get-tuple-element.338), channel_id=1, source_target_pairs={{0,16},{4,20},{8,24},{12,28},{16,0},{20,4},{24,8},{28,12},{1,17},{... | collective-permute-start | bytes 1806344 | tf_op jit(solution)/shard_map/ppermute | solution.py:271
  81.1 2.8 %all-gather.4 = bf16[336,1536]{1,0:T(8,128)(2,1)S(1)} all-gather(bf16[168,1536]{1,0:T(8,128)(2,1)S(1)} %get-tuple-element.320.refs_24_.refs_4_.refs_20_.refs_10_), channel_id=6, replica_groups=mesh['dev'=8,'ha'=2,'wa'=2] {'wa'}, dimensions={0}, use_global_device_ids=true | all-gather | bytes 1548288 | tf_op jit(solution)/shard_map/all_gather | solution.py:375
  85.6 2.0 %back_0.1 = (bf16[147,384]{1,0:T(8,128)(2,1)S(1)}, bf16[224,384]{1,0:T(8,128)(2,1)S(1)}, f32[32,384]{1,0:T(8,128)S(1)}, f32[8,128]{1,0:T(8,128)S(1)}) custom-call(f32[168,768]{1,0:T(8,128)S(1)} %get-tuple-element.308.refs_22_.refs_10_.refs_0_, f32[168,768]{1,0:T(8,128)S(1)} %get-tuple-element.216.refs_0_.refs_14_.refs_15_.refs_10_.refs_13_.refs_21_.refs_11_.refs_17_.refs_1_, ...), custom_call_target="tpu_custom_call" | custom-call | tf_op jit(solution)/shard_map/back_0/pallas_call | solution.py:55
  87.6 2.1 %all-gather.5 = bf16[448,384]{1,0:T(8,128)(2,1)S(1)} all-gather(bf16[224,384]{1,0:T(8,128)(2,1)S(1)} %get-tuple-element.324), channel_id=7, replica_groups=mesh['dev'=8,'ha'=2,'wa'=2] {'wa'}, dimensions={0}, use_global_device_ids=true | all-gather | bytes 516096 | tf_op jit(solution)/shard_map/all_gather | solution.py:1095
  90.3 5.9 %collective-permute-done.32.refs_1_ = bf16[224,384]{1,0:T(8,128)(2,1)S(1)} collective-permute-done((bf16[224,384]{1,0:T(8,128)(2,1)S(1)}, bf16[224,384]{1,0:T(8,128)(2,1)S(1)}, u32[]{:S(2)}, u32[]{:S(2)}) %collective-permute-start.32) | collective-permute-done | bytes 172064 | tf_op jit(solution)/shard_map/ppermute | solution.py:265
  99.3 3.1 %collective-permute-done.37.refs_3_ = bf16[768,384]{1,0:T(8,128)(2,1)S(1)} collective-permute-done((bf16[768,384]{1,0:T(8,128)(2,1)S(1)}, bf16[768,384]{1,0:T(8,128)(2,1)S(1)}, u32[]{:S(2)}, u32[]{:S(2)}) %collective-permute-start.37) | collective-permute-done | bytes 589856 | tf_op jit(solution)/shard_map/ppermute | solution.py:271
  103.5 4.0 %collective-permute-done.34.refs_3_.refs_5_ = bf16[784,384]{1,0:T(8,128)(2,1)S(1)} collective-permute-done((bf16[784,384]{1,0:T(8,128)(2,1)S(1)}, bf16[784,384]{1,0:T(8,128)(2,1)S(1)}, u32[]{:S(2)}, u32[]{:S(2)}) %collective-permute-start.34) | collective-permute-done | bytes 602144 | tf_op jit(solution)/shard_map/ppermute | solution.py:271
  110.5 2.9 %collective-permute-done.40.refs_1_ = bf16[384,384]{1,0:T(8,128)(2,1)S(1)} collective-permute-done((bf16[384,384]{1,0:T(8,128)(2,1)S(1)}, bf16[384,384]{1,0:T(8,128)(2,1)S(1)}, u32[]{:S(2)}, u32[]{:S(2)}) %collective-permute-start.40) | collective-permute-done | bytes 294944 | tf_op jit(solution)/shard_map/ppermute | solution.py:271
  114.9 9.0 %collective-permute-done.39.refs_1_ = bf16[448,384]{1,0:T(8,128)(2,1)S(1)} collective-permute-done((bf16[448,384]{1,0:T(8,128)(2,1)S(1)}, bf16[448,384]{1,0:T(8,128)(2,1)S(1)}, u32[]{:S(2)}, u32[]{:S(2)}) %collective-permute-start.39) | collective-permute-done | bytes 344096 | tf_op jit(solution)/shard_map/ppermute | solution.py:271
  126.5 2.5 %collective-permute-done.38.refs_1_ = bf16[147,384]{1,0:T(8,128)(2,1)S(1)} collective-permute-done((bf16[147,384]{1,0:T(8,128)(2,1)S(1)}, bf16[147,384]{1,0:T(8,128)(2,1)S(1)}, u32[]{:S(2)}, u32[]{:S(2)}) %collective-permute-start.38) | collective-permute-done | bytes 112928 | tf_op jit(solution)/shard_map/ppermute | solution.py:265
  130.4 3.6 %collective-permute-done.43.refs_5_.refs_7_ = bf16[384,384]{1,0:T(8,128)(2,1)S(1)} collective-permute-done((bf16[384,384]{1,0:T(8,128)(2,1)S(1)}, bf16[384,384]{1,0:T(8,128)(2,1)S(1)}, u32[]{:S(2)}, u32[]{:S(2)}) %collective-permute-start.43) | collective-permute-done | bytes 294944 | tf_op jit(solution)/shard_map/ppermute | solution.py:271
  134.0 2.4 %collective-permute-done.42.refs_1_.refs_3_ = bf16[256,384]{1,0:T(8,128)(2,1)S(1)} collective-permute-done((bf16[256,384]{1,0:T(8,128)(2,1)S(1)}, bf16[256,384]{1,0:T(8,128)(2,1)S(1)}, u32[]{:S(2)}, u32[]{:S(2)}) %collective-permute-start.42) | collective-permute-done | bytes 196640 | tf_op jit(solution)/shard_map/ppermute | solution.py:271
  (129 shorter events, 64.4 us)
Async XLA Ops:
  0.6 7.7 %collective-permute-start.1 = (bf16[2,3,384,384]{3,2,1,0:T(8,128)(2,1)}, bf16[2,3,384,384]{3,2,1,0:T(8,128)(2,1)S(1)}, u32[]{:S(2)}, u32[]{:S(2)}) collective-permute-start(bf16[2,3,384,384]{3,2,1,0:T(8,128)(2,1)} %bitcast.14), channel_id=1, source_target_pairs={{0,1},{1,0},{2,3},{3,2},{4,5},{5,4},{6,7},{7,6},{8,9},{9,8},{10,11... | collective-permute-start | bytes 5308424 | tf_op jit(solution)/shard_map/ppermute | solution.py:268
  1.2 7.2 %collective-permute-start.2 = (bf16[2,384,384]{2,1,0:T(8,128)(2,1)}, bf16[2,384,384]{2,1,0:T(8,128)(2,1)S(1)}, u32[]{:S(2)}, u32[]{:S(2)}) collective-permute-start(bf16[2,384,384]{2,1,0:T(8,128)(2,1)} %refs_8_.9), channel_id=1, source_target_pairs={{0,1},{1,0},{2,3},{3,2},{4,5},{5,4},{6,7},{7,6},{8,9},{9,8},{10,11... | collective-permute-start | bytes 1769480 | tf_op jit(solution)/shard_map/ppermute | solution.py:268
  1.2 7.1 %collective-permute-start = (bf16[147,384]{1,0:T(8,128)(2,1)}, bf16[147,384]{1,0:T(8,128)(2,1)S(1)}, u32[]{:S(2)}, u32[]{:S(2)}) collective-permute-start(bf16[147,384]{1,0:T(8,128)(2,1)} %refs_0_.2), channel_id=1, source_target_pairs={{0,2},{2,0},{1,3},{3,1},{4,6},{6,4},{5,7},{7,5},{8,10},{10,8},{9,1... | collective-permute-start | bytes 338696 | tf_op jit(solution)/shard_map/ppermute | solution.py:265
  10.8 9.6 %collective-permute-start.8 = (bf16[2,384,1536]{2,1,0:T(8,128)(2,1)S(1)}, bf16[2,384,1536]{2,1,0:T(8,128)(2,1)S(1)}, u32[]{:S(2)}, u32[]{:S(2)}) collective-permute-start(bf16[2,384,1536]{2,1,0:T(8,128)(2,1)S(1)} %copy-done.2), channel_id=1, source_target_pairs={{0,1},{1,0},{2,3},{3,2},{4,5},{5,4},{6,7},{7,6},{8,9},{9,8},{10,11... | collective-permute-start | bytes 7077896 | tf_op jit(solution)/shard_map/ppermute | solution.py:268
  10.8 9.6 %collective-permute-start.9 = (bf16[2,1536,384]{2,1,0:T(8,128)(2,1)S(1)}, bf16[2,1536,384]{2,1,0:T(8,128)(2,1)S(1)}, u32[]{:S(2)}, u32[]{:S(2)}) collective-permute-start(bf16[2,1536,384]{2,1,0:T(8,128)(2,1)S(1)} %copy-done), channel_id=1, source_target_pairs={{0,1},{1,0},{2,3},{3,2},{4,5},{5,4},{6,7},{7,6},{8,9},{9,8},{10,11... | collective-permute-start | bytes 7077896 | tf_op jit(solution)/shard_map/ppermute | solution.py:268
  13.2 7.2 %collective-permute-start.10 = (bf16[112,768]{1,0:T(8,128)(2,1)S(1)}, bf16[112,768]{1,0:T(8,128)(2,1)S(1)}, u32[]{:S(2)}, u32[]{:S(2)}) collective-permute-start(bf16[112,768]{1,0:T(8,128)(2,1)S(1)} %get-tuple-element.207.refs_13_.refs_1_), channel_id=1, source_target_pairs={{0,2},{2,0},{1,3},{3,1},{4,6},{6,4},{5,7},{7,5},{8,10},{10,8},{9,1... | collective-permute-start | bytes 516104 | tf_op jit(solution)/shard_map/ppermute | solution.py:265
  16.9 7.0 %collective-permute-start.7 = (bf16[56,768]{1,0:T(8,128)(2,1)S(1)}, bf16[56,768]{1,0:T(8,128)(2,1)S(1)}, u32[]{:S(2)}, u32[]{:S(2)}) collective-permute-start(bf16[56,768]{1,0:T(8,128)(2,1)S(1)} %get-tuple-element.217.refs_1_), channel_id=1, source_target_pairs={{0,2},{2,0},{1,3},{3,1},{4,6},{6,4},{5,7},{7,5},{8,10},{10,8},{9,1... | collective-permute-start | bytes 258056 | tf_op jit(solution)/shard_map/ppermute | solution.py:265
  40.0 8.6 %collective-permute-start.20 = (bf16[112,768]{1,0:T(8,128)(2,1)S(1)}, bf16[112,768]{1,0:T(8,128)(2,1)S(1)}, u32[]{:S(2)}, u32[]{:S(2)}) collective-permute-start(bf16[112,768]{1,0:T(8,128)(2,1)S(1)} %get-tuple-element.269.refs_38_.refs_12_), channel_id=1, source_target_pairs={{0,2},{2,0},{1,3},{3,1},{4,6},{6,4},{5,7},{7,5},{8,10},{10,8},{9,1... | collective-permute-start | bytes 516104 | tf_op jit(solution)/shard_map/ppermute | solution.py:265
  41.3 7.3 %collective-permute-start.21 = (bf16[56,768]{1,0:T(8,128)(2,1)S(1)}, bf16[56,768]{1,0:T(8,128)(2,1)S(1)}, u32[]{:S(2)}, u32[]{:S(2)}) collective-permute-start(bf16[56,768]{1,0:T(8,128)(2,1)S(1)} %get-tuple-element.278.refs_13_), channel_id=1, source_target_pairs={{0,2},{2,0},{1,3},{3,1},{4,6},{6,4},{5,7},{7,5},{8,10},{10,8},{9,1... | collective-permute-start | bytes 258056 | tf_op jit(solution)/shard_map/ppermute | solution.py:265
  44.5 15.4 %collective-permute-start.27 = (bf16[768,384]{1,0:T(8,128)(2,1)S(1)}, bf16[768,384]{1,0:T(8,128)(2,1)S(1)}, u32[]{:S(2)}, u32[]{:S(2)}) collective-permute-start(bf16[768,384]{1,0:T(8,128)(2,1)S(1)} %get-tuple-element.295), channel_id=1, source_target_pairs={{0,4},{4,0},{8,12},{12,8},{16,20},{20,16},{24,28},{28,24},{1,5},{5... | collective-permute-start | bytes 1769480 | tf_op jit(solution)/shard_map/ppermute | solution.py:271
  45.9 15.1 %collective-permute-start.28 = (bf16[768,384]{1,0:T(8,128)(2,1)S(1)}, bf16[768,384]{1,0:T(8,128)(2,1)S(1)}, u32[]{:S(2)}, u32[]{:S(2)}) collective-permute-start(bf16[768,384]{1,0:T(8,128)(2,1)S(1)} %get-tuple-element.297), channel_id=1, source_target_pairs={{0,8},{4,12},{8,0},{12,4},{16,24},{20,28},{24,16},{28,20},{1,9},{5... | collective-permute-start | bytes 1769480 | tf_op jit(solution)/shard_map/ppermute | solution.py:271
  50.8 8.6 %collective-permute-start.25 = (bf16[168,768]{1,0:T(8,128)(2,1)S(1)}, bf16[168,768]{1,0:T(8,128)(2,1)S(1)}, u32[]{:S(2)}, u32[]{:S(2)}) collective-permute-start(bf16[168,768]{1,0:T(8,128)(2,1)S(1)} %get-tuple-element.285.refs_38_.refs_1_), channel_id=1, source_target_pairs={{0,2},{2,0},{1,3},{3,1},{4,6},{6,4},{5,7},{7,5},{8,10},{10,8},{9,1... | collective-permute-start | bytes 774152 | tf_op jit(solution)/shard_map/ppermute | solution.py:265
  61.4 16.7 %collective-permute-start.30 = (bf16[768,384]{1,0:T(8,128)(2,1)S(1)}, bf16[768,384]{1,0:T(8,128)(2,1)S(1)}, u32[]{:S(2)}, u32[]{:S(2)}) collective-permute-start(bf16[768,384]{1,0:T(8,128)(2,1)S(1)} %get-tuple-element.312), channel_id=1, source_target_pairs={{0,8},{4,12},{8,0},{12,4},{16,24},{20,28},{24,16},{28,20},{1,9},{5... | collective-permute-start | bytes 1769480 | tf_op jit(solution)/shard_map/ppermute | solution.py:271
  63.0 15.1 %collective-permute-start.31 = (bf16[768,384]{1,0:T(8,128)(2,1)S(1)}, bf16[768,384]{1,0:T(8,128)(2,1)S(1)}, u32[]{:S(2)}, u32[]{:S(2)}) collective-permute-start(bf16[768,384]{1,0:T(8,128)(2,1)S(1)} %get-tuple-element.314), channel_id=1, source_target_pairs={{0,4},{4,0},{8,12},{12,8},{16,20},{20,16},{24,28},{28,24},{1,5},{5... | collective-permute-start | bytes 1769480 | tf_op jit(solution)/shard_map/ppermute | solution.py:271
  66.3 10.0 %collective-permute-start.29 = (bf16[168,768]{1,0:T(8,128)(2,1)S(1)}, bf16[168,768]{1,0:T(8,128)(2,1)S(1)}, u32[]{:S(2)}, u32[]{:S(2)}) collective-permute-start(bf16[168,768]{1,0:T(8,128)(2,1)S(1)} %get-tuple-element.301.refs_1_), channel_id=1, source_target_pairs={{0,2},{2,0},{1,3},{3,1},{4,6},{6,4},{5,7},{7,5},{8,10},{10,8},{9,1... | collective-permute-start | bytes 774152 | tf_op jit(solution)/shard_map/ppermute | solution.py:265
  74.3 25.0 %collective-permute-start.36 = (bf16[768,384]{1,0:T(8,128)(2,1)S(1)}, bf16[768,384]{1,0:T(8,128)(2,1)S(1)}, u32[]{:S(2)}, u32[]{:S(2)}) collective-permute-start(bf16[768,384]{1,0:T(8,128)(2,1)S(1)} %get-tuple-element.343), channel_id=1, source_target_pairs={{0,4},{4,0},{8,12},{12,8},{16,20},{20,16},{24,28},{28,24},{1,5},{5... | collective-permute-start | bytes 1769480 | tf_op jit(solution)/shard_map/ppermute | solution.py:271
  75.9 26.6 %collective-permute-start.37 = (bf16[768,384]{1,0:T(8,128)(2,1)S(1)}, bf16[768,384]{1,0:T(8,128)(2,1)S(1)}, u32[]{:S(2)}, u32[]{:S(2)}) collective-permute-start(bf16[768,384]{1,0:T(8,128)(2,1)S(1)} %get-tuple-element.345), channel_id=1, source_target_pairs={{0,8},{4,12},{8,0},{12,4},{16,24},{20,28},{24,16},{28,20},{1,9},{5... | collective-permute-start | bytes 1769480 | tf_op jit(solution)/shard_map/ppermute | solution.py:271
  78.4 29.1 %collective-permute-start.34 = (bf16[784,384]{1,0:T(8,128)(2,1)S(1)}, bf16[784,384]{1,0:T(8,128)(2,1)S(1)}, u32[]{:S(2)}, u32[]{:S(2)}) collective-permute-start(bf16[784,384]{1,0:T(8,128)(2,1)S(1)} %get-tuple-element.338), channel_id=1, source_target_pairs={{0,16},{4,20},{8,24},{12,28},{16,0},{20,4},{24,8},{28,12},{1,17},{... | collective-permute-start | bytes 1806344 | tf_op jit(solution)/shard_map/ppermute | solution.py:271
  84.9 18.5 %collective-permute-start.33 = (bf16[768,384]{1,0:T(8,128)(2,1)S(1)}, bf16[768,384]{1,0:T(8,128)(2,1)S(1)}, u32[]{:S(2)}, u32[]{:S(2)}) collective-permute-start(bf16[768,384]{1,0:T(8,128)(2,1)S(1)} %get-tuple-element.337), channel_id=1, source_target_pairs={{0,4},{4,0},{8,12},{12,8},{16,20},{20,16},{24,28},{28,24},{1,5},{5... | collective-permute-start | bytes 1769480 | tf_op jit(solution)/shard_map/ppermute | solution.py:271
  102.8 10.7 %collective-permute-start.40 = (bf16[384,384]{1,0:T(8,128)(2,1)S(1)}, bf16[384,384]{1,0:T(8,128)(2,1)S(1)}, u32[]{:S(2)}, u32[]{:S(2)}) collective-permute-start(bf16[384,384]{1,0:T(8,128)(2,1)S(1)} %get-tuple-element.355), channel_id=1, source_target_pairs={{0,8},{4,12},{8,0},{12,4},{16,24},{20,28},{24,16},{28,20},{1,9},{5... | collective-permute-start | bytes 884744 | tf_op jit(solution)/shard_map/ppermute | solution.py:271
  102.8 10.6 %collective-permute-start.41 = (bf16[384,384]{1,0:T(8,128)(2,1)S(1)}, bf16[384,384]{1,0:T(8,128)(2,1)S(1)}, u32[]{:S(2)}, u32[]{:S(2)}) collective-permute-start(bf16[384,384]{1,0:T(8,128)(2,1)S(1)} %get-tuple-element.357), channel_id=1, source_target_pairs={{0,4},{4,0},{8,12},{12,8},{16,20},{20,16},{24,28},{28,24},{1,5},{5... | collective-permute-start | bytes 884744 | tf_op jit(solution)/shard_map/ppermute | solution.py:271
  107.7 16.2 %collective-permute-start.39 = (bf16[448,384]{1,0:T(8,128)(2,1)S(1)}, bf16[448,384]{1,0:T(8,128)(2,1)S(1)}, u32[]{:S(2)}, u32[]{:S(2)}) collective-permute-start(bf16[448,384]{1,0:T(8,128)(2,1)S(1)} %get-tuple-element.352), channel_id=1, source_target_pairs={{0,8},{4,12},{8,0},{12,4},{16,24},{20,28},{24,16},{28,20},{1,9},{5... | collective-permute-start | bytes 1032200 | tf_op jit(solution)/shard_map/ppermute | solution.py:271
  113.7 20.4 %collective-permute-start.43 = (bf16[384,384]{1,0:T(8,128)(2,1)S(1)}, bf16[384,384]{1,0:T(8,128)(2,1)S(1)}, u32[]{:S(2)}, u32[]{:S(2)}) collective-permute-start(bf16[384,384]{1,0:T(8,128)(2,1)S(1)} %get-tuple-element.369), channel_id=1, source_target_pairs={{0,16},{4,20},{8,24},{12,28},{16,0},{20,4},{24,8},{28,12},{1,17},{... | collective-permute-start | bytes 884744 | tf_op jit(solution)/shard_map/ppermute | solution.py:271
  124.0 12.4 %collective-permute-start.42 = (bf16[256,384]{1,0:T(8,128)(2,1)S(1)}, bf16[256,384]{1,0:T(8,128)(2,1)S(1)}, u32[]{:S(2)}, u32[]{:S(2)}) collective-permute-start(bf16[256,384]{1,0:T(8,128)(2,1)S(1)} %get-tuple-element.366), channel_id=1, source_target_pairs={{0,16},{4,20},{8,24},{12,28},{16,0},{20,4},{24,8},{28,12},{1,17},{... | collective-permute-start | bytes 589832 | tf_op jit(solution)/shard_map/ppermute | solution.py:271
  (32 other events, 104.2 us)

commit v7 on v6

--- a/solution.py
+++ b/solution.py
@@ -531,20 +531,23 @@
 
             return carry
 
-        def in_chunks(name, make_body, ins, shapes, hold, extra=(), between=None):
+        def in_chunks(
+            name, make_body, ins, shapes, hold, extra=(), between=None, alone=True
+        ):
             arrays, parts, fars, more = None, [], [], []
             for at, (chunk, span) in enumerate(zip(chunks, spans)):
                 results = call(
                     make_body(chunk, span), f"{name}{at}", ins(at),
-                    [*shapes, part_shape(span), *(extra if at == 0 else ())],
+                    [*shapes, *([part_shape(span)] if alone else ()), *(extra if at == 0 else ())],
                     hold=[*hold, *more, *parts],
                     reuse=None if arrays is None else dict(enumerate(arrays)),
                     carry=carry_spans(at),
                 )
-                arrays, part = results[: len(shapes)], results[len(shapes)]
-                more = more or results[len(shapes) + 1 :]
-                parts.append(part)
-                fars.append(over_ha(part))
+                arrays, rest = results[: len(shapes)], results[len(shapes) :]
+                if alone:
+                    parts.append(rest[0])
+                    fars.append(over_ha(rest[0]))
+                more = more or rest[1:]
                 if at == 0 and between is not None:
                     between(arrays, more)
             return arrays, parts, fars, more
@@ -651,7 +654,7 @@
                 s_in, part_a, part_b, small_a, small_b, dhid_ref, g_oth, wu_a, wu_b,
                 s_ref, n_own, fore_ref, *refs,
             ):
-                *rear_refs, part_ref = refs
+                share, *rear_refs = refs
                 s_ref[span, :] = add_parts(s_in[span, :], part_a, part_b)
                 normed = to_normed(s_ref[span, :], (small_a, small_b), 3)
                 put_normed(n_own, [fore_ref], span, normed)
@@ -661,17 +664,18 @@
                 dpre = (dhid_ref[span, :].astype(F32) * (below + pre * bell)).astype(BF16)
                 put_rear(rear_refs, 0, g_oth[span, :], span)
                 put_rear(rear_refs, half, dpre, span)
-                part_ref[:, :half] = mm(dpre, wu_a[1], 1, 1).astype(BF16)
-                part_ref[:, half:] = mm(dpre, wu_b[1], 1, 1).astype(BF16)
+                share[span, :half] = mm(dpre, wu_a[1], 1, 1).astype(BF16)
+                share[span, half:] = mm(dpre, wu_b[1], 1, 1).astype(BF16)
 
             return body
 
-        (s5, n3_own, fore3, *rear3), back3, far_back3, _ = in_chunks(
+        (s5, n3_own, fore3, back3, *rear3), _, _, _ = in_chunks(
             "mlp_d", last_body,
             lambda at: [s4, part2[at], far2[at], *small, dhid3, g3_oth, *wu],
-            [full, half_low, fore_mlp, *rear_shapes(rear_width_mlp, 2)],
-            [*keep_a, *keep_b, *keep_c, *fore2[1], g3_own, *wq, *wp, *wd],
-        )
+            [full, half_low, fore_mlp, full_low, *rear_shapes(rear_width_mlp, 2)],
+            [*keep_a, *keep_b, *keep_c, *fore2[1], g3_own, *wq, *wp, *wd], alone=False,
+        )
+        far_back3 = over_ha(back3)
         fore3 = both_rear([fore3], False)
         keep_c += fore2[1]
         rear3 = both_rear(rear3, False)
@@ -776,13 +780,8 @@
             for stream in streams:
                 stream.got, stream.step = over_dev(stream.sent, stream.bits[0]), 1
 
-        def split_low(values):
-            high = values.astype(BF16)
-            return high, (values - high.astype(F32)).astype(BF16)
-
-        def joined(ref, at):
-            high = ref[at : at + sum_rows, :].astype(F32)
-            return high + ref[at + sum_rows : at + 2 * sum_rows, :].astype(F32)
+        def sums_in(ref, at):
+            return ref[at : at + sum_rows, :].astype(F32)
 
         def last_sum(stream, kept, got):
             return kept[...].astype(F32) + got[
@@ -830,11 +829,11 @@
             if sums is not None:
                 total_at = place_of(sums[0])
                 sums_got = None if sums[1] is None else place_of(sums[1])
-                sums_room = room(sums[3], 2 * sum_rows)
+                sums_room = room(sums[3], sum_rows)
                 sums_out = len(outs)
                 outs.append(sds((sum_rows, half)))
             if spare is not None:
-                spare_at = room(spare, 16)
+                spare_at = room(*spare)
             bits_used = sorted(sizes)
             buffer_at = {bit: len(outs) + at for at, bit in enumerate(bits_used)}
             outs += [sds((sizes[bit], half), BF16) for bit in bits_used]
@@ -853,18 +852,16 @@
                         + got[got_row + size : got_row + 2 * size, :].astype(F32)
                     ).astype(BF16)
                 if spare is not None:
-                    out_refs[buffer_at[spare]][spare_at:, :] = jnp.zeros((16, half), BF16)
+                    out_refs[buffer_at[spare[0]]][spare_at:, :] = jnp.zeros((spare[1], half), BF16)
                 for stream, kept_in, got_in, out_at in plan_ending:
                     out_refs[out_at][...] = last_sum(stream, in_refs[kept_in], in_refs[got_in])
                 if sums is not None:
                     total = in_refs[total_at][...]
                     if sums_got is not None:
-                        total = total + joined(in_refs[sums_got], sums[2])
-                    high, low = split_low(total)
-                    out_refs[sums_out][...] = high.astype(F32) + low.astype(F32)
-                    buffer = out_refs[buffer_at[sums[3]]]
-                    buffer[sums_room : sums_room + sum_rows, :] = high
-                    buffer[sums_room + sum_rows : sums_room + 2 * sum_rows, :] = low
+                        total = total + sums_in(in_refs[sums_got], sums[2])
+                    low = total.astype(BF16)
+                    out_refs[sums_out][...] = low.astype(F32)
+                    out_refs[buffer_at[sums[3]]][sums_room : sums_room + sum_rows, :] = low
 
             results = call(body, name, ins, outs, hold=hold)
             for stream, _, _, out_at in plan_ending:
@@ -930,12 +927,7 @@
             g_in_own, g_in_oth, s_in, small_a, small_b, mask_ref, qkv_ref, probs_ref,
             wp_a, wp_b, wq_a, wq_b, *refs,
         ):
-            count = len(chunks)
-            part_a, part_b = (
-                jnp.concatenate([ref[...] for ref in refs[at : at + count]], axis=0)
-                for at in (0, count)
-            )
-            g_ref, g_own, part_ref, sums_ref, *rear_refs = refs[2 * count :]
+            part_a, part_b, g_ref, g_own, part_ref, sums_ref, *rear_refs = refs
             grad = jnp.concatenate([g_in_own[...], g_in_oth[...]], axis=1).astype(F32)
             gain = gain_row((small_a, small_b), 3)
             grad = add_norm_back(grad, part_a, part_b, s_in[...], gain, sums_ref)
@@ -954,7 +946,7 @@
         late = [*fore3[0], *wd, s5]
         (g2, g2_own, back2, sums3, *rear2) = call(
             channel_back_body, "back_c",
-            [g3_own, g3_oth, s5, *small, mask, qkv2, probs2, *wp, *wq, *back3, *far_back3],
+            [g3_own, g3_oth, s5, *small, mask, qkv2, probs2, *wp, *wq, back3, far_back3],
             [full, half_low, full_low, sds((2, width)), *rear_shapes(rear_width_attn, 1)],
             flops=attn_flops,
             hold=[*keep_a, *keep_b, s3, s4, n2_own, *fore2[0], *fore2[1], *wu, *wd, *fore3[0]],
@@ -1028,7 +1020,7 @@
         )
         every = [*streams_d, *streams_c]
         depart = prepare_slot(
-            "slot_cd", moving=every, spare=2,
+            "slot_cd", moving=every, spare=(2, 16),
             hold=[x0, n0_own, *fore0[0], *fore0[1], s1, *small, *wq, *late, sums1, sums2, sums3,
                   g0, g0_own, *rear0],
         )
@@ -1043,12 +1035,10 @@
 
         sums_at = -(-rows_in // 16) * 16
         sums_half = sds((sum_rows, half))
-        with_sums = sds((sums_at + 2 * sum_rows, half), BF16)
+        with_sums = sds((sums_at + sum_rows, half), BF16)
 
         def put_sums(ref, total):
-            high, low = split_low(total)
-            ref[sums_at : sums_at + sum_rows, :] = high
-            ref[sums_at + sum_rows :, :] = low
+            ref[sums_at:, :] = total.astype(BF16)
 
         def first_back_body(
             g_in, s_in, x_ref, small_a, small_b, wq_a, wq_b, sums_one, sums_two, sums_three, *refs
@@ -1086,9 +1076,9 @@
         def fold_tokens(kept, both, sums_a, stay, go, sums_ref):
             received = other_core(both)
             fold(kept, received, stay, go)
-            total = sums_a[...] + joined(received, sums_at)
+            total = sums_a[...] + sums_in(received, sums_at)
             put_sums(go, total)
-            sums_ref[...] = joined(go, sums_at)
+            sums_ref[...] = sums_in(go, sums_at)
 
         token_stay, token_go, sums_chip = call(
             fold_tokens, "fold_tokens",
@@ -1099,7 +1089,7 @@
 
         def join_tokens(stay, received, sums_chip, out_ref, sums_ref):
             join(stay, received, out_ref)
-            sums_ref[...] = sums_chip[...] + joined(received, sums_at)
+            sums_ref[...] = sums_chip[...] + sums_in(received, sums_at)
 
         owned = sds((rows_in, half))
         grad_tokens, sums_ha = call(
@@ -1108,7 +1098,7 @@
         )
         left_bits = list(range(bits))
         sums = [sums_ha, None, 0, left_bits.pop(0)]
-        slot("sums_x", sums=sums, hold=late)
+        slot("sums_x", sums=sums, spare=(0, 96), hold=late)
         out_kept, out_sent = call(
             out_body, "out_d", [s5, *fore3[0], *wd], shipped, flops=mlp_flops // 2
         )
@@ -1124,10 +1114,11 @@
         while left_bits or any(stream.step < bits for stream in every):
             turn += 1
             arrived = [s for s in every if s.step == bits and s.final is None]
-            first = [*streams_b, *streams_c] if turn > 1 else streams_b
-            slot(f"slot_b{turn}", moving=[s for s in first if s.step < bits])
+            slot(f"slot_b{turn}", moving=[s for s in streams_b if s.step < bits])
             second = [s for s in [*streams_d, *streams_a] if s.step < bits]
             slot(f"slot_a{turn}", moving=second, ending=arrived, sums=hop())
+            if turn > 1:
+                slot(f"slot_c{turn}", moving=[s for s in streams_c if s.step < bits])
             if turn == 1:
                 out_stay, out_go = call(
                     lambda kept, both, *refs: fold(kept, other_core(both), *refs),
@@ -1139,7 +1130,7 @@
         def finish_body(*refs):
             (up, down, qkv, proj, taps_ref, gain_ref, shift_ref) = refs[-7:]
             at = iter(refs)
-            total = next(at)[...] + joined(next(at), sums[2])
+            total = next(at)[...] + sums_in(next(at), sums[2])
             for branch, row in enumerate((0, 11, 13, 24)):
                 gain_ref[branch : branch + 1, :] = total[row : row + 1]
                 shift_ref[branch : branch + 1, :] = total[row + 1 : row + 2]

time: 138 us -> 137 us (level)
    ppermute x14 -> x13, starting transfers between devices: 16.1 us -> 15.3 us  [over_ha(): return lax.ppermute(values, 'ha', swap)]
    ppermute x14 -> x13, waiting for transfers between devices: 18.2 us -> 17.5 us  [over_ha(): return lax.ppermute(values, 'ha', swap)]
    pallas_call x34 -> x35, Pallas kernels: 32.9 us -> 32.9 us  [kernel_call(): pl.pallas_call(wrapped, in_specs=[pl.BlockSpec(memory_space=pltpu.VMEM)]...]
  transfers between devices with their start and end apart: 46 -> 45, of which waited for: 22 -> 22; matrix products, arithmetic and copies ran while one was open for 0% -> 0% of each run, Pallas kernels for 22% -> 22%
where the time goes in v7:
time: 137 us
  waiting for transfers between devices  47.6 us (35%)
  starting transfers between devices  35.6 us (26%)
  Pallas kernels  32.9 us (24%)
  blocking collectives  15.9 us (12%)
  local copies, waits for them, and re-layouts  3.6 us (3%)
    pallas_call x35, Pallas kernels, kernel_call(): pl.pallas_call(wrapped, in_specs=[pl.BlockSpec(memory_space=pltpu.VMEM)]...  32.9 us
    ppermute x16, waiting for transfers between devices, over_dev(): lax.ppermute(values, 'dev', [(i, i ^ 1 << bit) for i in range(n_dev)])  26.9 us
    ppermute x13, waiting for transfers between devices, over_ha(): return lax.ppermute(values, 'ha', swap)  17.5 us
    ppermute x16, starting transfers between devices, over_dev(): lax.ppermute(values, 'dev', [(i, i ^ 1 << bit) for i in range(n_dev)])  16.6 us
    ppermute x13, starting transfers between devices, over_ha(): return lax.ppermute(values, 'ha', swap)  15.3 us
    all_gather x3, blocking collectives, both_rear(): return (pieces, [lax.all_gather(piece, 'wa') for piece in pieces])  7.26 us
    all_gather x2, blocking collectives, on_device(): lax.all_gather(later(values, g2), 'wa')  4.69 us
    ppermute x16, starting transfers between devices, over_wa(): return lax.ppermute(values, 'wa', swap)  3.64 us
  transfers between devices with their start and end apart: 45, of which 22 were waited for; matrix products, arithmetic and copies ran while one was open for 0% of the time, Pallas kernels for 22%

profile of v7, /device:TPU:0, one launch (start us, length us, event | category | flops | bytes accessed | tf_op | source)
XLA Modules:
  0.0 136.6 jit_solution(15126886731164857844)
XLA Ops:
  1.2 2.9 %collective-permute-start = (bf16[147,384]{1,0:T(8,128)(2,1)}, bf16[147,384]{1,0:T(8,128)(2,1)S(1)}, u32[]{:S(2)}, u32[]{:S(2)}) collective-permute-start(bf16[147,384]{1,0:T(8,128)(2,1)} %refs_0_.2), channel_id=1, source_target_pairs={{0,2},{2,0},{1,3},{3,1},{4,6},{6,4},{5,7},{7,5},{8,10},{10,8},{9,1... | collective-permute-start | bytes 338696 | tf_op jit(solution)/shard_map/ppermute | solution.py:265
  13.2 2.1 %collective-permute-start.10 = (bf16[112,768]{1,0:T(8,128)(2,1)S(1)}, bf16[112,768]{1,0:T(8,128)(2,1)S(1)}, u32[]{:S(2)}, u32[]{:S(2)}) collective-permute-start(bf16[112,768]{1,0:T(8,128)(2,1)S(1)} %get-tuple-element.208.refs_13_.refs_1_), channel_id=1, source_target_pairs={{0,2},{2,0},{1,3},{3,1},{4,6},{6,4},{5,7},{7,5},{8,10},{10,8},{9,1... | collective-permute-start | bytes 516104 | tf_op jit(solution)/shard_map/ppermute | solution.py:265
  16.9 3.4 %collective-permute-done.10.refs_2_ = bf16[112,768]{1,0:T(8,128)(2,1)S(1)} collective-permute-done((bf16[112,768]{1,0:T(8,128)(2,1)S(1)}, bf16[112,768]{1,0:T(8,128)(2,1)S(1)}, u32[]{:S(2)}, u32[]{:S(2)}) %collective-permute-start.10) | collective-permute-done | bytes 172064 | tf_op jit(solution)/shard_map/ppermute | solution.py:265
  21.7 2.1 %collective-permute-start.15 = (bf16[112,768]{1,0:T(8,128)(2,1)S(1)}, bf16[112,768]{1,0:T(8,128)(2,1)S(1)}, u32[]{:S(2)}, u32[]{:S(2)}) collective-permute-start(bf16[112,768]{1,0:T(8,128)(2,1)S(1)} %get-tuple-element.230.refs_22_.refs_1_), channel_id=1, source_target_pairs={{0,2},{2,0},{1,3},{3,1},{4,6},{6,4},{5,7},{7,5},{8,10},{10,8},{9,1... | collective-permute-start | bytes 516104 | tf_op jit(solution)/shard_map/ppermute | solution.py:265
  28.9 2.5 %collective-permute-start.19 = (bf16[112,768]{1,0:T(8,128)(2,1)S(1)}, bf16[112,768]{1,0:T(8,128)(2,1)S(1)}, u32[]{:S(2)}, u32[]{:S(2)}) collective-permute-start(bf16[112,768]{1,0:T(8,128)(2,1)S(1)} %get-tuple-element.246.refs_29_.refs_1_), channel_id=1, source_target_pairs={{0,2},{2,0},{1,3},{3,1},{4,6},{6,4},{5,7},{7,5},{8,10},{10,8},{9,1... | collective-permute-start | bytes 516104 | tf_op jit(solution)/shard_map/ppermute | solution.py:265
  42.5 2.1 %wgrad_d.1 = (bf16[768,384]{1,0:T(8,128)(2,1)S(1)}, bf16[768,384]{1,0:T(8,128)(2,1)S(1)}, bf16[768,384]{1,0:T(8,128)(2,1)S(1)}, bf16[768,384]{1,0:T(8,128)(2,1)S(1)}, f32[8,128]{1,0:T(8,128)S(1)}) custom-call(bf16[168,384]{1,0:T(8,128)(2,1)S(1)} %get-tuple-element.280.refs_0_, bf16[168,384]{1,0:T(8,128)(2,1)S(1)} %get-tuple-element.268.refs_31_.refs_1_.refs_0_, ...), custom_call_target="tpu_custom_call" | custom-call | tf_op jit(solution)/shard_map/wgrad_d/pallas_call | solution.py:55
  48.6 2.1 %back_c.1 = (f32[168,768]{1,0:T(8,128)S(1)}, bf16[168,384]{1,0:T(8,128)(2,1)S(1)}, bf16[168,768]{1,0:T(8,128)(2,1)S(1)}, f32[2,768]{1,0:T(2,128)S(1)}, bf16[168,...) custom-call(bf16[168,384]{1,0:T(8,128)(2,1)S(1)} %get-tuple-element.268.refs_31_.refs_1_.refs_0_, ...), custom_call_target="tpu_custom_call" | custom-call | tf_op jit(solution)/shard_map/back_c/pallas_call | solution.py:55
  52.1 2.2 %all-gather = bf16[336,768]{1,0:T(8,128)(2,1)S(1)} all-gather(bf16[168,768]{1,0:T(8,128)(2,1)S(1)} %get-tuple-element.287.refs_11_.refs_12_.refs_7_.refs_10_.refs_16_.refs_8_.refs_14_.refs_2_), channel_id=2, replica_groups=mesh['dev'=8,'ha'=2,'wa'=2] {'wa'}, dimensions={0}, use_global_device_ids=true | all-gather | bytes 774144 | tf_op jit(solution)/shard_map/all_gather | solution.py:957
  54.3 2.5 %all-gather.1 = bf16[336,1536]{1,0:T(8,128)(2,1)S(1)} all-gather(bf16[168,1536]{1,0:T(8,128)(2,1)S(1)} %get-tuple-element.288.refs_19_.refs_14_.refs_18_.refs_17_.refs_23_.refs_16_.refs_22_.refs_3_), channel_id=3, replica_groups=mesh['dev'=8,'ha'=2,'wa'=2] {'wa'}, dimensions={0}, use_global_device_ids=true | all-gather | bytes 1548288 | tf_op jit(solution)/shard_map/all_gather | solution.py:957
  63.6 2.8 %back_b.1 = (f32[168,768]{1,0:T(8,128)S(1)}, bf16[168,384]{1,0:T(8,128)(2,1)S(1)}, bf16[168,768]{1,0:T(8,128)(2,1)S(1)}, f32[11,768]{1,0:T(8,128)S(1)}, bf16[168...) custom-call(f32[168,768]{1,0:T(8,128)S(1)} %get-tuple-element.285.refs_34_.refs_32_.refs_0_, ...), custom_call_target="tpu_custom_call" | custom-call | tf_op jit(solution)/shard_map/back_b/pallas_call | solution.py:55
  67.9 2.2 %all-gather.3 = bf16[336,896]{1,0:T(8,128)(2,1)S(1)} all-gather(bf16[168,896]{1,0:T(8,128)(2,1)S(1)} %get-tuple-element.306.refs_7_), channel_id=5, replica_groups=mesh['dev'=8,'ha'=2,'wa'=2] {'wa'}, dimensions={0}, use_global_device_ids=true | all-gather | bytes 903168 | tf_op jit(solution)/shard_map/all_gather | solution.py:375
  70.2 2.3 %all-gather.2 = bf16[336,1024]{1,0:T(8,128)(2,1)S(1)} all-gather(bf16[168,1024]{1,0:T(8,128)(2,1)S(1)} %get-tuple-element.305.refs_6_), channel_id=4, replica_groups=mesh['dev'=8,'ha'=2,'wa'=2] {'wa'}, dimensions={0}, use_global_device_ids=true | all-gather | bytes 1032192 | tf_op jit(solution)/shard_map/all_gather | solution.py:375
  78.4 2.6 %collective-permute-start.33 = (bf16[784,384]{1,0:T(8,128)(2,1)S(1)}, bf16[784,384]{1,0:T(8,128)(2,1)S(1)}, u32[]{:S(2)}, u32[]{:S(2)}) collective-permute-start(bf16[784,384]{1,0:T(8,128)(2,1)S(1)} %get-tuple-element.339), channel_id=1, source_target_pairs={{0,16},{4,20},{8,24},{12,28},{16,0},{20,4},{24,8},{28,12},{1,17},{... | collective-permute-start | bytes 1806344 | tf_op jit(solution)/shard_map/ppermute | solution.py:271
  81.1 2.8 %all-gather.4 = bf16[336,1536]{1,0:T(8,128)(2,1)S(1)} all-gather(bf16[168,1536]{1,0:T(8,128)(2,1)S(1)} %get-tuple-element.321.refs_24_.refs_4_.refs_20_.refs_10_), channel_id=6, replica_groups=mesh['dev'=8,'ha'=2,'wa'=2] {'wa'}, dimensions={0}, use_global_device_ids=true | all-gather | bytes 1548288 | tf_op jit(solution)/shard_map/all_gather | solution.py:375
  85.6 2.0 %back_0.1 = (bf16[147,384]{1,0:T(8,128)(2,1)S(1)}, bf16[192,384]{1,0:T(8,128)(2,1)S(1)}, f32[32,384]{1,0:T(8,128)S(1)}, f32[8,128]{1,0:T(8,128)S(1)}) custom-call(f32[168,768]{1,0:T(8,128)S(1)} %get-tuple-element.309.refs_22_.refs_10_.refs_0_, f32[168,768]{1,0:T(8,128)S(1)} %get-tuple-element.217.refs_0_.refs_14_.refs_15_.refs_10_.refs_13_.refs_19_.refs_11_.refs_17_.refs_1_, ...), custom_call_target="tpu_custom_call" | custom-call | tf_op jit(solution)/shard_map/back_0/pallas_call | solution.py:55
  87.6 2.0 %all-gather.5 = bf16[384,384]{1,0:T(8,128)(2,1)S(1)} all-gather(bf16[192,384]{1,0:T(8,128)(2,1)S(1)} %get-tuple-element.325), channel_id=7, replica_groups=mesh['dev'=8,'ha'=2,'wa'=2] {'wa'}, dimensions={0}, use_global_device_ids=true | all-gather | bytes 442368 | tf_op jit(solution)/shard_map/all_gather | solution.py:1085
  90.3 5.4 %collective-permute-done.31.refs_1_ = bf16[192,384]{1,0:T(8,128)(2,1)S(1)} collective-permute-done((bf16[192,384]{1,0:T(8,128)(2,1)S(1)}, bf16[192,384]{1,0:T(8,128)(2,1)S(1)}, u32[]{:S(2)}, u32[]{:S(2)}) %collective-permute-start.31) | collective-permute-done | bytes 147488 | tf_op jit(solution)/shard_map/ppermute | solution.py:265
  98.8 3.7 %collective-permute-done.36.refs_3_ = bf16[768,384]{1,0:T(8,128)(2,1)S(1)} collective-permute-done((bf16[768,384]{1,0:T(8,128)(2,1)S(1)}, bf16[768,384]{1,0:T(8,128)(2,1)S(1)}, u32[]{:S(2)}, u32[]{:S(2)}) %collective-permute-start.36) | collective-permute-done | bytes 589856 | tf_op jit(solution)/shard_map/ppermute | solution.py:271
  104.5 3.0 %collective-permute-done.33.refs_3_.refs_1_ = bf16[784,384]{1,0:T(8,128)(2,1)S(1)} collective-permute-done((bf16[784,384]{1,0:T(8,128)(2,1)S(1)}, bf16[784,384]{1,0:T(8,128)(2,1)S(1)}, u32[]{:S(2)}, u32[]{:S(2)}) %collective-permute-start.33) | collective-permute-done | bytes 602144 | tf_op jit(solution)/shard_map/ppermute | solution.py:271
  108.5 2.0 %all-gather.7.refs_1_ = bf16[2,147,384]{2,1,0:T(8,128)(2,1)S(1)} all-gather(bf16[1,147,384]{2,1,0:T(8,128)(2,1)S(1)} %bitcast.50), channel_id=8, replica_groups=mesh['dev'=8,'ha'=2,'wa'=2] {'wa'}, dimensions={0}, use_global_device_ids=true | all-gather | bytes 338688 | tf_op jit(solution)/shard_map/all_gather | solution.py:1105
  110.5 2.9 %collective-permute-done.39.refs_1_ = bf16[384,384]{1,0:T(8,128)(2,1)S(1)} collective-permute-done((bf16[384,384]{1,0:T(8,128)(2,1)S(1)}, bf16[384,384]{1,0:T(8,128)(2,1)S(1)}, u32[]{:S(2)}, u32[]{:S(2)}) %collective-permute-start.39) | collective-permute-done | bytes 294944 | tf_op jit(solution)/shard_map/ppermute | solution.py:271
  114.8 8.1 %collective-permute-done.38.refs_1_ = bf16[416,384]{1,0:T(8,128)(2,1)S(1)} collective-permute-done((bf16[416,384]{1,0:T(8,128)(2,1)S(1)}, bf16[416,384]{1,0:T(8,128)(2,1)S(1)}, u32[]{:S(2)}, u32[]{:S(2)}) %collective-permute-start.38) | collective-permute-done | bytes 319520 | tf_op jit(solution)/shard_map/ppermute | solution.py:271
  125.7 2.3 %collective-permute-done.37.refs_1_ = bf16[147,384]{1,0:T(8,128)(2,1)S(1)} collective-permute-done((bf16[147,384]{1,0:T(8,128)(2,1)S(1)}, bf16[147,384]{1,0:T(8,128)(2,1)S(1)}, u32[]{:S(2)}, u32[]{:S(2)}) %collective-permute-start.37) | collective-permute-done | bytes 112928 | tf_op jit(solution)/shard_map/ppermute | solution.py:265
  128.7 4.7 %collective-permute-done.42.refs_5_.refs_7_ = bf16[384,384]{1,0:T(8,128)(2,1)S(1)} collective-permute-done((bf16[384,384]{1,0:T(8,128)(2,1)S(1)}, bf16[384,384]{1,0:T(8,128)(2,1)S(1)}, u32[]{:S(2)}, u32[]{:S(2)}) %collective-permute-start.42) | collective-permute-done | bytes 294944 | tf_op jit(solution)/shard_map/ppermute | solution.py:271
  (128 shorter events, 64.7 us)
Async XLA Ops:
  0.6 7.7 %collective-permute-start.1 = (bf16[2,3,384,384]{3,2,1,0:T(8,128)(2,1)}, bf16[2,3,384,384]{3,2,1,0:T(8,128)(2,1)S(1)}, u32[]{:S(2)}, u32[]{:S(2)}) collective-permute-start(bf16[2,3,384,384]{3,2,1,0:T(8,128)(2,1)} %bitcast.14), channel_id=1, source_target_pairs={{0,1},{1,0},{2,3},{3,2},{4,5},{5,4},{6,7},{7,6},{8,9},{9,8},{10,11... | collective-permute-start | bytes 5308424 | tf_op jit(solution)/shard_map/ppermute | solution.py:268
  1.2 7.2 %collective-permute-start.2 = (bf16[2,384,384]{2,1,0:T(8,128)(2,1)}, bf16[2,384,384]{2,1,0:T(8,128)(2,1)S(1)}, u32[]{:S(2)}, u32[]{:S(2)}) collective-permute-start(bf16[2,384,384]{2,1,0:T(8,128)(2,1)} %refs_8_.9), channel_id=1, source_target_pairs={{0,1},{1,0},{2,3},{3,2},{4,5},{5,4},{6,7},{7,6},{8,9},{9,8},{10,11... | collective-permute-start | bytes 1769480 | tf_op jit(solution)/shard_map/ppermute | solution.py:268
  10.8 9.6 %collective-permute-start.8 = (bf16[2,384,1536]{2,1,0:T(8,128)(2,1)S(1)}, bf16[2,384,1536]{2,1,0:T(8,128)(2,1)S(1)}, u32[]{:S(2)}, u32[]{:S(2)}) collective-permute-start(bf16[2,384,1536]{2,1,0:T(8,128)(2,1)S(1)} %copy-done.2), channel_id=1, source_target_pairs={{0,1},{1,0},{2,3},{3,2},{4,5},{5,4},{6,7},{7,6},{8,9},{9,8},{10,11... | collective-permute-start | bytes 7077896 | tf_op jit(solution)/shard_map/ppermute | solution.py:268
  10.8 9.6 %collective-permute-start.9 = (bf16[2,1536,384]{2,1,0:T(8,128)(2,1)S(1)}, bf16[2,1536,384]{2,1,0:T(8,128)(2,1)S(1)}, u32[]{:S(2)}, u32[]{:S(2)}) collective-permute-start(bf16[2,1536,384]{2,1,0:T(8,128)(2,1)S(1)} %copy-done), channel_id=1, source_target_pairs={{0,1},{1,0},{2,3},{3,2},{4,5},{5,4},{6,7},{7,6},{8,9},{9,8},{10,11... | collective-permute-start | bytes 7077896 | tf_op jit(solution)/shard_map/ppermute | solution.py:268
  13.2 7.2 %collective-permute-start.10 = (bf16[112,768]{1,0:T(8,128)(2,1)S(1)}, bf16[112,768]{1,0:T(8,128)(2,1)S(1)}, u32[]{:S(2)}, u32[]{:S(2)}) collective-permute-start(bf16[112,768]{1,0:T(8,128)(2,1)S(1)} %get-tuple-element.208.refs_13_.refs_1_), channel_id=1, source_target_pairs={{0,2},{2,0},{1,3},{3,1},{4,6},{6,4},{5,7},{7,5},{8,10},{10,8},{9,1... | collective-permute-start | bytes 516104 | tf_op jit(solution)/shard_map/ppermute | solution.py:265
  40.0 8.6 %collective-permute-start.20 = (bf16[168,768]{1,0:T(8,128)(2,1)S(1)}, bf16[168,768]{1,0:T(8,128)(2,1)S(1)}, u32[]{:S(2)}, u32[]{:S(2)}) collective-permute-start(bf16[168,768]{1,0:T(8,128)(2,1)S(1)} %get-tuple-element.279.refs_12_), channel_id=1, source_target_pairs={{0,2},{2,0},{1,3},{3,1},{4,6},{6,4},{5,7},{7,5},{8,10},{10,8},{9,1... | collective-permute-start | bytes 774152 | tf_op jit(solution)/shard_map/ppermute | solution.py:265
  44.5 15.4 %collective-permute-start.26 = (bf16[768,384]{1,0:T(8,128)(2,1)S(1)}, bf16[768,384]{1,0:T(8,128)(2,1)S(1)}, u32[]{:S(2)}, u32[]{:S(2)}) collective-permute-start(bf16[768,384]{1,0:T(8,128)(2,1)S(1)} %get-tuple-element.296), channel_id=1, source_target_pairs={{0,4},{4,0},{8,12},{12,8},{16,20},{20,16},{24,28},{28,24},{1,5},{5... | collective-permute-start | bytes 1769480 | tf_op jit(solution)/shard_map/ppermute | solution.py:271
  46.0 15.1 %collective-permute-start.27 = (bf16[768,384]{1,0:T(8,128)(2,1)S(1)}, bf16[768,384]{1,0:T(8,128)(2,1)S(1)}, u32[]{:S(2)}, u32[]{:S(2)}) collective-permute-start(bf16[768,384]{1,0:T(8,128)(2,1)S(1)} %get-tuple-element.298), channel_id=1, source_target_pairs={{0,8},{4,12},{8,0},{12,4},{16,24},{20,28},{24,16},{28,20},{1,9},{5... | collective-permute-start | bytes 1769480 | tf_op jit(solution)/shard_map/ppermute | solution.py:271
  50.8 8.6 %collective-permute-start.24 = (bf16[168,768]{1,0:T(8,128)(2,1)S(1)}, bf16[168,768]{1,0:T(8,128)(2,1)S(1)}, u32[]{:S(2)}, u32[]{:S(2)}) collective-permute-start(bf16[168,768]{1,0:T(8,128)(2,1)S(1)} %get-tuple-element.286.refs_38_.refs_1_), channel_id=1, source_target_pairs={{0,2},{2,0},{1,3},{3,1},{4,6},{6,4},{5,7},{7,5},{8,10},{10,8},{9,1... | collective-permute-start | bytes 774152 | tf_op jit(solution)/shard_map/ppermute | solution.py:265
  61.4 16.7 %collective-permute-start.29 = (bf16[768,384]{1,0:T(8,128)(2,1)S(1)}, bf16[768,384]{1,0:T(8,128)(2,1)S(1)}, u32[]{:S(2)}, u32[]{:S(2)}) collective-permute-start(bf16[768,384]{1,0:T(8,128)(2,1)S(1)} %get-tuple-element.313), channel_id=1, source_target_pairs={{0,8},{4,12},{8,0},{12,4},{16,24},{20,28},{24,16},{28,20},{1,9},{5... | collective-permute-start | bytes 1769480 | tf_op jit(solution)/shard_map/ppermute | solution.py:271
  63.0 15.1 %collective-permute-start.30 = (bf16[768,384]{1,0:T(8,128)(2,1)S(1)}, bf16[768,384]{1,0:T(8,128)(2,1)S(1)}, u32[]{:S(2)}, u32[]{:S(2)}) collective-permute-start(bf16[768,384]{1,0:T(8,128)(2,1)S(1)} %get-tuple-element.315), channel_id=1, source_target_pairs={{0,4},{4,0},{8,12},{12,8},{16,20},{20,16},{24,28},{28,24},{1,5},{5... | collective-permute-start | bytes 1769480 | tf_op jit(solution)/shard_map/ppermute | solution.py:271
  66.4 10.0 %collective-permute-start.28 = (bf16[168,768]{1,0:T(8,128)(2,1)S(1)}, bf16[168,768]{1,0:T(8,128)(2,1)S(1)}, u32[]{:S(2)}, u32[]{:S(2)}) collective-permute-start(bf16[168,768]{1,0:T(8,128)(2,1)S(1)} %get-tuple-element.302.refs_1_), channel_id=1, source_target_pairs={{0,2},{2,0},{1,3},{3,1},{4,6},{6,4},{5,7},{7,5},{8,10},{10,8},{9,1... | collective-permute-start | bytes 774152 | tf_op jit(solution)/shard_map/ppermute | solution.py:265
  74.3 24.4 %collective-permute-start.35 = (bf16[768,384]{1,0:T(8,128)(2,1)S(1)}, bf16[768,384]{1,0:T(8,128)(2,1)S(1)}, u32[]{:S(2)}, u32[]{:S(2)}) collective-permute-start(bf16[768,384]{1,0:T(8,128)(2,1)S(1)} %get-tuple-element.344), channel_id=1, source_target_pairs={{0,4},{4,0},{8,12},{12,8},{16,20},{20,16},{24,28},{28,24},{1,5},{5... | collective-permute-start | bytes 1769480 | tf_op jit(solution)/shard_map/ppermute | solution.py:271
  75.9 26.6 %collective-permute-start.36 = (bf16[768,384]{1,0:T(8,128)(2,1)S(1)}, bf16[768,384]{1,0:T(8,128)(2,1)S(1)}, u32[]{:S(2)}, u32[]{:S(2)}) collective-permute-start(bf16[768,384]{1,0:T(8,128)(2,1)S(1)} %get-tuple-element.346), channel_id=1, source_target_pairs={{0,8},{4,12},{8,0},{12,4},{16,24},{20,28},{24,16},{28,20},{1,9},{5... | collective-permute-start | bytes 1769480 | tf_op jit(solution)/shard_map/ppermute | solution.py:271
  78.4 29.1 %collective-permute-start.33 = (bf16[784,384]{1,0:T(8,128)(2,1)S(1)}, bf16[784,384]{1,0:T(8,128)(2,1)S(1)}, u32[]{:S(2)}, u32[]{:S(2)}) collective-permute-start(bf16[784,384]{1,0:T(8,128)(2,1)S(1)} %get-tuple-element.339), channel_id=1, source_target_pairs={{0,16},{4,20},{8,24},{12,28},{16,0},{20,4},{24,8},{28,12},{1,17},{... | collective-permute-start | bytes 1806344 | tf_op jit(solution)/shard_map/ppermute | solution.py:271
  85.0 19.6 %collective-permute-start.32 = (bf16[768,384]{1,0:T(8,128)(2,1)S(1)}, bf16[768,384]{1,0:T(8,128)(2,1)S(1)}, u32[]{:S(2)}, u32[]{:S(2)}) collective-permute-start(bf16[768,384]{1,0:T(8,128)(2,1)S(1)} %get-tuple-element.338), channel_id=1, source_target_pairs={{0,4},{4,0},{8,12},{12,8},{16,20},{20,16},{24,28},{28,24},{1,5},{5... | collective-permute-start | bytes 1769480 | tf_op jit(solution)/shard_map/ppermute | solution.py:271
  96.4 8.2 %collective-permute-start.34 = (bf16[128,384]{1,0:T(8,128)(2,1)S(1)}, bf16[128,384]{1,0:T(8,128)(2,1)S(1)}, u32[]{:S(2)}, u32[]{:S(2)}) collective-permute-start(bf16[128,384]{1,0:T(8,128)(2,1)S(1)} %get-tuple-element.342), channel_id=1, source_target_pairs={{0,4},{4,0},{8,12},{12,8},{16,20},{20,16},{24,28},{28,24},{1,5},{5... | collective-permute-start | bytes 294920 | tf_op jit(solution)/shard_map/ppermute | solution.py:271
  102.8 10.7 %collective-permute-start.39 = (bf16[384,384]{1,0:T(8,128)(2,1)S(1)}, bf16[384,384]{1,0:T(8,128)(2,1)S(1)}, u32[]{:S(2)}, u32[]{:S(2)}) collective-permute-start(bf16[384,384]{1,0:T(8,128)(2,1)S(1)} %get-tuple-element.358), channel_id=1, source_target_pairs={{0,8},{4,12},{8,0},{12,4},{16,24},{20,28},{24,16},{28,20},{1,9},{5... | collective-permute-start | bytes 884744 | tf_op jit(solution)/shard_map/ppermute | solution.py:271
  102.9 10.6 %collective-permute-start.40 = (bf16[384,384]{1,0:T(8,128)(2,1)S(1)}, bf16[384,384]{1,0:T(8,128)(2,1)S(1)}, u32[]{:S(2)}, u32[]{:S(2)}) collective-permute-start(bf16[384,384]{1,0:T(8,128)(2,1)S(1)} %get-tuple-element.360), channel_id=1, source_target_pairs={{0,4},{4,0},{8,12},{12,8},{16,20},{20,16},{24,28},{28,24},{1,5},{5... | collective-permute-start | bytes 884744 | tf_op jit(solution)/shard_map/ppermute | solution.py:271
  107.7 15.2 %collective-permute-start.38 = (bf16[416,384]{1,0:T(8,128)(2,1)S(1)}, bf16[416,384]{1,0:T(8,128)(2,1)S(1)}, u32[]{:S(2)}, u32[]{:S(2)}) collective-permute-start(bf16[416,384]{1,0:T(8,128)(2,1)S(1)} %get-tuple-element.355), channel_id=1, source_target_pairs={{0,8},{4,12},{8,0},{12,4},{16,24},{20,28},{24,16},{28,20},{1,9},{5... | collective-permute-start | bytes 958472 | tf_op jit(solution)/shard_map/ppermute | solution.py:271
  113.6 19.8 %collective-permute-start.42 = (bf16[384,384]{1,0:T(8,128)(2,1)S(1)}, bf16[384,384]{1,0:T(8,128)(2,1)S(1)}, u32[]{:S(2)}, u32[]{:S(2)}) collective-permute-start(bf16[384,384]{1,0:T(8,128)(2,1)S(1)} %get-tuple-element.371), channel_id=1, source_target_pairs={{0,16},{4,20},{8,24},{12,28},{16,0},{20,4},{24,8},{28,12},{1,17},{... | collective-permute-start | bytes 884744 | tf_op jit(solution)/shard_map/ppermute | solution.py:271
  123.0 12.2 %collective-permute-start.41 = (bf16[224,384]{1,0:T(8,128)(2,1)S(1)}, bf16[224,384]{1,0:T(8,128)(2,1)S(1)}, u32[]{:S(2)}, u32[]{:S(2)}) collective-permute-start(bf16[224,384]{1,0:T(8,128)(2,1)S(1)} %get-tuple-element.368), channel_id=1, source_target_pairs={{0,16},{4,20},{8,24},{12,28},{16,0},{20,4},{24,8},{28,12},{1,17},{... | collective-permute-start | bytes 516104 | tf_op jit(solution)/shard_map/ppermute | solution.py:271
  123.8 9.6 %collective-permute-start.43 = (bf16[96,384]{1,0:T(8,128)(2,1)S(1)}, bf16[96,384]{1,0:T(8,128)(2,1)S(1)}, u32[]{:S(2)}, u32[]{:S(2)}) collective-permute-start(bf16[96,384]{1,0:T(8,128)(2,1)S(1)} %get-tuple-element.374), channel_id=1, source_target_pairs={{0,8},{4,12},{8,0},{12,4},{16,24},{20,28},{24,16},{28,20},{1,9},{5... | collective-permute-start | bytes 221192 | tf_op jit(solution)/shard_map/ppermute | solution.py:271
  125.3 8.2 %collective-permute-start.44 = (bf16[96,384]{1,0:T(8,128)(2,1)S(1)}, bf16[96,384]{1,0:T(8,128)(2,1)S(1)}, u32[]{:S(2)}, u32[]{:S(2)}) collective-permute-start(bf16[96,384]{1,0:T(8,128)(2,1)S(1)} %get-tuple-element.376), channel_id=1, source_target_pairs={{0,4},{4,0},{8,12},{12,8},{16,20},{20,16},{24,28},{28,24},{1,5},{5... | collective-permute-start | bytes 221192 | tf_op jit(solution)/shard_map/ppermute | solution.py:271
  (31 other events, 101.9 us)

commit v8 on v7

--- a/solution.py
+++ b/solution.py
@@ -267,8 +267,12 @@
     def over_wa(values):
         return lax.ppermute(values, "wa", swap)
 
+    partner = [1 << bit for bit in range(bits)]
+    if bits > 2:
+        partner[2] = 6
+
     def over_dev(values, bit):
-        return lax.ppermute(values, "dev", [(i, i ^ (1 << bit)) for i in range(n_dev)])
+        return lax.ppermute(values, "dev", [(i, i ^ partner[bit]) for i in range(n_dev)])
 
     def on_device(
         tokens, cotangent, conv_taps, norm_gain, norm_shift, w_qkv, w_proj, w_up, w_down, valid
@@ -290,7 +294,7 @@
         def chunk_at(place, which):
             found = 0
             for step, bit in enumerate(orders[which]):
-                found |= ((place >> (bits - 1 - step)) & 1) << bit
+                found ^= ((place >> (bits - 1 - step)) & 1) * partner[bit]
             return found ^ here("dev")
 
         order = Order()

time: 137 us -> 135 us (0.985)
  waiting for transfers between devices: 47.6 us -> 37.3 us
  starting transfers between devices: 35.6 us -> 44 us
    ppermute x16, waiting for transfers between devices: 26.9 us -> 15.3 us  [over_dev(): lax.ppermute(values, 'dev', [(i, i ^ partner[bit]) for i in range(n_dev)])]
    ppermute x16, starting transfers between devices: 16.6 us -> 25.1 us  [over_dev(): lax.ppermute(values, 'dev', [(i, i ^ partner[bit]) for i in range(n_dev)])]
  transfers between devices with their start and end apart: 45 -> 45, of which waited for: 22 -> 19; matrix products, arithmetic and copies ran while one was open for 0% -> 0% of each run, Pallas kernels for 22% -> 22%
where the time goes in v8:
time: 135 us
  starting transfers between devices  44 us (33%)
  waiting for transfers between devices  37.3 us (28%)
  Pallas kernels  32.9 us (24%)
  blocking collectives  15.9 us (12%)
  local copies, waits for them, and re-layouts  3.6 us (3%)
    pallas_call x35, Pallas kernels, kernel_call(): pl.pallas_call(wrapped, in_specs=[pl.BlockSpec(memory_space=pltpu.VMEM)]...  32.9 us
    ppermute x16, starting transfers between devices, over_dev(): lax.ppermute(values, 'dev', [(i, i ^ partner[bit]) for i in range(n_dev)])  25.1 us
    ppermute x13, waiting for transfers between devices, over_ha(): return lax.ppermute(values, 'ha', swap)  18.8 us
    ppermute x16, waiting for transfers between devices, over_dev(): lax.ppermute(values, 'dev', [(i, i ^ partner[bit]) for i in range(n_dev)])  15.3 us
    ppermute x13, starting transfers between devices, over_ha(): return lax.ppermute(values, 'ha', swap)  15.2 us
    all_gather x3, blocking collectives, both_rear(): return (pieces, [lax.all_gather(piece, 'wa') for piece in pieces])  7.26 us
    all_gather x2, blocking collectives, on_device(): lax.all_gather(later(values, g2), 'wa')  4.69 us
    ppermute x16, starting transfers between devices, over_wa(): return lax.ppermute(values, 'wa', swap)  3.64 us
  transfers between devices with their start and end apart: 45, of which 19 were waited for; matrix products, arithmetic and copies ran while one was open for 0% of the time, Pallas kernels for 22%

profile of v8, /device:TPU:0, one launch (start us, length us, event | category | flops | bytes accessed | tf_op | source)
XLA Modules:
  0.0 134.7 jit_solution(15990650073979123764)
XLA Ops:
  1.2 2.9 %collective-permute-start = (bf16[147,384]{1,0:T(8,128)(2,1)}, bf16[147,384]{1,0:T(8,128)(2,1)S(1)}, u32[]{:S(2)}, u32[]{:S(2)}) collective-permute-start(bf16[147,384]{1,0:T(8,128)(2,1)} %refs_0_.2), channel_id=1, source_target_pairs={{0,2},{2,0},{1,3},{3,1},{4,6},{6,4},{5,7},{7,5},{8,10},{10,8},{9,1... | collective-permute-start | bytes 338696 | tf_op jit(solution)/shard_map/ppermute | solution.py:265
  13.2 2.1 %collective-permute-start.10 = (bf16[112,768]{1,0:T(8,128)(2,1)S(1)}, bf16[112,768]{1,0:T(8,128)(2,1)S(1)}, u32[]{:S(2)}, u32[]{:S(2)}) collective-permute-start(bf16[112,768]{1,0:T(8,128)(2,1)S(1)} %get-tuple-element.208.refs_13_.refs_1_), channel_id=1, source_target_pairs={{0,2},{2,0},{1,3},{3,1},{4,6},{6,4},{5,7},{7,5},{8,10},{10,8},{9,1... | collective-permute-start | bytes 516104 | tf_op jit(solution)/shard_map/ppermute | solution.py:265
  16.9 3.4 %collective-permute-done.10.refs_2_ = bf16[112,768]{1,0:T(8,128)(2,1)S(1)} collective-permute-done((bf16[112,768]{1,0:T(8,128)(2,1)S(1)}, bf16[112,768]{1,0:T(8,128)(2,1)S(1)}, u32[]{:S(2)}, u32[]{:S(2)}) %collective-permute-start.10) | collective-permute-done | bytes 172064 | tf_op jit(solution)/shard_map/ppermute | solution.py:265
  21.7 2.1 %collective-permute-start.15 = (bf16[112,768]{1,0:T(8,128)(2,1)S(1)}, bf16[112,768]{1,0:T(8,128)(2,1)S(1)}, u32[]{:S(2)}, u32[]{:S(2)}) collective-permute-start(bf16[112,768]{1,0:T(8,128)(2,1)S(1)} %get-tuple-element.230.refs_22_.refs_1_), channel_id=1, source_target_pairs={{0,2},{2,0},{1,3},{3,1},{4,6},{6,4},{5,7},{7,5},{8,10},{10,8},{9,1... | collective-permute-start | bytes 516104 | tf_op jit(solution)/shard_map/ppermute | solution.py:265
  28.9 2.5 %collective-permute-start.19 = (bf16[112,768]{1,0:T(8,128)(2,1)S(1)}, bf16[112,768]{1,0:T(8,128)(2,1)S(1)}, u32[]{:S(2)}, u32[]{:S(2)}) collective-permute-start(bf16[112,768]{1,0:T(8,128)(2,1)S(1)} %get-tuple-element.246.refs_29_.refs_1_), channel_id=1, source_target_pairs={{0,2},{2,0},{1,3},{3,1},{4,6},{6,4},{5,7},{7,5},{8,10},{10,8},{9,1... | collective-permute-start | bytes 516104 | tf_op jit(solution)/shard_map/ppermute | solution.py:265
  42.5 2.1 %wgrad_d.1 = (bf16[768,384]{1,0:T(8,128)(2,1)S(1)}, bf16[768,384]{1,0:T(8,128)(2,1)S(1)}, bf16[768,384]{1,0:T(8,128)(2,1)S(1)}, bf16[768,384]{1,0:T(8,128)(2,1)S(1)}, f32[8,128]{1,0:T(8,128)S(1)}) custom-call(bf16[168,384]{1,0:T(8,128)(2,1)S(1)} %get-tuple-element.280.refs_0_, bf16[168,384]{1,0:T(8,128)(2,1)S(1)} %get-tuple-element.268.refs_31_.refs_1_.refs_0_, ...), custom_call_target="tpu_custom_call" | custom-call | tf_op jit(solution)/shard_map/wgrad_d/pallas_call | solution.py:55
  48.6 2.1 %back_c.1 = (f32[168,768]{1,0:T(8,128)S(1)}, bf16[168,384]{1,0:T(8,128)(2,1)S(1)}, bf16[168,768]{1,0:T(8,128)(2,1)S(1)}, f32[2,768]{1,0:T(2,128)S(1)}, bf16[168,...) custom-call(bf16[168,384]{1,0:T(8,128)(2,1)S(1)} %get-tuple-element.268.refs_31_.refs_1_.refs_0_, ...), custom_call_target="tpu_custom_call" | custom-call | tf_op jit(solution)/shard_map/back_c/pallas_call | solution.py:55
  52.1 2.2 %all-gather = bf16[336,768]{1,0:T(8,128)(2,1)S(1)} all-gather(bf16[168,768]{1,0:T(8,128)(2,1)S(1)} %get-tuple-element.287.refs_11_.refs_12_.refs_7_.refs_10_.refs_16_.refs_8_.refs_14_.refs_2_), channel_id=2, replica_groups=mesh['dev'=8,'ha'=2,'wa'=2] {'wa'}, dimensions={0}, use_global_device_ids=true | all-gather | bytes 774144 | tf_op jit(solution)/shard_map/all_gather | solution.py:961
  54.3 2.5 %all-gather.1 = bf16[336,1536]{1,0:T(8,128)(2,1)S(1)} all-gather(bf16[168,1536]{1,0:T(8,128)(2,1)S(1)} %get-tuple-element.288.refs_19_.refs_14_.refs_18_.refs_17_.refs_23_.refs_16_.refs_22_.refs_3_), channel_id=3, replica_groups=mesh['dev'=8,'ha'=2,'wa'=2] {'wa'}, dimensions={0}, use_global_device_ids=true | all-gather | bytes 1548288 | tf_op jit(solution)/shard_map/all_gather | solution.py:961
  63.6 2.8 %back_b.1 = (f32[168,768]{1,0:T(8,128)S(1)}, bf16[168,384]{1,0:T(8,128)(2,1)S(1)}, bf16[168,768]{1,0:T(8,128)(2,1)S(1)}, f32[11,768]{1,0:T(8,128)S(1)}, bf16[168...) custom-call(f32[168,768]{1,0:T(8,128)S(1)} %get-tuple-element.285.refs_34_.refs_32_.refs_0_, ...), custom_call_target="tpu_custom_call" | custom-call | tf_op jit(solution)/shard_map/back_b/pallas_call | solution.py:55
  67.9 2.2 %all-gather.3 = bf16[336,896]{1,0:T(8,128)(2,1)S(1)} all-gather(bf16[168,896]{1,0:T(8,128)(2,1)S(1)} %get-tuple-element.306.refs_7_), channel_id=5, replica_groups=mesh['dev'=8,'ha'=2,'wa'=2] {'wa'}, dimensions={0}, use_global_device_ids=true | all-gather | bytes 903168 | tf_op jit(solution)/shard_map/all_gather | solution.py:379
  70.2 2.3 %all-gather.2 = bf16[336,1024]{1,0:T(8,128)(2,1)S(1)} all-gather(bf16[168,1024]{1,0:T(8,128)(2,1)S(1)} %get-tuple-element.305.refs_6_), channel_id=4, replica_groups=mesh['dev'=8,'ha'=2,'wa'=2] {'wa'}, dimensions={0}, use_global_device_ids=true | all-gather | bytes 1032192 | tf_op jit(solution)/shard_map/all_gather | solution.py:379
  78.4 3.7 %collective-permute-start.33 = (bf16[784,384]{1,0:T(8,128)(2,1)S(1)}, bf16[784,384]{1,0:T(8,128)(2,1)S(1)}, u32[]{:S(2)}, u32[]{:S(2)}) collective-permute-start(bf16[784,384]{1,0:T(8,128)(2,1)S(1)} %get-tuple-element.339), channel_id=1, source_target_pairs={{0,24},{4,28},{8,16},{12,20},{16,8},{20,12},{24,0},{28,4},{1,25},{... | collective-permute-start | bytes 1806344 | tf_op jit(solution)/shard_map/ppermute | solution.py:275
  82.1 2.8 %all-gather.4 = bf16[336,1536]{1,0:T(8,128)(2,1)S(1)} all-gather(bf16[168,1536]{1,0:T(8,128)(2,1)S(1)} %get-tuple-element.321.refs_24_.refs_4_.refs_20_.refs_10_), channel_id=6, replica_groups=mesh['dev'=8,'ha'=2,'wa'=2] {'wa'}, dimensions={0}, use_global_device_ids=true | all-gather | bytes 1548288 | tf_op jit(solution)/shard_map/all_gather | solution.py:379
  86.6 2.0 %back_0.1 = (bf16[147,384]{1,0:T(8,128)(2,1)S(1)}, bf16[192,384]{1,0:T(8,128)(2,1)S(1)}, f32[32,384]{1,0:T(8,128)S(1)}, f32[8,128]{1,0:T(8,128)S(1)}) custom-call(f32[168,768]{1,0:T(8,128)S(1)} %get-tuple-element.309.refs_22_.refs_10_.refs_0_, f32[168,768]{1,0:T(8,128)S(1)} %get-tuple-element.217.refs_0_.refs_14_.refs_15_.refs_10_.refs_13_.refs_19_.refs_11_.refs_17_.refs_1_, ...), custom_call_target="tpu_custom_call" | custom-call | tf_op jit(solution)/shard_map/back_0/pallas_call | solution.py:55
  88.6 2.0 %all-gather.5 = bf16[384,384]{1,0:T(8,128)(2,1)S(1)} all-gather(bf16[192,384]{1,0:T(8,128)(2,1)S(1)} %get-tuple-element.325), channel_id=7, replica_groups=mesh['dev'=8,'ha'=2,'wa'=2] {'wa'}, dimensions={0}, use_global_device_ids=true | all-gather | bytes 442368 | tf_op jit(solution)/shard_map/all_gather | solution.py:1089
  91.2 5.4 %collective-permute-done.31.refs_1_ = bf16[192,384]{1,0:T(8,128)(2,1)S(1)} collective-permute-done((bf16[192,384]{1,0:T(8,128)(2,1)S(1)}, bf16[192,384]{1,0:T(8,128)(2,1)S(1)}, u32[]{:S(2)}, u32[]{:S(2)}) %collective-permute-start.31) | collective-permute-done | bytes 147488 | tf_op jit(solution)/shard_map/ppermute | solution.py:265
  100.8 4.5 %collective-permute-done.34.refs_6_ = bf16[128,384]{1,0:T(8,128)(2,1)S(1)} collective-permute-done((bf16[128,384]{1,0:T(8,128)(2,1)S(1)}, bf16[128,384]{1,0:T(8,128)(2,1)S(1)}, u32[]{:S(2)}, u32[]{:S(2)}) %collective-permute-start.34) | collective-permute-done | bytes 98336 | tf_op jit(solution)/shard_map/ppermute | solution.py:275
  108.3 2.0 %all-gather.7.refs_1_ = bf16[2,147,384]{2,1,0:T(8,128)(2,1)S(1)} all-gather(bf16[1,147,384]{2,1,0:T(8,128)(2,1)S(1)} %bitcast.50), channel_id=8, replica_groups=mesh['dev'=8,'ha'=2,'wa'=2] {'wa'}, dimensions={0}, use_global_device_ids=true | all-gather | bytes 338688 | tf_op jit(solution)/shard_map/all_gather | solution.py:1109
  110.3 2.1 %collective-permute-done.39.refs_1_ = bf16[384,384]{1,0:T(8,128)(2,1)S(1)} collective-permute-done((bf16[384,384]{1,0:T(8,128)(2,1)S(1)}, bf16[384,384]{1,0:T(8,128)(2,1)S(1)}, u32[]{:S(2)}, u32[]{:S(2)}) %collective-permute-start.39) | collective-permute-done | bytes 294944 | tf_op jit(solution)/shard_map/ppermute | solution.py:275
  112.6 2.7 %collective-permute-start.42 = (bf16[384,384]{1,0:T(8,128)(2,1)S(1)}, bf16[384,384]{1,0:T(8,128)(2,1)S(1)}, u32[]{:S(2)}, u32[]{:S(2)}) collective-permute-start(bf16[384,384]{1,0:T(8,128)(2,1)S(1)} %get-tuple-element.371), channel_id=1, source_target_pairs={{0,24},{4,28},{8,16},{12,20},{16,8},{20,12},{24,0},{28,4},{1,25},{... | collective-permute-start | bytes 884744 | tf_op jit(solution)/shard_map/ppermute | solution.py:275
  115.2 5.3 %collective-permute-done.38.refs_1_ = bf16[416,384]{1,0:T(8,128)(2,1)S(1)} collective-permute-done((bf16[416,384]{1,0:T(8,128)(2,1)S(1)}, bf16[416,384]{1,0:T(8,128)(2,1)S(1)}, u32[]{:S(2)}, u32[]{:S(2)}) %collective-permute-start.38) | collective-permute-done | bytes 319520 | tf_op jit(solution)/shard_map/ppermute | solution.py:275
  120.7 7.2 %collective-permute-start.41 = (bf16[224,384]{1,0:T(8,128)(2,1)S(1)}, bf16[224,384]{1,0:T(8,128)(2,1)S(1)}, u32[]{:S(2)}, u32[]{:S(2)}) collective-permute-start(bf16[224,384]{1,0:T(8,128)(2,1)S(1)} %get-tuple-element.368), channel_id=1, source_target_pairs={{0,24},{4,28},{8,16},{12,20},{16,8},{20,12},{24,0},{28,4},{1,25},{... | collective-permute-start | bytes 516104 | tf_op jit(solution)/shard_map/ppermute | solution.py:275
  129.1 3.6 %collective-permute-done.37.refs_1_ = bf16[147,384]{1,0:T(8,128)(2,1)S(1)} collective-permute-done((bf16[147,384]{1,0:T(8,128)(2,1)S(1)}, bf16[147,384]{1,0:T(8,128)(2,1)S(1)}, u32[]{:S(2)}, u32[]{:S(2)}) %collective-permute-start.37) | collective-permute-done | bytes 112928 | tf_op jit(solution)/shard_map/ppermute | solution.py:265
  (128 shorter events, 61.2 us)
Async XLA Ops:
  0.6 7.7 %collective-permute-start.1 = (bf16[2,3,384,384]{3,2,1,0:T(8,128)(2,1)}, bf16[2,3,384,384]{3,2,1,0:T(8,128)(2,1)S(1)}, u32[]{:S(2)}, u32[]{:S(2)}) collective-permute-start(bf16[2,3,384,384]{3,2,1,0:T(8,128)(2,1)} %bitcast.14), channel_id=1, source_target_pairs={{0,1},{1,0},{2,3},{3,2},{4,5},{5,4},{6,7},{7,6},{8,9},{9,8},{10,11... | collective-permute-start | bytes 5308424 | tf_op jit(solution)/shard_map/ppermute | solution.py:268
  1.2 7.2 %collective-permute-start.2 = (bf16[2,384,384]{2,1,0:T(8,128)(2,1)}, bf16[2,384,384]{2,1,0:T(8,128)(2,1)S(1)}, u32[]{:S(2)}, u32[]{:S(2)}) collective-permute-start(bf16[2,384,384]{2,1,0:T(8,128)(2,1)} %refs_8_.9), channel_id=1, source_target_pairs={{0,1},{1,0},{2,3},{3,2},{4,5},{5,4},{6,7},{7,6},{8,9},{9,8},{10,11... | collective-permute-start | bytes 1769480 | tf_op jit(solution)/shard_map/ppermute | solution.py:268
  1.2 7.1 %collective-permute-start = (bf16[147,384]{1,0:T(8,128)(2,1)}, bf16[147,384]{1,0:T(8,128)(2,1)S(1)}, u32[]{:S(2)}, u32[]{:S(2)}) collective-permute-start(bf16[147,384]{1,0:T(8,128)(2,1)} %refs_0_.2), channel_id=1, source_target_pairs={{0,2},{2,0},{1,3},{3,1},{4,6},{6,4},{5,7},{7,5},{8,10},{10,8},{9,1... | collective-permute-start | bytes 338696 | tf_op jit(solution)/shard_map/ppermute | solution.py:265
  10.8 9.6 %collective-permute-start.8 = (bf16[2,384,1536]{2,1,0:T(8,128)(2,1)S(1)}, bf16[2,384,1536]{2,1,0:T(8,128)(2,1)S(1)}, u32[]{:S(2)}, u32[]{:S(2)}) collective-permute-start(bf16[2,384,1536]{2,1,0:T(8,128)(2,1)S(1)} %copy-done.2), channel_id=1, source_target_pairs={{0,1},{1,0},{2,3},{3,2},{4,5},{5,4},{6,7},{7,6},{8,9},{9,8},{10,11... | collective-permute-start | bytes 7077896 | tf_op jit(solution)/shard_map/ppermute | solution.py:268
  10.8 9.6 %collective-permute-start.9 = (bf16[2,1536,384]{2,1,0:T(8,128)(2,1)S(1)}, bf16[2,1536,384]{2,1,0:T(8,128)(2,1)S(1)}, u32[]{:S(2)}, u32[]{:S(2)}) collective-permute-start(bf16[2,1536,384]{2,1,0:T(8,128)(2,1)S(1)} %copy-done), channel_id=1, source_target_pairs={{0,1},{1,0},{2,3},{3,2},{4,5},{5,4},{6,7},{7,6},{8,9},{9,8},{10,11... | collective-permute-start | bytes 7077896 | tf_op jit(solution)/shard_map/ppermute | solution.py:268
  13.2 7.2 %collective-permute-start.10 = (bf16[112,768]{1,0:T(8,128)(2,1)S(1)}, bf16[112,768]{1,0:T(8,128)(2,1)S(1)}, u32[]{:S(2)}, u32[]{:S(2)}) collective-permute-start(bf16[112,768]{1,0:T(8,128)(2,1)S(1)} %get-tuple-element.208.refs_13_.refs_1_), channel_id=1, source_target_pairs={{0,2},{2,0},{1,3},{3,1},{4,6},{6,4},{5,7},{7,5},{8,10},{10,8},{9,1... | collective-permute-start | bytes 516104 | tf_op jit(solution)/shard_map/ppermute | solution.py:265
  16.9 7.0 %collective-permute-start.7 = (bf16[56,768]{1,0:T(8,128)(2,1)S(1)}, bf16[56,768]{1,0:T(8,128)(2,1)S(1)}, u32[]{:S(2)}, u32[]{:S(2)}) collective-permute-start(bf16[56,768]{1,0:T(8,128)(2,1)S(1)} %get-tuple-element.218.refs_1_), channel_id=1, source_target_pairs={{0,2},{2,0},{1,3},{3,1},{4,6},{6,4},{5,7},{7,5},{8,10},{10,8},{9,1... | collective-permute-start | bytes 258056 | tf_op jit(solution)/shard_map/ppermute | solution.py:265
  40.0 8.6 %collective-permute-start.20 = (bf16[168,768]{1,0:T(8,128)(2,1)S(1)}, bf16[168,768]{1,0:T(8,128)(2,1)S(1)}, u32[]{:S(2)}, u32[]{:S(2)}) collective-permute-start(bf16[168,768]{1,0:T(8,128)(2,1)S(1)} %get-tuple-element.279.refs_12_), channel_id=1, source_target_pairs={{0,2},{2,0},{1,3},{3,1},{4,6},{6,4},{5,7},{7,5},{8,10},{10,8},{9,1... | collective-permute-start | bytes 774152 | tf_op jit(solution)/shard_map/ppermute | solution.py:265
  44.5 15.4 %collective-permute-start.26 = (bf16[768,384]{1,0:T(8,128)(2,1)S(1)}, bf16[768,384]{1,0:T(8,128)(2,1)S(1)}, u32[]{:S(2)}, u32[]{:S(2)}) collective-permute-start(bf16[768,384]{1,0:T(8,128)(2,1)S(1)} %get-tuple-element.296), channel_id=1, source_target_pairs={{0,4},{4,0},{8,12},{12,8},{16,20},{20,16},{24,28},{28,24},{1,5},{5... | collective-permute-start | bytes 1769480 | tf_op jit(solution)/shard_map/ppermute | solution.py:275
  46.0 15.1 %collective-permute-start.27 = (bf16[768,384]{1,0:T(8,128)(2,1)S(1)}, bf16[768,384]{1,0:T(8,128)(2,1)S(1)}, u32[]{:S(2)}, u32[]{:S(2)}) collective-permute-start(bf16[768,384]{1,0:T(8,128)(2,1)S(1)} %get-tuple-element.298), channel_id=1, source_target_pairs={{0,8},{4,12},{8,0},{12,4},{16,24},{20,28},{24,16},{28,20},{1,9},{5... | collective-permute-start | bytes 1769480 | tf_op jit(solution)/shard_map/ppermute | solution.py:275
  50.8 8.6 %collective-permute-start.24 = (bf16[168,768]{1,0:T(8,128)(2,1)S(1)}, bf16[168,768]{1,0:T(8,128)(2,1)S(1)}, u32[]{:S(2)}, u32[]{:S(2)}) collective-permute-start(bf16[168,768]{1,0:T(8,128)(2,1)S(1)} %get-tuple-element.286.refs_38_.refs_1_), channel_id=1, source_target_pairs={{0,2},{2,0},{1,3},{3,1},{4,6},{6,4},{5,7},{7,5},{8,10},{10,8},{9,1... | collective-permute-start | bytes 774152 | tf_op jit(solution)/shard_map/ppermute | solution.py:265
  61.4 16.7 %collective-permute-start.29 = (bf16[768,384]{1,0:T(8,128)(2,1)S(1)}, bf16[768,384]{1,0:T(8,128)(2,1)S(1)}, u32[]{:S(2)}, u32[]{:S(2)}) collective-permute-start(bf16[768,384]{1,0:T(8,128)(2,1)S(1)} %get-tuple-element.313), channel_id=1, source_target_pairs={{0,8},{4,12},{8,0},{12,4},{16,24},{20,28},{24,16},{28,20},{1,9},{5... | collective-permute-start | bytes 1769480 | tf_op jit(solution)/shard_map/ppermute | solution.py:275
  63.0 15.1 %collective-permute-start.30 = (bf16[768,384]{1,0:T(8,128)(2,1)S(1)}, bf16[768,384]{1,0:T(8,128)(2,1)S(1)}, u32[]{:S(2)}, u32[]{:S(2)}) collective-permute-start(bf16[768,384]{1,0:T(8,128)(2,1)S(1)} %get-tuple-element.315), channel_id=1, source_target_pairs={{0,4},{4,0},{8,12},{12,8},{16,20},{20,16},{24,28},{28,24},{1,5},{5... | collective-permute-start | bytes 1769480 | tf_op jit(solution)/shard_map/ppermute | solution.py:275
  66.4 10.0 %collective-permute-start.28 = (bf16[168,768]{1,0:T(8,128)(2,1)S(1)}, bf16[168,768]{1,0:T(8,128)(2,1)S(1)}, u32[]{:S(2)}, u32[]{:S(2)}) collective-permute-start(bf16[168,768]{1,0:T(8,128)(2,1)S(1)} %get-tuple-element.302.refs_1_), channel_id=1, source_target_pairs={{0,2},{2,0},{1,3},{3,1},{4,6},{6,4},{5,7},{7,5},{8,10},{10,8},{9,1... | collective-permute-start | bytes 774152 | tf_op jit(solution)/shard_map/ppermute | solution.py:265
  74.3 25.5 %collective-permute-start.35 = (bf16[768,384]{1,0:T(8,128)(2,1)S(1)}, bf16[768,384]{1,0:T(8,128)(2,1)S(1)}, u32[]{:S(2)}, u32[]{:S(2)}) collective-permute-start(bf16[768,384]{1,0:T(8,128)(2,1)S(1)} %get-tuple-element.344), channel_id=1, source_target_pairs={{0,4},{4,0},{8,12},{12,8},{16,20},{20,16},{24,28},{28,24},{1,5},{5... | collective-permute-start | bytes 1769480 | tf_op jit(solution)/shard_map/ppermute | solution.py:275
  75.9 23.9 %collective-permute-start.36 = (bf16[768,384]{1,0:T(8,128)(2,1)S(1)}, bf16[768,384]{1,0:T(8,128)(2,1)S(1)}, u32[]{:S(2)}, u32[]{:S(2)}) collective-permute-start(bf16[768,384]{1,0:T(8,128)(2,1)S(1)} %get-tuple-element.346), channel_id=1, source_target_pairs={{0,8},{4,12},{8,0},{12,4},{16,24},{20,28},{24,16},{28,20},{1,9},{5... | collective-permute-start | bytes 1769480 | tf_op jit(solution)/shard_map/ppermute | solution.py:275
  78.4 28.7 %collective-permute-start.33 = (bf16[784,384]{1,0:T(8,128)(2,1)S(1)}, bf16[784,384]{1,0:T(8,128)(2,1)S(1)}, u32[]{:S(2)}, u32[]{:S(2)}) collective-permute-start(bf16[784,384]{1,0:T(8,128)(2,1)S(1)} %get-tuple-element.339), channel_id=1, source_target_pairs={{0,24},{4,28},{8,16},{12,20},{16,8},{20,12},{24,0},{28,4},{1,25},{... | collective-permute-start | bytes 1806344 | tf_op jit(solution)/shard_map/ppermute | solution.py:275
  86.0 19.3 %collective-permute-start.32 = (bf16[768,384]{1,0:T(8,128)(2,1)S(1)}, bf16[768,384]{1,0:T(8,128)(2,1)S(1)}, u32[]{:S(2)}, u32[]{:S(2)}) collective-permute-start(bf16[768,384]{1,0:T(8,128)(2,1)S(1)} %get-tuple-element.338), channel_id=1, source_target_pairs={{0,4},{4,0},{8,12},{12,8},{16,20},{20,16},{24,28},{28,24},{1,5},{5... | collective-permute-start | bytes 1769480 | tf_op jit(solution)/shard_map/ppermute | solution.py:275
  97.4 8.0 %collective-permute-start.34 = (bf16[128,384]{1,0:T(8,128)(2,1)S(1)}, bf16[128,384]{1,0:T(8,128)(2,1)S(1)}, u32[]{:S(2)}, u32[]{:S(2)}) collective-permute-start(bf16[128,384]{1,0:T(8,128)(2,1)S(1)} %get-tuple-element.342), channel_id=1, source_target_pairs={{0,4},{4,0},{8,12},{12,8},{16,20},{20,16},{24,28},{28,24},{1,5},{5... | collective-permute-start | bytes 294920 | tf_op jit(solution)/shard_map/ppermute | solution.py:275
  100.1 12.3 %collective-permute-start.39 = (bf16[384,384]{1,0:T(8,128)(2,1)S(1)}, bf16[384,384]{1,0:T(8,128)(2,1)S(1)}, u32[]{:S(2)}, u32[]{:S(2)}) collective-permute-start(bf16[384,384]{1,0:T(8,128)(2,1)S(1)} %get-tuple-element.358), channel_id=1, source_target_pairs={{0,8},{4,12},{8,0},{12,4},{16,24},{20,28},{24,16},{28,20},{1,9},{5... | collective-permute-start | bytes 884744 | tf_op jit(solution)/shard_map/ppermute | solution.py:275
  100.2 12.2 %collective-permute-start.40 = (bf16[384,384]{1,0:T(8,128)(2,1)S(1)}, bf16[384,384]{1,0:T(8,128)(2,1)S(1)}, u32[]{:S(2)}, u32[]{:S(2)}) collective-permute-start(bf16[384,384]{1,0:T(8,128)(2,1)S(1)} %get-tuple-element.360), channel_id=1, source_target_pairs={{0,4},{4,0},{8,12},{12,8},{16,20},{20,16},{24,28},{28,24},{1,5},{5... | collective-permute-start | bytes 884744 | tf_op jit(solution)/shard_map/ppermute | solution.py:275
  107.4 13.2 %collective-permute-start.38 = (bf16[416,384]{1,0:T(8,128)(2,1)S(1)}, bf16[416,384]{1,0:T(8,128)(2,1)S(1)}, u32[]{:S(2)}, u32[]{:S(2)}) collective-permute-start(bf16[416,384]{1,0:T(8,128)(2,1)S(1)} %get-tuple-element.355), channel_id=1, source_target_pairs={{0,8},{4,12},{8,0},{12,4},{16,24},{20,28},{24,16},{28,20},{1,9},{5... | collective-permute-start | bytes 958472 | tf_op jit(solution)/shard_map/ppermute | solution.py:275
  112.6 20.8 %collective-permute-start.42 = (bf16[384,384]{1,0:T(8,128)(2,1)S(1)}, bf16[384,384]{1,0:T(8,128)(2,1)S(1)}, u32[]{:S(2)}, u32[]{:S(2)}) collective-permute-start(bf16[384,384]{1,0:T(8,128)(2,1)S(1)} %get-tuple-element.371), channel_id=1, source_target_pairs={{0,24},{4,28},{8,16},{12,20},{16,8},{20,12},{24,0},{28,4},{1,25},{... | collective-permute-start | bytes 884744 | tf_op jit(solution)/shard_map/ppermute | solution.py:275
  120.7 12.7 %collective-permute-start.41 = (bf16[224,384]{1,0:T(8,128)(2,1)S(1)}, bf16[224,384]{1,0:T(8,128)(2,1)S(1)}, u32[]{:S(2)}, u32[]{:S(2)}) collective-permute-start(bf16[224,384]{1,0:T(8,128)(2,1)S(1)} %get-tuple-element.368), channel_id=1, source_target_pairs={{0,24},{4,28},{8,16},{12,20},{16,8},{20,12},{24,0},{28,4},{1,25},{... | collective-permute-start | bytes 516104 | tf_op jit(solution)/shard_map/ppermute | solution.py:275
  (31 other events, 97.4 us)

commit v9 on v8

--- a/solution.py
+++ b/solution.py
@@ -873,8 +873,11 @@
             for stream, (_, _, _, _, kept_at, _, _) in zip(moving, plan_moving):
                 stream.kept = results[kept_at]
 
-            def depart():
-                received = {bit: over_dev(results[buffer_at[bit]], bit) for bit in bits_used}
+            def depart(event=None):
+                buffers = {bit: results[buffer_at[bit]] for bit in bits_used}
+                if event is not None:
+                    buffers = later(buffers, event)
+                received = {bit: over_dev(buffers[bit], bit) for bit in bits_used}
                 for stream, (_, _, bit, at) in zip(fresh, plan_fresh):
                     stream.got, stream.at, stream.step = received[bit], at, 1
                 for stream, (_, _, _, _, _, bit, at) in zip(moving, plan_moving):
@@ -1106,8 +1109,6 @@
         out_kept, out_sent = call(
             out_body, "out_d", [s5, *fore3[0], *wd], shipped, flops=mlp_flops // 2
         )
-        out_both = lax.all_gather(out_sent, "wa")
-
         def hop():
             if not left_bits:
                 return None
@@ -1120,15 +1121,18 @@
             arrived = [s for s in every if s.step == bits and s.final is None]
             slot(f"slot_b{turn}", moving=[s for s in streams_b if s.step < bits])
             second = [s for s in [*streams_d, *streams_a] if s.step < bits]
-            slot(f"slot_a{turn}", moving=second, ending=arrived, sums=hop())
+            depart = prepare_slot(f"slot_a{turn}", moving=second, ending=arrived, sums=hop())
             if turn > 1:
+                depart()
                 slot(f"slot_c{turn}", moving=[s for s in streams_c if s.step < bits])
-            if turn == 1:
-                out_stay, out_go = call(
-                    lambda kept, both, *refs: fold(kept, other_core(both), *refs),
-                    "fold_out", [out_kept, out_both], shipped,
-                )
-                out_got = over_ha(out_go)
+                continue
+            out_both = lax.all_gather(later(out_sent, streams_a[0].kept), "wa")
+            out_stay, out_go = call(
+                lambda kept, both, *refs: fold(kept, other_core(both), *refs),
+                "fold_out", [out_kept, out_both], shipped,
+            )
+            depart(out_stay)
+            out_got = over_ha(out_go)
         output = call(join, "join_out", [out_stay, out_got], [owned])[0]
 
         def finish_body(*refs):

time: 135 us -> 134 us (level)
  starting transfers between devices: 44 us -> 38.2 us
  waiting for transfers between devices: 37.3 us -> 41.8 us
    ppermute x16, waiting for transfers between devices: 15.3 us -> 21.3 us  [over_dev(): lax.ppermute(values, 'dev', [(i, i ^ partner[bit]) for i in range(n_dev)])]
    ppermute x16, starting transfers between devices: 25.1 us -> 19.4 us  [over_dev(): lax.ppermute(values, 'dev', [(i, i ^ partner[bit]) for i in range(n_dev)])]
    ppermute x13, waiting for transfers between devices: 18.8 us -> 17.2 us  [over_ha(): return lax.ppermute(values, 'ha', swap)]
  transfers between devices with their start and end apart: 45 -> 45, of which waited for: 19 -> 21; matrix products, arithmetic and copies ran while one was open for 0% -> 0% of each run, Pallas kernels for 22% -> 22%
where the time goes in v9:
time: 134 us; the launch traced here: 133 us
  waiting for transfers between devices  41.8 us (31%)
  starting transfers between devices  38.2 us (29%)
  Pallas kernels  32.9 us (25%)
  blocking collectives  15.9 us (12%)
  local copies, waits for them, and re-layouts  3.6 us (3%)
    pallas_call x35, Pallas kernels, kernel_call(): pl.pallas_call(wrapped, in_specs=[pl.BlockSpec(memory_space=pltpu.VMEM)]...  32.9 us
    ppermute x16, waiting for transfers between devices, over_dev(): lax.ppermute(values, 'dev', [(i, i ^ partner[bit]) for i in range(n_dev)])  21.3 us
    ppermute x16, starting transfers between devices, over_dev(): lax.ppermute(values, 'dev', [(i, i ^ partner[bit]) for i in range(n_dev)])  19.4 us
    ppermute x13, waiting for transfers between devices, over_ha(): return lax.ppermute(values, 'ha', swap)  17.2 us
    ppermute x13, starting transfers between devices, over_ha(): return lax.ppermute(values, 'ha', swap)  15.2 us
    all_gather x3, blocking collectives, both_rear(): return (pieces, [lax.all_gather(piece, 'wa') for piece in pieces])  7.26 us
    all_gather x2, blocking collectives, on_device(): lax.all_gather(later(values, g2), 'wa')  4.69 us
    ppermute x16, starting transfers between devices, over_wa(): return lax.ppermute(values, 'wa', swap)  3.64 us
  transfers between devices with their start and end apart: 45, of which 21 were waited for; matrix products, arithmetic and copies ran while one was open for 0% of the time, Pallas kernels for 22%

profile of v9, /device:TPU:0, one launch (start us, length us, event | category | flops | bytes accessed | tf_op | source)
XLA Modules:
  0.0 133.4 jit_solution(17928154074739295937)
XLA Ops:
  1.2 2.9 %collective-permute-start = (bf16[147,384]{1,0:T(8,128)(2,1)}, bf16[147,384]{1,0:T(8,128)(2,1)S(1)}, u32[]{:S(2)}, u32[]{:S(2)}) collective-permute-start(bf16[147,384]{1,0:T(8,128)(2,1)} %refs_0_.2), channel_id=1, source_target_pairs={{0,2},{2,0},{1,3},{3,1},{4,6},{6,4},{5,7},{7,5},{8,10},{10,8},{9,1... | collective-permute-start | bytes 338696 | tf_op jit(solution)/shard_map/ppermute | solution.py:265
  13.2 2.1 %collective-permute-start.10 = (bf16[112,768]{1,0:T(8,128)(2,1)S(1)}, bf16[112,768]{1,0:T(8,128)(2,1)S(1)}, u32[]{:S(2)}, u32[]{:S(2)}) collective-permute-start(bf16[112,768]{1,0:T(8,128)(2,1)S(1)} %get-tuple-element.210.refs_13_.refs_1_), channel_id=1, source_target_pairs={{0,2},{2,0},{1,3},{3,1},{4,6},{6,4},{5,7},{7,5},{8,10},{10,8},{9,1... | collective-permute-start | bytes 516104 | tf_op jit(solution)/shard_map/ppermute | solution.py:265
  16.9 3.4 %collective-permute-done.10.refs_2_ = bf16[112,768]{1,0:T(8,128)(2,1)S(1)} collective-permute-done((bf16[112,768]{1,0:T(8,128)(2,1)S(1)}, bf16[112,768]{1,0:T(8,128)(2,1)S(1)}, u32[]{:S(2)}, u32[]{:S(2)}) %collective-permute-start.10) | collective-permute-done | bytes 172064 | tf_op jit(solution)/shard_map/ppermute | solution.py:265
  21.7 2.1 %collective-permute-start.15 = (bf16[112,768]{1,0:T(8,128)(2,1)S(1)}, bf16[112,768]{1,0:T(8,128)(2,1)S(1)}, u32[]{:S(2)}, u32[]{:S(2)}) collective-permute-start(bf16[112,768]{1,0:T(8,128)(2,1)S(1)} %get-tuple-element.232.refs_22_.refs_1_), channel_id=1, source_target_pairs={{0,2},{2,0},{1,3},{3,1},{4,6},{6,4},{5,7},{7,5},{8,10},{10,8},{9,1... | collective-permute-start | bytes 516104 | tf_op jit(solution)/shard_map/ppermute | solution.py:265
  28.9 2.5 %collective-permute-start.19 = (bf16[112,768]{1,0:T(8,128)(2,1)S(1)}, bf16[112,768]{1,0:T(8,128)(2,1)S(1)}, u32[]{:S(2)}, u32[]{:S(2)}) collective-permute-start(bf16[112,768]{1,0:T(8,128)(2,1)S(1)} %get-tuple-element.248.refs_29_.refs_1_), channel_id=1, source_target_pairs={{0,2},{2,0},{1,3},{3,1},{4,6},{6,4},{5,7},{7,5},{8,10},{10,8},{9,1... | collective-permute-start | bytes 516104 | tf_op jit(solution)/shard_map/ppermute | solution.py:265
  42.5 2.1 %wgrad_d.1 = (bf16[768,384]{1,0:T(8,128)(2,1)S(1)}, bf16[768,384]{1,0:T(8,128)(2,1)S(1)}, bf16[768,384]{1,0:T(8,128)(2,1)S(1)}, bf16[768,384]{1,0:T(8,128)(2,1)S(1)}, f32[8,128]{1,0:T(8,128)S(1)}) custom-call(bf16[168,384]{1,0:T(8,128)(2,1)S(1)} %get-tuple-element.282.refs_0_, bf16[168,384]{1,0:T(8,128)(2,1)S(1)} %get-tuple-element.270.refs_31_.refs_1_.refs_0_, ...), custom_call_target="tpu_custom_call" | custom-call | tf_op jit(solution)/shard_map/wgrad_d/pallas_call | solution.py:55
  48.6 2.1 %back_c.1 = (f32[168,768]{1,0:T(8,128)S(1)}, bf16[168,384]{1,0:T(8,128)(2,1)S(1)}, bf16[168,768]{1,0:T(8,128)(2,1)S(1)}, f32[2,768]{1,0:T(2,128)S(1)}, bf16[168,...) custom-call(bf16[168,384]{1,0:T(8,128)(2,1)S(1)} %get-tuple-element.270.refs_31_.refs_1_.refs_0_, ...), custom_call_target="tpu_custom_call" | custom-call | tf_op jit(solution)/shard_map/back_c/pallas_call | solution.py:55
  52.1 2.2 %all-gather = bf16[336,768]{1,0:T(8,128)(2,1)S(1)} all-gather(bf16[168,768]{1,0:T(8,128)(2,1)S(1)} %get-tuple-element.289.refs_11_.refs_12_.refs_7_.refs_10_.refs_16_.refs_8_.refs_14_.refs_2_), channel_id=2, replica_groups=mesh['dev'=8,'ha'=2,'wa'=2] {'wa'}, dimensions={0}, use_global_device_ids=true | all-gather | bytes 774144 | tf_op jit(solution)/shard_map/all_gather | solution.py:964
  54.3 2.5 %all-gather.1 = bf16[336,1536]{1,0:T(8,128)(2,1)S(1)} all-gather(bf16[168,1536]{1,0:T(8,128)(2,1)S(1)} %get-tuple-element.290.refs_19_.refs_14_.refs_18_.refs_17_.refs_23_.refs_16_.refs_22_.refs_3_), channel_id=3, replica_groups=mesh['dev'=8,'ha'=2,'wa'=2] {'wa'}, dimensions={0}, use_global_device_ids=true | all-gather | bytes 1548288 | tf_op jit(solution)/shard_map/all_gather | solution.py:964
  63.6 2.8 %back_b.1 = (f32[168,768]{1,0:T(8,128)S(1)}, bf16[168,384]{1,0:T(8,128)(2,1)S(1)}, bf16[168,768]{1,0:T(8,128)(2,1)S(1)}, f32[11,768]{1,0:T(8,128)S(1)}, bf16[168...) custom-call(f32[168,768]{1,0:T(8,128)S(1)} %get-tuple-element.287.refs_34_.refs_32_.refs_0_, ...), custom_call_target="tpu_custom_call" | custom-call | tf_op jit(solution)/shard_map/back_b/pallas_call | solution.py:55
  67.9 2.2 %all-gather.3 = bf16[336,896]{1,0:T(8,128)(2,1)S(1)} all-gather(bf16[168,896]{1,0:T(8,128)(2,1)S(1)} %get-tuple-element.308.refs_7_), channel_id=5, replica_groups=mesh['dev'=8,'ha'=2,'wa'=2] {'wa'}, dimensions={0}, use_global_device_ids=true | all-gather | bytes 903168 | tf_op jit(solution)/shard_map/all_gather | solution.py:379
  70.2 2.3 %all-gather.2 = bf16[336,1024]{1,0:T(8,128)(2,1)S(1)} all-gather(bf16[168,1024]{1,0:T(8,128)(2,1)S(1)} %get-tuple-element.307.refs_6_), channel_id=4, replica_groups=mesh['dev'=8,'ha'=2,'wa'=2] {'wa'}, dimensions={0}, use_global_device_ids=true | all-gather | bytes 1032192 | tf_op jit(solution)/shard_map/all_gather | solution.py:379
  72.5 1.9 %wgrad_b.1 = (bf16[768,384]{1,0:T(8,128)(2,1)S(1)}, bf16[768,384]{1,0:T(8,128)(2,1)S(1)}, bf16[768,384]{1,0:T(8,128)(2,1)S(1)}, bf16[768,384]{1,0:T(8,128)(2,1)S(1)}, f32[8,128]{1,0:T(8,128)S(1)}) custom-call(bf16[168,384]{1,0:T(8,128)(2,1)S(1)} %get-tuple-element.241.refs_17_.refs_12_.refs_16_.refs_15_.refs_21_.refs_14_.refs_20_.refs_0_, ...), custom_call_target="tpu_custom_call" | custom-call | tf_op jit(solution)/shard_map/wgrad_b/pallas_call | solution.py:55
  78.4 3.7 %collective-permute-start.33 = (bf16[784,384]{1,0:T(8,128)(2,1)S(1)}, bf16[784,384]{1,0:T(8,128)(2,1)S(1)}, u32[]{:S(2)}, u32[]{:S(2)}) collective-permute-start(bf16[784,384]{1,0:T(8,128)(2,1)S(1)} %get-tuple-element.341), channel_id=1, source_target_pairs={{0,24},{4,28},{8,16},{12,20},{16,8},{20,12},{24,0},{28,4},{1,25},{... | collective-permute-start | bytes 1806344 | tf_op jit(solution)/shard_map/ppermute | solution.py:275
  82.1 2.8 %all-gather.4 = bf16[336,1536]{1,0:T(8,128)(2,1)S(1)} all-gather(bf16[168,1536]{1,0:T(8,128)(2,1)S(1)} %get-tuple-element.323.refs_24_.refs_4_.refs_20_.refs_10_), channel_id=6, replica_groups=mesh['dev'=8,'ha'=2,'wa'=2] {'wa'}, dimensions={0}, use_global_device_ids=true | all-gather | bytes 1548288 | tf_op jit(solution)/shard_map/all_gather | solution.py:379
  86.6 2.0 %back_0.1 = (bf16[147,384]{1,0:T(8,128)(2,1)S(1)}, bf16[192,384]{1,0:T(8,128)(2,1)S(1)}, f32[32,384]{1,0:T(8,128)S(1)}, f32[8,128]{1,0:T(8,128)S(1)}) custom-call(f32[168,768]{1,0:T(8,128)S(1)} %get-tuple-element.311.refs_22_.refs_10_.refs_0_, f32[168,768]{1,0:T(8,128)S(1)} %get-tuple-element.219.refs_0_.refs_14_.refs_15_.refs_10_.refs_13_.refs_19_.refs_11_.refs_17_.refs_1_, ...), custom_call_target="tpu_custom_call" | custom-call | tf_op jit(solution)/shard_map/back_0/pallas_call | solution.py:55
  88.6 2.0 %all-gather.5 = bf16[384,384]{1,0:T(8,128)(2,1)S(1)} all-gather(bf16[192,384]{1,0:T(8,128)(2,1)S(1)} %get-tuple-element.327), channel_id=7, replica_groups=mesh['dev'=8,'ha'=2,'wa'=2] {'wa'}, dimensions={0}, use_global_device_ids=true | all-gather | bytes 442368 | tf_op jit(solution)/shard_map/all_gather | solution.py:1092
  91.2 5.4 %collective-permute-done.31.refs_1_ = bf16[192,384]{1,0:T(8,128)(2,1)S(1)} collective-permute-done((bf16[192,384]{1,0:T(8,128)(2,1)S(1)}, bf16[192,384]{1,0:T(8,128)(2,1)S(1)}, u32[]{:S(2)}, u32[]{:S(2)}) %collective-permute-start.31) | collective-permute-done | bytes 147488 | tf_op jit(solution)/shard_map/ppermute | solution.py:265
  100.8 4.5 %collective-permute-done.34.refs_6_ = bf16[128,384]{1,0:T(8,128)(2,1)S(1)} collective-permute-done((bf16[128,384]{1,0:T(8,128)(2,1)S(1)}, bf16[128,384]{1,0:T(8,128)(2,1)S(1)}, u32[]{:S(2)}, u32[]{:S(2)}) %collective-permute-start.34) | collective-permute-done | bytes 98336 | tf_op jit(solution)/shard_map/ppermute | solution.py:275
  107.4 2.0 %all-gather.7.refs_1_ = bf16[2,147,384]{2,1,0:T(8,128)(2,1)S(1)} all-gather(bf16[1,147,384]{2,1,0:T(8,128)(2,1)S(1)} %bitcast.50), channel_id=8, replica_groups=mesh['dev'=8,'ha'=2,'wa'=2] {'wa'}, dimensions={0}, use_global_device_ids=true | all-gather | bytes 338688 | tf_op jit(solution)/shard_map/all_gather | solution.py:1129
  110.3 2.1 %collective-permute-done.39.refs_1_ = bf16[384,384]{1,0:T(8,128)(2,1)S(1)} collective-permute-done((bf16[384,384]{1,0:T(8,128)(2,1)S(1)}, bf16[384,384]{1,0:T(8,128)(2,1)S(1)}, u32[]{:S(2)}, u32[]{:S(2)}) %collective-permute-start.39) | collective-permute-done | bytes 294944 | tf_op jit(solution)/shard_map/ppermute | solution.py:275
  113.5 5.6 %collective-permute-done.38.refs_1_ = bf16[416,384]{1,0:T(8,128)(2,1)S(1)} collective-permute-done((bf16[416,384]{1,0:T(8,128)(2,1)S(1)}, bf16[416,384]{1,0:T(8,128)(2,1)S(1)}, u32[]{:S(2)}, u32[]{:S(2)}) %collective-permute-start.38) | collective-permute-done | bytes 319520 | tf_op jit(solution)/shard_map/ppermute | solution.py:275
  123.6 2.0 %collective-permute-done.37.refs_1_ = bf16[147,384]{1,0:T(8,128)(2,1)S(1)} collective-permute-done((bf16[147,384]{1,0:T(8,128)(2,1)S(1)}, bf16[147,384]{1,0:T(8,128)(2,1)S(1)}, u32[]{:S(2)}, u32[]{:S(2)}) %collective-permute-start.37) | collective-permute-done | bytes 112928 | tf_op jit(solution)/shard_map/ppermute | solution.py:265
  127.7 4.4 %collective-permute-done.43.refs_9_ = bf16[96,384]{1,0:T(8,128)(2,1)S(1)} collective-permute-done((bf16[96,384]{1,0:T(8,128)(2,1)S(1)}, bf16[96,384]{1,0:T(8,128)(2,1)S(1)}, u32[]{:S(2)}, u32[]{:S(2)}) %collective-permute-start.43) | collective-permute-done | bytes 73760 | tf_op jit(solution)/shard_map/ppermute | solution.py:275
  (128 shorter events, 64.7 us)
Async XLA Ops:
  0.6 7.7 %collective-permute-start.1 = (bf16[2,3,384,384]{3,2,1,0:T(8,128)(2,1)}, bf16[2,3,384,384]{3,2,1,0:T(8,128)(2,1)S(1)}, u32[]{:S(2)}, u32[]{:S(2)}) collective-permute-start(bf16[2,3,384,384]{3,2,1,0:T(8,128)(2,1)} %bitcast.14), channel_id=1, source_target_pairs={{0,1},{1,0},{2,3},{3,2},{4,5},{5,4},{6,7},{7,6},{8,9},{9,8},{10,11... | collective-permute-start | bytes 5308424 | tf_op jit(solution)/shard_map/ppermute | solution.py:268
  1.2 7.2 %collective-permute-start.2 = (bf16[2,384,384]{2,1,0:T(8,128)(2,1)}, bf16[2,384,384]{2,1,0:T(8,128)(2,1)S(1)}, u32[]{:S(2)}, u32[]{:S(2)}) collective-permute-start(bf16[2,384,384]{2,1,0:T(8,128)(2,1)} %refs_8_.9), channel_id=1, source_target_pairs={{0,1},{1,0},{2,3},{3,2},{4,5},{5,4},{6,7},{7,6},{8,9},{9,8},{10,11... | collective-permute-start | bytes 1769480 | tf_op jit(solution)/shard_map/ppermute | solution.py:268
  10.8 9.6 %collective-permute-start.8 = (bf16[2,384,1536]{2,1,0:T(8,128)(2,1)S(1)}, bf16[2,384,1536]{2,1,0:T(8,128)(2,1)S(1)}, u32[]{:S(2)}, u32[]{:S(2)}) collective-permute-start(bf16[2,384,1536]{2,1,0:T(8,128)(2,1)S(1)} %copy-done.2), channel_id=1, source_target_pairs={{0,1},{1,0},{2,3},{3,2},{4,5},{5,4},{6,7},{7,6},{8,9},{9,8},{10,11... | collective-permute-start | bytes 7077896 | tf_op jit(solution)/shard_map/ppermute | solution.py:268
  10.8 9.6 %collective-permute-start.9 = (bf16[2,1536,384]{2,1,0:T(8,128)(2,1)S(1)}, bf16[2,1536,384]{2,1,0:T(8,128)(2,1)S(1)}, u32[]{:S(2)}, u32[]{:S(2)}) collective-permute-start(bf16[2,1536,384]{2,1,0:T(8,128)(2,1)S(1)} %copy-done), channel_id=1, source_target_pairs={{0,1},{1,0},{2,3},{3,2},{4,5},{5,4},{6,7},{7,6},{8,9},{9,8},{10,11... | collective-permute-start | bytes 7077896 | tf_op jit(solution)/shard_map/ppermute | solution.py:268
  13.2 7.2 %collective-permute-start.10 = (bf16[112,768]{1,0:T(8,128)(2,1)S(1)}, bf16[112,768]{1,0:T(8,128)(2,1)S(1)}, u32[]{:S(2)}, u32[]{:S(2)}) collective-permute-start(bf16[112,768]{1,0:T(8,128)(2,1)S(1)} %get-tuple-element.210.refs_13_.refs_1_), channel_id=1, source_target_pairs={{0,2},{2,0},{1,3},{3,1},{4,6},{6,4},{5,7},{7,5},{8,10},{10,8},{9,1... | collective-permute-start | bytes 516104 | tf_op jit(solution)/shard_map/ppermute | solution.py:265
  40.0 8.6 %collective-permute-start.20 = (bf16[168,768]{1,0:T(8,128)(2,1)S(1)}, bf16[168,768]{1,0:T(8,128)(2,1)S(1)}, u32[]{:S(2)}, u32[]{:S(2)}) collective-permute-start(bf16[168,768]{1,0:T(8,128)(2,1)S(1)} %get-tuple-element.281.refs_12_), channel_id=1, source_target_pairs={{0,2},{2,0},{1,3},{3,1},{4,6},{6,4},{5,7},{7,5},{8,10},{10,8},{9,1... | collective-permute-start | bytes 774152 | tf_op jit(solution)/shard_map/ppermute | solution.py:265
  44.5 15.4 %collective-permute-start.26 = (bf16[768,384]{1,0:T(8,128)(2,1)S(1)}, bf16[768,384]{1,0:T(8,128)(2,1)S(1)}, u32[]{:S(2)}, u32[]{:S(2)}) collective-permute-start(bf16[768,384]{1,0:T(8,128)(2,1)S(1)} %get-tuple-element.298), channel_id=1, source_target_pairs={{0,4},{4,0},{8,12},{12,8},{16,20},{20,16},{24,28},{28,24},{1,5},{5... | collective-permute-start | bytes 1769480 | tf_op jit(solution)/shard_map/ppermute | solution.py:275
  46.0 15.1 %collective-permute-start.27 = (bf16[768,384]{1,0:T(8,128)(2,1)S(1)}, bf16[768,384]{1,0:T(8,128)(2,1)S(1)}, u32[]{:S(2)}, u32[]{:S(2)}) collective-permute-start(bf16[768,384]{1,0:T(8,128)(2,1)S(1)} %get-tuple-element.300), channel_id=1, source_target_pairs={{0,8},{4,12},{8,0},{12,4},{16,24},{20,28},{24,16},{28,20},{1,9},{5... | collective-permute-start | bytes 1769480 | tf_op jit(solution)/shard_map/ppermute | solution.py:275
  50.8 8.6 %collective-permute-start.24 = (bf16[168,768]{1,0:T(8,128)(2,1)S(1)}, bf16[168,768]{1,0:T(8,128)(2,1)S(1)}, u32[]{:S(2)}, u32[]{:S(2)}) collective-permute-start(bf16[168,768]{1,0:T(8,128)(2,1)S(1)} %get-tuple-element.288.refs_38_.refs_1_), channel_id=1, source_target_pairs={{0,2},{2,0},{1,3},{3,1},{4,6},{6,4},{5,7},{7,5},{8,10},{10,8},{9,1... | collective-permute-start | bytes 774152 | tf_op jit(solution)/shard_map/ppermute | solution.py:265
  61.4 16.7 %collective-permute-start.29 = (bf16[768,384]{1,0:T(8,128)(2,1)S(1)}, bf16[768,384]{1,0:T(8,128)(2,1)S(1)}, u32[]{:S(2)}, u32[]{:S(2)}) collective-permute-start(bf16[768,384]{1,0:T(8,128)(2,1)S(1)} %get-tuple-element.315), channel_id=1, source_target_pairs={{0,8},{4,12},{8,0},{12,4},{16,24},{20,28},{24,16},{28,20},{1,9},{5... | collective-permute-start | bytes 1769480 | tf_op jit(solution)/shard_map/ppermute | solution.py:275
  63.0 15.1 %collective-permute-start.30 = (bf16[768,384]{1,0:T(8,128)(2,1)S(1)}, bf16[768,384]{1,0:T(8,128)(2,1)S(1)}, u32[]{:S(2)}, u32[]{:S(2)}) collective-permute-start(bf16[768,384]{1,0:T(8,128)(2,1)S(1)} %get-tuple-element.317), channel_id=1, source_target_pairs={{0,4},{4,0},{8,12},{12,8},{16,20},{20,16},{24,28},{28,24},{1,5},{5... | collective-permute-start | bytes 1769480 | tf_op jit(solution)/shard_map/ppermute | solution.py:275
  66.4 10.0 %collective-permute-start.28 = (bf16[168,768]{1,0:T(8,128)(2,1)S(1)}, bf16[168,768]{1,0:T(8,128)(2,1)S(1)}, u32[]{:S(2)}, u32[]{:S(2)}) collective-permute-start(bf16[168,768]{1,0:T(8,128)(2,1)S(1)} %get-tuple-element.304.refs_1_), channel_id=1, source_target_pairs={{0,2},{2,0},{1,3},{3,1},{4,6},{6,4},{5,7},{7,5},{8,10},{10,8},{9,1... | collective-permute-start | bytes 774152 | tf_op jit(solution)/shard_map/ppermute | solution.py:265
  74.3 25.5 %collective-permute-start.35 = (bf16[768,384]{1,0:T(8,128)(2,1)S(1)}, bf16[768,384]{1,0:T(8,128)(2,1)S(1)}, u32[]{:S(2)}, u32[]{:S(2)}) collective-permute-start(bf16[768,384]{1,0:T(8,128)(2,1)S(1)} %get-tuple-element.346), channel_id=1, source_target_pairs={{0,4},{4,0},{8,12},{12,8},{16,20},{20,16},{24,28},{28,24},{1,5},{5... | collective-permute-start | bytes 1769480 | tf_op jit(solution)/shard_map/ppermute | solution.py:275
  75.9 23.9 %collective-permute-start.36 = (bf16[768,384]{1,0:T(8,128)(2,1)S(1)}, bf16[768,384]{1,0:T(8,128)(2,1)S(1)}, u32[]{:S(2)}, u32[]{:S(2)}) collective-permute-start(bf16[768,384]{1,0:T(8,128)(2,1)S(1)} %get-tuple-element.348), channel_id=1, source_target_pairs={{0,8},{4,12},{8,0},{12,4},{16,24},{20,28},{24,16},{28,20},{1,9},{5... | collective-permute-start | bytes 1769480 | tf_op jit(solution)/shard_map/ppermute | solution.py:275
  78.4 28.7 %collective-permute-start.33 = (bf16[784,384]{1,0:T(8,128)(2,1)S(1)}, bf16[784,384]{1,0:T(8,128)(2,1)S(1)}, u32[]{:S(2)}, u32[]{:S(2)}) collective-permute-start(bf16[784,384]{1,0:T(8,128)(2,1)S(1)} %get-tuple-element.341), channel_id=1, source_target_pairs={{0,24},{4,28},{8,16},{12,20},{16,8},{20,12},{24,0},{28,4},{1,25},{... | collective-permute-start | bytes 1806344 | tf_op jit(solution)/shard_map/ppermute | solution.py:275
  86.0 19.3 %collective-permute-start.32 = (bf16[768,384]{1,0:T(8,128)(2,1)S(1)}, bf16[768,384]{1,0:T(8,128)(2,1)S(1)}, u32[]{:S(2)}, u32[]{:S(2)}) collective-permute-start(bf16[768,384]{1,0:T(8,128)(2,1)S(1)} %get-tuple-element.340), channel_id=1, source_target_pairs={{0,4},{4,0},{8,12},{12,8},{16,20},{20,16},{24,28},{28,24},{1,5},{5... | collective-permute-start | bytes 1769480 | tf_op jit(solution)/shard_map/ppermute | solution.py:275
  97.4 8.0 %collective-permute-start.34 = (bf16[128,384]{1,0:T(8,128)(2,1)S(1)}, bf16[128,384]{1,0:T(8,128)(2,1)S(1)}, u32[]{:S(2)}, u32[]{:S(2)}) collective-permute-start(bf16[128,384]{1,0:T(8,128)(2,1)S(1)} %get-tuple-element.344), channel_id=1, source_target_pairs={{0,4},{4,0},{8,12},{12,8},{16,20},{20,16},{24,28},{28,24},{1,5},{5... | collective-permute-start | bytes 294920 | tf_op jit(solution)/shard_map/ppermute | solution.py:275
  100.1 12.3 %collective-permute-start.39 = (bf16[384,384]{1,0:T(8,128)(2,1)S(1)}, bf16[384,384]{1,0:T(8,128)(2,1)S(1)}, u32[]{:S(2)}, u32[]{:S(2)}) collective-permute-start(bf16[384,384]{1,0:T(8,128)(2,1)S(1)} %get-tuple-element.362), channel_id=1, source_target_pairs={{0,8},{4,12},{8,0},{12,4},{16,24},{20,28},{24,16},{28,20},{1,9},{5... | collective-permute-start | bytes 884744 | tf_op jit(solution)/shard_map/ppermute | solution.py:275
  100.2 12.2 %collective-permute-start.40 = (bf16[384,384]{1,0:T(8,128)(2,1)S(1)}, bf16[384,384]{1,0:T(8,128)(2,1)S(1)}, u32[]{:S(2)}, u32[]{:S(2)}) collective-permute-start(bf16[384,384]{1,0:T(8,128)(2,1)S(1)} %get-tuple-element.364), channel_id=1, source_target_pairs={{0,4},{4,0},{8,12},{12,8},{16,20},{20,16},{24,28},{28,24},{1,5},{5... | collective-permute-start | bytes 884744 | tf_op jit(solution)/shard_map/ppermute | solution.py:275
  109.4 9.8 %collective-permute-start.38 = (bf16[416,384]{1,0:T(8,128)(2,1)S(1)}, bf16[416,384]{1,0:T(8,128)(2,1)S(1)}, u32[]{:S(2)}, u32[]{:S(2)}) collective-permute-start(bf16[416,384]{1,0:T(8,128)(2,1)S(1)} %get-tuple-element.359), channel_id=1, source_target_pairs={{0,8},{4,12},{8,0},{12,4},{16,24},{20,28},{24,16},{28,20},{1,9},{5... | collective-permute-start | bytes 958472 | tf_op jit(solution)/shard_map/ppermute | solution.py:275
  112.6 15.1 %collective-permute-start.42 = (bf16[384,384]{1,0:T(8,128)(2,1)S(1)}, bf16[384,384]{1,0:T(8,128)(2,1)S(1)}, u32[]{:S(2)}, u32[]{:S(2)}) collective-permute-start(bf16[384,384]{1,0:T(8,128)(2,1)S(1)} %get-tuple-element.375), channel_id=1, source_target_pairs={{0,24},{4,28},{8,16},{12,20},{16,8},{20,12},{24,0},{28,4},{1,25},{... | collective-permute-start | bytes 884744 | tf_op jit(solution)/shard_map/ppermute | solution.py:275
  119.3 12.8 %collective-permute-start.41 = (bf16[224,384]{1,0:T(8,128)(2,1)S(1)}, bf16[224,384]{1,0:T(8,128)(2,1)S(1)}, u32[]{:S(2)}, u32[]{:S(2)}) collective-permute-start(bf16[224,384]{1,0:T(8,128)(2,1)S(1)} %get-tuple-element.372), channel_id=1, source_target_pairs={{0,24},{4,28},{8,16},{12,20},{16,8},{20,12},{24,0},{28,4},{1,25},{... | collective-permute-start | bytes 516104 | tf_op jit(solution)/shard_map/ppermute | solution.py:275
  121.5 10.6 %collective-permute-start.43 = (bf16[96,384]{1,0:T(8,128)(2,1)S(1)}, bf16[96,384]{1,0:T(8,128)(2,1)S(1)}, u32[]{:S(2)}, u32[]{:S(2)}) collective-permute-start(bf16[96,384]{1,0:T(8,128)(2,1)S(1)} %get-tuple-element.378), channel_id=1, source_target_pairs={{0,8},{4,12},{8,0},{12,4},{16,24},{20,28},{24,16},{28,20},{1,9},{5... | collective-permute-start | bytes 221192 | tf_op jit(solution)/shard_map/ppermute | solution.py:275
  123.1 8.9 %collective-permute-start.44 = (bf16[96,384]{1,0:T(8,128)(2,1)S(1)}, bf16[96,384]{1,0:T(8,128)(2,1)S(1)}, u32[]{:S(2)}, u32[]{:S(2)}) collective-permute-start(bf16[96,384]{1,0:T(8,128)(2,1)S(1)} %get-tuple-element.380), channel_id=1, source_target_pairs={{0,4},{4,0},{8,12},{12,8},{16,20},{20,16},{24,28},{28,24},{1,5},{5... | collective-permute-start | bytes 221192 | tf_op jit(solution)/shard_map/ppermute | solution.py:275
  (31 other events, 101.8 us)

commit v10 on v9

--- a/solution.py
+++ b/solution.py
@@ -1106,9 +1106,6 @@
         left_bits = list(range(bits))
         sums = [sums_ha, None, 0, left_bits.pop(0)]
         slot("sums_x", sums=sums, spare=(0, 96), hold=late)
-        out_kept, out_sent = call(
-            out_body, "out_d", [s5, *fore3[0], *wd], shipped, flops=mlp_flops // 2
-        )
         def hop():
             if not left_bits:
                 return None
@@ -1119,7 +1116,14 @@
         while left_bits or any(stream.step < bits for stream in every):
             turn += 1
             arrived = [s for s in every if s.step == bits and s.final is None]
-            slot(f"slot_b{turn}", moving=[s for s in streams_b if s.step < bits])
+            slot(
+                f"slot_b{turn}", moving=[s for s in streams_b if s.step < bits],
+                hold=late if turn == 1 else (),
+            )
+            if turn == 1:
+                out_kept, out_sent = call(
+                    out_body, "out_d", [s5, *fore3[0], *wd], shipped, flops=mlp_flops // 2
+                )
             second = [s for s in [*streams_d, *streams_a] if s.step < bits]
             depart = prepare_slot(f"slot_a{turn}", moving=second, ending=arrived, sums=hop())
             if turn > 1:

time: 134 us -> 134 us (level)
    unnamed x20 -> x22, local copies, waits for them, and re-layouts: 3.6 us -> 3.61 us
where the time goes in v10:
time: 134 us; the launch traced here: 133 us
  waiting for transfers between devices  41.7 us (31%)
  starting transfers between devices  38.2 us (29%)
  Pallas kernels  32.9 us (25%)
  blocking collectives  15.9 us (12%)
  local copies, waits for them, and re-layouts  3.61 us (3%)
    pallas_call x35, Pallas kernels, kernel_call(): pl.pallas_call(wrapped, in_specs=[pl.BlockSpec(memory_space=pltpu.VMEM)]...  32.9 us
    ppermute x16, waiting for transfers between devices, over_dev(): lax.ppermute(values, 'dev', [(i, i ^ partner[bit]) for i in range(n_dev)])  21.3 us
    ppermute x16, starting transfers between devices, over_dev(): lax.ppermute(values, 'dev', [(i, i ^ partner[bit]) for i in range(n_dev)])  19.4 us
    ppermute x13, waiting for transfers between devices, over_ha(): return lax.ppermute(values, 'ha', swap)  17.2 us
    ppermute x13, starting transfers between devices, over_ha(): return lax.ppermute(values, 'ha', swap)  15.2 us
    all_gather x3, blocking collectives, both_rear(): return (pieces, [lax.all_gather(piece, 'wa') for piece in pieces])  7.26 us
    all_gather x2, blocking collectives, on_device(): lax.all_gather(later(values, g2), 'wa')  4.69 us
    ppermute x16, starting transfers between devices, over_wa(): return lax.ppermute(values, 'wa', swap)  3.64 us
  transfers between devices with their start and end apart: 45, of which 21 were waited for; matrix products, arithmetic and copies ran while one was open for 0% of the time, Pallas kernels for 22%

profile of v10, /device:TPU:0, one launch (start us, length us, event | category | flops | bytes accessed | tf_op | source)
XLA Modules:
  0.0 133.4 jit_solution(7923139768570700211)
XLA Ops:
  1.2 2.9 %collective-permute-start = (bf16[147,384]{1,0:T(8,128)(2,1)}, bf16[147,384]{1,0:T(8,128)(2,1)S(1)}, u32[]{:S(2)}, u32[]{:S(2)}) collective-permute-start(bf16[147,384]{1,0:T(8,128)(2,1)} %refs_0_.2), channel_id=1, source_target_pairs={{0,2},{2,0},{1,3},{3,1},{4,6},{6,4},{5,7},{7,5},{8,10},{10,8},{9,1... | collective-permute-start | bytes 338696 | tf_op jit(solution)/shard_map/ppermute | solution.py:265
  13.2 2.1 %collective-permute-start.10 = (bf16[112,768]{1,0:T(8,128)(2,1)S(1)}, bf16[112,768]{1,0:T(8,128)(2,1)S(1)}, u32[]{:S(2)}, u32[]{:S(2)}) collective-permute-start(bf16[112,768]{1,0:T(8,128)(2,1)S(1)} %get-tuple-element.210.refs_13_.refs_1_), channel_id=1, source_target_pairs={{0,2},{2,0},{1,3},{3,1},{4,6},{6,4},{5,7},{7,5},{8,10},{10,8},{9,1... | collective-permute-start | bytes 516104 | tf_op jit(solution)/shard_map/ppermute | solution.py:265
  16.9 3.4 %collective-permute-done.10.refs_2_ = bf16[112,768]{1,0:T(8,128)(2,1)S(1)} collective-permute-done((bf16[112,768]{1,0:T(8,128)(2,1)S(1)}, bf16[112,768]{1,0:T(8,128)(2,1)S(1)}, u32[]{:S(2)}, u32[]{:S(2)}) %collective-permute-start.10) | collective-permute-done | bytes 172064 | tf_op jit(solution)/shard_map/ppermute | solution.py:265
  21.7 2.1 %collective-permute-start.15 = (bf16[112,768]{1,0:T(8,128)(2,1)S(1)}, bf16[112,768]{1,0:T(8,128)(2,1)S(1)}, u32[]{:S(2)}, u32[]{:S(2)}) collective-permute-start(bf16[112,768]{1,0:T(8,128)(2,1)S(1)} %get-tuple-element.232.refs_22_.refs_1_), channel_id=1, source_target_pairs={{0,2},{2,0},{1,3},{3,1},{4,6},{6,4},{5,7},{7,5},{8,10},{10,8},{9,1... | collective-permute-start | bytes 516104 | tf_op jit(solution)/shard_map/ppermute | solution.py:265
  28.9 2.5 %collective-permute-start.19 = (bf16[112,768]{1,0:T(8,128)(2,1)S(1)}, bf16[112,768]{1,0:T(8,128)(2,1)S(1)}, u32[]{:S(2)}, u32[]{:S(2)}) collective-permute-start(bf16[112,768]{1,0:T(8,128)(2,1)S(1)} %get-tuple-element.248.refs_29_.refs_1_), channel_id=1, source_target_pairs={{0,2},{2,0},{1,3},{3,1},{4,6},{6,4},{5,7},{7,5},{8,10},{10,8},{9,1... | collective-permute-start | bytes 516104 | tf_op jit(solution)/shard_map/ppermute | solution.py:265
  42.5 2.1 %wgrad_d.1 = (bf16[768,384]{1,0:T(8,128)(2,1)S(1)}, bf16[768,384]{1,0:T(8,128)(2,1)S(1)}, bf16[768,384]{1,0:T(8,128)(2,1)S(1)}, bf16[768,384]{1,0:T(8,128)(2,1)S(1)}, f32[8,128]{1,0:T(8,128)S(1)}) custom-call(bf16[168,384]{1,0:T(8,128)(2,1)S(1)} %get-tuple-element.282.refs_0_, bf16[168,384]{1,0:T(8,128)(2,1)S(1)} %get-tuple-element.270.refs_31_.refs_1_.refs_0_, ...), custom_call_target="tpu_custom_call" | custom-call | tf_op jit(solution)/shard_map/wgrad_d/pallas_call | solution.py:55
  48.6 2.1 %back_c.1 = (f32[168,768]{1,0:T(8,128)S(1)}, bf16[168,384]{1,0:T(8,128)(2,1)S(1)}, bf16[168,768]{1,0:T(8,128)(2,1)S(1)}, f32[2,768]{1,0:T(2,128)S(1)}, bf16[168,...) custom-call(bf16[168,384]{1,0:T(8,128)(2,1)S(1)} %get-tuple-element.270.refs_31_.refs_1_.refs_0_, ...), custom_call_target="tpu_custom_call" | custom-call | tf_op jit(solution)/shard_map/back_c/pallas_call | solution.py:55
  52.1 2.2 %all-gather = bf16[336,768]{1,0:T(8,128)(2,1)S(1)} all-gather(bf16[168,768]{1,0:T(8,128)(2,1)S(1)} %get-tuple-element.289.refs_11_.refs_12_.refs_7_.refs_10_.refs_16_.refs_8_.refs_14_.refs_2_), channel_id=2, replica_groups=mesh['dev'=8,'ha'=2,'wa'=2] {'wa'}, dimensions={0}, use_global_device_ids=true | all-gather | bytes 774144 | tf_op jit(solution)/shard_map/all_gather | solution.py:964
  54.3 2.5 %all-gather.1 = bf16[336,1536]{1,0:T(8,128)(2,1)S(1)} all-gather(bf16[168,1536]{1,0:T(8,128)(2,1)S(1)} %get-tuple-element.290.refs_19_.refs_14_.refs_18_.refs_17_.refs_23_.refs_16_.refs_22_.refs_3_), channel_id=3, replica_groups=mesh['dev'=8,'ha'=2,'wa'=2] {'wa'}, dimensions={0}, use_global_device_ids=true | all-gather | bytes 1548288 | tf_op jit(solution)/shard_map/all_gather | solution.py:964
  63.6 2.8 %back_b.1 = (f32[168,768]{1,0:T(8,128)S(1)}, bf16[168,384]{1,0:T(8,128)(2,1)S(1)}, bf16[168,768]{1,0:T(8,128)(2,1)S(1)}, f32[11,768]{1,0:T(8,128)S(1)}, bf16[168...) custom-call(f32[168,768]{1,0:T(8,128)S(1)} %get-tuple-element.287.refs_34_.refs_32_.refs_0_, ...), custom_call_target="tpu_custom_call" | custom-call | tf_op jit(solution)/shard_map/back_b/pallas_call | solution.py:55
  67.9 2.2 %all-gather.3 = bf16[336,896]{1,0:T(8,128)(2,1)S(1)} all-gather(bf16[168,896]{1,0:T(8,128)(2,1)S(1)} %get-tuple-element.305.refs_7_), channel_id=5, replica_groups=mesh['dev'=8,'ha'=2,'wa'=2] {'wa'}, dimensions={0}, use_global_device_ids=true | all-gather | bytes 903168 | tf_op jit(solution)/shard_map/all_gather | solution.py:379
  70.2 2.3 %all-gather.2 = bf16[336,1024]{1,0:T(8,128)(2,1)S(1)} all-gather(bf16[168,1024]{1,0:T(8,128)(2,1)S(1)} %get-tuple-element.304.refs_6_), channel_id=4, replica_groups=mesh['dev'=8,'ha'=2,'wa'=2] {'wa'}, dimensions={0}, use_global_device_ids=true | all-gather | bytes 1032192 | tf_op jit(solution)/shard_map/all_gather | solution.py:379
  72.4 1.9 %wgrad_b.1 = (bf16[768,384]{1,0:T(8,128)(2,1)S(1)}, bf16[768,384]{1,0:T(8,128)(2,1)S(1)}, bf16[768,384]{1,0:T(8,128)(2,1)S(1)}, bf16[768,384]{1,0:T(8,128)(2,1)S(1)}, f32[8,128]{1,0:T(8,128)S(1)}) custom-call(bf16[168,384]{1,0:T(8,128)(2,1)S(1)} %get-tuple-element.241.refs_17_.refs_12_.refs_16_.refs_15_.refs_21_.refs_14_.refs_20_.refs_0_, ...), custom_call_target="tpu_custom_call" | custom-call | tf_op jit(solution)/shard_map/wgrad_b/pallas_call | solution.py:55
  78.4 3.7 %collective-permute-start.35 = (bf16[784,384]{1,0:T(8,128)(2,1)S(1)}, bf16[784,384]{1,0:T(8,128)(2,1)S(1)}, u32[]{:S(2)}, u32[]{:S(2)}) collective-permute-start(bf16[784,384]{1,0:T(8,128)(2,1)S(1)} %get-tuple-element.346), channel_id=1, source_target_pairs={{0,24},{4,28},{8,16},{12,20},{16,8},{20,12},{24,0},{28,4},{1,25},{... | collective-permute-start | bytes 1806344 | tf_op jit(solution)/shard_map/ppermute | solution.py:275
  82.1 2.8 %all-gather.4 = bf16[336,1536]{1,0:T(8,128)(2,1)S(1)} all-gather(bf16[168,1536]{1,0:T(8,128)(2,1)S(1)} %get-tuple-element.327.refs_24_.refs_4_.refs_20_.refs_10_), channel_id=6, replica_groups=mesh['dev'=8,'ha'=2,'wa'=2] {'wa'}, dimensions={0}, use_global_device_ids=true | all-gather | bytes 1548288 | tf_op jit(solution)/shard_map/all_gather | solution.py:379
  86.6 2.0 %back_0.1 = (bf16[147,384]{1,0:T(8,128)(2,1)S(1)}, bf16[192,384]{1,0:T(8,128)(2,1)S(1)}, f32[32,384]{1,0:T(8,128)S(1)}, f32[8,128]{1,0:T(8,128)S(1)}) custom-call(f32[168,768]{1,0:T(8,128)S(1)} %get-tuple-element.315.refs_22_.refs_10_.refs_0_, f32[168,768]{1,0:T(8,128)S(1)} %get-tuple-element.219.refs_0_.refs_14_.refs_15_.refs_10_.refs_13_.refs_19_.refs_11_.refs_17_.refs_1_, ...), custom_call_target="tpu_custom_call" | custom-call | tf_op jit(solution)/shard_map/back_0/pallas_call | solution.py:55
  88.6 2.0 %all-gather.5 = bf16[384,384]{1,0:T(8,128)(2,1)S(1)} all-gather(bf16[192,384]{1,0:T(8,128)(2,1)S(1)} %get-tuple-element.331), channel_id=7, replica_groups=mesh['dev'=8,'ha'=2,'wa'=2] {'wa'}, dimensions={0}, use_global_device_ids=true | all-gather | bytes 442368 | tf_op jit(solution)/shard_map/all_gather | solution.py:1092
  91.3 5.4 %collective-permute-done.33.refs_1_ = bf16[192,384]{1,0:T(8,128)(2,1)S(1)} collective-permute-done((bf16[192,384]{1,0:T(8,128)(2,1)S(1)}, bf16[192,384]{1,0:T(8,128)(2,1)S(1)}, u32[]{:S(2)}, u32[]{:S(2)}) %collective-permute-start.33) | collective-permute-done | bytes 147488 | tf_op jit(solution)/shard_map/ppermute | solution.py:265
  100.8 4.5 %collective-permute-done.36.refs_6_ = bf16[128,384]{1,0:T(8,128)(2,1)S(1)} collective-permute-done((bf16[128,384]{1,0:T(8,128)(2,1)S(1)}, bf16[128,384]{1,0:T(8,128)(2,1)S(1)}, u32[]{:S(2)}, u32[]{:S(2)}) %collective-permute-start.36) | collective-permute-done | bytes 98336 | tf_op jit(solution)/shard_map/ppermute | solution.py:275
  107.3 2.0 %all-gather.7.refs_1_ = bf16[2,147,384]{2,1,0:T(8,128)(2,1)S(1)} all-gather(bf16[1,147,384]{2,1,0:T(8,128)(2,1)S(1)} %bitcast.50), channel_id=8, replica_groups=mesh['dev'=8,'ha'=2,'wa'=2] {'wa'}, dimensions={0}, use_global_device_ids=true | all-gather | bytes 338688 | tf_op jit(solution)/shard_map/all_gather | solution.py:1133
  110.3 2.1 %collective-permute-done.39.refs_1_ = bf16[384,384]{1,0:T(8,128)(2,1)S(1)} collective-permute-done((bf16[384,384]{1,0:T(8,128)(2,1)S(1)}, bf16[384,384]{1,0:T(8,128)(2,1)S(1)}, u32[]{:S(2)}, u32[]{:S(2)}) %collective-permute-start.39) | collective-permute-done | bytes 294944 | tf_op jit(solution)/shard_map/ppermute | solution.py:275
  113.5 5.6 %collective-permute-done.38.refs_1_ = bf16[416,384]{1,0:T(8,128)(2,1)S(1)} collective-permute-done((bf16[416,384]{1,0:T(8,128)(2,1)S(1)}, bf16[416,384]{1,0:T(8,128)(2,1)S(1)}, u32[]{:S(2)}, u32[]{:S(2)}) %collective-permute-start.38) | collective-permute-done | bytes 319520 | tf_op jit(solution)/shard_map/ppermute | solution.py:275
  123.7 2.0 %collective-permute-done.37.refs_1_ = bf16[147,384]{1,0:T(8,128)(2,1)S(1)} collective-permute-done((bf16[147,384]{1,0:T(8,128)(2,1)S(1)}, bf16[147,384]{1,0:T(8,128)(2,1)S(1)}, u32[]{:S(2)}, u32[]{:S(2)}) %collective-permute-start.37) | collective-permute-done | bytes 112928 | tf_op jit(solution)/shard_map/ppermute | solution.py:265
  127.7 4.4 %collective-permute-done.43.refs_9_ = bf16[96,384]{1,0:T(8,128)(2,1)S(1)} collective-permute-done((bf16[96,384]{1,0:T(8,128)(2,1)S(1)}, bf16[96,384]{1,0:T(8,128)(2,1)S(1)}, u32[]{:S(2)}, u32[]{:S(2)}) %collective-permute-start.43) | collective-permute-done | bytes 73760 | tf_op jit(solution)/shard_map/ppermute | solution.py:275
  (130 shorter events, 64.8 us)
Async XLA Ops:
  0.6 7.7 %collective-permute-start.1 = (bf16[2,3,384,384]{3,2,1,0:T(8,128)(2,1)}, bf16[2,3,384,384]{3,2,1,0:T(8,128)(2,1)S(1)}, u32[]{:S(2)}, u32[]{:S(2)}) collective-permute-start(bf16[2,3,384,384]{3,2,1,0:T(8,128)(2,1)} %bitcast.14), channel_id=1, source_target_pairs={{0,1},{1,0},{2,3},{3,2},{4,5},{5,4},{6,7},{7,6},{8,9},{9,8},{10,11... | collective-permute-start | bytes 5308424 | tf_op jit(solution)/shard_map/ppermute | solution.py:268
  1.2 7.2 %collective-permute-start.2 = (bf16[2,384,384]{2,1,0:T(8,128)(2,1)}, bf16[2,384,384]{2,1,0:T(8,128)(2,1)S(1)}, u32[]{:S(2)}, u32[]{:S(2)}) collective-permute-start(bf16[2,384,384]{2,1,0:T(8,128)(2,1)} %refs_8_.9), channel_id=1, source_target_pairs={{0,1},{1,0},{2,3},{3,2},{4,5},{5,4},{6,7},{7,6},{8,9},{9,8},{10,11... | collective-permute-start | bytes 1769480 | tf_op jit(solution)/shard_map/ppermute | solution.py:268
  10.8 9.6 %collective-permute-start.8 = (bf16[2,384,1536]{2,1,0:T(8,128)(2,1)S(1)}, bf16[2,384,1536]{2,1,0:T(8,128)(2,1)S(1)}, u32[]{:S(2)}, u32[]{:S(2)}) collective-permute-start(bf16[2,384,1536]{2,1,0:T(8,128)(2,1)S(1)} %copy-done.2), channel_id=1, source_target_pairs={{0,1},{1,0},{2,3},{3,2},{4,5},{5,4},{6,7},{7,6},{8,9},{9,8},{10,11... | collective-permute-start | bytes 7077896 | tf_op jit(solution)/shard_map/ppermute | solution.py:268
  10.8 9.6 %collective-permute-start.9 = (bf16[2,1536,384]{2,1,0:T(8,128)(2,1)S(1)}, bf16[2,1536,384]{2,1,0:T(8,128)(2,1)S(1)}, u32[]{:S(2)}, u32[]{:S(2)}) collective-permute-start(bf16[2,1536,384]{2,1,0:T(8,128)(2,1)S(1)} %copy-done), channel_id=1, source_target_pairs={{0,1},{1,0},{2,3},{3,2},{4,5},{5,4},{6,7},{7,6},{8,9},{9,8},{10,11... | collective-permute-start | bytes 7077896 | tf_op jit(solution)/shard_map/ppermute | solution.py:268
  13.2 7.2 %collective-permute-start.10 = (bf16[112,768]{1,0:T(8,128)(2,1)S(1)}, bf16[112,768]{1,0:T(8,128)(2,1)S(1)}, u32[]{:S(2)}, u32[]{:S(2)}) collective-permute-start(bf16[112,768]{1,0:T(8,128)(2,1)S(1)} %get-tuple-element.210.refs_13_.refs_1_), channel_id=1, source_target_pairs={{0,2},{2,0},{1,3},{3,1},{4,6},{6,4},{5,7},{7,5},{8,10},{10,8},{9,1... | collective-permute-start | bytes 516104 | tf_op jit(solution)/shard_map/ppermute | solution.py:265
  40.0 8.6 %collective-permute-start.20 = (bf16[168,768]{1,0:T(8,128)(2,1)S(1)}, bf16[168,768]{1,0:T(8,128)(2,1)S(1)}, u32[]{:S(2)}, u32[]{:S(2)}) collective-permute-start(bf16[168,768]{1,0:T(8,128)(2,1)S(1)} %get-tuple-element.281.refs_12_), channel_id=1, source_target_pairs={{0,2},{2,0},{1,3},{3,1},{4,6},{6,4},{5,7},{7,5},{8,10},{10,8},{9,1... | collective-permute-start | bytes 774152 | tf_op jit(solution)/shard_map/ppermute | solution.py:265
  44.6 15.4 %collective-permute-start.26 = (bf16[768,384]{1,0:T(8,128)(2,1)S(1)}, bf16[768,384]{1,0:T(8,128)(2,1)S(1)}, u32[]{:S(2)}, u32[]{:S(2)}) collective-permute-start(bf16[768,384]{1,0:T(8,128)(2,1)S(1)} %get-tuple-element.298), channel_id=1, source_target_pairs={{0,4},{4,0},{8,12},{12,8},{16,20},{20,16},{24,28},{28,24},{1,5},{5... | collective-permute-start | bytes 1769480 | tf_op jit(solution)/shard_map/ppermute | solution.py:275
  46.0 15.1 %collective-permute-start.27 = (bf16[768,384]{1,0:T(8,128)(2,1)S(1)}, bf16[768,384]{1,0:T(8,128)(2,1)S(1)}, u32[]{:S(2)}, u32[]{:S(2)}) collective-permute-start(bf16[768,384]{1,0:T(8,128)(2,1)S(1)} %get-tuple-element.300), channel_id=1, source_target_pairs={{0,8},{4,12},{8,0},{12,4},{16,24},{20,28},{24,16},{28,20},{1,9},{5... | collective-permute-start | bytes 1769480 | tf_op jit(solution)/shard_map/ppermute | solution.py:275
  50.8 8.6 %collective-permute-start.24 = (bf16[168,768]{1,0:T(8,128)(2,1)S(1)}, bf16[168,768]{1,0:T(8,128)(2,1)S(1)}, u32[]{:S(2)}, u32[]{:S(2)}) collective-permute-start(bf16[168,768]{1,0:T(8,128)(2,1)S(1)} %get-tuple-element.288.refs_38_.refs_1_), channel_id=1, source_target_pairs={{0,2},{2,0},{1,3},{3,1},{4,6},{6,4},{5,7},{7,5},{8,10},{10,8},{9,1... | collective-permute-start | bytes 774152 | tf_op jit(solution)/shard_map/ppermute | solution.py:265
  61.4 16.7 %collective-permute-start.31 = (bf16[768,384]{1,0:T(8,128)(2,1)S(1)}, bf16[768,384]{1,0:T(8,128)(2,1)S(1)}, u32[]{:S(2)}, u32[]{:S(2)}) collective-permute-start(bf16[768,384]{1,0:T(8,128)(2,1)S(1)} %get-tuple-element.319), channel_id=1, source_target_pairs={{0,8},{4,12},{8,0},{12,4},{16,24},{20,28},{24,16},{28,20},{1,9},{5... | collective-permute-start | bytes 1769480 | tf_op jit(solution)/shard_map/ppermute | solution.py:275
  63.1 15.1 %collective-permute-start.32 = (bf16[768,384]{1,0:T(8,128)(2,1)S(1)}, bf16[768,384]{1,0:T(8,128)(2,1)S(1)}, u32[]{:S(2)}, u32[]{:S(2)}) collective-permute-start(bf16[768,384]{1,0:T(8,128)(2,1)S(1)} %get-tuple-element.321), channel_id=1, source_target_pairs={{0,4},{4,0},{8,12},{12,8},{16,20},{20,16},{24,28},{28,24},{1,5},{5... | collective-permute-start | bytes 1769480 | tf_op jit(solution)/shard_map/ppermute | solution.py:275
  66.4 9.9 %collective-permute-start.30 = (bf16[168,768]{1,0:T(8,128)(2,1)S(1)}, bf16[168,768]{1,0:T(8,128)(2,1)S(1)}, u32[]{:S(2)}, u32[]{:S(2)}) collective-permute-start(bf16[168,768]{1,0:T(8,128)(2,1)S(1)} %get-tuple-element.313.refs_1_), channel_id=1, source_target_pairs={{0,2},{2,0},{1,3},{3,1},{4,6},{6,4},{5,7},{7,5},{8,10},{10,8},{9,1... | collective-permute-start | bytes 774152 | tf_op jit(solution)/shard_map/ppermute | solution.py:265
  74.3 24.6 %collective-permute-start.28 = (bf16[768,384]{1,0:T(8,128)(2,1)S(1)}, bf16[768,384]{1,0:T(8,128)(2,1)S(1)}, u32[]{:S(2)}, u32[]{:S(2)}) collective-permute-start(bf16[768,384]{1,0:T(8,128)(2,1)S(1)} %get-tuple-element.310), channel_id=1, source_target_pairs={{0,4},{4,0},{8,12},{12,8},{16,20},{20,16},{24,28},{28,24},{1,5},{5... | collective-permute-start | bytes 1769480 | tf_op jit(solution)/shard_map/ppermute | solution.py:275
  75.9 23.1 %collective-permute-start.29 = (bf16[768,384]{1,0:T(8,128)(2,1)S(1)}, bf16[768,384]{1,0:T(8,128)(2,1)S(1)}, u32[]{:S(2)}, u32[]{:S(2)}) collective-permute-start(bf16[768,384]{1,0:T(8,128)(2,1)S(1)} %get-tuple-element.312), channel_id=1, source_target_pairs={{0,8},{4,12},{8,0},{12,4},{16,24},{20,28},{24,16},{28,20},{1,9},{5... | collective-permute-start | bytes 1769480 | tf_op jit(solution)/shard_map/ppermute | solution.py:275
  78.4 28.7 %collective-permute-start.35 = (bf16[784,384]{1,0:T(8,128)(2,1)S(1)}, bf16[784,384]{1,0:T(8,128)(2,1)S(1)}, u32[]{:S(2)}, u32[]{:S(2)}) collective-permute-start(bf16[784,384]{1,0:T(8,128)(2,1)S(1)} %get-tuple-element.346), channel_id=1, source_target_pairs={{0,24},{4,28},{8,16},{12,20},{16,8},{20,12},{24,0},{28,4},{1,25},{... | collective-permute-start | bytes 1806344 | tf_op jit(solution)/shard_map/ppermute | solution.py:275
  86.0 19.3 %collective-permute-start.34 = (bf16[768,384]{1,0:T(8,128)(2,1)S(1)}, bf16[768,384]{1,0:T(8,128)(2,1)S(1)}, u32[]{:S(2)}, u32[]{:S(2)}) collective-permute-start(bf16[768,384]{1,0:T(8,128)(2,1)S(1)} %get-tuple-element.345), channel_id=1, source_target_pairs={{0,4},{4,0},{8,12},{12,8},{16,20},{20,16},{24,28},{28,24},{1,5},{5... | collective-permute-start | bytes 1769480 | tf_op jit(solution)/shard_map/ppermute | solution.py:275
  97.4 7.9 %collective-permute-start.36 = (bf16[128,384]{1,0:T(8,128)(2,1)S(1)}, bf16[128,384]{1,0:T(8,128)(2,1)S(1)}, u32[]{:S(2)}, u32[]{:S(2)}) collective-permute-start(bf16[128,384]{1,0:T(8,128)(2,1)S(1)} %get-tuple-element.349), channel_id=1, source_target_pairs={{0,4},{4,0},{8,12},{12,8},{16,20},{20,16},{24,28},{28,24},{1,5},{5... | collective-permute-start | bytes 294920 | tf_op jit(solution)/shard_map/ppermute | solution.py:275
  99.2 13.2 %collective-permute-start.39 = (bf16[384,384]{1,0:T(8,128)(2,1)S(1)}, bf16[384,384]{1,0:T(8,128)(2,1)S(1)}, u32[]{:S(2)}, u32[]{:S(2)}) collective-permute-start(bf16[384,384]{1,0:T(8,128)(2,1)S(1)} %get-tuple-element.362), channel_id=1, source_target_pairs={{0,8},{4,12},{8,0},{12,4},{16,24},{20,28},{24,16},{28,20},{1,9},{5... | collective-permute-start | bytes 884744 | tf_op jit(solution)/shard_map/ppermute | solution.py:275
  99.3 13.1 %collective-permute-start.40 = (bf16[384,384]{1,0:T(8,128)(2,1)S(1)}, bf16[384,384]{1,0:T(8,128)(2,1)S(1)}, u32[]{:S(2)}, u32[]{:S(2)}) collective-permute-start(bf16[384,384]{1,0:T(8,128)(2,1)S(1)} %get-tuple-element.364), channel_id=1, source_target_pairs={{0,4},{4,0},{8,12},{12,8},{16,20},{20,16},{24,28},{28,24},{1,5},{5... | collective-permute-start | bytes 884744 | tf_op jit(solution)/shard_map/ppermute | solution.py:275
  109.4 9.8 %collective-permute-start.38 = (bf16[416,384]{1,0:T(8,128)(2,1)S(1)}, bf16[416,384]{1,0:T(8,128)(2,1)S(1)}, u32[]{:S(2)}, u32[]{:S(2)}) collective-permute-start(bf16[416,384]{1,0:T(8,128)(2,1)S(1)} %get-tuple-element.359), channel_id=1, source_target_pairs={{0,8},{4,12},{8,0},{12,4},{16,24},{20,28},{24,16},{28,20},{1,9},{5... | collective-permute-start | bytes 958472 | tf_op jit(solution)/shard_map/ppermute | solution.py:275
  112.6 15.1 %collective-permute-start.42 = (bf16[384,384]{1,0:T(8,128)(2,1)S(1)}, bf16[384,384]{1,0:T(8,128)(2,1)S(1)}, u32[]{:S(2)}, u32[]{:S(2)}) collective-permute-start(bf16[384,384]{1,0:T(8,128)(2,1)S(1)} %get-tuple-element.375), channel_id=1, source_target_pairs={{0,24},{4,28},{8,16},{12,20},{16,8},{20,12},{24,0},{28,4},{1,25},{... | collective-permute-start | bytes 884744 | tf_op jit(solution)/shard_map/ppermute | solution.py:275
  119.3 12.8 %collective-permute-start.41 = (bf16[224,384]{1,0:T(8,128)(2,1)S(1)}, bf16[224,384]{1,0:T(8,128)(2,1)S(1)}, u32[]{:S(2)}, u32[]{:S(2)}) collective-permute-start(bf16[224,384]{1,0:T(8,128)(2,1)S(1)} %get-tuple-element.372), channel_id=1, source_target_pairs={{0,24},{4,28},{8,16},{12,20},{16,8},{20,12},{24,0},{28,4},{1,25},{... | collective-permute-start | bytes 516104 | tf_op jit(solution)/shard_map/ppermute | solution.py:275
  121.5 10.5 %collective-permute-start.43 = (bf16[96,384]{1,0:T(8,128)(2,1)S(1)}, bf16[96,384]{1,0:T(8,128)(2,1)S(1)}, u32[]{:S(2)}, u32[]{:S(2)}) collective-permute-start(bf16[96,384]{1,0:T(8,128)(2,1)S(1)} %get-tuple-element.378), channel_id=1, source_target_pairs={{0,8},{4,12},{8,0},{12,4},{16,24},{20,28},{24,16},{28,20},{1,9},{5... | collective-permute-start | bytes 221192 | tf_op jit(solution)/shard_map/ppermute | solution.py:275
  123.2 8.9 %collective-permute-start.44 = (bf16[96,384]{1,0:T(8,128)(2,1)S(1)}, bf16[96,384]{1,0:T(8,128)(2,1)S(1)}, u32[]{:S(2)}, u32[]{:S(2)}) collective-permute-start(bf16[96,384]{1,0:T(8,128)(2,1)S(1)} %get-tuple-element.380), channel_id=1, source_target_pairs={{0,4},{4,0},{8,12},{12,8},{16,20},{20,16},{24,28},{28,24},{1,5},{5... | collective-permute-start | bytes 221192 | tf_op jit(solution)/shard_map/ppermute | solution.py:275
  (32 other events, 102.9 us)
